TPU v7x, 32 devices: a whole 2x2x4 slice. The times are simulated.
32 devices in a mesh: slab: 4 (over y, x), energy: 4 (over z), mom: 2 (over core).
Axes of the slice: x: 2, y: 2, z: 4, core: 2. Of those that a mesh axis runs over, the one named last changes fastest.
Arguments:
- onsite: float32 [2, 4, 256], P('mom', 'slab'), may hold values from -0.5 to 0.5
- hop: float32 [2, 4, 2, 256, 256], P('mom', 'slab'), may hold values from -0.0234375 to 0.0234375
- couple: float32 [2, 4, 2, 256, 256], P('mom', 'slab'), may hold values from -2 to 2
- sigma_in: float32 [8, 4, 2, 256, 256], P('energy', 'slab'), may hold values from -0.03125 to 0.03125
- shifts: int32 [4], replicated, may hold values from 1 to 7
- mode_weight: float32 [2, 4], replicated, may hold values from 0.2 to 1
Outputs:
- sigma_out: float32 [8, 4, 2, 256, 256], P(None, 'slab', None, 'energy')
Inputs may be any that keep to these rules, and one draw needn't show every extreme that they name: `shifts`: energy-index offsets of the phonon modes.
All inputs are finite; a program needn't handle non-finite values.
Results may differ from a plain program's by a relative error of at most 0.00025.
Values sent between devices are 32-bit elements; how exact they have to be, the bound alone decides.
No kernel may reach another device: no remote copies, remote signals or barrier semaphores. Data moves between devices by JAX's collectives and lax.ppermute only.
A program may use at most 128 MiB of HBM per device.

v0:
```python
import jax
import jax.numpy as jnp
from jax import lax
from jax.sharding import PartitionSpec as P

ETA = 0.5
HIGH = lax.Precision.HIGHEST


def shifted(shard, axis, by):
    length = lax.axis_size(axis)
    pairs = [(i, i + by) for i in range(length) if 0 <= i + by < length]
    return lax.ppermute(shard, axis, pairs)


def complex_mul(form, left, right):

    def product(first, second):
        return jnp.einsum(form, first, second, precision=HIGH)

    return (
        product(left[0], right[0]) - product(left[1], right[1]),
        product(left[0], right[1]) + product(left[1], right[0]),
    )


def newton_inverse(mat_real, mat_imag, form, identity):
    diag_real = jnp.diagonal(mat_real, axis1=-2, axis2=-1)
    diag_imag = jnp.diagonal(mat_imag, axis1=-2, axis2=-1)
    denom = diag_real * diag_real + diag_imag * diag_imag
    x_real = diag_real / denom
    x_imag = -diag_imag / denom
    rows_real = x_real[..., :, None] * mat_real - x_imag[..., :, None] * mat_imag
    rows_imag = x_real[..., :, None] * mat_imag + x_imag[..., :, None] * mat_real
    both_real = rows_real * x_real[..., None, :] - rows_imag * x_imag[..., None, :]
    both_imag = rows_real * x_imag[..., None, :] + rows_imag * x_real[..., None, :]
    first = (
        2.0 * identity * x_real[..., None, :] - both_real,
        2.0 * identity * x_imag[..., None, :] - both_imag,
    )
    resid = complex_mul(form, (mat_real, mat_imag), first)
    second = complex_mul(form, first, resid)
    return (2.0 * first[0] - second[0], 2.0 * first[1] - second[1])


def phonon_matrix(shifts, mode_weight, count):
    rows = jnp.arange(count)[:, None, None]
    cols = jnp.arange(count)[None, :, None]
    offset = shifts[None, None, :]
    upper = (cols == rows + offset).astype(jnp.float32)
    lower = (cols == rows - offset).astype(jnp.float32)
    return jnp.sum(upper * mode_weight[0] + lower * mode_weight[1], axis=2)


def body(onsite, hop, couple, sigma_in, shifts, mode_weight):
    e_local = sigma_in.shape[0]
    width = onsite.shape[-1]
    slab_count = lax.axis_size("slab")
    slab_index = lax.axis_index("slab")
    energy_count = lax.axis_size("energy")
    mom_count = lax.axis_size("mom")
    total = e_local * energy_count
    identity = jnp.eye(width, dtype=jnp.float32)
    global_index = lax.axis_index("energy") * e_local + jnp.arange(e_local)
    energy = -0.5 + (global_index.astype(jnp.float32) + 0.5) / total
    coupling = (couple[0, 0, 0], couple[0, 0, 1])
    adjoint = (coupling[0].T, -coupling[1].T)
    hopping = (hop[0, 0, 0], hop[0, 0, 1])
    level = onsite[0, 0]
    sigma = sigma_in[:, 0]

    def forward(received, energies, sig):
        temp = complex_mul("ij,ejl->eil", coupling, (received[:, 0], received[:, 1]))
        left = complex_mul("eij,jl->eil", temp, adjoint)
        z_real = energies[:, None] - level[None, :]
        mat_real = identity * z_real[:, None, :] - hopping[0] - sig[:, 0] - left[0]
        mat_imag = identity * ETA - hopping[1] - sig[:, 1] - left[1]
        green = newton_inverse(mat_real, mat_imag, "eij,ejl->eil", identity)
        return jnp.stack(green, axis=1)

    def backward(green, received):
        pair = (green[:, 0], green[:, 1])
        temp = complex_mul("eij,ejl->eil", pair, (received[:, 0], received[:, 1]))
        extra = complex_mul("eij,ejl->eil", temp, pair)
        full = (pair[0] + extra[0], pair[1] + extra[1])
        temp = complex_mul("ij,ejl->eil", adjoint, full)
        coupled = complex_mul("eij,jl->eil", temp, coupling)
        return (jnp.stack(full, axis=1), jnp.stack(coupled, axis=1))

    empty = jnp.zeros((e_local, 2, width, width), jnp.float32)

    def forward_step(step, green_all):
        received = shifted(green_all, "slab", 1)
        return lax.cond(
            slab_index == step, lambda: forward(received, energy, sigma), lambda: green_all
        )

    green_all = lax.fori_loop(0, slab_count, forward_step, empty)

    def backward_step(step, carry):
        received = shifted(carry[1], "slab", -1)
        return lax.cond(
            slab_index == slab_count - 1 - step,
            lambda: backward(green_all, received),
            lambda: carry,
        )

    full_all, coupled_all = lax.fori_loop(0, slab_count, backward_step, (empty, empty))
    phonon = phonon_matrix(shifts, mode_weight, total)
    blocks = full_all[:, None]
    mixed = jnp.einsum(
        "ef,fsrjl->esrjl",
        phonon,
        lax.all_to_all(blocks, "energy", split_axis=3, concat_axis=0, tiled=True),
        precision=HIGH,
    )
    result = lax.psum(mixed, "mom") / mom_count
    return result


def solution(mesh):
    in_specs = (
        P("mom", "slab", None),
        P("mom", "slab", None, None, None),
        P("mom", "slab", None, None, None),
        P("energy", "slab", None, None, None),
        P(),
        P(),
    )
    out_specs = P(None, "slab", None, "energy", None)
    return jax.shard_map(body, mesh=mesh, in_specs=in_specs, out_specs=out_specs, check_vma=False)
```

profile of v0, /device:TPU:0, one launch (start us, length us, event | category | flops | bytes accessed | tf_op | source)
XLA Modules:
  0.0 540.1 jit_solution(15320253141992246850)
XLA Ops:
  6.5 1.8 slice_bitcast_fusion
  9.7 2.3 copy.152
  12.0 212.6 %while.34 = (s32[]{:T(128)}, f32[2,2,256,256]{3,2,0,1:T(8,128)S(1)}, s32[]{:T(128)}, f32[1,1,256]{2,1,0:T(1,128)}, f32[1,1,1,256,256]{4,3,2,1,0:T(8,128)}, /*ind...) while((s32[]{:T(128)}, ...), condition=%wide.region_4.5_spmd.clone.clone, body=%wide.region_1.4_spmd.clone.clone.sunk | while | flops 6447567360 | bytes 44865880 | solution.py:98
  12.0 1.3 copy.154
  13.4 4.9 collective-permute-start.1
  18.3 22.6 %collective-permute-done.1 = f32[2,2,256,256]{2,3,0,1:T(8,128)S(1)} collective-permute-done((f32[2,2,256,256]{2,3,0,1:T(8,128)}, f32[2,2,256,256]{2,3,0,1:T(8,128)S(1)}, u32[]{:S(2)}, u32[]{:S(2)}) %collective-permute-start.1) | collective-permute-done | bytes 1048608 | tf_op jit(solution)/shard_map/while/body/eval_jaxpr/ppermute | solution.py:13
  40.9 53.2 %conditional.7 = (f32[2,2,256,256]{3,2,0,1:T(8,128)S(1)}) conditional(s32[]{:T(128)} %convert_element_type.49, f32[2,2,256,256]{3,2,0,1:T(8,128)S(1)} %get-tuple-element.764, (f32[256,256]{1,0:T(8,128)S(1)}, f32[256,256]{1,0:T(8,128)S(1)}, f32[256,256]{1,0:T(8,128)S(1)}, f32[2]{0:T(128)S(1)}, f32[1,1,256]{2,1,0:T(1,128)}, ...), branch_computations={%region_2.2_spmd, %region_3.3_spmd.clone} | conditional | flops 6447436288 | bytes 38311968 | solution.py:94
  46.2 2.1 fusion.55
  48.4 2.0 fusion.54
  50.5 16.5 %copy.145 = f32[2,256,256]{0,2,1:T(8,128)} copy(f32[2,256,256]{2,1,0:T(8,128)S(1)} %fusion.54) | data formatting | bytes 1048576 | tf_op jit(solution)/shard_map/while/body/eval_jaxpr/cond/branch_1_fun/sub | solution.py:77
  67.0 2.3 gather_fusion.1
  69.4 16.5 %copy.143 = f32[2,256,256]{0,2,1:T(8,128)} copy(f32[2,256,256]{2,1,0:T(8,128)S(1)} %fusion.55) | data formatting | bytes 1048576 | tf_op jit(solution)/shard_map/while/body/eval_jaxpr/cond/branch_1_fun/sub | solution.py:76
  85.9 2.3 gather_fusion
  95.4 1.3 collective-permute-start.1
  96.8 22.0 %collective-permute-done.1 = f32[2,2,256,256]{2,3,0,1:T(8,128)S(1)} collective-permute-done((f32[2,2,256,256]{2,3,0,1:T(8,128)}, f32[2,2,256,256]{2,3,0,1:T(8,128)S(1)}, u32[]{:S(2)}, u32[]{:S(2)}) %collective-permute-start.1) | collective-permute-done | bytes 1048608 | tf_op jit(solution)/shard_map/while/body/eval_jaxpr/ppermute | solution.py:13
  120.1 57.5 %collective-permute-start.1 = (f32[2,2,256,256]{2,3,0,1:T(8,128)}, f32[2,2,256,256]{2,3,0,1:T(8,128)S(1)}, u32[]{:S(2)}, u32[]{:S(2)}) collective-permute-start(f32[2,2,256,256]{2,3,0,1:T(8,128)} %copy.154), channel_id=1, source_target_pairs={{0,8},{8,16},{16,24},{1,9},{9,17},{17,25},{2,10},{10,18},{18,26},{... | collective-permute-start | bytes 3145736 | tf_op jit(solution)/shard_map/while/body/eval_jaxpr/ppermute | solution.py:13
  177.7 21.1 %collective-permute-done.1 = f32[2,2,256,256]{2,3,0,1:T(8,128)S(1)} collective-permute-done((f32[2,2,256,256]{2,3,0,1:T(8,128)}, f32[2,2,256,256]{2,3,0,1:T(8,128)S(1)}, u32[]{:S(2)}, u32[]{:S(2)}) %collective-permute-start.1) | collective-permute-done | bytes 1048608 | tf_op jit(solution)/shard_map/while/body/eval_jaxpr/ppermute | solution.py:13
  200.1 4.3 collective-permute-start.1
  204.5 20.1 %collective-permute-done.1 = f32[2,2,256,256]{2,3,0,1:T(8,128)S(1)} collective-permute-done((f32[2,2,256,256]{2,3,0,1:T(8,128)}, f32[2,2,256,256]{2,3,0,1:T(8,128)S(1)}, u32[]{:S(2)}, u32[]{:S(2)}) %collective-permute-start.1) | collective-permute-done | bytes 1048608 | tf_op jit(solution)/shard_map/while/body/eval_jaxpr/ppermute | solution.py:13
  226.8 255.3 %while.33 = (s32[]{:T(128)}, f32[2,2,256,256]{3,2,0,1:T(8,128)}, f32[2,2,256,256]{3,2,0,1:T(8,128)}, s32[]{:T(128)}, f32[2,2,256,256]{3,2,0,1:T(8,128)S(1)}, /*i...) while((s32[]{:T(128)}, f32[2,2,256,256]{3,2,0,1:T(8,128)}, ...), condition=%wide.region_8.9_spmd, body=%wide.region_5.8_spmd.sunk | while | flops 6444285952 | bytes 36700408 | solution.py:108
  226.8 1.4 collective-permute-start
  228.2 75.5 %collective-permute-done = f32[2,2,256,256]{3,2,0,1:T(8,128)S(1)} collective-permute-done((f32[2,2,256,256]{3,2,0,1:T(8,128)}, f32[2,2,256,256]{3,2,0,1:T(8,128)S(1)}, u32[]{:S(2)}, u32[]{:S(2)}) %collective-permute-start) | collective-permute-done | bytes 1048608 | tf_op jit(solution)/shard_map/while/body/eval_jaxpr/ppermute | solution.py:13
  305.0 23.5 %collective-permute-done = f32[2,2,256,256]{3,2,0,1:T(8,128)S(1)} collective-permute-done((f32[2,2,256,256]{3,2,0,1:T(8,128)}, f32[2,2,256,256]{3,2,0,1:T(8,128)S(1)}, u32[]{:S(2)}, u32[]{:S(2)}) %collective-permute-start) | collective-permute-done | bytes 1048608 | tf_op jit(solution)/shard_map/while/body/eval_jaxpr/ppermute | solution.py:13
  329.8 72.5 %collective-permute-done = f32[2,2,256,256]{3,2,0,1:T(8,128)S(1)} collective-permute-done((f32[2,2,256,256]{3,2,0,1:T(8,128)}, f32[2,2,256,256]{3,2,0,1:T(8,128)S(1)}, u32[]{:S(2)}, u32[]{:S(2)}) %collective-permute-start) | collective-permute-done | bytes 1048608 | tf_op jit(solution)/shard_map/while/body/eval_jaxpr/ppermute | solution.py:13
  403.6 63.4 %collective-permute-done = f32[2,2,256,256]{3,2,0,1:T(8,128)S(1)} collective-permute-done((f32[2,2,256,256]{3,2,0,1:T(8,128)}, f32[2,2,256,256]{3,2,0,1:T(8,128)S(1)}, u32[]{:S(2)}, u32[]{:S(2)}) %collective-permute-start) | collective-permute-done | bytes 1048608 | tf_op jit(solution)/shard_map/while/body/eval_jaxpr/ppermute | solution.py:13
  467.0 15.1 %conditional.6 = ((f32[2,2,256,256]{3,2,0,1:T(8,128)}, f32[2,2,256,256]{3,2,0,1:T(8,128)})) conditional(s32[]{:T(128)} %convert_element_type.46, (f32[2,2,256,256]{3,2,0,1:T(8,128)}, f32[2,2,256,256]{3,2,0,1:T(8,128)}) %tuple.94, (f32[2,2,256,256]{3,2,0,1:T(8,128)S(1)}, f32[2,2,256,256]{3,2,0,1:T(8,128)S(1)}, f32[256,256]{1,0:T(8,128)S(1)}, ...), branch_computations={%region_6.6_spmd, %region_7.7_spmd} | conditional | flops 6444285952 | bytes 32505864 | solution.py:102
  480.5 1.5 pad_maximum_fusion
  482.0 3.0 copy.151
  485.0 5.2 all-to-all-start
  490.4 20.2 %all-to-all-done = f32[2,1,2,256,256]{4,0,2,1,3:T(2,128)S(1)} async-done(((f32[2,1,2,256,256]{4,0,2,1,3:T(2,128)}), f32[2,1,2,256,256]{4,0,2,1,3:T(2,128)S(1)}, u32[]{:S(2)}, u32[]{:S(2)}) %all-to-all-start) | async-done | bytes 1048608 | tf_op jit(solution)/shard_map/all_to_all | solution.py:114
  511.7 1.9 convolution_bitcast_fusion
  513.6 17.0 %all-reduce.2.cloned.1.call-done = f32[8,1,2,64,256]{4,0,3,2,1:T(8,128)} async-done(((f32[8,1,2,64,256]{4,0,3,2,1:T(8,128)}), f32[8,1,2,64,256]{4,0,3,2,1:T(8,128)}) %all-reduce.2.cloned.1.call-update) | async-done | bytes 1048592 | tf_op jit(solution)/shard_map/psum | solution.py:117
  (80 shorter events, 40.0 us)
Async XLA Ops:
  13.4 27.6 %collective-permute-start.1 = (f32[2,2,256,256]{2,3,0,1:T(8,128)}, f32[2,2,256,256]{2,3,0,1:T(8,128)S(1)}, u32[]{:S(2)}, u32[]{:S(2)}) collective-permute-start(f32[2,2,256,256]{2,3,0,1:T(8,128)} %copy.154), channel_id=1, source_target_pairs={{0,8},{8,16},{16,24},{1,9},{9,17},{17,25},{2,10},{10,18},{18,26},{... | collective-permute-start | bytes 3145736 | tf_op jit(solution)/shard_map/while/body/eval_jaxpr/ppermute | solution.py:13
  95.4 23.4 %collective-permute-start.1 = (f32[2,2,256,256]{2,3,0,1:T(8,128)}, f32[2,2,256,256]{2,3,0,1:T(8,128)S(1)}, u32[]{:S(2)}, u32[]{:S(2)}) collective-permute-start(f32[2,2,256,256]{2,3,0,1:T(8,128)} %copy.154), channel_id=1, source_target_pairs={{0,8},{8,16},{16,24},{1,9},{9,17},{17,25},{2,10},{10,18},{18,26},{... | collective-permute-start | bytes 3145736 | tf_op jit(solution)/shard_map/while/body/eval_jaxpr/ppermute | solution.py:13
  120.1 78.6 %collective-permute-start.1 = (f32[2,2,256,256]{2,3,0,1:T(8,128)}, f32[2,2,256,256]{2,3,0,1:T(8,128)S(1)}, u32[]{:S(2)}, u32[]{:S(2)}) collective-permute-start(f32[2,2,256,256]{2,3,0,1:T(8,128)} %copy.154), channel_id=1, source_target_pairs={{0,8},{8,16},{16,24},{1,9},{9,17},{17,25},{2,10},{10,18},{18,26},{... | collective-permute-start | bytes 3145736 | tf_op jit(solution)/shard_map/while/body/eval_jaxpr/ppermute | solution.py:13
  200.1 24.5 %collective-permute-start.1 = (f32[2,2,256,256]{2,3,0,1:T(8,128)}, f32[2,2,256,256]{2,3,0,1:T(8,128)S(1)}, u32[]{:S(2)}, u32[]{:S(2)}) collective-permute-start(f32[2,2,256,256]{2,3,0,1:T(8,128)} %copy.154), channel_id=1, source_target_pairs={{0,8},{8,16},{16,24},{1,9},{9,17},{17,25},{2,10},{10,18},{18,26},{... | collective-permute-start | bytes 3145736 | tf_op jit(solution)/shard_map/while/body/eval_jaxpr/ppermute | solution.py:13
  226.8 263.4 %copy-start = (f32[2,4]{1,0:T(2,128)S(1)}, f32[2,4]{1,0:T(2,128)}, u32[]{:S(2)}) copy-start(f32[2,4]{1,0:T(2,128)} %param.19) | copy-start | bytes 100
  226.8 263.4 %copy-start.1 = (s32[4]{0:T(128)S(1)}, s32[4]{0:T(128)}, u32[]{:S(2)}) copy-start(s32[4]{0:T(128)} %param.18) | copy-start | bytes 52
  226.8 76.9 %collective-permute-start = (f32[2,2,256,256]{3,2,0,1:T(8,128)}, f32[2,2,256,256]{3,2,0,1:T(8,128)S(1)}, u32[]{:S(2)}, u32[]{:S(2)}) collective-permute-start(f32[2,2,256,256]{3,2,0,1:T(8,128)} %get-tuple-element.802), channel_id=1, source_target_pairs={{8,0},{16,8},{24,16},{9,1},{17,9},{25,17},{10,2},{18,10},{26,18},{... | collective-permute-start | bytes 3145736 | tf_op jit(solution)/shard_map/while/body/eval_jaxpr/ppermute | solution.py:13
  303.7 24.8 %collective-permute-start = (f32[2,2,256,256]{3,2,0,1:T(8,128)}, f32[2,2,256,256]{3,2,0,1:T(8,128)S(1)}, u32[]{:S(2)}, u32[]{:S(2)}) collective-permute-start(f32[2,2,256,256]{3,2,0,1:T(8,128)} %get-tuple-element.802), channel_id=1, source_target_pairs={{8,0},{16,8},{24,16},{9,1},{17,9},{25,17},{10,2},{18,10},{26,18},{... | collective-permute-start | bytes 3145736 | tf_op jit(solution)/shard_map/while/body/eval_jaxpr/ppermute | solution.py:13
  328.5 73.8 %collective-permute-start = (f32[2,2,256,256]{3,2,0,1:T(8,128)}, f32[2,2,256,256]{3,2,0,1:T(8,128)S(1)}, u32[]{:S(2)}, u32[]{:S(2)}) collective-permute-start(f32[2,2,256,256]{3,2,0,1:T(8,128)} %get-tuple-element.802), channel_id=1, source_target_pairs={{8,0},{16,8},{24,16},{9,1},{17,9},{25,17},{10,2},{18,10},{26,18},{... | collective-permute-start | bytes 3145736 | tf_op jit(solution)/shard_map/while/body/eval_jaxpr/ppermute | solution.py:13
  402.3 64.7 %collective-permute-start = (f32[2,2,256,256]{3,2,0,1:T(8,128)}, f32[2,2,256,256]{3,2,0,1:T(8,128)S(1)}, u32[]{:S(2)}, u32[]{:S(2)}) collective-permute-start(f32[2,2,256,256]{3,2,0,1:T(8,128)} %get-tuple-element.802), channel_id=1, source_target_pairs={{8,0},{16,8},{24,16},{9,1},{17,9},{25,17},{10,2},{18,10},{26,18},{... | collective-permute-start | bytes 3145736 | tf_op jit(solution)/shard_map/while/body/eval_jaxpr/ppermute | solution.py:13
  485.0 25.5 %all-to-all-start = ((f32[2,1,2,256,256]{4,0,2,1,3:T(2,128)}), f32[2,1,2,256,256]{4,0,2,1,3:T(2,128)S(1)}, u32[]{:S(2)}, u32[]{:S(2)}) async-start(f32[2,1,2,256,256]{4,0,2,1,3:T(2,128)} %bitcast.207), calls=%async_computation | async-start | bytes 2097152 | tf_op jit(solution)/shard_map/all_to_all | solution.py:114
  490.2 40.4 %all-reduce.2.cloned.1.call-start = ((), (), s32[]{:S(2)}) async-start(), calls=%async_computation.1 | async-start | bytes 2097152 | tf_op jit(solution)/shard_map/psum | solution.py:117
Sparse Core Ops, SparseCore 0:
  513.8 16.8 all-reduce.1
where the time goes:
time: 541 us; the launch traced here: 540 us
  waiting for transfers between devices  358 us (66%)
  starting transfers between devices  78.5 us (15%)
  local copies, waits for them, and re-layouts  56 us (10%)
  matrix products  29.3 us (5%)
  between operations  13.5 us (2%)
    ppermute x8, waiting for transfers between devices, shifted(): return lax.ppermute(shard, axis, pairs)  321 us
    ppermute x8, starting transfers between devices, shifted(): return lax.ppermute(shard, axis, pairs)  73.3 us
    dot_general x32, matrix products, product(): return jnp.einsum(form, first, second, precision=HIGH)  27.4 us
    all_to_all x1, waiting for transfers between devices, body(): lax.all_to_all(blocks, 'energy', split_axis=3, concat_axis=0, tiled=True)  20.2 us
    psum x1, waiting for transfers between devices, body(): result = lax.psum(mixed, 'mom') / mom_count  17 us
    sub x1, local copies, waits for them, and re-layouts, forward(): mat_imag = identity * ETA - hopping[1] - sig[:, 1] - left[1]  16.5 us
    sub x1, local copies, waits for them, and re-layouts, forward(): mat_real = identity * z_real[:, None, :] - hopping[0] - sig[:, 0] - left[0]  16.5 us
  transfers between devices with their start and end apart: 10, of which 10 were waited for; matrix products, arithmetic and copies ran while one was open for 0% of the time, Pallas kernels for 0%

commit v1 on v0

--- a/solution.py
+++ b/solution.py
@@ -1,6 +1,10 @@
+import functools
+
 import jax
 import jax.numpy as jnp
 from jax import lax
+from jax.experimental import pallas as pl
+from jax.experimental.pallas import tpu as pltpu
 from jax.sharding import PartitionSpec as P
 
 ETA = 0.5
@@ -52,7 +56,7 @@
     return jnp.sum(upper * mode_weight[0] + lower * mode_weight[1], axis=2)
 
 
-def body(onsite, hop, couple, sigma_in, shifts, mode_weight):
+def chain_body(onsite, hop, couple, sigma_in, shifts, mode_weight):
     e_local = sigma_in.shape[0]
     width = onsite.shape[-1]
     slab_count = lax.axis_size("slab")
@@ -118,6 +122,295 @@
     return result
 
 
+VMEM_BYTES = 48 * 1024 * 1024
+
+
+def halves(value):
+    high = value.astype(jnp.bfloat16)
+    low = (value - high.astype(jnp.float32)).astype(jnp.bfloat16)
+    return high, low
+
+
+def form(pair):
+    return halves(pair[0]), halves(pair[1]), halves(pair[0] + pair[1])
+
+
+def real_dot(left, right, flip):
+    lhs = jnp.concatenate([left[0], left[1], left[0]], axis=1)
+    axis = 1 if flip else 0
+    rhs = jnp.concatenate([right[0], right[0], right[1]], axis=axis)
+    return lax.dot_general(
+        lhs, rhs, (((1,), (axis,)), ((), ())), preferred_element_type=jnp.float32
+    )
+
+
+def mul(left, right):
+    first = real_dot(left[0], right[0], False)
+    second = real_dot(left[1], right[1], False)
+    third = real_dot(left[2], right[2], False)
+    return first - second, third - first - second
+
+
+def mul_adjoint(left, right, difference):
+    first = real_dot(left[0], right[0], True)
+    second = real_dot(left[1], right[1], True)
+    third = real_dot(left[2], difference, True)
+    return first + second, third - first + second
+
+
+def adjoint_form(pair):
+    real = pair[0].T
+    imag = -pair[1].T
+    return form((real, imag))
+
+
+def add(left, right):
+    return left[0] + right[0], left[1] + right[1]
+
+
+def read(ref):
+    return ref[0], ref[1]
+
+
+def write(ref, pair):
+    ref[0] = pair[0]
+    ref[1] = pair[1]
+
+
+def choose(cond, left, right):
+    return jnp.where(cond, left[0], right[0]), jnp.where(cond, left[1], right[1])
+
+
+def inverse(mat):
+    width = mat[0].shape[0]
+    eye = lax.broadcasted_iota(jnp.int32, (width, width), 0) == lax.broadcasted_iota(
+        jnp.int32, (width, width), 1
+    )
+    on_r = jnp.where(eye, mat[0], 0.0)
+    on_i = jnp.where(eye, mat[1], 0.0)
+    row_r = jnp.sum(on_r, axis=0, keepdims=True)
+    row_i = jnp.sum(on_i, axis=0, keepdims=True)
+    col_r = jnp.sum(on_r, axis=1, keepdims=True)
+    col_i = jnp.sum(on_i, axis=1, keepdims=True)
+
+    def invert(real, imag):
+        denom = real * real + imag * imag
+        return real / denom, -imag / denom
+
+    xr, xi = invert(row_r, row_i)
+    yr, yi = invert(col_r, col_i)
+    off_r = jnp.where(eye, 0.0, mat[0])
+    off_i = jnp.where(eye, 0.0, mat[1])
+    e_r = off_r * xr - off_i * xi
+    e_i = off_r * xi + off_i * xr
+    e_form = form((e_r, e_i))
+    sq = mul(e_form, e_form)
+    cube = mul(e_form, form(sq))
+    t_r = jnp.where(eye, 1.0, 0.0) - e_r + sq[0] - cube[0]
+    t_i = sq[1] - e_i - cube[1]
+    return yr * t_r - yi * t_i, yr * t_i + yi * t_r
+
+
+def pick_block(y, x, slab, own, x_side, y_side, far):
+    same_y = y == slab // 2
+    same_x = x == slab % 2
+    near = choose(same_x, read(own), read(x_side))
+    away = choose(same_x, read(y_side), read(far))
+    return choose(same_y, near, away)
+
+
+def left_term(coupling, green_form):
+    c_form = form(coupling)
+    inner = mul_adjoint(green_form, c_form, halves(coupling[0] - coupling[1]))
+    return mul(c_form, form(inner))
+
+
+def minus(left, right):
+    return left[0] - right[0], left[1] - right[1]
+
+
+def forward_kernel(
+    place, b_own, b_x, b_y, b_far, c_own, c_x, c_third,
+    g0_ref, g1_ref, p1_ref, q1_ref, k1_ref, g2_ref, p2_ref, q2_ref, k2_ref,
+):
+    y, x = place[0], place[1]
+    blocks = (b_own, b_x, b_y, b_far)
+    green = inverse(pick_block(y, x, 0, *blocks))
+    write(g0_ref, green)
+    couplings = (
+        choose(y == 0, choose(x == 1, read(c_own), read(c_x)), read(c_third)),
+        choose(y == 1, choose(x == 0, read(c_own), read(c_x)), read(c_third)),
+    )
+    outs = ((g1_ref, p1_ref, q1_ref, k1_ref), (g2_ref, p2_ref, q2_ref, k2_ref))
+    for slab in (1, 2):
+        coupling = couplings[slab - 1]
+        mat = minus(pick_block(y, x, slab, *blocks), left_term(coupling, form(green)))
+        green = inverse(mat)
+        g_form = form(green)
+        adjoint = adjoint_form(coupling)
+        right = mul(g_form, form(coupling))
+        g_ref, p_ref, q_ref, k_ref = outs[slab - 1]
+        write(g_ref, green)
+        write(p_ref, right)
+        write(q_ref, mul(adjoint, g_form))
+        write(k_ref, mul(adjoint, form(right)))
+
+
+def upper_kernel(
+    place, b_own, b_x, b_y, b_far, c_own, c_x, c_last, g2_ref, p2_ref, q2_ref, k2_ref,
+    keep_ref, send_ref, y2_ref,
+):
+    y, x = place[0], place[1]
+    coupling = choose(y == 0, read(c_last), choose(x == 1, read(c_own), read(c_x)))
+    green2 = read(g2_ref)
+    form2 = form(green2)
+    mat = minus(pick_block(y, x, 3, b_own, b_x, b_y, b_far), left_term(coupling, form2))
+    green3 = inverse(mat)
+    inner = mul(form(green3), form(coupling))
+    y3_form = form(mul(adjoint_form(coupling), form(inner)))
+    y2 = add(read(k2_ref), mul(form(read(q2_ref)), form(mul(y3_form, form(read(p2_ref))))))
+    write(y2_ref, y2)
+    full2 = add(green2, mul(form2, form(mul(y3_form, form2))))
+    write(keep_ref, choose(x == 0, full2, green3))
+    write(send_ref, choose(x == 0, green3, full2))
+
+
+def lower_kernel(place, y2_ref, g1_ref, p1_ref, q1_ref, k1_ref, g0_ref, keep_ref, send_ref):
+    x = place[1]
+    green1 = read(g1_ref)
+    form1 = form(green1)
+    y2_form = form(read(y2_ref))
+    y1 = add(read(k1_ref), mul(form(read(q1_ref)), form(mul(y2_form, form(read(p1_ref))))))
+    full1 = add(green1, mul(form1, form(mul(y2_form, form1))))
+    green0 = read(g0_ref)
+    form0 = form(green0)
+    full0 = add(green0, mul(form0, form(mul(form(y1), form0))))
+    write(keep_ref, choose(x == 0, full0, full1))
+    write(send_ref, choose(x == 0, full1, full0))
+
+
+def mix_kernel(weight, *refs):
+    *parts, out_ref = refs
+    rows = parts[0].shape[1]
+    step = 8
+    for part in range(2):
+        for row in range(0, rows, step):
+            values = [ref[part, row : row + step, :] for ref in parts]
+            for energy in range(out_ref.shape[0]):
+                total = weight[energy, 0] * values[0]
+                for slot in range(1, len(values)):
+                    total = total + weight[energy, slot] * values[slot]
+                out_ref[energy, part, row : row + step, :] = total
+
+
+def call(kernel, place, arrays, count, products):
+    shape = jax.ShapeDtypeStruct(arrays[0].shape, jnp.float32)
+    width = arrays[0].shape[-1]
+    vmem = pl.BlockSpec(memory_space=pltpu.VMEM)
+    return pl.pallas_call(
+        kernel,
+        out_shape=[shape] * count,
+        in_specs=[pl.BlockSpec(memory_space=pltpu.SMEM)] + [vmem] * len(arrays),
+        out_specs=[vmem] * count,
+        compiler_params=pltpu.CompilerParams(vmem_limit_bytes=VMEM_BYTES),
+        cost_estimate=pl.CostEstimate(
+            flops=products * 9 * 2 * width**3,
+            bytes_accessed=(len(arrays) + count) * 2 * width * width * 4,
+            transcendentals=0,
+        ),
+    )(place, *arrays)
+
+
+def owner_body(onsite, hop, couple, sigma_in, shifts, mode_weight):
+    e_local = sigma_in.shape[0]
+    width = onsite.shape[-1]
+    energy_count = lax.axis_size("energy")
+    mom_count = lax.axis_size("mom")
+    total = e_local * energy_count
+    axes = ("slab", "energy", "mom")
+    slab = lax.axis_index("slab")
+    z = lax.axis_index("energy")
+    k = lax.axis_index("mom")
+    y, x = slab // 2, slab % 2
+    place = jnp.stack([y, x]).astype(jnp.int32)
+    active = k == x
+
+    def device(yy, xx, zz, kk):
+        return ((2 * yy + xx) * energy_count + zz) * mom_count + kk
+
+    chips = [(yy, xx, zz) for yy in range(2) for xx in range(2) for zz in range(energy_count)]
+    x_feed = [(device(a, b, c, 1 - b), device(a, 1 - b, c, 1 - b)) for a, b, c in chips]
+    x_feed_c = [(device(a, b, c, 1 - b), device(a, 1 - b, c, 1 - b)) for a, b, c in chips if a + b > 0]
+    y_pass = [(device(a, b, c, b), device(1 - a, b, c, b)) for a, b, c in chips]
+    y_down = [(device(a, b, c, b), device(1 - a, b, c, b)) for a, b, c in chips if a == 1]
+    x_swap = [(device(a, b, c, b), device(a, 1 - b, c, 1 - b)) for a, b, c in chips]
+    core = [(device(a, b, c, b), device(a, b, c, 1 - b)) for a, b, c in chips]
+
+    def send(value, pairs):
+        return lax.ppermute(value, axes, pairs)
+
+    eye = jnp.eye(width, dtype=bool)
+
+    def block(local):
+        index = (z * e_local + local).astype(jnp.float32)
+        energy = -0.5 + (index + 0.5) / total
+        sigma = lax.dynamic_index_in_dim(sigma_in[:, 0], local, 0, keepdims=False)
+        real = jnp.where(eye, (energy - onsite[0, 0])[None, :], 0.0) - hop[0, 0, 0] - sigma[0]
+        imag = jnp.where(eye, ETA, 0.0) - hop[0, 0, 1] - sigma[1]
+        return jnp.stack([real, imag])
+
+    coupling = couple[0, 0]
+    b_other = block(1 - y)
+    b_own = block(y)
+    b_far_sent = send(b_other, x_feed)
+    b_y = send(b_other, y_pass)
+    c_x = send(coupling, x_feed_c)
+    b_far = send(b_far_sent, y_pass)
+    b_x = send(b_own, x_feed)
+    c_third = send(jnp.where(x != y, coupling, c_x), y_pass)
+    c_last = send(jnp.where(x == 1, coupling, c_x), y_down)
+
+    blocks = (b_own, b_x, b_y, b_far)
+    g0, g1, p1, q1, k1, g2, p2, q2, k2 = call(
+        forward_kernel, place, (*blocks, coupling, c_x, c_third), 9, 16
+    )
+    keep_up, send_up, y2 = call(
+        upper_kernel, place, (*blocks, coupling, c_x, c_last, g2, p2, q2, k2), 3, 10
+    )
+    up = keep_up + send(send_up, x_swap)
+    keep_low, send_low = call(lower_kernel, place, (y2, g1, p1, q1, k1, g0), 2, 6)
+    low = keep_low + send(send_low, x_swap)
+
+    sum_own = jnp.where(y == 0, low, up)
+    sum_other = send(jnp.where(y == 0, up, low), y_pass)
+
+    rows = width // energy_count
+    phonon = phonon_matrix(shifts, mode_weight, total) / mom_count
+    parts, columns = [], []
+    for source, local in ((sum_own, y), (sum_other, 1 - y)):
+        for flip in range(energy_count):
+            peer = z ^ flip
+            piece = lax.dynamic_slice_in_dim(source, peer * rows, rows, axis=1)
+            if flip:
+                pairs = [(device(a, b, c, b), device(a, b, c ^ flip, b)) for a, b, c in chips]
+                piece = send(piece, pairs)
+            parts.append(piece)
+            columns.append(
+                lax.dynamic_index_in_dim(phonon, peer * e_local + local, 1, keepdims=False)
+            )
+    weight = jnp.stack(columns, axis=1)
+    vmem = pl.BlockSpec(memory_space=pltpu.VMEM)
+    mixed = pl.pallas_call(
+        mix_kernel,
+        out_shape=jax.ShapeDtypeStruct((total, 2, rows, width), jnp.float32),
+        in_specs=[pl.BlockSpec(memory_space=pltpu.SMEM)] + [vmem] * len(parts),
+        out_specs=vmem,
+        compiler_params=pltpu.CompilerParams(vmem_limit_bytes=VMEM_BYTES),
+    )(weight, *parts)
+    result = jnp.where(active, mixed, send(mixed, core))
+    return result[:, None]
+
+
 def solution(mesh):
     in_specs = (
         P("mom", "slab", None),
@@ -128,4 +421,20 @@
         P(),
     )
     out_specs = P(None, "slab", None, "energy", None)
-    return jax.shard_map(body, mesh=mesh, in_specs=in_specs, out_specs=out_specs, check_vma=False)
+    count = mesh.shape["energy"]
+
+    def run(onsite, hop, couple, sigma_in, shifts, mode_weight):
+        owned = (
+            mesh.shape["slab"] == 4
+            and mesh.shape["mom"] == 2
+            and couple.shape[:2] == (2, 4)
+            and sigma_in.shape[0] == 2 * count
+            and count & (count - 1) == 0
+        )
+        inner = owner_body if owned else chain_body
+        sharded = jax.shard_map(
+            inner, mesh=mesh, in_specs=in_specs, out_specs=out_specs, check_vma=False
+        )
+        return sharded(onsite, hop, couple, sigma_in, shifts, mode_weight)
+
+    return run

time: 541 us -> 109 us (0.20)
  waiting for transfers between devices: 358 us -> 27.7 us
  local copies, waits for them, and re-layouts: 56 us -> 7.56 us
  matrix products: 29.3 us -> 0 us
  starting transfers between devices: 78.5 us -> 50.1 us
  Pallas kernels: 0 us -> 19.6 us
  between operations: 13.5 us -> 0.48 us
    ppermute x8 -> x17, waiting for transfers between devices: 321 us -> 27.7 us  [send(): return lax.ppermute(value, axes, pairs)]
    sub x2 -> x0, local copies, waits for them, and re-layouts: 33 us -> none  [the longest x1 16.5 us: forward(): mat_imag = identity * ETA - hopping[1] - sig[:, 1] - left[1]]
    dot_general x33 -> x0, matrix products: 29.3 us -> none  [the longest x32 27.4 us: product(): return jnp.einsum(form, first, second, precision=HIGH)]
    ppermute x8 -> x17, starting transfers between devices: 73.3 us -> 50.1 us  [send(): return lax.ppermute(value, axes, pairs)]
    all_to_all x1 -> x0, waiting for transfers between devices: 20.2 us -> none  [body(): lax.all_to_all(blocks, 'energy', split_axis=3, concat_axis=0, tiled=True)]
    pallas_call x0 -> x4, Pallas kernels: none -> 19.6 us  [the longest x3 18.4 us: call(): pl.pallas_call(kernel, out_shape=[shape] * count, in_specs=[pl.BlockSpec(...]
    psum x1 -> x0, waiting for transfers between devices: 17 us -> none  [body(): result = lax.psum(mixed, 'mom') / mom_count]
    while x5 -> x0, local copies, waits for them, and re-layouts: 8.31 us -> none
  transfers between devices with their start and end apart: 10 -> 17, of which waited for: 10 -> 8; matrix products, arithmetic and copies ran while one was open for 0% -> 1% of each run, Pallas kernels for 0% -> 8%
where the time goes in v1:
time: 109 us
  starting transfers between devices  50.1 us (46%)
  waiting for transfers between devices  27.7 us (25%)
  Pallas kernels  19.6 us (18%)
  local copies, waits for them, and re-layouts  7.56 us (7%)
  other arithmetic  3.13 us (3%)
    ppermute x17, starting transfers between devices, send(): return lax.ppermute(value, axes, pairs)  50.1 us
    ppermute x17, waiting for transfers between devices, send(): return lax.ppermute(value, axes, pairs)  27.7 us
    pallas_call x3, Pallas kernels, call(): pl.pallas_call(kernel, out_shape=[shape] * count, in_specs=[pl.BlockSpec(...  18.4 us
    unnamed x30, local copies, waits for them, and re-layouts  7.3 us
  transfers between devices with their start and end apart: 17, of which 8 were waited for; matrix products, arithmetic and copies ran while one was open for 1% of the time, Pallas kernels for 8%

profile of v1, /device:TPU:0, one launch (start us, length us, event | category | flops | bytes accessed | tf_op | source)
XLA Modules:
  0.0 108.6 jit_solution(18437841261453393547)
XLA Ops:
  0.7 1.5 %fusion.1 = (f32[1,256,256]{2,1,0:T(8,128)S(1)}, f32[1,256,256]{2,1,0:T(8,128)S(1)}, f32[1,256,256]{2,1,0:T(8,128)S(1)}, f32[1,256,256]{2,1,0:T(8,128)S(1)}) fusion(f32[2,1,2,256,256]{4,3,2,1,0:T(8,128)} %param.9, s32[]{:T(128)S(6)} %select_n.144, f32[1,1,2,256,256]{4,3,2,1,0:T(8,128)} %param.7, f32[256]{0:T(256)S(1)} %bitcast.47, s32[]{:T(128)S(6)} %select_n.141, ...), kind=kLoop, calls=%fused_computation.6 | loop fusion | flops 720896 | bytes 2623500 | tf_op jit(solution)/shard_map/sub | solution.py:358
  2.2 1.4 %collective-permute-start.2 = (f32[2,256,256]{2,1,0:T(8,128)S(1)}, f32[2,256,256]{2,1,0:T(8,128)}, u32[]{:S(2)}, u32[]{:S(2)}) collective-permute-start(f32[2,256,256]{2,1,0:T(8,128)S(1)} %pad_maximum_fusion.1), channel_id=1, source_target_pairs={{1,9},{3,11},{5,13},{7,15},{8,0},{10,2},{12,4},{14,6},{17,25},{19,... | collective-permute-start | bytes 1572872 | tf_op jit(solution)/shard_map/ppermute | solution.py:350
  3.7 1.3 %collective-permute-start.4 = (f32[2,256,256]{2,1,0:T(8,128)S(1)}, f32[2,256,256]{2,1,0:T(8,128)S(1)}, u32[]{:S(2)}, u32[]{:S(2)}) collective-permute-start(f32[2,256,256]{2,1,0:T(8,128)S(1)} %bitcast.45), channel_id=1, source_target_pairs={{8,0},{10,2},{12,4},{14,6},{17,25},{19,27},{21,29},{23,31},{24,16}... | collective-permute-start | bytes 1572872 | tf_op jit(solution)/shard_map/ppermute | solution.py:350
  5.0 4.9 %collective-permute-start.1 = (f32[2,256,256]{2,1,0:T(8,128)S(1)}, f32[2,256,256]{2,1,0:T(8,128)S(1)}, u32[]{:S(2)}, u32[]{:S(2)}) collective-permute-start(f32[2,256,256]{2,1,0:T(8,128)S(1)} %pad_maximum_fusion.1), channel_id=1, source_target_pairs={{0,16},{2,18},{4,20},{6,22},{9,25},{11,27},{13,29},{15,31},{16,0},... | collective-permute-start | bytes 1572872 | tf_op jit(solution)/shard_map/ppermute | solution.py:350
  9.9 1.3 %collective-permute-start = (f32[2,256,256]{2,1,0:T(8,128)S(1)}, f32[2,256,256]{2,1,0:T(8,128)S(1)}, u32[]{:S(2)}, u32[]{:S(2)}) collective-permute-start(f32[2,256,256]{2,1,0:T(8,128)S(1)} %pad_maximum_fusion.b_own), channel_id=1, source_target_pairs={{1,9},{3,11},{5,13},{7,15},{8,0},{10,2},{12,4},{14,6},{17,25},{19,... | collective-permute-start | bytes 1572872 | tf_op jit(solution)/shard_map/ppermute | solution.py:350
  11.2 2.6 %collective-permute-done.2 = f32[2,256,256]{2,1,0:T(8,128)} collective-permute-done((f32[2,256,256]{2,1,0:T(8,128)S(1)}, f32[2,256,256]{2,1,0:T(8,128)}, u32[]{:S(2)}, u32[]{:S(2)}) %collective-permute-start.2) | collective-permute-done | bytes 524320 | tf_op jit(solution)/shard_map/ppermute | solution.py:350
  13.8 4.6 %collective-permute-start.3 = (f32[2,256,256]{2,1,0:T(8,128)}, f32[2,256,256]{2,1,0:T(8,128)S(1)}, u32[]{:S(2)}, u32[]{:S(2)}) collective-permute-start(f32[2,256,256]{2,1,0:T(8,128)} %collective-permute-done.2), channel_id=1, source_target_pairs={{0,16},{2,18},{4,20},{6,22},{9,25},{11,27},{13,29},{15,31},{16,0},... | collective-permute-start | bytes 1572872 | tf_op jit(solution)/shard_map/ppermute | solution.py:350
  20.1 4.6 %collective-permute-start.6 = (f32[2,256,256]{2,1,0:T(8,128)S(1)}, f32[2,256,256]{2,1,0:T(8,128)S(1)}, u32[]{:S(2)}, u32[]{:S(2)}) collective-permute-start(f32[2,256,256]{2,1,0:T(8,128)S(1)} %get-tuple-element.39), channel_id=1, source_target_pairs={{0,16},{2,18},{4,20},{6,22},{9,25},{11,27},{13,29},{15,31},{16,0},... | collective-permute-start | bytes 1572872 | tf_op jit(solution)/shard_map/ppermute | solution.py:350
  24.7 1.3 %collective-permute-start.5 = (f32[2,256,256]{2,1,0:T(8,128)S(1)}, f32[2,256,256]{2,1,0:T(8,128)S(1)}, u32[]{:S(2)}, u32[]{:S(2)}) collective-permute-start(f32[2,256,256]{2,1,0:T(8,128)S(1)} %get-tuple-element.40), channel_id=1, source_target_pairs={{16,0},{18,2},{20,4},{22,6},{25,9},{27,11},{29,13},{31,15}} | collective-permute-start | bytes 1572872 | tf_op jit(solution)/shard_map/ppermute | solution.py:350
  26.1 5.7 %collective-permute-done.6.c_third = f32[2,256,256]{2,1,0:T(8,128)S(1)} collective-permute-done((f32[2,256,256]{2,1,0:T(8,128)S(1)}, f32[2,256,256]{2,1,0:T(8,128)S(1)}, u32[]{:S(2)}, u32[]{:S(2)}) %collective-permute-start.6) | collective-permute-done | bytes 524320 | tf_op jit(solution)/shard_map/ppermute | solution.py:350
  32.6 9.1 %shard_map.64 = (f32[2,256,256]{2,1,0:T(8,128)S(1)}, f32[2,256,256]{2,1,0:T(8,128)S(1)}, f32[2,256,256]{2,1,0:T(8,128)S(1)}, f32[2,256,256]{2,1,0:T(8,128)S(1)},...) custom-call(s32[2]{0:T(128)S(1)} %pad_add_fusion.place, ...), custom_call_target="tpu_custom_call" | custom-call | flops 4831838208 | bytes 8388608 | tf_op jit(solution)/shard_map/pallas_call | solution.py:310
  44.2 1.0 copy-done.5
  45.2 1.0 copy-done.7
  46.2 6.0 %shard_map.65 = (f32[2,256,256]{2,1,0:T(8,128)S(1)}, f32[2,256,256]{2,1,0:T(8,128)S(1)}, f32[2,256,256]{2,1,0:T(8,128)S(1)}) custom-call(s32[2]{0:T(128)S(1)} %pad_add_fusion.place, f32[2,256,256]{2,1,0:T(8,128)S(1)} %pad_maximum_fusion.b_own, f32[2,256,256]{2,1,0:T(8,128)S(1)} %collective-permute-done.b_x, f32[2,256,256]{2,1,0:T(8,128)S(1)} %copy-done.5, ...), custom_call_target="tpu_custom_call" | custom-call | flops 3019898880 | bytes 7340032 | tf_op jit(solution)/shard_map/pallas_call | solution.py:310
  52.2 3.4 %shard_map.66 = (f32[2,256,256]{2,1,0:T(8,128)S(1)}, f32[2,256,256]{2,1,0:T(8,128)S(1)}) custom-call(s32[2]{0:T(128)S(1)} %pad_add_fusion.place, f32[2,256,256]{2,1,0:T(8,128)S(1)} %get-tuple-element.23.y2_ref, f32[2,256,256]{2,1,0:T(8,128)S(1)} %get-tuple-element.24.g1_ref, f32[2,256,256]{2,1,0:T(8,128)S(1)} %get-tuple-element.25.p1_ref, ...), custom_call_target="tpu_custom_call" | custom-call | flops 1811939328 | bytes 4194304 | tf_op jit(solution)/shard_map/pallas_call | solution.py:310
  55.6 1.9 %collective-permute-start.7 = (f32[2,256,256]{2,1,0:T(8,128)S(1)}, f32[2,256,256]{2,1,0:T(8,128)S(1)}, u32[]{:S(2)}, u32[]{:S(2)}) collective-permute-start(f32[2,256,256]{2,1,0:T(8,128)S(1)} %get-tuple-element.30), channel_id=1, source_target_pairs={{0,9},{2,11},{4,13},{6,15},{9,0},{11,2},{13,4},{15,6},{16,25},{18,... | collective-permute-start | bytes 1572872 | tf_op jit(solution)/shard_map/ppermute | solution.py:350
  57.5 3.6 %collective-permute-start.8 = (f32[2,256,256]{2,1,0:T(8,128)S(1)}, f32[2,256,256]{2,1,0:T(8,128)S(1)}, u32[]{:S(2)}, u32[]{:S(2)}) collective-permute-start(f32[2,256,256]{2,1,0:T(8,128)S(1)} %get-tuple-element.32), channel_id=1, source_target_pairs={{0,9},{2,11},{4,13},{6,15},{9,0},{11,2},{13,4},{15,6},{16,25},{18,... | collective-permute-start | bytes 1572872 | tf_op jit(solution)/shard_map/ppermute | solution.py:350
  61.2 4.9 %collective-permute-done.7 = f32[2,256,256]{2,1,0:T(8,128)S(1)} collective-permute-done((f32[2,256,256]{2,1,0:T(8,128)S(1)}, f32[2,256,256]{2,1,0:T(8,128)S(1)}, u32[]{:S(2)}, u32[]{:S(2)}) %collective-permute-start.7) | collective-permute-done | bytes 524320 | tf_op jit(solution)/shard_map/ppermute | solution.py:350
  66.1 5.6 %collective-permute-done.8 = f32[2,256,256]{2,1,0:T(8,128)S(1)} collective-permute-done((f32[2,256,256]{2,1,0:T(8,128)S(1)}, f32[2,256,256]{2,1,0:T(8,128)S(1)}, u32[]{:S(2)}, u32[]{:S(2)}) %collective-permute-start.8) | collective-permute-done | bytes 524320 | tf_op jit(solution)/shard_map/ppermute | solution.py:350
  71.8 3.9 %collective-permute-start.12 = (f32[2,256,256]{2,1,0:T(8,128)S(1)}, f32[2,256,256]{2,1,0:T(8,128)S(1)}, u32[]{:S(2)}, u32[]{:S(2)}) collective-permute-start(f32[2,256,256]{2,1,0:T(8,128)S(1)} %get-tuple-element.33), channel_id=1, source_target_pairs={{0,16},{2,18},{4,20},{6,22},{9,25},{11,27},{13,29},{15,31},{16,0},... | collective-permute-start | bytes 1572872 | tf_op jit(solution)/shard_map/ppermute | solution.py:350
  76.6 4.5 %collective-permute-start.10 = (f32[2,64,256]{2,1,0:T(8,128)S(1)}, f32[2,64,256]{2,1,0:T(8,128)S(1)}, u32[]{:S(2)}, u32[]{:S(2)}) collective-permute-start(f32[2,64,256]{2,1,0:T(8,128)S(1)} %get-tuple-element.46), channel_id=1, source_target_pairs={{0,4},{2,6},{4,0},{6,2},{9,13},{11,15},{13,9},{15,11},{16,20},{18,... | collective-permute-start | bytes 393224 | tf_op jit(solution)/shard_map/ppermute | solution.py:350
  81.2 3.3 %collective-permute-start.11 = (f32[2,64,256]{2,1,0:T(8,128)S(1)}, f32[2,64,256]{2,1,0:T(8,128)S(1)}, u32[]{:S(2)}, u32[]{:S(2)}) collective-permute-start(f32[2,64,256]{2,1,0:T(8,128)S(1)} %get-tuple-element.45), channel_id=1, source_target_pairs={{0,6},{2,4},{4,2},{6,0},{9,15},{11,13},{13,11},{15,9},{16,22},{18,... | collective-permute-start | bytes 393224 | tf_op jit(solution)/shard_map/ppermute | solution.py:350
  84.4 2.2 %collective-permute-start.9 = (f32[2,64,256]{2,1,0:T(8,128)S(1)}, f32[2,64,256]{2,1,0:T(8,128)S(1)}, u32[]{:S(2)}, u32[]{:S(2)}) collective-permute-start(f32[2,64,256]{2,1,0:T(8,128)S(1)} %get-tuple-element.47), channel_id=1, source_target_pairs={{0,2},{2,0},{4,6},{6,4},{9,11},{11,9},{13,15},{15,13},{16,18},{18,... | collective-permute-start | bytes 393224 | tf_op jit(solution)/shard_map/ppermute | solution.py:350
  86.7 3.7 %collective-permute-start.13 = (f32[2,64,256]{2,1,0:T(8,128)S(1)}, f32[2,64,256]{2,1,0:T(8,128)S(1)}, u32[]{:S(2)}, u32[]{:S(2)}) collective-permute-start(f32[2,64,256]{2,1,0:T(8,128)S(1)} %get-tuple-element.43), channel_id=1, source_target_pairs={{0,2},{2,0},{4,6},{6,4},{9,11},{11,9},{13,15},{15,13},{16,18},{18,... | collective-permute-start | bytes 393224 | tf_op jit(solution)/shard_map/ppermute | solution.py:350
  90.4 3.6 %collective-permute-start.14 = (f32[2,64,256]{2,1,0:T(8,128)S(1)}, f32[2,64,256]{2,1,0:T(8,128)S(1)}, u32[]{:S(2)}, u32[]{:S(2)}) collective-permute-start(f32[2,64,256]{2,1,0:T(8,128)S(1)} %get-tuple-element.42), channel_id=1, source_target_pairs={{0,4},{2,6},{4,0},{6,2},{9,13},{11,15},{13,9},{15,11},{16,20},{18,... | collective-permute-start | bytes 393224 | tf_op jit(solution)/shard_map/ppermute | solution.py:350
  94.0 2.8 %collective-permute-start.15 = (f32[2,64,256]{2,1,0:T(8,128)S(1)}, f32[2,64,256]{2,1,0:T(8,128)S(1)}, u32[]{:S(2)}, u32[]{:S(2)}) collective-permute-start(f32[2,64,256]{2,1,0:T(8,128)S(1)} %get-tuple-element.41), channel_id=1, source_target_pairs={{0,6},{2,4},{4,2},{6,0},{9,15},{11,13},{13,11},{15,9},{16,22},{18,... | collective-permute-start | bytes 393224 | tf_op jit(solution)/shard_map/ppermute | solution.py:350
  97.1 2.1 %collective-permute-done.14.refs_6_ = f32[2,64,256]{2,1,0:T(8,128)S(1)} collective-permute-done((f32[2,64,256]{2,1,0:T(8,128)S(1)}, f32[2,64,256]{2,1,0:T(8,128)S(1)}, u32[]{:S(2)}, u32[]{:S(2)}) %collective-permute-start.14) | collective-permute-done | bytes 131104 | tf_op jit(solution)/shard_map/ppermute | solution.py:350
  99.2 3.5 %collective-permute-done.15.refs_7_ = f32[2,64,256]{2,1,0:T(8,128)S(1)} collective-permute-done((f32[2,64,256]{2,1,0:T(8,128)S(1)}, f32[2,64,256]{2,1,0:T(8,128)S(1)}, u32[]{:S(2)}, u32[]{:S(2)}) %collective-permute-start.15) | collective-permute-done | bytes 131104 | tf_op jit(solution)/shard_map/ppermute | solution.py:350
  102.7 1.2 %shard_map.67 = f32[8,2,64,256]{3,2,1,0:T(8,128)S(1)} custom-call(f32[8,8]{1,0:T(8,128)S(1)} %stack.12.weight, f32[2,64,256]{2,1,0:T(8,128)S(1)} %get-tuple-element.48.refs_0_, f32[2,64,256]{2,1,0:T(8,128)S(1)} %collective-permute-done.9.refs_1_, f32[2,64,256]{2,1,0:T(8,128)S(1)} %collective-permute-done.10.refs_2_, ...), custom_call_target="tpu_custom_call" | custom-call | tf_op jit(solution)/shard_map/pallas_call | solution.py:403
  103.9 1.4 %collective-permute-start.16 = (f32[8,2,64,256]{3,2,1,0:T(8,128)S(1)}, f32[8,2,64,256]{3,2,1,0:T(8,128)S(1)}, u32[]{:S(2)}, u32[]{:S(2)}) collective-permute-start(f32[8,2,64,256]{3,2,1,0:T(8,128)S(1)} %shard_map.67), channel_id=1, source_target_pairs={{0,1},{2,3},{4,5},{6,7},{9,8},{11,10},{13,12},{15,14},{16,17},{18,... | collective-permute-start | bytes 3145736 | tf_op jit(solution)/shard_map/ppermute | solution.py:350
  105.3 2.2 %collective-permute-done.16 = f32[8,2,64,256]{3,2,1,0:T(8,128)S(1)} collective-permute-done((f32[8,2,64,256]{3,2,1,0:T(8,128)S(1)}, f32[8,2,64,256]{3,2,1,0:T(8,128)S(1)}, u32[]{:S(2)}, u32[]{:S(2)}) %collective-permute-start.16) | collective-permute-done | bytes 1048608 | tf_op jit(solution)/shard_map/ppermute | solution.py:350
  107.5 1.1 %select_bitcast_fusion = f32[8,1,2,64,256]{4,3,2,1,0:T(8,128)} fusion(f32[8,2,64,256]{3,2,1,0:T(8,128)S(1)} %shard_map.67, f32[8,2,64,256]{3,2,1,0:T(8,128)S(1)} %collective-permute-done.16, pred[]{:T(512)S(6)} %eq.64), kind=kLoop, calls=%fused_computation | loop fusion | flops 262144 | bytes 3145729 | tf_op jit(solution)/shard_map/broadcast_in_dim | solution.py:411
  (52 shorter events, 7.0 us)
Async XLA Ops:
  0.0 0.7 copy-start.12
  2.2 1.5 %copy-start = (f32[1,1,2,256,256]{4,3,2,1,0:T(8,128)S(1)}, f32[1,1,2,256,256]{4,3,2,1,0:T(8,128)}, u32[]{:S(2)}) copy-start(f32[1,1,2,256,256]{4,3,2,1,0:T(8,128)} %param.8) | copy-start | bytes 1572868
  2.2 11.6 %collective-permute-start.2 = (f32[2,256,256]{2,1,0:T(8,128)S(1)}, f32[2,256,256]{2,1,0:T(8,128)}, u32[]{:S(2)}, u32[]{:S(2)}) collective-permute-start(f32[2,256,256]{2,1,0:T(8,128)S(1)} %pad_maximum_fusion.1), channel_id=1, source_target_pairs={{1,9},{3,11},{5,13},{7,15},{8,0},{10,2},{12,4},{14,6},{17,25},{19,... | collective-permute-start | bytes 1572872 | tf_op jit(solution)/shard_map/ppermute | solution.py:350
  3.7 15.7 %collective-permute-start.4 = (f32[2,256,256]{2,1,0:T(8,128)S(1)}, f32[2,256,256]{2,1,0:T(8,128)S(1)}, u32[]{:S(2)}, u32[]{:S(2)}) collective-permute-start(f32[2,256,256]{2,1,0:T(8,128)S(1)} %bitcast.45), channel_id=1, source_target_pairs={{8,0},{10,2},{12,4},{14,6},{17,25},{19,27},{21,29},{23,31},{24,16}... | collective-permute-start | bytes 1572872 | tf_op jit(solution)/shard_map/ppermute | solution.py:350
  5.0 21.1 %collective-permute-start.1 = (f32[2,256,256]{2,1,0:T(8,128)S(1)}, f32[2,256,256]{2,1,0:T(8,128)S(1)}, u32[]{:S(2)}, u32[]{:S(2)}) collective-permute-start(f32[2,256,256]{2,1,0:T(8,128)S(1)} %pad_maximum_fusion.1), channel_id=1, source_target_pairs={{0,16},{2,18},{4,20},{6,22},{9,25},{11,27},{13,29},{15,31},{16,0},... | collective-permute-start | bytes 1572872 | tf_op jit(solution)/shard_map/ppermute | solution.py:350
  9.9 16.2 %collective-permute-start = (f32[2,256,256]{2,1,0:T(8,128)S(1)}, f32[2,256,256]{2,1,0:T(8,128)S(1)}, u32[]{:S(2)}, u32[]{:S(2)}) collective-permute-start(f32[2,256,256]{2,1,0:T(8,128)S(1)} %pad_maximum_fusion.b_own), channel_id=1, source_target_pairs={{1,9},{3,11},{5,13},{7,15},{8,0},{10,2},{12,4},{14,6},{17,25},{19,... | collective-permute-start | bytes 1572872 | tf_op jit(solution)/shard_map/ppermute | solution.py:350
  13.8 12.3 %collective-permute-start.3 = (f32[2,256,256]{2,1,0:T(8,128)}, f32[2,256,256]{2,1,0:T(8,128)S(1)}, u32[]{:S(2)}, u32[]{:S(2)}) collective-permute-start(f32[2,256,256]{2,1,0:T(8,128)} %collective-permute-done.2), channel_id=1, source_target_pairs={{0,16},{2,18},{4,20},{6,22},{9,25},{11,27},{13,29},{15,31},{16,0},... | collective-permute-start | bytes 1572872 | tf_op jit(solution)/shard_map/ppermute | solution.py:350
  19.4 0.8 copy-start.2
  20.1 11.7 %collective-permute-start.6 = (f32[2,256,256]{2,1,0:T(8,128)S(1)}, f32[2,256,256]{2,1,0:T(8,128)S(1)}, u32[]{:S(2)}, u32[]{:S(2)}) collective-permute-start(f32[2,256,256]{2,1,0:T(8,128)S(1)} %get-tuple-element.39), channel_id=1, source_target_pairs={{0,16},{2,18},{4,20},{6,22},{9,25},{11,27},{13,29},{15,31},{16,0},... | collective-permute-start | bytes 1572872 | tf_op jit(solution)/shard_map/ppermute | solution.py:350
  24.7 19.4 %collective-permute-start.5 = (f32[2,256,256]{2,1,0:T(8,128)S(1)}, f32[2,256,256]{2,1,0:T(8,128)S(1)}, u32[]{:S(2)}, u32[]{:S(2)}) collective-permute-start(f32[2,256,256]{2,1,0:T(8,128)S(1)} %get-tuple-element.40), channel_id=1, source_target_pairs={{16,0},{18,2},{20,4},{22,6},{25,9},{27,11},{29,13},{31,15}} | collective-permute-start | bytes 1572872 | tf_op jit(solution)/shard_map/ppermute | solution.py:350
  26.1 18.0 %copy-start.1 = (f32[1,1,2,256,256]{4,3,2,1,0:T(8,128)S(1)}, f32[1,1,2,256,256]{4,3,2,1,0:T(8,128)}, u32[]{:S(2)}) copy-start(f32[1,1,2,256,256]{4,3,2,1,0:T(8,128)} %param.8) | copy-start | bytes 1572868
  26.1 18.0 %copy-start.3 = (f32[2,256,256]{2,1,0:T(8,128)S(1)}, f32[2,256,256]{2,1,0:T(8,128)}, u32[]{:S(2)}) copy-start(f32[2,256,256]{2,1,0:T(8,128)} %copy-done.2) | copy-start | bytes 1572868
  26.1 5.8 %copy-start.4 = (f32[2,256,256]{2,1,0:T(8,128)}, f32[2,256,256]{2,1,0:T(8,128)S(1)}, u32[]{:S(2)}) copy-start(f32[2,256,256]{2,1,0:T(8,128)S(1)} %collective-permute-done.1.b_y) | copy-start | bytes 1572868
  26.1 5.7 %copy-start.6 = (f32[2,256,256]{2,1,0:T(8,128)}, f32[2,256,256]{2,1,0:T(8,128)S(1)}, u32[]{:S(2)}) copy-start(f32[2,256,256]{2,1,0:T(8,128)S(1)} %collective-permute-done.3.b_far) | copy-start | bytes 1572868
  31.9 0.8 copy-start.14
  41.7 0.8 copy-start.8
  42.5 0.8 copy-start.9
  43.3 0.8 copy-start.10
  44.1 1.0 copy-start.5
  45.2 1.0 copy-start.7
  55.6 10.5 %collective-permute-start.7 = (f32[2,256,256]{2,1,0:T(8,128)S(1)}, f32[2,256,256]{2,1,0:T(8,128)S(1)}, u32[]{:S(2)}, u32[]{:S(2)}) collective-permute-start(f32[2,256,256]{2,1,0:T(8,128)S(1)} %get-tuple-element.30), channel_id=1, source_target_pairs={{0,9},{2,11},{4,13},{6,15},{9,0},{11,2},{13,4},{15,6},{16,25},{18,... | collective-permute-start | bytes 1572872 | tf_op jit(solution)/shard_map/ppermute | solution.py:350
  57.5 14.2 %collective-permute-start.8 = (f32[2,256,256]{2,1,0:T(8,128)S(1)}, f32[2,256,256]{2,1,0:T(8,128)S(1)}, u32[]{:S(2)}, u32[]{:S(2)}) collective-permute-start(f32[2,256,256]{2,1,0:T(8,128)S(1)} %get-tuple-element.32), channel_id=1, source_target_pairs={{0,9},{2,11},{4,13},{6,15},{9,0},{11,2},{13,4},{15,6},{16,25},{18,... | collective-permute-start | bytes 1572872 | tf_op jit(solution)/shard_map/ppermute | solution.py:350
  71.8 3.9 %copy-start.11 = (f32[2,4]{1,0:T(2,128)S(1)}, f32[2,4]{1,0:T(2,128)}, u32[]{:S(2)}) copy-start(f32[2,4]{1,0:T(2,128)} %param.11) | copy-start | bytes 100
  71.8 14.7 %collective-permute-start.12 = (f32[2,256,256]{2,1,0:T(8,128)S(1)}, f32[2,256,256]{2,1,0:T(8,128)S(1)}, u32[]{:S(2)}, u32[]{:S(2)}) collective-permute-start(f32[2,256,256]{2,1,0:T(8,128)S(1)} %get-tuple-element.33), channel_id=1, source_target_pairs={{0,16},{2,18},{4,20},{6,22},{9,25},{11,27},{13,29},{15,31},{16,0},... | collective-permute-start | bytes 1572872 | tf_op jit(solution)/shard_map/ppermute | solution.py:350
  75.8 0.7 copy-start.13
  76.6 17.4 %collective-permute-start.10 = (f32[2,64,256]{2,1,0:T(8,128)S(1)}, f32[2,64,256]{2,1,0:T(8,128)S(1)}, u32[]{:S(2)}, u32[]{:S(2)}) collective-permute-start(f32[2,64,256]{2,1,0:T(8,128)S(1)} %get-tuple-element.46), channel_id=1, source_target_pairs={{0,4},{2,6},{4,0},{6,2},{9,13},{11,15},{13,9},{15,11},{16,20},{18,... | collective-permute-start | bytes 393224 | tf_op jit(solution)/shard_map/ppermute | solution.py:350
  81.2 15.9 %collective-permute-start.11 = (f32[2,64,256]{2,1,0:T(8,128)S(1)}, f32[2,64,256]{2,1,0:T(8,128)S(1)}, u32[]{:S(2)}, u32[]{:S(2)}) collective-permute-start(f32[2,64,256]{2,1,0:T(8,128)S(1)} %get-tuple-element.45), channel_id=1, source_target_pairs={{0,6},{2,4},{4,2},{6,0},{9,15},{11,13},{13,11},{15,9},{16,22},{18,... | collective-permute-start | bytes 393224 | tf_op jit(solution)/shard_map/ppermute | solution.py:350
  84.4 12.6 %collective-permute-start.9 = (f32[2,64,256]{2,1,0:T(8,128)S(1)}, f32[2,64,256]{2,1,0:T(8,128)S(1)}, u32[]{:S(2)}, u32[]{:S(2)}) collective-permute-start(f32[2,64,256]{2,1,0:T(8,128)S(1)} %get-tuple-element.47), channel_id=1, source_target_pairs={{0,2},{2,0},{4,6},{6,4},{9,11},{11,9},{13,15},{15,13},{16,18},{18,... | collective-permute-start | bytes 393224 | tf_op jit(solution)/shard_map/ppermute | solution.py:350
  86.7 10.4 %collective-permute-start.13 = (f32[2,64,256]{2,1,0:T(8,128)S(1)}, f32[2,64,256]{2,1,0:T(8,128)S(1)}, u32[]{:S(2)}, u32[]{:S(2)}) collective-permute-start(f32[2,64,256]{2,1,0:T(8,128)S(1)} %get-tuple-element.43), channel_id=1, source_target_pairs={{0,2},{2,0},{4,6},{6,4},{9,11},{11,9},{13,15},{15,13},{16,18},{18,... | collective-permute-start | bytes 393224 | tf_op jit(solution)/shard_map/ppermute | solution.py:350
  90.4 8.8 %collective-permute-start.14 = (f32[2,64,256]{2,1,0:T(8,128)S(1)}, f32[2,64,256]{2,1,0:T(8,128)S(1)}, u32[]{:S(2)}, u32[]{:S(2)}) collective-permute-start(f32[2,64,256]{2,1,0:T(8,128)S(1)} %get-tuple-element.42), channel_id=1, source_target_pairs={{0,4},{2,6},{4,0},{6,2},{9,13},{11,15},{13,9},{15,11},{16,20},{18,... | collective-permute-start | bytes 393224 | tf_op jit(solution)/shard_map/ppermute | solution.py:350
  94.0 8.8 %collective-permute-start.15 = (f32[2,64,256]{2,1,0:T(8,128)S(1)}, f32[2,64,256]{2,1,0:T(8,128)S(1)}, u32[]{:S(2)}, u32[]{:S(2)}) collective-permute-start(f32[2,64,256]{2,1,0:T(8,128)S(1)} %get-tuple-element.41), channel_id=1, source_target_pairs={{0,6},{2,4},{4,2},{6,0},{9,15},{11,13},{13,11},{15,9},{16,22},{18,... | collective-permute-start | bytes 393224 | tf_op jit(solution)/shard_map/ppermute | solution.py:350
  103.9 3.6 %collective-permute-start.16 = (f32[8,2,64,256]{3,2,1,0:T(8,128)S(1)}, f32[8,2,64,256]{3,2,1,0:T(8,128)S(1)}, u32[]{:S(2)}, u32[]{:S(2)}) collective-permute-start(f32[8,2,64,256]{3,2,1,0:T(8,128)S(1)} %shard_map.67), channel_id=1, source_target_pairs={{0,1},{2,3},{4,5},{6,7},{9,8},{11,10},{13,12},{15,14},{16,17},{18,... | collective-permute-start | bytes 3145736 | tf_op jit(solution)/shard_map/ppermute | solution.py:350

commit v2 on v1

--- a/solution.py
+++ b/solution.py
@@ -122,7 +122,7 @@
     return result
 
 
-VMEM_BYTES = 48 * 1024 * 1024
+VMEM_BYTES = 24 * 1024 * 1024
 
 
 def halves(value):
@@ -132,30 +132,44 @@
 
 
 def form(pair):
-    return halves(pair[0]), halves(pair[1]), halves(pair[0] + pair[1])
-
-
-def real_dot(left, right, flip):
-    lhs = jnp.concatenate([left[0], left[1], left[0]], axis=1)
-    axis = 1 if flip else 0
-    rhs = jnp.concatenate([right[0], right[0], right[1]], axis=axis)
-    return lax.dot_general(
-        lhs, rhs, (((1,), (axis,)), ((), ())), preferred_element_type=jnp.float32
-    )
+    return halves(pair[0]), halves(pair[1])
+
+
+def left_side(operand):
+    (rh, rl), (ih, il) = operand
+    return jnp.concatenate([rh, ih, rl, il, rh, ih], axis=1)
 
 
 def mul(left, right):
-    first = real_dot(left[0], right[0], False)
-    second = real_dot(left[1], right[1], False)
-    third = real_dot(left[2], right[2], False)
-    return first - second, third - first - second
-
-
-def mul_adjoint(left, right, difference):
-    first = real_dot(left[0], right[0], True)
-    second = real_dot(left[1], right[1], True)
-    third = real_dot(left[2], difference, True)
-    return first + second, third - first + second
+    (rh, rl), (ih, il) = right
+    high_r, low_r = jnp.concatenate([rh, -ih], axis=0), jnp.concatenate([rl, -il], axis=0)
+    high_i, low_i = jnp.concatenate([ih, rh], axis=0), jnp.concatenate([il, rl], axis=0)
+    rhs = jnp.concatenate(
+        [
+            jnp.concatenate([high_r, high_r, low_r], axis=0),
+            jnp.concatenate([high_i, high_i, low_i], axis=0),
+        ],
+        axis=1,
+    )
+    out = jnp.dot(left_side(left), rhs, preferred_element_type=jnp.float32)
+    width = rh.shape[0]
+    return out[:, :width], out[:, width:]
+
+
+def mul_adjoint(left, right):
+    (rh, rl), (ih, il) = right
+    rhs = jnp.concatenate(
+        [
+            jnp.concatenate([rh, ih, rh, ih, rl, il], axis=1),
+            jnp.concatenate([-ih, rh, -ih, rh, -il, rl], axis=1),
+        ],
+        axis=0,
+    )
+    out = lax.dot_general(
+        left_side(left), rhs, (((1,), (1,)), ((), ())), preferred_element_type=jnp.float32
+    )
+    width = rh.shape[0]
+    return out[:, :width], out[:, width:]
 
 
 def adjoint_form(pair):
@@ -221,7 +235,7 @@
 
 def left_term(coupling, green_form):
     c_form = form(coupling)
-    inner = mul_adjoint(green_form, c_form, halves(coupling[0] - coupling[1]))
+    inner = mul_adjoint(green_form, c_form)
     return mul(c_form, form(inner))
 
 
@@ -289,18 +303,33 @@
     write(send_ref, choose(x == 0, full1, full0))
 
 
-def mix_kernel(weight, *refs):
-    *parts, out_ref = refs
+def mix_kernel(place, weight, *refs):
+    *parts, other_ref, out_ref = refs
+    slots = len(parts) // 2
     rows = parts[0].shape[1]
+    upper = place[0] == 1
     step = 8
     for part in range(2):
         for row in range(0, rows, step):
-            values = [ref[part, row : row + step, :] for ref in parts]
+            here = (part, slice(row, row + step), slice(None))
+            values = [jnp.where(upper, parts[i][here], parts[slots + i][here]) for i in range(slots)]
+            values += [other_ref[(i, *here)] for i in range(slots)]
             for energy in range(out_ref.shape[0]):
                 total = weight[energy, 0] * values[0]
                 for slot in range(1, len(values)):
                     total = total + weight[energy, slot] * values[slot]
                 out_ref[energy, part, row : row + step, :] = total
+
+
+def prepare_kernel(place, scale, onsite_ref, hop_ref, sigma_ref, own_ref, other_ref):
+    width = hop_ref.shape[-1]
+    eye = lax.broadcasted_iota(jnp.int32, (width, width), 0) == lax.broadcasted_iota(
+        jnp.int32, (width, width), 1
+    )
+    for ref, local, energy in ((other_ref, 1 - place[0], scale[1]), (own_ref, place[0], scale[0])):
+        level = energy - onsite_ref[...]
+        ref[0] = jnp.where(eye, level, 0.0) - hop_ref[0] - sigma_ref[local, 0]
+        ref[1] = jnp.where(eye, ETA, 0.0) - hop_ref[1] - sigma_ref[local, 1]
 
 
 def call(kernel, place, arrays, count, products):
@@ -349,26 +378,30 @@
     def send(value, pairs):
         return lax.ppermute(value, axes, pairs)
 
-    eye = jnp.eye(width, dtype=bool)
-
-    def block(local):
-        index = (z * e_local + local).astype(jnp.float32)
-        energy = -0.5 + (index + 0.5) / total
-        sigma = lax.dynamic_index_in_dim(sigma_in[:, 0], local, 0, keepdims=False)
-        real = jnp.where(eye, (energy - onsite[0, 0])[None, :], 0.0) - hop[0, 0, 0] - sigma[0]
-        imag = jnp.where(eye, ETA, 0.0) - hop[0, 0, 1] - sigma[1]
-        return jnp.stack([real, imag])
+    def after(value, earlier):
+        return lax.optimization_barrier((value, earlier))[0]
+
+    locals_ = jnp.stack([y, 1 - y])
+    energies = -0.5 + ((z * e_local + locals_).astype(jnp.float32) + 0.5) / total
+    smem = pl.BlockSpec(memory_space=pltpu.SMEM)
+    vmem = pl.BlockSpec(memory_space=pltpu.VMEM)
+    block_shape = jax.ShapeDtypeStruct((2, width, width), jnp.float32)
+    b_own, b_other = pl.pallas_call(
+        prepare_kernel,
+        out_shape=[block_shape] * 2,
+        in_specs=[smem, smem, vmem, vmem, vmem],
+        out_specs=[vmem] * 2,
+        compiler_params=pltpu.CompilerParams(vmem_limit_bytes=VMEM_BYTES),
+    )(place, energies, onsite[0], hop[0, 0], sigma_in[:, 0])
 
     coupling = couple[0, 0]
-    b_other = block(1 - y)
-    b_own = block(y)
     b_far_sent = send(b_other, x_feed)
     b_y = send(b_other, y_pass)
-    c_x = send(coupling, x_feed_c)
-    b_far = send(b_far_sent, y_pass)
-    b_x = send(b_own, x_feed)
-    c_third = send(jnp.where(x != y, coupling, c_x), y_pass)
-    c_last = send(jnp.where(x == 1, coupling, c_x), y_down)
+    c_x = send(after(coupling, b_far_sent), x_feed_c)
+    b_far = send(after(b_far_sent, b_y), y_pass)
+    b_x = send(after(b_own, c_x), x_feed)
+    c_third = send(after(jnp.where(x != y, coupling, c_x), b_far), y_pass)
+    c_last = send(after(jnp.where(x == 1, coupling, c_x), c_third), y_down)
 
     blocks = (b_own, b_x, b_y, b_far)
     g0, g1, p1, q1, k1, g2, p2, q2, k2 = call(
@@ -377,36 +410,40 @@
     keep_up, send_up, y2 = call(
         upper_kernel, place, (*blocks, coupling, c_x, c_last, g2, p2, q2, k2), 3, 10
     )
-    up = keep_up + send(send_up, x_swap)
+    got_up = send(send_up, x_swap)
     keep_low, send_low = call(lower_kernel, place, (y2, g1, p1, q1, k1, g0), 2, 6)
-    low = keep_low + send(send_low, x_swap)
-
-    sum_own = jnp.where(y == 0, low, up)
-    sum_other = send(jnp.where(y == 0, up, low), y_pass)
+    got_low = send(after(send_low, got_up), x_swap)
 
     rows = width // energy_count
-    phonon = phonon_matrix(shifts, mode_weight, total) / mom_count
-    parts, columns = [], []
-    for source, local in ((sum_own, y), (sum_other, 1 - y)):
+
+    def over_planes(value):
+        parts = []
         for flip in range(energy_count):
-            peer = z ^ flip
-            piece = lax.dynamic_slice_in_dim(source, peer * rows, rows, axis=1)
+            piece = lax.dynamic_slice_in_dim(value, (z ^ flip) * rows, rows, axis=1)
             if flip:
                 pairs = [(device(a, b, c, b), device(a, b, c ^ flip, b)) for a, b, c in chips]
                 piece = send(piece, pairs)
             parts.append(piece)
-            columns.append(
-                lax.dynamic_index_in_dim(phonon, peer * e_local + local, 1, keepdims=False)
-            )
+        return parts
+
+    up = over_planes(keep_up + got_up)
+    low = over_planes(keep_low + got_low)
+    other = send(jnp.where(y == 0, jnp.stack(up), jnp.stack(low)), y_pass)
+
+    phonon = phonon_matrix(shifts, mode_weight, total) / mom_count
+    columns = [
+        lax.dynamic_index_in_dim(phonon, (z ^ flip) * e_local + local, 1, keepdims=False)
+        for local in (y, 1 - y)
+        for flip in range(energy_count)
+    ]
     weight = jnp.stack(columns, axis=1)
-    vmem = pl.BlockSpec(memory_space=pltpu.VMEM)
     mixed = pl.pallas_call(
         mix_kernel,
         out_shape=jax.ShapeDtypeStruct((total, 2, rows, width), jnp.float32),
-        in_specs=[pl.BlockSpec(memory_space=pltpu.SMEM)] + [vmem] * len(parts),
+        in_specs=[smem, smem] + [vmem] * (2 * energy_count + 1),
         out_specs=vmem,
         compiler_params=pltpu.CompilerParams(vmem_limit_bytes=VMEM_BYTES),
-    )(weight, *parts)
+    )(place, weight, *up, *low, other)
     result = jnp.where(active, mixed, send(mixed, core))
     return result[:, None]
 

time: 109 us -> 116 us (1.064)
  waiting for transfers between devices: 27.7 us -> 43 us
  local copies, waits for them, and re-layouts: 7.56 us -> 3.23 us
  starting transfers between devices: 50.1 us -> 45.9 us
  other arithmetic: 3.13 us -> 1.73 us
  Pallas kernels: 19.6 us -> 20.9 us
    ppermute x17, waiting for transfers between devices: 27.7 us -> 43 us  [send(): return lax.ppermute(value, axes, pairs)]
    unnamed x30 -> x12, local copies, waits for them, and re-layouts: 7.3 us -> 2.96 us
    ppermute x17, starting transfers between devices: 50.1 us -> 45.9 us  [send(): return lax.ppermute(value, axes, pairs)]
    sub x2 -> x0, other arithmetic: 1.48 us -> none  [the longest x1 1.48 us: block(): jnp.where(eye, (energy - onsite[0, 0])[None, :], 0.0) - hop[0, 0, 0]]
  transfers between devices with their start and end apart: 17 -> 17, of which waited for: 8 -> 11; matrix products, arithmetic and copies ran while one was open for 1% -> 1% of each run, Pallas kernels for 8% -> 11%
where the time goes in v2:
time: 116 us; the launch traced here: 115 us
  starting transfers between devices  45.9 us (40%)
  waiting for transfers between devices  43 us (37%)
  Pallas kernels  20.9 us (18%)
  local copies, waits for them, and re-layouts  3.23 us (3%)
  other arithmetic  1.73 us (1%)
    ppermute x17, starting transfers between devices, send(): return lax.ppermute(value, axes, pairs)  45.9 us
    ppermute x17, waiting for transfers between devices, send(): return lax.ppermute(value, axes, pairs)  43 us
    pallas_call x3, Pallas kernels, call(): pl.pallas_call(kernel, out_shape=[shape] * count, in_specs=[pl.BlockSpec(...  19 us
    unnamed x12, local copies, waits for them, and re-layouts  2.96 us
  transfers between devices with their start and end apart: 17, of which 11 were waited for; matrix products, arithmetic and copies ran while one was open for 1% of the time, Pallas kernels for 11%

profile of v2, /device:TPU:0, one launch (start us, length us, event | category | flops | bytes accessed | tf_op | source)
XLA Modules:
  0.0 115.1 jit_solution(5591280867666544584)
XLA Ops:
  0.8 1.2 %copy-done = f32[2,1,2,256,256]{4,3,2,1,0:T(8,128)S(1)} copy-done((f32[2,1,2,256,256]{4,3,2,1,0:T(8,128)S(1)}, f32[2,1,2,256,256]{4,3,2,1,0:T(8,128)}, u32[]{:S(2)}) %copy-start) | copy-done | bytes 1048600
  3.8 1.3 %collective-permute-start = (f32[2,256,256]{2,1,0:T(8,128)S(1)}, f32[2,256,256]{2,1,0:T(8,128)S(1)}, u32[]{:S(2)}, u32[]{:S(2)}) collective-permute-start(f32[2,256,256]{2,1,0:T(8,128)S(1)} %get-tuple-element.28), channel_id=1, source_target_pairs={{1,9},{3,11},{5,13},{7,15},{8,0},{10,2},{12,4},{14,6},{17,25},{19,... | collective-permute-start | bytes 1572872 | tf_op jit(solution)/shard_map/ppermute | solution.py:379
  5.1 4.9 %collective-permute-start.3 = (f32[2,256,256]{2,1,0:T(8,128)S(1)}, f32[2,256,256]{2,1,0:T(8,128)S(1)}, u32[]{:S(2)}, u32[]{:S(2)}) collective-permute-start(f32[2,256,256]{2,1,0:T(8,128)S(1)} %get-tuple-element.28), channel_id=1, source_target_pairs={{0,16},{2,18},{4,20},{6,22},{9,25},{11,27},{13,29},{15,31},{16,0},... | collective-permute-start | bytes 1572872 | tf_op jit(solution)/shard_map/ppermute | solution.py:379
  10.0 5.2 %collective-permute-done = f32[2,256,256]{2,1,0:T(8,128)S(1)} collective-permute-done((f32[2,256,256]{2,1,0:T(8,128)S(1)}, f32[2,256,256]{2,1,0:T(8,128)S(1)}, u32[]{:S(2)}, u32[]{:S(2)}) %collective-permute-start) | collective-permute-done | bytes 524320 | tf_op jit(solution)/shard_map/ppermute | solution.py:379
  15.2 1.3 %collective-permute-start.1 = (f32[2,256,256]{2,1,0:T(8,128)S(1)}, f32[2,256,256]{2,1,0:T(8,128)S(1)}, u32[]{:S(2)}, u32[]{:S(2)}) collective-permute-start(f32[2,256,256]{2,1,0:T(8,128)S(1)} %bitcast.35), channel_id=1, source_target_pairs={{8,0},{10,2},{12,4},{14,6},{17,25},{19,27},{21,29},{23,31},{24,16}... | collective-permute-start | bytes 1572872 | tf_op jit(solution)/shard_map/ppermute | solution.py:379
  17.1 3.9 %collective-permute-start.4 = (f32[2,256,256]{2,1,0:T(8,128)S(1)}, f32[2,256,256]{2,1,0:T(8,128)S(1)}, u32[]{:S(2)}, u32[]{:S(2)}) collective-permute-start(f32[2,256,256]{2,1,0:T(8,128)S(1)} %collective-permute-done), channel_id=1, source_target_pairs={{0,16},{2,18},{4,20},{6,22},{9,25},{11,27},{13,29},{15,31},{16,0},... | collective-permute-start | bytes 1572872 | tf_op jit(solution)/shard_map/ppermute | solution.py:379
  21.0 5.2 %collective-permute-done.1.c_x = f32[2,256,256]{2,1,0:T(8,128)S(1)} collective-permute-done((f32[2,256,256]{2,1,0:T(8,128)S(1)}, f32[2,256,256]{2,1,0:T(8,128)S(1)}, u32[]{:S(2)}, u32[]{:S(2)}) %collective-permute-start.1) | collective-permute-done | bytes 524320 | tf_op jit(solution)/shard_map/ppermute | solution.py:379
  26.3 1.9 %collective-permute-done.4.b_far = f32[2,256,256]{2,1,0:T(8,128)S(1)} collective-permute-done((f32[2,256,256]{2,1,0:T(8,128)S(1)}, f32[2,256,256]{2,1,0:T(8,128)S(1)}, u32[]{:S(2)}, u32[]{:S(2)}) %collective-permute-start.4) | collective-permute-done | bytes 524320 | tf_op jit(solution)/shard_map/ppermute | solution.py:379
  28.2 3.9 %collective-permute-start.5 = (f32[2,256,256]{2,1,0:T(8,128)S(1)}, f32[2,256,256]{2,1,0:T(8,128)S(1)}, u32[]{:S(2)}, u32[]{:S(2)}) collective-permute-start(f32[2,256,256]{2,1,0:T(8,128)S(1)} %get-tuple-element.32), channel_id=1, source_target_pairs={{0,16},{2,18},{4,20},{6,22},{9,25},{11,27},{13,29},{15,31},{16,0},... | collective-permute-start | bytes 1572872 | tf_op jit(solution)/shard_map/ppermute | solution.py:379
  32.1 1.3 %collective-permute-start.2 = (f32[2,256,256]{2,1,0:T(8,128)S(1)}, f32[2,256,256]{2,1,0:T(8,128)S(1)}, u32[]{:S(2)}, u32[]{:S(2)}) collective-permute-start(f32[2,256,256]{2,1,0:T(8,128)S(1)} %get-tuple-element.30.b_own), channel_id=1, source_target_pairs={{1,9},{3,11},{5,13},{7,15},{8,0},{10,2},{12,4},{14,6},{17,25},{19,... | collective-permute-start | bytes 1572872 | tf_op jit(solution)/shard_map/ppermute | solution.py:379
  33.4 5.8 %collective-permute-done.5.c_third = f32[2,256,256]{2,1,0:T(8,128)S(1)} collective-permute-done((f32[2,256,256]{2,1,0:T(8,128)S(1)}, f32[2,256,256]{2,1,0:T(8,128)S(1)}, u32[]{:S(2)}, u32[]{:S(2)}) %collective-permute-start.5) | collective-permute-done | bytes 524320 | tf_op jit(solution)/shard_map/ppermute | solution.py:379
  39.2 1.3 %collective-permute-start.6 = (f32[2,256,256]{2,1,0:T(8,128)S(1)}, f32[2,256,256]{2,1,0:T(8,128)S(1)}, u32[]{:S(2)}, u32[]{:S(2)}) collective-permute-start(f32[2,256,256]{2,1,0:T(8,128)S(1)} %get-tuple-element.33), channel_id=1, source_target_pairs={{16,0},{18,2},{20,4},{22,6},{25,9},{27,11},{29,13},{31,15}} | collective-permute-start | bytes 1572872 | tf_op jit(solution)/shard_map/ppermute | solution.py:379
  40.5 2.6 %collective-permute-done.2.b_x = f32[2,256,256]{2,1,0:T(8,128)S(1)} collective-permute-done((f32[2,256,256]{2,1,0:T(8,128)S(1)}, f32[2,256,256]{2,1,0:T(8,128)S(1)}, u32[]{:S(2)}, u32[]{:S(2)}) %collective-permute-start.2) | collective-permute-done | bytes 524320 | tf_op jit(solution)/shard_map/ppermute | solution.py:379
  43.2 9.2 %shard_map.65 = (f32[2,256,256]{2,1,0:T(8,128)S(1)}, f32[2,256,256]{2,1,0:T(8,128)S(1)}, f32[2,256,256]{2,1,0:T(8,128)S(1)}, f32[2,256,256]{2,1,0:T(8,128)S(1)},...) custom-call(s32[2]{0:T(128)S(1)} %pad_add_fusion.place, ...), custom_call_target="tpu_custom_call" | custom-call | flops 4831838208 | bytes 8388608 | tf_op jit(solution)/shard_map/pallas_call | solution.py:339
  52.4 6.1 %shard_map.66 = (f32[2,256,256]{2,1,0:T(8,128)S(1)}, f32[2,256,256]{2,1,0:T(8,128)S(1)}, f32[2,256,256]{2,1,0:T(8,128)S(1)}) custom-call(s32[2]{0:T(128)S(1)} %pad_add_fusion.place, f32[2,256,256]{2,1,0:T(8,128)S(1)} %get-tuple-element.30.b_own, f32[2,256,256]{2,1,0:T(8,128)S(1)} %collective-permute-done.2.b_x, ...), custom_call_target="tpu_custom_call" | custom-call | flops 3019898880 | bytes 7340032 | tf_op jit(solution)/shard_map/pallas_call | solution.py:339
  58.5 2.1 %collective-permute-start.7 = (f32[2,256,256]{2,1,0:T(8,128)S(1)}, f32[2,256,256]{2,1,0:T(8,128)S(1)}, u32[]{:S(2)}, u32[]{:S(2)}) collective-permute-start(f32[2,256,256]{2,1,0:T(8,128)S(1)} %get-tuple-element.39), channel_id=1, source_target_pairs={{0,9},{2,11},{4,13},{6,15},{9,0},{11,2},{13,4},{15,6},{16,25},{18,... | collective-permute-start | bytes 1572872 | tf_op jit(solution)/shard_map/ppermute | solution.py:379
  60.7 3.6 %shard_map.67 = (f32[2,256,256]{2,1,0:T(8,128)S(1)}, f32[2,256,256]{2,1,0:T(8,128)S(1)}) custom-call(s32[2]{0:T(128)S(1)} %pad_add_fusion.place, f32[2,256,256]{2,1,0:T(8,128)S(1)} %get-tuple-element.40.y2_ref, f32[2,256,256]{2,1,0:T(8,128)S(1)} %get-tuple-element.41.g1_ref, f32[2,256,256]{2,1,0:T(8,128)S(1)} %get-tuple-element.42.p1_ref, ...), custom_call_target="tpu_custom_call" | custom-call | flops 1811939328 | bytes 4194304 | tf_op jit(solution)/shard_map/pallas_call | solution.py:339
  64.3 4.7 %collective-permute-done.7 = f32[2,256,256]{2,1,0:T(8,128)S(1)} collective-permute-done((f32[2,256,256]{2,1,0:T(8,128)S(1)}, f32[2,256,256]{2,1,0:T(8,128)S(1)}, u32[]{:S(2)}, u32[]{:S(2)}) %collective-permute-start.7) | collective-permute-done | bytes 524320 | tf_op jit(solution)/shard_map/ppermute | solution.py:379
  69.0 1.9 %collective-permute-start.11 = (f32[2,256,256]{2,1,0:T(8,128)S(1)}, f32[2,256,256]{2,1,0:T(8,128)S(1)}, u32[]{:S(2)}, u32[]{:S(2)}) collective-permute-start(f32[2,256,256]{2,1,0:T(8,128)S(1)} %get-tuple-element.48), channel_id=1, source_target_pairs={{0,9},{2,11},{4,13},{6,15},{9,0},{11,2},{13,4},{15,6},{16,25},{18,... | collective-permute-start | bytes 1572872 | tf_op jit(solution)/shard_map/ppermute | solution.py:379
  71.1 3.5 %collective-permute-start.8 = (f32[2,64,256]{2,1,0:T(8,128)S(1)}, f32[2,64,256]{2,1,0:T(8,128)S(1)}, u32[]{:S(2)}, u32[]{:S(2)}) collective-permute-start(f32[2,64,256]{2,1,0:T(8,128)S(1)} %get-tuple-element.57), channel_id=1, source_target_pairs={{0,2},{2,0},{4,6},{6,4},{9,11},{11,9},{13,15},{15,13},{16,18},{18,... | collective-permute-start | bytes 393224 | tf_op jit(solution)/shard_map/ppermute | solution.py:379
  74.6 4.5 %collective-permute-start.9 = (f32[2,64,256]{2,1,0:T(8,128)S(1)}, f32[2,64,256]{2,1,0:T(8,128)S(1)}, u32[]{:S(2)}, u32[]{:S(2)}) collective-permute-start(f32[2,64,256]{2,1,0:T(8,128)S(1)} %get-tuple-element.56), channel_id=1, source_target_pairs={{0,4},{2,6},{4,0},{6,2},{9,13},{11,15},{13,9},{15,11},{16,20},{18,... | collective-permute-start | bytes 393224 | tf_op jit(solution)/shard_map/ppermute | solution.py:379
  79.1 2.1 %collective-permute-start.10 = (f32[2,64,256]{2,1,0:T(8,128)S(1)}, f32[2,64,256]{2,1,0:T(8,128)S(1)}, u32[]{:S(2)}, u32[]{:S(2)}) collective-permute-start(f32[2,64,256]{2,1,0:T(8,128)S(1)} %get-tuple-element.55), channel_id=1, source_target_pairs={{0,6},{2,4},{4,2},{6,0},{9,15},{11,13},{13,11},{15,9},{16,22},{18,... | collective-permute-start | bytes 393224 | tf_op jit(solution)/shard_map/ppermute | solution.py:379
  81.4 2.6 %collective-permute-start.12 = (f32[2,64,256]{2,1,0:T(8,128)S(1)}, f32[2,64,256]{2,1,0:T(8,128)S(1)}, u32[]{:S(2)}, u32[]{:S(2)}) collective-permute-start(f32[2,64,256]{2,1,0:T(8,128)S(1)} %get-tuple-element.53), channel_id=1, source_target_pairs={{0,2},{2,0},{4,6},{6,4},{9,11},{11,9},{13,15},{15,13},{16,18},{18,... | collective-permute-start | bytes 393224 | tf_op jit(solution)/shard_map/ppermute | solution.py:379
  84.0 5.4 %collective-permute-start.13 = (f32[2,64,256]{2,1,0:T(8,128)S(1)}, f32[2,64,256]{2,1,0:T(8,128)S(1)}, u32[]{:S(2)}, u32[]{:S(2)}) collective-permute-start(f32[2,64,256]{2,1,0:T(8,128)S(1)} %get-tuple-element.52), channel_id=1, source_target_pairs={{0,4},{2,6},{4,0},{6,2},{9,13},{11,15},{13,9},{15,11},{16,20},{18,... | collective-permute-start | bytes 393224 | tf_op jit(solution)/shard_map/ppermute | solution.py:379
  89.4 2.1 %collective-permute-start.14 = (f32[2,64,256]{2,1,0:T(8,128)S(1)}, f32[2,64,256]{2,1,0:T(8,128)S(1)}, u32[]{:S(2)}, u32[]{:S(2)}) collective-permute-start(f32[2,64,256]{2,1,0:T(8,128)S(1)} %get-tuple-element.51), channel_id=1, source_target_pairs={{0,6},{2,4},{4,2},{6,0},{9,15},{11,13},{13,11},{15,9},{16,22},{18,... | collective-permute-start | bytes 393224 | tf_op jit(solution)/shard_map/ppermute | solution.py:379
  91.7 2.1 %collective-permute-done.13.refs_6_ = f32[2,64,256]{2,1,0:T(8,128)S(1)} collective-permute-done((f32[2,64,256]{2,1,0:T(8,128)S(1)}, f32[2,64,256]{2,1,0:T(8,128)S(1)}, u32[]{:S(2)}, u32[]{:S(2)}) %collective-permute-start.13) | collective-permute-done | bytes 131104 | tf_op jit(solution)/shard_map/ppermute | solution.py:379
  93.7 4.3 %collective-permute-done.14.refs_7_ = f32[2,64,256]{2,1,0:T(8,128)S(1)} collective-permute-done((f32[2,64,256]{2,1,0:T(8,128)S(1)}, f32[2,64,256]{2,1,0:T(8,128)S(1)}, u32[]{:S(2)}, u32[]{:S(2)}) %collective-permute-start.14) | collective-permute-done | bytes 131104 | tf_op jit(solution)/shard_map/ppermute | solution.py:379
  98.1 2.5 %collective-permute-start.15 = (f32[4,2,64,256]{3,2,1,0:T(8,128)S(1)}, f32[4,2,64,256]{3,2,1,0:T(8,128)S(1)}, u32[]{:S(2)}, u32[]{:S(2)}) collective-permute-start(f32[4,2,64,256]{3,2,1,0:T(8,128)S(1)} %maximum_select_fusion), channel_id=1, source_target_pairs={{0,16},{2,18},{4,20},{6,22},{9,25},{11,27},{13,29},{15,31},{16,0},... | collective-permute-start | bytes 1572872 | tf_op jit(solution)/shard_map/ppermute | solution.py:379
  101.0 8.3 %collective-permute-done.15.refs_8_ = f32[4,2,64,256]{3,2,1,0:T(8,128)S(1)} collective-permute-done((f32[4,2,64,256]{3,2,1,0:T(8,128)S(1)}, f32[4,2,64,256]{3,2,1,0:T(8,128)S(1)}, u32[]{:S(2)}, u32[]{:S(2)}) %collective-permute-start.15) | collective-permute-done | bytes 524320 | tf_op jit(solution)/shard_map/ppermute | solution.py:379
  109.2 1.2 %shard_map.68 = f32[8,2,64,256]{3,2,1,0:T(8,128)S(1)} custom-call(s32[2]{0:T(128)S(1)} %pad_add_fusion.place, f32[8,8]{1,0:T(8,128)S(1)} %stack.60.weight, f32[2,64,256]{2,1,0:T(8,128)S(1)} %get-tuple-element.58.refs_0_, f32[2,64,256]{2,1,0:T(8,128)S(1)} %collective-permute-done.8.refs_1_, f32[2,64,256]{2,1,0:T(8,128)S(1)} %collective-permute-done.9.refs_2_, ...), custom_call_target="tpu_custom_call" | custom-call | tf_op jit(solution)/shard_map/pallas_call | solution.py:440
  110.4 1.4 %collective-permute-start.16 = (f32[8,2,64,256]{3,2,1,0:T(8,128)S(1)}, f32[8,2,64,256]{3,2,1,0:T(8,128)S(1)}, u32[]{:S(2)}, u32[]{:S(2)}) collective-permute-start(f32[8,2,64,256]{3,2,1,0:T(8,128)S(1)} %shard_map.68), channel_id=1, source_target_pairs={{0,1},{2,3},{4,5},{6,7},{9,8},{11,10},{13,12},{15,14},{16,17},{18,... | collective-permute-start | bytes 3145736 | tf_op jit(solution)/shard_map/ppermute | solution.py:379
  111.8 2.2 %collective-permute-done.16 = f32[8,2,64,256]{3,2,1,0:T(8,128)S(1)} collective-permute-done((f32[8,2,64,256]{3,2,1,0:T(8,128)S(1)}, f32[8,2,64,256]{3,2,1,0:T(8,128)S(1)}, u32[]{:S(2)}, u32[]{:S(2)}) %collective-permute-start.16) | collective-permute-done | bytes 1048608 | tf_op jit(solution)/shard_map/ppermute | solution.py:379
  (34 shorter events, 5.1 us)
Async XLA Ops:
  0.2 0.7 copy-start.3
  0.8 1.2 %copy-start = (f32[2,1,2,256,256]{4,3,2,1,0:T(8,128)S(1)}, f32[2,1,2,256,256]{4,3,2,1,0:T(8,128)}, u32[]{:S(2)}) copy-start(f32[2,1,2,256,256]{4,3,2,1,0:T(8,128)} %param.9) | copy-start | bytes 3145732
  2.1 1.0 copy-start.1
  3.1 12.1 %copy-start.2 = (f32[1,1,2,256,256]{4,3,2,1,0:T(8,128)S(1)}, f32[1,1,2,256,256]{4,3,2,1,0:T(8,128)}, u32[]{:S(2)}) copy-start(f32[1,1,2,256,256]{4,3,2,1,0:T(8,128)} %param.8) | copy-start | bytes 1572868
  3.8 11.4 %collective-permute-start = (f32[2,256,256]{2,1,0:T(8,128)S(1)}, f32[2,256,256]{2,1,0:T(8,128)S(1)}, u32[]{:S(2)}, u32[]{:S(2)}) collective-permute-start(f32[2,256,256]{2,1,0:T(8,128)S(1)} %get-tuple-element.28), channel_id=1, source_target_pairs={{1,9},{3,11},{5,13},{7,15},{8,0},{10,2},{12,4},{14,6},{17,25},{19,... | collective-permute-start | bytes 1572872 | tf_op jit(solution)/shard_map/ppermute | solution.py:379
  5.1 12.0 %collective-permute-start.3 = (f32[2,256,256]{2,1,0:T(8,128)S(1)}, f32[2,256,256]{2,1,0:T(8,128)S(1)}, u32[]{:S(2)}, u32[]{:S(2)}) collective-permute-start(f32[2,256,256]{2,1,0:T(8,128)S(1)} %get-tuple-element.28), channel_id=1, source_target_pairs={{0,16},{2,18},{4,20},{6,22},{9,25},{11,27},{13,29},{15,31},{16,0},... | collective-permute-start | bytes 1572872 | tf_op jit(solution)/shard_map/ppermute | solution.py:379
  15.2 11.1 %collective-permute-start.1 = (f32[2,256,256]{2,1,0:T(8,128)S(1)}, f32[2,256,256]{2,1,0:T(8,128)S(1)}, u32[]{:S(2)}, u32[]{:S(2)}) collective-permute-start(f32[2,256,256]{2,1,0:T(8,128)S(1)} %bitcast.35), channel_id=1, source_target_pairs={{8,0},{10,2},{12,4},{14,6},{17,25},{19,27},{21,29},{23,31},{24,16}... | collective-permute-start | bytes 1572872 | tf_op jit(solution)/shard_map/ppermute | solution.py:379
  17.1 11.1 %collective-permute-start.4 = (f32[2,256,256]{2,1,0:T(8,128)S(1)}, f32[2,256,256]{2,1,0:T(8,128)S(1)}, u32[]{:S(2)}, u32[]{:S(2)}) collective-permute-start(f32[2,256,256]{2,1,0:T(8,128)S(1)} %collective-permute-done), channel_id=1, source_target_pairs={{0,16},{2,18},{4,20},{6,22},{9,25},{11,27},{13,29},{15,31},{16,0},... | collective-permute-start | bytes 1572872 | tf_op jit(solution)/shard_map/ppermute | solution.py:379
  28.2 11.1 %collective-permute-start.5 = (f32[2,256,256]{2,1,0:T(8,128)S(1)}, f32[2,256,256]{2,1,0:T(8,128)S(1)}, u32[]{:S(2)}, u32[]{:S(2)}) collective-permute-start(f32[2,256,256]{2,1,0:T(8,128)S(1)} %get-tuple-element.32), channel_id=1, source_target_pairs={{0,16},{2,18},{4,20},{6,22},{9,25},{11,27},{13,29},{15,31},{16,0},... | collective-permute-start | bytes 1572872 | tf_op jit(solution)/shard_map/ppermute | solution.py:379
  32.1 11.1 %collective-permute-start.2 = (f32[2,256,256]{2,1,0:T(8,128)S(1)}, f32[2,256,256]{2,1,0:T(8,128)S(1)}, u32[]{:S(2)}, u32[]{:S(2)}) collective-permute-start(f32[2,256,256]{2,1,0:T(8,128)S(1)} %get-tuple-element.30.b_own), channel_id=1, source_target_pairs={{1,9},{3,11},{5,13},{7,15},{8,0},{10,2},{12,4},{14,6},{17,25},{19,... | collective-permute-start | bytes 1572872 | tf_op jit(solution)/shard_map/ppermute | solution.py:379
  39.2 13.2 %collective-permute-start.6 = (f32[2,256,256]{2,1,0:T(8,128)S(1)}, f32[2,256,256]{2,1,0:T(8,128)S(1)}, u32[]{:S(2)}, u32[]{:S(2)}) collective-permute-start(f32[2,256,256]{2,1,0:T(8,128)S(1)} %get-tuple-element.33), channel_id=1, source_target_pairs={{16,0},{18,2},{20,4},{22,6},{25,9},{27,11},{29,13},{31,15}} | collective-permute-start | bytes 1572872 | tf_op jit(solution)/shard_map/ppermute | solution.py:379
  58.5 10.5 %collective-permute-start.7 = (f32[2,256,256]{2,1,0:T(8,128)S(1)}, f32[2,256,256]{2,1,0:T(8,128)S(1)}, u32[]{:S(2)}, u32[]{:S(2)}) collective-permute-start(f32[2,256,256]{2,1,0:T(8,128)S(1)} %get-tuple-element.39), channel_id=1, source_target_pairs={{0,9},{2,11},{4,13},{6,15},{9,0},{11,2},{13,4},{15,6},{16,25},{18,... | collective-permute-start | bytes 1572872 | tf_op jit(solution)/shard_map/ppermute | solution.py:379
  69.0 12.2 %collective-permute-start.11 = (f32[2,256,256]{2,1,0:T(8,128)S(1)}, f32[2,256,256]{2,1,0:T(8,128)S(1)}, u32[]{:S(2)}, u32[]{:S(2)}) collective-permute-start(f32[2,256,256]{2,1,0:T(8,128)S(1)} %get-tuple-element.48), channel_id=1, source_target_pairs={{0,9},{2,11},{4,13},{6,15},{9,0},{11,2},{13,4},{15,6},{16,25},{18,... | collective-permute-start | bytes 1572872 | tf_op jit(solution)/shard_map/ppermute | solution.py:379
  71.1 18.3 %collective-permute-start.8 = (f32[2,64,256]{2,1,0:T(8,128)S(1)}, f32[2,64,256]{2,1,0:T(8,128)S(1)}, u32[]{:S(2)}, u32[]{:S(2)}) collective-permute-start(f32[2,64,256]{2,1,0:T(8,128)S(1)} %get-tuple-element.57), channel_id=1, source_target_pairs={{0,2},{2,0},{4,6},{6,4},{9,11},{11,9},{13,15},{15,13},{16,18},{18,... | collective-permute-start | bytes 393224 | tf_op jit(solution)/shard_map/ppermute | solution.py:379
  74.6 17.0 %collective-permute-start.9 = (f32[2,64,256]{2,1,0:T(8,128)S(1)}, f32[2,64,256]{2,1,0:T(8,128)S(1)}, u32[]{:S(2)}, u32[]{:S(2)}) collective-permute-start(f32[2,64,256]{2,1,0:T(8,128)S(1)} %get-tuple-element.56), channel_id=1, source_target_pairs={{0,4},{2,6},{4,0},{6,2},{9,13},{11,15},{13,9},{15,11},{16,20},{18,... | collective-permute-start | bytes 393224 | tf_op jit(solution)/shard_map/ppermute | solution.py:379
  79.1 12.5 %collective-permute-start.10 = (f32[2,64,256]{2,1,0:T(8,128)S(1)}, f32[2,64,256]{2,1,0:T(8,128)S(1)}, u32[]{:S(2)}, u32[]{:S(2)}) collective-permute-start(f32[2,64,256]{2,1,0:T(8,128)S(1)} %get-tuple-element.55), channel_id=1, source_target_pairs={{0,6},{2,4},{4,2},{6,0},{9,15},{11,13},{13,11},{15,9},{16,22},{18,... | collective-permute-start | bytes 393224 | tf_op jit(solution)/shard_map/ppermute | solution.py:379
  81.4 10.2 %collective-permute-start.12 = (f32[2,64,256]{2,1,0:T(8,128)S(1)}, f32[2,64,256]{2,1,0:T(8,128)S(1)}, u32[]{:S(2)}, u32[]{:S(2)}) collective-permute-start(f32[2,64,256]{2,1,0:T(8,128)S(1)} %get-tuple-element.53), channel_id=1, source_target_pairs={{0,2},{2,0},{4,6},{6,4},{9,11},{11,9},{13,15},{15,13},{16,18},{18,... | collective-permute-start | bytes 393224 | tf_op jit(solution)/shard_map/ppermute | solution.py:379
  84.0 7.6 %copy-start.5 = (s32[4]{0:T(128)S(1)}, s32[4]{0:T(128)}, u32[]{:S(2)}) copy-start(s32[4]{0:T(128)} %param.10) | copy-start | bytes 52
  84.0 9.7 %collective-permute-start.13 = (f32[2,64,256]{2,1,0:T(8,128)S(1)}, f32[2,64,256]{2,1,0:T(8,128)S(1)}, u32[]{:S(2)}, u32[]{:S(2)}) collective-permute-start(f32[2,64,256]{2,1,0:T(8,128)S(1)} %get-tuple-element.52), channel_id=1, source_target_pairs={{0,4},{2,6},{4,0},{6,2},{9,13},{11,15},{13,9},{15,11},{16,20},{18,... | collective-permute-start | bytes 393224 | tf_op jit(solution)/shard_map/ppermute | solution.py:379
  89.4 8.7 %collective-permute-start.14 = (f32[2,64,256]{2,1,0:T(8,128)S(1)}, f32[2,64,256]{2,1,0:T(8,128)S(1)}, u32[]{:S(2)}, u32[]{:S(2)}) collective-permute-start(f32[2,64,256]{2,1,0:T(8,128)S(1)} %get-tuple-element.51), channel_id=1, source_target_pairs={{0,6},{2,4},{4,2},{6,0},{9,15},{11,13},{13,11},{15,9},{16,22},{18,... | collective-permute-start | bytes 393224 | tf_op jit(solution)/shard_map/ppermute | solution.py:379
  98.1 2.5 %copy-start.4 = (f32[2,4]{1,0:T(2,128)S(1)}, f32[2,4]{1,0:T(2,128)}, u32[]{:S(2)}) copy-start(f32[2,4]{1,0:T(2,128)} %param.11) | copy-start | bytes 100
  98.1 11.1 %collective-permute-start.15 = (f32[4,2,64,256]{3,2,1,0:T(8,128)S(1)}, f32[4,2,64,256]{3,2,1,0:T(8,128)S(1)}, u32[]{:S(2)}, u32[]{:S(2)}) collective-permute-start(f32[4,2,64,256]{3,2,1,0:T(8,128)S(1)} %maximum_select_fusion), channel_id=1, source_target_pairs={{0,16},{2,18},{4,20},{6,22},{9,25},{11,27},{13,29},{15,31},{16,0},... | collective-permute-start | bytes 1572872 | tf_op jit(solution)/shard_map/ppermute | solution.py:379
  110.4 3.6 %collective-permute-start.16 = (f32[8,2,64,256]{3,2,1,0:T(8,128)S(1)}, f32[8,2,64,256]{3,2,1,0:T(8,128)S(1)}, u32[]{:S(2)}, u32[]{:S(2)}) collective-permute-start(f32[8,2,64,256]{3,2,1,0:T(8,128)S(1)} %shard_map.68), channel_id=1, source_target_pairs={{0,1},{2,3},{4,5},{6,7},{9,8},{11,10},{13,12},{15,14},{16,17},{18,... | collective-permute-start | bytes 3145736 | tf_op jit(solution)/shard_map/ppermute | solution.py:379

commit v3 on v2

--- a/solution.py
+++ b/solution.py
@@ -135,41 +135,38 @@
     return halves(pair[0]), halves(pair[1])
 
 
-def left_side(operand):
-    (rh, rl), (ih, il) = operand
-    return jnp.concatenate([rh, ih, rl, il, rh, ih], axis=1)
+def three_terms(left, high, low, axis):
+    (rh, rl), (ih, il) = left
+    top = jnp.concatenate([rh, ih], axis=1)
+    both = jnp.concatenate([top, jnp.concatenate([rl, il], axis=1)], axis=0)
+    numbers = (((1,), (axis,)), ((), ()))
+    main = lax.dot_general(both, high, numbers, preferred_element_type=jnp.float32)
+    rest = lax.dot_general(top, low, numbers, preferred_element_type=jnp.float32)
+    width = rh.shape[0]
+    out = main[:width] + main[width:] + rest
+    return out[:, :width], out[:, width:]
 
 
 def mul(left, right):
     (rh, rl), (ih, il) = right
-    high_r, low_r = jnp.concatenate([rh, -ih], axis=0), jnp.concatenate([rl, -il], axis=0)
-    high_i, low_i = jnp.concatenate([ih, rh], axis=0), jnp.concatenate([il, rl], axis=0)
-    rhs = jnp.concatenate(
-        [
-            jnp.concatenate([high_r, high_r, low_r], axis=0),
-            jnp.concatenate([high_i, high_i, low_i], axis=0),
-        ],
-        axis=1,
-    )
-    out = jnp.dot(left_side(left), rhs, preferred_element_type=jnp.float32)
-    width = rh.shape[0]
-    return out[:, :width], out[:, width:]
+
+    def grid(real, imag):
+        return jnp.concatenate(
+            [jnp.concatenate([real, imag], axis=1), jnp.concatenate([-imag, real], axis=1)], axis=0
+        )
+
+    return three_terms(left, grid(rh, ih), grid(rl, il), 0)
 
 
 def mul_adjoint(left, right):
     (rh, rl), (ih, il) = right
-    rhs = jnp.concatenate(
-        [
-            jnp.concatenate([rh, ih, rh, ih, rl, il], axis=1),
-            jnp.concatenate([-ih, rh, -ih, rh, -il, rl], axis=1),
-        ],
-        axis=0,
-    )
-    out = lax.dot_general(
-        left_side(left), rhs, (((1,), (1,)), ((), ())), preferred_element_type=jnp.float32
-    )
-    width = rh.shape[0]
-    return out[:, :width], out[:, width:]
+
+    def grid(real, imag):
+        return jnp.concatenate(
+            [jnp.concatenate([real, imag], axis=1), jnp.concatenate([-imag, real], axis=1)], axis=0
+        )
+
+    return three_terms(left, grid(rh, ih), grid(rl, il), 1)
 
 
 def adjoint_form(pair):
@@ -270,55 +267,57 @@
         write(k_ref, mul(adjoint, form(right)))
 
 
-def upper_kernel(
-    place, b_own, b_x, b_y, b_far, c_own, c_x, c_last, g2_ref, p2_ref, q2_ref, k2_ref,
-    keep_ref, send_ref, y2_ref,
+def backward_kernel(
+    place, b_own, b_x, b_y, b_far, c_own, c_x, c_last,
+    g0_ref, g1_ref, p1_ref, q1_ref, k1_ref, g2_ref, p2_ref, q2_ref, k2_ref,
+    keep_ref, give_ref,
 ):
     y, x = place[0], place[1]
+
+    def finish(slab, full):
+        keep_ref[slab] = jnp.where(x == 0, full[0], full[1])
+        give_ref[slab] = jnp.where(x == 0, full[1], full[0])
+
     coupling = choose(y == 0, read(c_last), choose(x == 1, read(c_own), read(c_x)))
     green2 = read(g2_ref)
     form2 = form(green2)
     mat = minus(pick_block(y, x, 3, b_own, b_x, b_y, b_far), left_term(coupling, form2))
     green3 = inverse(mat)
+    finish(3, green3)
     inner = mul(form(green3), form(coupling))
     y3_form = form(mul(adjoint_form(coupling), form(inner)))
     y2 = add(read(k2_ref), mul(form(read(q2_ref)), form(mul(y3_form, form(read(p2_ref))))))
-    write(y2_ref, y2)
-    full2 = add(green2, mul(form2, form(mul(y3_form, form2))))
-    write(keep_ref, choose(x == 0, full2, green3))
-    write(send_ref, choose(x == 0, green3, full2))
-
-
-def lower_kernel(place, y2_ref, g1_ref, p1_ref, q1_ref, k1_ref, g0_ref, keep_ref, send_ref):
-    x = place[1]
+    finish(2, add(green2, mul(form2, form(mul(y3_form, form2)))))
     green1 = read(g1_ref)
     form1 = form(green1)
-    y2_form = form(read(y2_ref))
+    y2_form = form(y2)
     y1 = add(read(k1_ref), mul(form(read(q1_ref)), form(mul(y2_form, form(read(p1_ref))))))
-    full1 = add(green1, mul(form1, form(mul(y2_form, form1))))
+    finish(1, add(green1, mul(form1, form(mul(y2_form, form1)))))
     green0 = read(g0_ref)
     form0 = form(green0)
-    full0 = add(green0, mul(form0, form(mul(form(y1), form0))))
-    write(keep_ref, choose(x == 0, full0, full1))
-    write(send_ref, choose(x == 0, full1, full0))
-
-
-def mix_kernel(place, weight, *refs):
-    *parts, other_ref, out_ref = refs
-    slots = len(parts) // 2
-    rows = parts[0].shape[1]
-    upper = place[0] == 1
-    step = 8
-    for part in range(2):
-        for row in range(0, rows, step):
-            here = (part, slice(row, row + step), slice(None))
-            values = [jnp.where(upper, parts[i][here], parts[slots + i][here]) for i in range(slots)]
-            values += [other_ref[(i, *here)] for i in range(slots)]
-            for energy in range(out_ref.shape[0]):
-                total = weight[energy, 0] * values[0]
-                for slot in range(1, len(values)):
-                    total = total + weight[energy, slot] * values[slot]
-                out_ref[energy, part, row : row + step, :] = total
+    finish(0, add(green0, mul(form0, form(mul(form(y1), form0)))))
+
+
+def mix_kernel(phonon, parts_ref, out_ref):
+    slots, rows, _ = parts_ref.shape
+    energies = out_ref.shape[0]
+    planes, step = slots // 4, 8
+
+    def source(slot):
+        return 2 * (slot % planes) + slot // planes // 2
+
+    for row in range(0, rows, step):
+        here = slice(row, row + step)
+        values = [None] * energies
+        for slot in range(slots):
+            value = parts_ref[slot, here, :]
+            held = values[source(slot)]
+            values[source(slot)] = value if held is None else held + value
+        for energy in range(energies):
+            total = phonon[energy, 0] * values[0]
+            for other in range(1, energies):
+                total = total + phonon[energy, other] * values[other]
+            out_ref[energy, here, :] = total
 
 
 def prepare_kernel(place, scale, onsite_ref, hop_ref, sigma_ref, own_ref, other_ref):
@@ -332,13 +331,12 @@
         ref[1] = jnp.where(eye, ETA, 0.0) - hop_ref[1] - sigma_ref[local, 1]
 
 
-def call(kernel, place, arrays, count, products):
-    shape = jax.ShapeDtypeStruct(arrays[0].shape, jnp.float32)
+def call(kernel, place, arrays, shape, count, products):
     width = arrays[0].shape[-1]
     vmem = pl.BlockSpec(memory_space=pltpu.VMEM)
     return pl.pallas_call(
         kernel,
-        out_shape=[shape] * count,
+        out_shape=[jax.ShapeDtypeStruct(shape, jnp.float32)] * count,
         in_specs=[pl.BlockSpec(memory_space=pltpu.SMEM)] + [vmem] * len(arrays),
         out_specs=[vmem] * count,
         compiler_params=pltpu.CompilerParams(vmem_limit_bytes=VMEM_BYTES),
@@ -372,8 +370,8 @@
     x_feed_c = [(device(a, b, c, 1 - b), device(a, 1 - b, c, 1 - b)) for a, b, c in chips if a + b > 0]
     y_pass = [(device(a, b, c, b), device(1 - a, b, c, b)) for a, b, c in chips]
     y_down = [(device(a, b, c, b), device(1 - a, b, c, b)) for a, b, c in chips if a == 1]
-    x_swap = [(device(a, b, c, b), device(a, 1 - b, c, 1 - b)) for a, b, c in chips]
-    core = [(device(a, b, c, b), device(a, b, c, 1 - b)) for a, b, c in chips]
+    siblings = [(device(a, b, c, d), device(a, b, c, 1 - d)) for a, b, c in chips for d in range(2)]
+    gift = [(device(a, b, c, b), device(a, b, c, 1 - b)) for a, b, c in chips]
 
     def send(value, pairs):
         return lax.ppermute(value, axes, pairs)
@@ -396,55 +394,38 @@
 
     coupling = couple[0, 0]
     b_far_sent = send(b_other, x_feed)
+    c_x = send(coupling, x_feed_c)
     b_y = send(b_other, y_pass)
-    c_x = send(after(coupling, b_far_sent), x_feed_c)
+    b_x = send(after(b_own, c_x), x_feed)
     b_far = send(after(b_far_sent, b_y), y_pass)
-    b_x = send(after(b_own, c_x), x_feed)
-    c_third = send(after(jnp.where(x != y, coupling, c_x), b_far), y_pass)
+    c_third = send(jnp.where(x != y, coupling, c_x), y_pass)
     c_last = send(after(jnp.where(x == 1, coupling, c_x), c_third), y_down)
 
     blocks = (b_own, b_x, b_y, b_far)
-    g0, g1, p1, q1, k1, g2, p2, q2, k2 = call(
-        forward_kernel, place, (*blocks, coupling, c_x, c_third), 9, 16
-    )
-    keep_up, send_up, y2 = call(
-        upper_kernel, place, (*blocks, coupling, c_x, c_last, g2, p2, q2, k2), 3, 10
-    )
-    got_up = send(send_up, x_swap)
-    keep_low, send_low = call(lower_kernel, place, (y2, g1, p1, q1, k1, g0), 2, 6)
-    got_low = send(after(send_low, got_up), x_swap)
+    shape = (2, width, width)
+    chain = call(forward_kernel, place, (*blocks, coupling, c_x, c_third), shape, 9, 16)
+    shape = (4, width, width)
+    keep, give = call(
+        backward_kernel, place, (*blocks, coupling, c_x, c_last, *chain), shape, 2, 16
+    )
+    half = jnp.where(active, keep, send(give, gift))
 
     rows = width // energy_count
-
-    def over_planes(value):
-        parts = []
-        for flip in range(energy_count):
-            piece = lax.dynamic_slice_in_dim(value, (z ^ flip) * rows, rows, axis=1)
-            if flip:
-                pairs = [(device(a, b, c, b), device(a, b, c ^ flip, b)) for a, b, c in chips]
-                piece = send(piece, pairs)
-            parts.append(piece)
-        return parts
-
-    up = over_planes(keep_up + got_up)
-    low = over_planes(keep_low + got_low)
-    other = send(jnp.where(y == 0, jnp.stack(up), jnp.stack(low)), y_pass)
-
+    slots = 4 * energy_count
+    parts = lax.all_to_all(
+        half.reshape(slots, rows, width), ("slab", "energy"), 0, 0, tiled=True
+    )
     phonon = phonon_matrix(shifts, mode_weight, total) / mom_count
-    columns = [
-        lax.dynamic_index_in_dim(phonon, (z ^ flip) * e_local + local, 1, keepdims=False)
-        for local in (y, 1 - y)
-        for flip in range(energy_count)
-    ]
-    weight = jnp.stack(columns, axis=1)
     mixed = pl.pallas_call(
         mix_kernel,
-        out_shape=jax.ShapeDtypeStruct((total, 2, rows, width), jnp.float32),
-        in_specs=[smem, smem] + [vmem] * (2 * energy_count + 1),
+        out_shape=jax.ShapeDtypeStruct((total, rows, width), jnp.float32),
+        in_specs=[smem, vmem],
         out_specs=vmem,
         compiler_params=pltpu.CompilerParams(vmem_limit_bytes=VMEM_BYTES),
-    )(place, weight, *up, *low, other)
-    result = jnp.where(active, mixed, send(mixed, core))
+    )(phonon, parts)
+    other = send(mixed, siblings)
+    mine = jnp.arange(2)[:, None, None] == k
+    result = jnp.where(mine, mixed[:, None], other[:, None])
     return result[:, None]
 
 

time: 116 us -> 98.4 us (0.85)
  starting transfers between devices: 45.9 us -> 24.5 us
  local copies, waits for them, and re-layouts: 3.23 us -> 5.68 us
  waiting for transfers between devices: 43 us -> 44.8 us
    ppermute x17 -> x9, starting transfers between devices: 45.9 us -> 17.9 us  [send(): return lax.ppermute(value, axes, pairs)]
    all_to_all x0 -> x1, waiting for transfers between devices: none -> 27.2 us  [owner_body(): lax.all_to_all(half.reshape(slots, rows, width), ('slab', 'energy'), 0, 0...]
    ppermute x17 -> x9, waiting for transfers between devices: 43 us -> 17.6 us  [send(): return lax.ppermute(value, axes, pairs)]
    all_to_all x0 -> x1, starting transfers between devices: none -> 6.57 us  [owner_body(): lax.all_to_all(half.reshape(slots, rows, width), ('slab', 'energy'), 0, 0...]
    unnamed x12 -> x20, local copies, waits for them, and re-layouts: 2.96 us -> 5.68 us
    select_n x2 -> x3, other arithmetic: 0.16 us -> 2.34 us  [the longest x1 1.15 us: owner_body(): result = jnp.where(mine, mixed[:, None], other[:, None])]
    pallas_call x4 -> x3, Pallas kernels: 20.2 us -> 19.2 us  [the longest x2 18.3 us: call(): pl.pallas_call(kernel, out_shape=[jax.ShapeDtypeStruct(shape, jnp.float32...]
  transfers between devices with their start and end apart: 17 -> 10, of which waited for: 11 -> 8; matrix products, arithmetic and copies ran while one was open for 1% -> 0% of each run, Pallas kernels for 11% -> 10%
where the time goes in v3:
time: 98.4 us; the launch traced here: 97.8 us
  waiting for transfers between devices  44.8 us (46%)
  starting transfers between devices  24.5 us (25%)
  Pallas kernels  19.9 us (20%)
  local copies, waits for them, and re-layouts  5.68 us (6%)
  other arithmetic  2.66 us (3%)
    all_to_all x1, waiting for transfers between devices, owner_body(): lax.all_to_all(half.reshape(slots, rows, width), ('slab', 'energy'), 0, 0...  27.2 us
    pallas_call x2, Pallas kernels, call(): pl.pallas_call(kernel, out_shape=[jax.ShapeDtypeStruct(shape, jnp.float32...  18.3 us
    ppermute x9, starting transfers between devices, send(): return lax.ppermute(value, axes, pairs)  17.9 us
    ppermute x9, waiting for transfers between devices, send(): return lax.ppermute(value, axes, pairs)  17.6 us
    all_to_all x1, starting transfers between devices, owner_body(): lax.all_to_all(half.reshape(slots, rows, width), ('slab', 'energy'), 0, 0...  6.57 us
    unnamed x20, local copies, waits for them, and re-layouts  5.68 us
  transfers between devices with their start and end apart: 10, of which 8 were waited for; matrix products, arithmetic and copies ran while one was open for 0% of the time, Pallas kernels for 10%

profile of v3, /device:TPU:0, one launch (start us, length us, event | category | flops | bytes accessed | tf_op | source)
XLA Modules:
  0.0 97.8 jit_solution(10622422823882969179)
XLA Ops:
  0.0 1.3 %collective-permute-start = (f32[2,256,256]{2,1,0:T(8,128)}, f32[2,256,256]{2,1,0:T(8,128)S(1)}, u32[]{:S(2)}, u32[]{:S(2)}) collective-permute-start(f32[2,256,256]{2,1,0:T(8,128)} %bitcast.16), channel_id=1, source_target_pairs={{8,0},{10,2},{12,4},{14,6},{17,25},{19,27},{21,29},{23,31},{24,16}... | collective-permute-start | bytes 1572872 | tf_op jit(solution)/shard_map/ppermute | solution.py:377
  1.4 0.1 multiply_add_fusion.scale
  1.5 0.7 copy-done.3
  2.1 1.2 %copy-done = f32[2,1,2,256,256]{4,3,2,1,0:T(8,128)S(1)} copy-done((f32[2,1,2,256,256]{4,3,2,1,0:T(8,128)S(1)}, f32[2,1,2,256,256]{4,3,2,1,0:T(8,128)}, u32[]{:S(2)}) %copy-start) | copy-done | bytes 1048600
  3.4 1.0 %copy-done.1 = f32[1,1,2,256,256]{4,3,2,1,0:T(8,128)S(1)} copy-done((f32[1,1,2,256,256]{4,3,2,1,0:T(8,128)S(1)}, f32[1,1,2,256,256]{4,3,2,1,0:T(8,128)}, u32[]{:S(2)}) %copy-start.1) | copy-done | bytes 524312
  4.4 0.7 shard_map.64
  5.1 4.9 %collective-permute-start.2 = (f32[2,256,256]{2,1,0:T(8,128)S(1)}, f32[2,256,256]{2,1,0:T(8,128)S(1)}, u32[]{:S(2)}, u32[]{:S(2)}) collective-permute-start(f32[2,256,256]{2,1,0:T(8,128)S(1)} %get-tuple-element.23), channel_id=1, source_target_pairs={{0,16},{2,18},{4,20},{6,22},{9,25},{11,27},{13,29},{15,31},{16,0},... | collective-permute-start | bytes 1572872 | tf_op jit(solution)/shard_map/ppermute | solution.py:377
  10.0 1.3 %collective-permute-start.3 = (f32[2,256,256]{2,1,0:T(8,128)S(1)}, f32[2,256,256]{2,1,0:T(8,128)S(1)}, u32[]{:S(2)}, u32[]{:S(2)}) collective-permute-start(f32[2,256,256]{2,1,0:T(8,128)S(1)} %get-tuple-element.23), channel_id=1, source_target_pairs={{1,9},{3,11},{5,13},{7,15},{8,0},{10,2},{12,4},{14,6},{17,25},{19,... | collective-permute-start | bytes 1572872 | tf_op jit(solution)/shard_map/ppermute | solution.py:377
  11.3 0.3 collective-permute-done.c_x
  11.6 0.1 broadcast_select_fusion.2
  11.7 4.6 %collective-permute-start.5 = (f32[2,256,256]{2,1,0:T(8,128)S(1)}, f32[2,256,256]{2,1,0:T(8,128)S(1)}, u32[]{:S(2)}, u32[]{:S(2)}) collective-permute-start(f32[2,256,256]{2,1,0:T(8,128)S(1)} %get-tuple-element.37), channel_id=1, source_target_pairs={{0,16},{2,18},{4,20},{6,22},{9,25},{11,27},{13,29},{15,31},{16,0},... | collective-permute-start | bytes 1572872 | tf_op jit(solution)/shard_map/ppermute | solution.py:377
  16.3 0.9 collective-permute-done.2.b_y
  17.1 3.9 %collective-permute-done.3 = f32[2,256,256]{2,1,0:T(8,128)S(1)} collective-permute-done((f32[2,256,256]{2,1,0:T(8,128)S(1)}, f32[2,256,256]{2,1,0:T(8,128)S(1)}, u32[]{:S(2)}, u32[]{:S(2)}) %collective-permute-start.3) | collective-permute-done | bytes 524320 | tf_op jit(solution)/shard_map/ppermute | solution.py:377
  21.1 1.9 %collective-permute-start.4 = (f32[2,256,256]{2,1,0:T(8,128)S(1)}, f32[2,256,256]{2,1,0:T(8,128)S(1)}, u32[]{:S(2)}, u32[]{:S(2)}) collective-permute-start(f32[2,256,256]{2,1,0:T(8,128)S(1)} %collective-permute-done.3), channel_id=1, source_target_pairs={{0,16},{2,18},{4,20},{6,22},{9,25},{11,27},{13,29},{15,31},{16,0},... | collective-permute-start | bytes 1572872 | tf_op jit(solution)/shard_map/ppermute | solution.py:377
  23.0 1.3 %collective-permute-start.1 = (f32[2,256,256]{2,1,0:T(8,128)S(1)}, f32[2,256,256]{2,1,0:T(8,128)S(1)}, u32[]{:S(2)}, u32[]{:S(2)}) collective-permute-start(f32[2,256,256]{2,1,0:T(8,128)S(1)} %get-tuple-element.22.b_own), channel_id=1, source_target_pairs={{1,9},{3,11},{5,13},{7,15},{8,0},{10,2},{12,4},{14,6},{17,25},{19,... | collective-permute-start | bytes 1572872 | tf_op jit(solution)/shard_map/ppermute | solution.py:377
  24.3 1.3 %collective-permute-start.6 = (f32[2,256,256]{2,1,0:T(8,128)S(1)}, f32[2,256,256]{2,1,0:T(8,128)S(1)}, u32[]{:S(2)}, u32[]{:S(2)}) collective-permute-start(f32[2,256,256]{2,1,0:T(8,128)S(1)} %get-tuple-element.25), channel_id=1, source_target_pairs={{16,0},{18,2},{20,4},{22,6},{25,9},{27,11},{29,13},{31,15}} | collective-permute-start | bytes 1572872 | tf_op jit(solution)/shard_map/ppermute | solution.py:377
  25.6 6.5 %collective-permute-done.4.b_far = f32[2,256,256]{2,1,0:T(8,128)S(1)} collective-permute-done((f32[2,256,256]{2,1,0:T(8,128)S(1)}, f32[2,256,256]{2,1,0:T(8,128)S(1)}, u32[]{:S(2)}, u32[]{:S(2)}) %collective-permute-start.4) | collective-permute-done | bytes 524320 | tf_op jit(solution)/shard_map/ppermute | solution.py:377
  32.1 1.9 %collective-permute-done.1.b_x = f32[2,256,256]{2,1,0:T(8,128)S(1)} collective-permute-done((f32[2,256,256]{2,1,0:T(8,128)S(1)}, f32[2,256,256]{2,1,0:T(8,128)S(1)}, u32[]{:S(2)}, u32[]{:S(2)}) %collective-permute-start.1) | collective-permute-done | bytes 524320 | tf_op jit(solution)/shard_map/ppermute | solution.py:377
  34.1 9.3 %shard_map.65 = (f32[2,256,256]{2,1,0:T(8,128)S(1)}, f32[2,256,256]{2,1,0:T(8,128)S(1)}, f32[2,256,256]{2,1,0:T(8,128)S(1)}, f32[2,256,256]{2,1,0:T(8,128)S(1)},...) custom-call(s32[2]{0:T(128)S(1)} %pad_add_fusion.place, ...), custom_call_target="tpu_custom_call" | custom-call | flops 4831838208 | bytes 8388608 | tf_op jit(solution)/shard_map/pallas_call | solution.py:337
  43.4 1.0 %copy-done.5 = f32[2,256,256]{2,1,0:T(8,128)S(1)} copy-done((f32[2,256,256]{2,1,0:T(8,128)S(1)}, f32[2,256,256]{2,1,0:T(8,128)}, u32[]{:S(2)}) %copy-start.5) | copy-done | bytes 524312
  44.5 1.0 %copy-done.7 = f32[2,256,256]{2,1,0:T(8,128)S(1)} copy-done((f32[2,256,256]{2,1,0:T(8,128)S(1)}, f32[2,256,256]{2,1,0:T(8,128)}, u32[]{:S(2)}) %copy-start.7) | copy-done | bytes 524312
  45.5 9.0 %shard_map.66 = (f32[4,256,256]{2,1,0:T(8,128)S(1)}, f32[4,256,256]{2,1,0:T(8,128)S(1)}) custom-call(s32[2]{0:T(128)S(1)} %pad_add_fusion.place, f32[2,256,256]{2,1,0:T(8,128)S(1)} %copy-done.5, f32[2,256,256]{2,1,0:T(8,128)S(1)} %collective-permute-done.1.b_x, f32[2,256,256]{2,1,0:T(8,128)S(1)} %copy-done.7, ...), custom_call_target="tpu_custom_call" | custom-call | flops 4831838208 | bytes 9437184 | tf_op jit(solution)/shard_map/pallas_call | solution.py:337
  54.5 1.4 %collective-permute-start.7 = (f32[4,256,256]{2,1,0:T(8,128)S(1)}, f32[4,256,256]{2,1,0:T(8,128)S(1)}, u32[]{:S(2)}, u32[]{:S(2)}) collective-permute-start(f32[4,256,256]{2,1,0:T(8,128)S(1)} %get-tuple-element.36), channel_id=1, source_target_pairs={{0,1},{2,3},{4,5},{6,7},{9,8},{11,10},{13,12},{15,14},{16,17},{18,... | collective-permute-start | bytes 3145736 | tf_op jit(solution)/shard_map/ppermute | solution.py:377
  55.8 2.2 %collective-permute-done.7 = f32[4,256,256]{2,1,0:T(8,128)S(1)} collective-permute-done((f32[4,256,256]{2,1,0:T(8,128)S(1)}, f32[4,256,256]{2,1,0:T(8,128)S(1)}, u32[]{:S(2)}, u32[]{:S(2)}) %collective-permute-start.7) | collective-permute-done | bytes 1048608 | tf_op jit(solution)/shard_map/ppermute | solution.py:377
  58.0 1.1 %broadcast_select_fusion.1 = f32[4,256,256]{2,1,0:T(8,128)} fusion(f32[4,256,256]{2,1,0:T(8,128)S(1)} %get-tuple-element.35, f32[4,256,256]{2,1,0:T(8,128)S(1)} %collective-permute-done.7, pred[]{:T(512)S(6)} %eq.51), kind=kLoop, calls=%fused_computation.1 | loop fusion | flops 262144 | bytes 3145729 | tf_op jit(solution)/shard_map/jit(_where)/select_n | solution.py:411
  59.1 6.6 %all-to-all-start = ((f32[16,64,256]{2,1,0:T(8,128)}), f32[16,64,256]{2,1,0:T(8,128)S(1)}, u32[]{:S(2)}, u32[]{:S(2)}) async-start(f32[16,64,256]{2,1,0:T(8,128)} %bitcast.9), calls=%async_computation | async-start | bytes 2097152 | tf_op jit(solution)/shard_map/all_to_all | solution.py:415
  65.8 0.6 copy-done.9
  66.5 0.1 add_reduce_fusion
  66.6 27.2 %all-to-all-done.parts_ref = f32[16,64,256]{2,1,0:T(8,128)S(1)} async-done(((f32[16,64,256]{2,1,0:T(8,128)}), f32[16,64,256]{2,1,0:T(8,128)S(1)}, u32[]{:S(2)}, u32[]{:S(2)}) %all-to-all-start) | async-done | bytes 1048608 | tf_op jit(solution)/shard_map/all_to_all | solution.py:415
  93.7 0.9 shard_map.67
  94.7 1.9 %collective-permute-done.8 = f32[8,64,256]{2,1,0:T(8,128)S(1)} collective-permute-done((f32[8,64,256]{2,1,0:T(8,128)S(1)}, f32[8,64,256]{2,1,0:T(8,128)S(1)}, u32[]{:S(2)}, u32[]{:S(2)}) %collective-permute-start.8) | collective-permute-done | bytes 524320 | tf_op jit(solution)/shard_map/ppermute | solution.py:377
  96.6 1.1 %broadcast_select_fusion = f32[8,1,2,64,256]{4,3,2,1,0:T(8,128)} fusion(f32[8,64,256]{2,1,0:T(8,128)S(1)} %collective-permute-done.8, f32[8,64,256]{2,1,0:T(8,128)S(1)} %shard_map.67, pred[2]{0:T(512)(128)(4,1)S(1)} %iota_compare_fusion.2), kind=kLoop, calls=%fused_computation | loop fusion | flops 262144 | bytes 2097154 | tf_op jit(solution)/shard_map/jit(_where)/select_n | solution.py:428
  (22 shorter events, 0.3 us)
Async XLA Ops:
  0.0 11.6 %collective-permute-start = (f32[2,256,256]{2,1,0:T(8,128)}, f32[2,256,256]{2,1,0:T(8,128)S(1)}, u32[]{:S(2)}, u32[]{:S(2)}) collective-permute-start(f32[2,256,256]{2,1,0:T(8,128)} %bitcast.16), channel_id=1, source_target_pairs={{8,0},{10,2},{12,4},{14,6},{17,25},{19,27},{21,29},{23,31},{24,16}... | collective-permute-start | bytes 1572872 | tf_op jit(solution)/shard_map/ppermute | solution.py:377
  1.5 0.7 copy-start.3
  2.1 1.2 %copy-start = (f32[2,1,2,256,256]{4,3,2,1,0:T(8,128)S(1)}, f32[2,1,2,256,256]{4,3,2,1,0:T(8,128)}, u32[]{:S(2)}) copy-start(f32[2,1,2,256,256]{4,3,2,1,0:T(8,128)} %param.9) | copy-start | bytes 3145732
  3.4 1.0 %copy-start.1 = (f32[1,1,2,256,256]{4,3,2,1,0:T(8,128)S(1)}, f32[1,1,2,256,256]{4,3,2,1,0:T(8,128)}, u32[]{:S(2)}) copy-start(f32[1,1,2,256,256]{4,3,2,1,0:T(8,128)} %param.7) | copy-start | bytes 1572868
  4.4 7.2 %copy-start.2 = (f32[1,1,2,256,256]{4,3,2,1,0:T(8,128)S(1)}, f32[1,1,2,256,256]{4,3,2,1,0:T(8,128)}, u32[]{:S(2)}) copy-start(f32[1,1,2,256,256]{4,3,2,1,0:T(8,128)} %param.8) | copy-start | bytes 1572868
  5.1 29.0 %copy-start.4 = (f32[2,256,256]{2,1,0:T(8,128)}, f32[2,256,256]{2,1,0:T(8,128)S(1)}, u32[]{:S(2)}) copy-start(f32[2,256,256]{2,1,0:T(8,128)S(1)} %get-tuple-element.22.b_own) | copy-start | bytes 1572868
  5.1 12.0 %collective-permute-start.2 = (f32[2,256,256]{2,1,0:T(8,128)S(1)}, f32[2,256,256]{2,1,0:T(8,128)S(1)}, u32[]{:S(2)}, u32[]{:S(2)}) collective-permute-start(f32[2,256,256]{2,1,0:T(8,128)S(1)} %get-tuple-element.23), channel_id=1, source_target_pairs={{0,16},{2,18},{4,20},{6,22},{9,25},{11,27},{13,29},{15,31},{16,0},... | collective-permute-start | bytes 1572872 | tf_op jit(solution)/shard_map/ppermute | solution.py:377
  10.0 11.1 %collective-permute-start.3 = (f32[2,256,256]{2,1,0:T(8,128)S(1)}, f32[2,256,256]{2,1,0:T(8,128)S(1)}, u32[]{:S(2)}, u32[]{:S(2)}) collective-permute-start(f32[2,256,256]{2,1,0:T(8,128)S(1)} %get-tuple-element.23), channel_id=1, source_target_pairs={{1,9},{3,11},{5,13},{7,15},{8,0},{10,2},{12,4},{14,6},{17,25},{19,... | collective-permute-start | bytes 1572872 | tf_op jit(solution)/shard_map/ppermute | solution.py:377
  11.7 12.6 %collective-permute-start.5 = (f32[2,256,256]{2,1,0:T(8,128)S(1)}, f32[2,256,256]{2,1,0:T(8,128)S(1)}, u32[]{:S(2)}, u32[]{:S(2)}) collective-permute-start(f32[2,256,256]{2,1,0:T(8,128)S(1)} %get-tuple-element.37), channel_id=1, source_target_pairs={{0,16},{2,18},{4,20},{6,22},{9,25},{11,27},{13,29},{15,31},{16,0},... | collective-permute-start | bytes 1572872 | tf_op jit(solution)/shard_map/ppermute | solution.py:377
  17.1 26.3 %copy-start.6 = (f32[2,256,256]{2,1,0:T(8,128)}, f32[2,256,256]{2,1,0:T(8,128)S(1)}, u32[]{:S(2)}) copy-start(f32[2,256,256]{2,1,0:T(8,128)S(1)} %collective-permute-done.2.b_y) | copy-start | bytes 1572868
  21.1 11.1 %collective-permute-start.4 = (f32[2,256,256]{2,1,0:T(8,128)S(1)}, f32[2,256,256]{2,1,0:T(8,128)S(1)}, u32[]{:S(2)}, u32[]{:S(2)}) collective-permute-start(f32[2,256,256]{2,1,0:T(8,128)S(1)} %collective-permute-done.3), channel_id=1, source_target_pairs={{0,16},{2,18},{4,20},{6,22},{9,25},{11,27},{13,29},{15,31},{16,0},... | collective-permute-start | bytes 1572872 | tf_op jit(solution)/shard_map/ppermute | solution.py:377
  23.0 11.1 %collective-permute-start.1 = (f32[2,256,256]{2,1,0:T(8,128)S(1)}, f32[2,256,256]{2,1,0:T(8,128)S(1)}, u32[]{:S(2)}, u32[]{:S(2)}) collective-permute-start(f32[2,256,256]{2,1,0:T(8,128)S(1)} %get-tuple-element.22.b_own), channel_id=1, source_target_pairs={{1,9},{3,11},{5,13},{7,15},{8,0},{10,2},{12,4},{14,6},{17,25},{19,... | collective-permute-start | bytes 1572872 | tf_op jit(solution)/shard_map/ppermute | solution.py:377
  24.3 19.1 %collective-permute-start.6 = (f32[2,256,256]{2,1,0:T(8,128)S(1)}, f32[2,256,256]{2,1,0:T(8,128)S(1)}, u32[]{:S(2)}, u32[]{:S(2)}) collective-permute-start(f32[2,256,256]{2,1,0:T(8,128)S(1)} %get-tuple-element.25), channel_id=1, source_target_pairs={{16,0},{18,2},{20,4},{22,6},{25,9},{27,11},{29,13},{31,15}} | collective-permute-start | bytes 1572872 | tf_op jit(solution)/shard_map/ppermute | solution.py:377
  43.4 1.0 %copy-start.5 = (f32[2,256,256]{2,1,0:T(8,128)S(1)}, f32[2,256,256]{2,1,0:T(8,128)}, u32[]{:S(2)}) copy-start(f32[2,256,256]{2,1,0:T(8,128)} %copy-done.4) | copy-start | bytes 1572868
  44.4 1.0 %copy-start.7 = (f32[2,256,256]{2,1,0:T(8,128)S(1)}, f32[2,256,256]{2,1,0:T(8,128)}, u32[]{:S(2)}) copy-start(f32[2,256,256]{2,1,0:T(8,128)} %copy-done.6) | copy-start | bytes 1572868
  54.5 3.6 %collective-permute-start.7 = (f32[4,256,256]{2,1,0:T(8,128)S(1)}, f32[4,256,256]{2,1,0:T(8,128)S(1)}, u32[]{:S(2)}, u32[]{:S(2)}) collective-permute-start(f32[4,256,256]{2,1,0:T(8,128)S(1)} %get-tuple-element.36), channel_id=1, source_target_pairs={{0,1},{2,3},{4,5},{6,7},{9,8},{11,10},{13,12},{15,14},{16,17},{18,... | collective-permute-start | bytes 3145736 | tf_op jit(solution)/shard_map/ppermute | solution.py:377
  59.1 6.6 %copy-start.8 = (f32[2,4]{1,0:T(2,128)S(1)}, f32[2,4]{1,0:T(2,128)}, u32[]{:S(2)}) copy-start(f32[2,4]{1,0:T(2,128)} %param.11) | copy-start | bytes 100
  59.1 34.6 %all-to-all-start = ((f32[16,64,256]{2,1,0:T(8,128)}), f32[16,64,256]{2,1,0:T(8,128)S(1)}, u32[]{:S(2)}, u32[]{:S(2)}) async-start(f32[16,64,256]{2,1,0:T(8,128)} %bitcast.9), calls=%async_computation | async-start | bytes 2097152 | tf_op jit(solution)/shard_map/all_to_all | solution.py:415
  65.7 0.7 copy-start.9
  94.6 2.0 %collective-permute-start.8 = (f32[8,64,256]{2,1,0:T(8,128)S(1)}, f32[8,64,256]{2,1,0:T(8,128)S(1)}, u32[]{:S(2)}, u32[]{:S(2)}) collective-permute-start(f32[8,64,256]{2,1,0:T(8,128)S(1)} %shard_map.67), channel_id=1, source_target_pairs={{0,1},{1,0},{2,3},{3,2},{4,5},{5,4},{6,7},{7,6},{8,9},{9,8},{10,11... | collective-permute-start | bytes 1572872 | tf_op jit(solution)/shard_map/ppermute | solution.py:377

commit v4 on v3

--- a/solution.py
+++ b/solution.py
@@ -125,6 +125,9 @@
 VMEM_BYTES = 24 * 1024 * 1024
 
 
+BLOCKS = 2
+
+
 def halves(value):
     high = value.astype(jnp.bfloat16)
     low = (value - high.astype(jnp.float32)).astype(jnp.bfloat16)
@@ -132,94 +135,100 @@
 
 
 def form(pair):
-    return halves(pair[0]), halves(pair[1])
-
-
-def three_terms(left, high, low, axis):
-    (rh, rl), (ih, il) = left
-    top = jnp.concatenate([rh, ih], axis=1)
-    both = jnp.concatenate([top, jnp.concatenate([rl, il], axis=1)], axis=0)
+    return halves(pair[0]), halves(pair[1]), halves(pair[0] + pair[1])
+
+
+def adjoint_form(pair):
+    return halves(pair[0]), halves(-pair[1]), halves(pair[0] - pair[1])
+
+
+def real_dot(left, right, axis):
+    rows = left[0].shape[0]
     numbers = (((1,), (axis,)), ((), ()))
-    main = lax.dot_general(both, high, numbers, preferred_element_type=jnp.float32)
-    rest = lax.dot_general(top, low, numbers, preferred_element_type=jnp.float32)
-    width = rh.shape[0]
-    out = main[:width] + main[width:] + rest
-    return out[:, :width], out[:, width:]
-
-
-def mul(left, right):
-    (rh, rl), (ih, il) = right
-
-    def grid(real, imag):
-        return jnp.concatenate(
-            [jnp.concatenate([real, imag], axis=1), jnp.concatenate([-imag, real], axis=1)], axis=0
-        )
-
-    return three_terms(left, grid(rh, ih), grid(rl, il), 0)
-
-
-def mul_adjoint(left, right):
-    (rh, rl), (ih, il) = right
-
-    def grid(real, imag):
-        return jnp.concatenate(
-            [jnp.concatenate([real, imag], axis=1), jnp.concatenate([-imag, real], axis=1)], axis=0
-        )
-
-    return three_terms(left, grid(rh, ih), grid(rl, il), 1)
-
-
-def adjoint_form(pair):
-    real = pair[0].T
-    imag = -pair[1].T
-    return form((real, imag))
-
-
-def add(left, right):
-    return left[0] + right[0], left[1] + right[1]
+    both = jnp.concatenate([left[0], left[1]], axis=0)
+    main = lax.dot_general(both, right[0], numbers, preferred_element_type=jnp.float32)
+    rest = lax.dot_general(left[0], right[1], numbers, preferred_element_type=jnp.float32)
+    return main[:rows] + main[rows:] + rest
+
+
+def mul(left, right, axis=0):
+    first = real_dot(left[0], right[0], axis)
+    second = real_dot(left[1], right[1], axis)
+    third = real_dot(left[2], right[2], axis)
+    return first - second, third - first - second
+
+
+def mul_twice(blocks, right, last, axis=0):
+    inner = [mul(block, right) for block in blocks]
+    return [mul(form(block), last, axis) for block in inner]
+
+
+def split_rows(pair):
+    size = pair[0].shape[0] // BLOCKS
+    return [tuple(part[b * size : (b + 1) * size] for part in pair) for b in range(BLOCKS)]
+
+
+def join_rows(blocks):
+    return tuple(jnp.concatenate([block[i] for block in blocks], axis=0) for i in range(2))
+
+
+def form_rows(forms):
+    return tuple(
+        tuple(jnp.concatenate([f[plane][term] for f in forms], axis=0) for term in range(2))
+        for plane in range(3)
+    )
 
 
 def read(ref):
     return ref[0], ref[1]
 
 
-def write(ref, pair):
-    ref[0] = pair[0]
-    ref[1] = pair[1]
+def write(ref, blocks):
+    size = blocks[0][0].shape[0]
+    for b, block in enumerate(blocks):
+        ref[0, b * size : (b + 1) * size] = block[0]
+        ref[1, b * size : (b + 1) * size] = block[1]
 
 
 def choose(cond, left, right):
     return jnp.where(cond, left[0], right[0]), jnp.where(cond, left[1], right[1])
 
 
-def inverse(mat):
-    width = mat[0].shape[0]
-    eye = lax.broadcasted_iota(jnp.int32, (width, width), 0) == lax.broadcasted_iota(
-        jnp.int32, (width, width), 1
-    )
-    on_r = jnp.where(eye, mat[0], 0.0)
-    on_i = jnp.where(eye, mat[1], 0.0)
-    row_r = jnp.sum(on_r, axis=0, keepdims=True)
-    row_i = jnp.sum(on_i, axis=0, keepdims=True)
-    col_r = jnp.sum(on_r, axis=1, keepdims=True)
-    col_i = jnp.sum(on_i, axis=1, keepdims=True)
+def times(left, right):
+    return left[0] * right[0] - left[1] * right[1], left[0] * right[1] + left[1] * right[0]
+
+
+def inverse(mats):
+    size, width = mats[0][0].shape
 
     def invert(real, imag):
         denom = real * real + imag * imag
         return real / denom, -imag / denom
 
-    xr, xi = invert(row_r, row_i)
-    yr, yi = invert(col_r, col_i)
-    off_r = jnp.where(eye, 0.0, mat[0])
-    off_i = jnp.where(eye, 0.0, mat[1])
-    e_r = off_r * xr - off_i * xi
-    e_i = off_r * xi + off_i * xr
-    e_form = form((e_r, e_i))
-    sq = mul(e_form, e_form)
-    cube = mul(e_form, form(sq))
-    t_r = jnp.where(eye, 1.0, 0.0) - e_r + sq[0] - cube[0]
-    t_i = sq[1] - e_i - cube[1]
-    return yr * t_r - yi * t_i, yr * t_i + yi * t_r
+    eyes, scaled = [], []
+    across = (0.0, 0.0)
+    for b, mat in enumerate(mats):
+        eye = lax.broadcasted_iota(jnp.int32, (size, width), 0) + b * size == (
+            lax.broadcasted_iota(jnp.int32, (size, width), 1)
+        )
+        on = [jnp.where(eye, part, 0.0) for part in mat]
+        off = [jnp.where(eye, 0.0, part) for part in mat]
+        across = tuple(
+            total + jnp.sum(part, axis=0, keepdims=True) for total, part in zip(across, on)
+        )
+        down = invert(*(jnp.sum(part, axis=1, keepdims=True) for part in on))
+        eyes.append(eye)
+        scaled.append(times(down, off))
+    forms = [form(block) for block in scaled]
+    right = form_rows(forms)
+    squares = [mul(block, right) for block in forms]
+    cubes = [mul(form(block), right) for block in squares]
+    factor = invert(*across)
+    out = []
+    for eye, one, two, three in zip(eyes, scaled, squares, cubes):
+        real = jnp.where(eye, 1.0, 0.0) - one[0] + two[0] - three[0]
+        out.append(times((real, two[1] - one[1] - three[1]), factor))
+    return out
 
 
 def pick_block(y, x, slab, own, x_side, y_side, far):
@@ -230,72 +239,72 @@
     return choose(same_y, near, away)
 
 
-def left_term(coupling, green_form):
-    c_form = form(coupling)
-    inner = mul_adjoint(green_form, c_form)
-    return mul(c_form, form(inner))
-
-
-def minus(left, right):
-    return left[0] - right[0], left[1] - right[1]
-
-
-def forward_kernel(
-    place, b_own, b_x, b_y, b_far, c_own, c_x, c_third,
-    g0_ref, g1_ref, p1_ref, q1_ref, k1_ref, g2_ref, p2_ref, q2_ref, k2_ref,
+def forward(block, coupling, green_form):
+    lefts = [form(part) for part in split_rows(coupling)]
+    terms = mul_twice(lefts, green_form, adjoint_form(coupling), axis=1)
+    mats = [
+        (part[0] - term[0], part[1] - term[1]) for part, term in zip(split_rows(block), terms)
+    ]
+    return inverse(mats)
+
+
+def couple_down(coupling, full_form):
+    lefts = [form(part) for part in split_rows((coupling[0].T, -coupling[1].T))]
+    return mul_twice(lefts, full_form, form(coupling))
+
+
+def complete(greens, coupled_form):
+    forms = [form(block) for block in greens]
+    extra = mul_twice(forms, coupled_form, form_rows(forms))
+    return [(g[0] + e[0], g[1] + e[1]) for g, e in zip(greens, extra)]
+
+
+def whole_form(blocks):
+    return form_rows([form(block) for block in blocks])
+
+
+def first_kernel(place, b_own, b_x, b_y, b_far, g_ref):
+    y, x = place[0], place[1]
+    write(g_ref, inverse(split_rows(pick_block(y, x, 0, b_own, b_x, b_y, b_far))))
+
+
+def middle_coupling(y, x, slab, c_own, c_one, c_two):
+    if slab == 1:
+        return choose(x == y, read(c_one), choose(x == 1, read(c_own), read(c_two)))
+    return choose(x == y, read(c_two), choose(x == 1, read(c_one), read(c_own)))
+
+
+def forward_kernel(place, b_own, b_x, b_y, b_far, c_own, c_one, c_two, g0_ref, g1_ref, g2_ref):
+    y, x = place[0], place[1]
+    green_form = form(read(g0_ref))
+    for slab, ref in ((1, g1_ref), (2, g2_ref)):
+        block = pick_block(y, x, slab, b_own, b_x, b_y, b_far)
+        greens = forward(block, middle_coupling(y, x, slab, c_own, c_one, c_two), green_form)
+        write(ref, greens)
+        green_form = whole_form(greens)
+
+
+def backward_kernel(
+    place, b_own, b_x, b_y, b_far, c_own, c_one, c_two, c_last, c_last_x,
+    g0_ref, g1_ref, g2_ref, keep_ref, give_ref,
 ):
     y, x = place[0], place[1]
-    blocks = (b_own, b_x, b_y, b_far)
-    green = inverse(pick_block(y, x, 0, *blocks))
-    write(g0_ref, green)
-    couplings = (
-        choose(y == 0, choose(x == 1, read(c_own), read(c_x)), read(c_third)),
-        choose(y == 1, choose(x == 0, read(c_own), read(c_x)), read(c_third)),
-    )
-    outs = ((g1_ref, p1_ref, q1_ref, k1_ref), (g2_ref, p2_ref, q2_ref, k2_ref))
-    for slab in (1, 2):
-        coupling = couplings[slab - 1]
-        mat = minus(pick_block(y, x, slab, *blocks), left_term(coupling, form(green)))
-        green = inverse(mat)
-        g_form = form(green)
-        adjoint = adjoint_form(coupling)
-        right = mul(g_form, form(coupling))
-        g_ref, p_ref, q_ref, k_ref = outs[slab - 1]
-        write(g_ref, green)
-        write(p_ref, right)
-        write(q_ref, mul(adjoint, g_form))
-        write(k_ref, mul(adjoint, form(right)))
-
-
-def backward_kernel(
-    place, b_own, b_x, b_y, b_far, c_own, c_x, c_last,
-    g0_ref, g1_ref, p1_ref, q1_ref, k1_ref, g2_ref, p2_ref, q2_ref, k2_ref,
-    keep_ref, give_ref,
-):
-    y, x = place[0], place[1]
-
-    def finish(slab, full):
+
+    def finish(slab, blocks):
+        full = join_rows(blocks)
         keep_ref[slab] = jnp.where(x == 0, full[0], full[1])
         give_ref[slab] = jnp.where(x == 0, full[1], full[0])
 
-    coupling = choose(y == 0, read(c_last), choose(x == 1, read(c_own), read(c_x)))
-    green2 = read(g2_ref)
-    form2 = form(green2)
-    mat = minus(pick_block(y, x, 3, b_own, b_x, b_y, b_far), left_term(coupling, form2))
-    green3 = inverse(mat)
-    finish(3, green3)
-    inner = mul(form(green3), form(coupling))
-    y3_form = form(mul(adjoint_form(coupling), form(inner)))
-    y2 = add(read(k2_ref), mul(form(read(q2_ref)), form(mul(y3_form, form(read(p2_ref))))))
-    finish(2, add(green2, mul(form2, form(mul(y3_form, form2)))))
-    green1 = read(g1_ref)
-    form1 = form(green1)
-    y2_form = form(y2)
-    y1 = add(read(k1_ref), mul(form(read(q1_ref)), form(mul(y2_form, form(read(p1_ref))))))
-    finish(1, add(green1, mul(form1, form(mul(y2_form, form1)))))
-    green0 = read(g0_ref)
-    form0 = form(green0)
-    finish(0, add(green0, mul(form0, form(mul(form(y1), form0)))))
+    coupling = choose(y == 0, read(c_last), choose(x == 0, read(c_last_x), read(c_own)))
+    block = pick_block(y, x, 3, b_own, b_x, b_y, b_far)
+    fulls = forward(block, coupling, form(read(g2_ref)))
+    finish(3, fulls)
+    for slab, ref in ((2, g2_ref), (1, g1_ref), (0, g0_ref)):
+        coupled = couple_down(coupling, whole_form(fulls))
+        fulls = complete(split_rows(read(ref)), whole_form(coupled))
+        finish(slab, fulls)
+        if slab:
+            coupling = middle_coupling(y, x, slab, c_own, c_one, c_two)
 
 
 def mix_kernel(phonon, parts_ref, out_ref):
@@ -366,18 +375,22 @@
         return ((2 * yy + xx) * energy_count + zz) * mom_count + kk
 
     chips = [(yy, xx, zz) for yy in range(2) for xx in range(2) for zz in range(energy_count)]
-    x_feed = [(device(a, b, c, 1 - b), device(a, 1 - b, c, 1 - b)) for a, b, c in chips]
-    x_feed_c = [(device(a, b, c, 1 - b), device(a, 1 - b, c, 1 - b)) for a, b, c in chips if a + b > 0]
-    y_pass = [(device(a, b, c, b), device(1 - a, b, c, b)) for a, b, c in chips]
-    y_down = [(device(a, b, c, b), device(1 - a, b, c, b)) for a, b, c in chips if a == 1]
+    to_x = [(device(a, b, c, 1 - b), device(a, 1 - b, c, 1 - b)) for a, b, c in chips]
+    to_y = [(device(a, b, c, b), device(1 - a, b, c, b)) for a, b, c in chips]
+    to_far = [(device(a, b, c, 1 - b), device(1 - a, 1 - b, c, 1 - b)) for a, b, c in chips]
+
+    def routes(*pairs):
+        return [
+            (device(*divmod(s, 2), zz, t % 2), device(*divmod(t, 2), zz, t % 2))
+            for s, t in pairs
+            for zz in range(energy_count)
+        ]
+
     siblings = [(device(a, b, c, d), device(a, b, c, 1 - d)) for a, b, c in chips for d in range(2)]
     gift = [(device(a, b, c, b), device(a, b, c, 1 - b)) for a, b, c in chips]
 
     def send(value, pairs):
         return lax.ppermute(value, axes, pairs)
-
-    def after(value, earlier):
-        return lax.optimization_barrier((value, earlier))[0]
 
     locals_ = jnp.stack([y, 1 - y])
     energies = -0.5 + ((z * e_local + locals_).astype(jnp.float32) + 0.5) / total
@@ -393,20 +406,22 @@
     )(place, energies, onsite[0], hop[0, 0], sigma_in[:, 0])
 
     coupling = couple[0, 0]
-    b_far_sent = send(b_other, x_feed)
-    c_x = send(coupling, x_feed_c)
-    b_y = send(b_other, y_pass)
-    b_x = send(after(b_own, c_x), x_feed)
-    b_far = send(after(b_far_sent, b_y), y_pass)
-    c_third = send(jnp.where(x != y, coupling, c_x), y_pass)
-    c_last = send(after(jnp.where(x == 1, coupling, c_x), c_third), y_down)
+    c_one = send(coupling, routes((1, 0), (1, 3), (2, 1)))
+    c_two = send(coupling, routes((1, 2), (2, 0), (2, 3)))
+    b_far = send(b_other, to_far)
+    b_y = send(b_other, to_y)
+    b_x = send(b_own, to_x)
+    c_last = send(coupling, routes((3, 0), (3, 1)))
+    c_last_x = send(coupling, routes((3, 2)))
 
     blocks = (b_own, b_x, b_y, b_far)
     shape = (2, width, width)
-    chain = call(forward_kernel, place, (*blocks, coupling, c_x, c_third), shape, 9, 16)
+    (g0,) = call(first_kernel, place, blocks, shape, 1, 2)
+    middle = (coupling, c_one, c_two)
+    g1, g2 = call(forward_kernel, place, (*blocks, *middle, g0), shape, 2, 8)
     shape = (4, width, width)
     keep, give = call(
-        backward_kernel, place, (*blocks, coupling, c_x, c_last, *chain), shape, 2, 16
+        backward_kernel, place, (*blocks, *middle, c_last, c_last_x, g0, g1, g2), shape, 2, 16
     )
     half = jnp.where(active, keep, send(give, gift))
 

time: 98.4 us -> 88.9 us (0.903)
  starting transfers between devices: 24.5 us -> 18.9 us
  Pallas kernels: 19.9 us -> 15.2 us
  waiting for transfers between devices: 44.8 us -> 47.9 us
  local copies, waits for them, and re-layouts: 5.68 us -> 3.59 us
    pallas_call x2 -> x3, Pallas kernels: 18.3 us -> 13.7 us  [call(): pl.pallas_call(kernel, out_shape=[jax.ShapeDtypeStruct(shape, jnp.float32...]
    ppermute x9, starting transfers between devices: 17.9 us -> 13.4 us  [send(): return lax.ppermute(value, axes, pairs)]
    ppermute x9, waiting for transfers between devices: 17.6 us -> 20.8 us  [send(): return lax.ppermute(value, axes, pairs)]
    unnamed x20 -> x12, local copies, waits for them, and re-layouts: 5.68 us -> 3.59 us
    all_to_all x1, starting transfers between devices: 6.57 us -> 5.48 us  [owner_body(): lax.all_to_all(half.reshape(slots, rows, width), ('slab', 'energy'), 0, 0...]
  transfers between devices with their start and end apart: 10 -> 10, of which waited for: 8 -> 7; matrix products, arithmetic and copies ran while one was open for 0% -> 0% of each run, Pallas kernels for 10% -> 7%
where the time goes in v4:
time: 88.9 us; the launch traced here: 88.5 us
  waiting for transfers between devices  47.9 us (54%)
  starting transfers between devices  18.9 us (21%)
  Pallas kernels  15.2 us (17%)
  local copies, waits for them, and re-layouts  3.59 us (4%)
  other arithmetic  2.57 us (3%)
    all_to_all x1, waiting for transfers between devices, owner_body(): lax.all_to_all(half.reshape(slots, rows, width), ('slab', 'energy'), 0, 0...  27.2 us
    ppermute x9, waiting for transfers between devices, send(): return lax.ppermute(value, axes, pairs)  20.8 us
    pallas_call x3, Pallas kernels, call(): pl.pallas_call(kernel, out_shape=[jax.ShapeDtypeStruct(shape, jnp.float32...  13.7 us
    ppermute x9, starting transfers between devices, send(): return lax.ppermute(value, axes, pairs)  13.4 us
    all_to_all x1, starting transfers between devices, owner_body(): lax.all_to_all(half.reshape(slots, rows, width), ('slab', 'energy'), 0, 0...  5.48 us
    unnamed x12, local copies, waits for them, and re-layouts  3.59 us
  transfers between devices with their start and end apart: 10, of which 7 were waited for; matrix products, arithmetic and copies ran while one was open for 0% of the time, Pallas kernels for 7%

profile of v4, /device:TPU:0, one launch (start us, length us, event | category | flops | bytes accessed | tf_op | source)
XLA Modules:
  0.0 88.5 jit_solution(17643014323199207132)
XLA Ops:
  0.0 0.1 pad_add_fusion.place
  0.1 0.1 multiply_add_fusion.scale
  0.2 0.7 copy-done.2
  0.8 1.2 %copy-done = f32[2,1,2,256,256]{4,3,2,1,0:T(8,128)S(1)} copy-done((f32[2,1,2,256,256]{4,3,2,1,0:T(8,128)S(1)}, f32[2,1,2,256,256]{4,3,2,1,0:T(8,128)}, u32[]{:S(2)}) %copy-start) | copy-done | bytes 1048600
  2.1 1.0 %copy-done.1 = f32[1,1,2,256,256]{4,3,2,1,0:T(8,128)S(1)} copy-done((f32[1,1,2,256,256]{4,3,2,1,0:T(8,128)S(1)}, f32[1,1,2,256,256]{4,3,2,1,0:T(8,128)}, u32[]{:S(2)}) %copy-start.1) | copy-done | bytes 524312
  3.1 0.7 shard_map.64
  3.8 1.3 %collective-permute-start = (f32[2,256,256]{2,1,0:T(8,128)S(1)}, f32[2,256,256]{2,1,0:T(8,128)S(1)}, u32[]{:S(2)}, u32[]{:S(2)}) collective-permute-start(f32[2,256,256]{2,1,0:T(8,128)S(1)} %get-tuple-element.11.b_own), channel_id=1, source_target_pairs={{1,9},{3,11},{5,13},{7,15},{8,0},{10,2},{12,4},{14,6},{17,25},{19,... | collective-permute-start | bytes 1572872 | tf_op jit(solution)/shard_map/ppermute | solution.py:393
  5.1 4.9 %collective-permute-start.1 = (f32[2,256,256]{2,1,0:T(8,128)S(1)}, f32[2,256,256]{2,1,0:T(8,128)S(1)}, u32[]{:S(2)}, u32[]{:S(2)}) collective-permute-start(f32[2,256,256]{2,1,0:T(8,128)S(1)} %get-tuple-element.12), channel_id=1, source_target_pairs={{0,16},{2,18},{4,20},{6,22},{9,25},{11,27},{13,29},{15,31},{16,0},... | collective-permute-start | bytes 1572872 | tf_op jit(solution)/shard_map/ppermute | solution.py:393
  10.0 1.3 %collective-permute-start.2 = (f32[2,256,256]{2,1,0:T(8,128)S(1)}, f32[2,256,256]{2,1,0:T(8,128)S(1)}, u32[]{:S(2)}, u32[]{:S(2)}) collective-permute-start(f32[2,256,256]{2,1,0:T(8,128)S(1)} %get-tuple-element.12), channel_id=1, source_target_pairs={{1,25},{3,27},{5,29},{7,31},{8,16},{10,18},{12,20},{14,22},{17,9},... | collective-permute-start | bytes 1572872 | tf_op jit(solution)/shard_map/ppermute | solution.py:393
  11.3 1.3 %collective-permute-start.3 = (f32[2,256,256]{2,1,0:T(8,128)S(1)}, f32[2,256,256]{2,1,0:T(8,128)S(1)}, u32[]{:S(2)}, u32[]{:S(2)}) collective-permute-start(f32[2,256,256]{2,1,0:T(8,128)S(1)} %bitcast.15), channel_id=1, source_target_pairs={{8,0},{10,2},{12,4},{14,6},{9,25},{11,27},{13,29},{15,31},{17,9},{... | collective-permute-start | bytes 1572872 | tf_op jit(solution)/shard_map/ppermute | solution.py:393
  12.6 1.3 %collective-permute-start.4 = (f32[2,256,256]{2,1,0:T(8,128)S(1)}, f32[2,256,256]{2,1,0:T(8,128)S(1)}, u32[]{:S(2)}, u32[]{:S(2)}) collective-permute-start(f32[2,256,256]{2,1,0:T(8,128)S(1)} %bitcast.16), channel_id=1, source_target_pairs={{8,16},{10,18},{12,20},{14,22},{16,0},{18,2},{20,4},{22,6},{17,25}... | collective-permute-start | bytes 1572872 | tf_op jit(solution)/shard_map/ppermute | solution.py:393
  13.9 1.3 %collective-permute-done.b_x = f32[2,256,256]{2,1,0:T(8,128)S(1)} collective-permute-done((f32[2,256,256]{2,1,0:T(8,128)S(1)}, f32[2,256,256]{2,1,0:T(8,128)S(1)}, u32[]{:S(2)}, u32[]{:S(2)}) %collective-permute-start) | collective-permute-done | bytes 524320 | tf_op jit(solution)/shard_map/ppermute | solution.py:393
  15.2 1.3 %collective-permute-start.5 = (f32[2,256,256]{2,1,0:T(8,128)S(1)}, f32[2,256,256]{2,1,0:T(8,128)S(1)}, u32[]{:S(2)}, u32[]{:S(2)}) collective-permute-start(f32[2,256,256]{2,1,0:T(8,128)S(1)} %bitcast.17), channel_id=1, source_target_pairs={{24,0},{26,2},{28,4},{30,6},{25,9},{27,11},{29,13},{31,15}} | collective-permute-start | bytes 1572872 | tf_op jit(solution)/shard_map/ppermute | solution.py:393
  16.4 5.8 %collective-permute-done.1.b_y = f32[2,256,256]{2,1,0:T(8,128)S(1)} collective-permute-done((f32[2,256,256]{2,1,0:T(8,128)S(1)}, f32[2,256,256]{2,1,0:T(8,128)S(1)}, u32[]{:S(2)}, u32[]{:S(2)}) %collective-permute-start.1) | collective-permute-done | bytes 524320 | tf_op jit(solution)/shard_map/ppermute | solution.py:393
  22.3 0.7 collective-permute-start.6
  23.0 1.6 %shard_map.65.g0_ref = f32[2,256,256]{2,1,0:T(8,128)S(1)} custom-call(s32[2]{0:T(128)S(1)} %pad_add_fusion.place, f32[2,256,256]{2,1,0:T(8,128)S(1)} %get-tuple-element.11.b_own, f32[2,256,256]{2,1,0:T(8,128)S(1)} %collective-permute-done.b_x, f32[2,256,256]{2,1,0:T(8,128)S(1)} %collective-permute-done.1.b_y, f32[2,256,256]{2,1,0:T(8,128)S(1)} %collective-permute-done.2.b_far), custom_call_target="tpu_custom_call" | custom-call | flops 603979776 | bytes 2621440 | tf_op jit(solution)/shard_map/pallas_call | solution.py:346
  24.5 1.9 %collective-permute-done.3.c_one = f32[2,256,256]{2,1,0:T(8,128)S(1)} collective-permute-done((f32[2,256,256]{2,1,0:T(8,128)S(1)}, f32[2,256,256]{2,1,0:T(8,128)S(1)}, u32[]{:S(2)}, u32[]{:S(2)}) %collective-permute-start.3) | collective-permute-done | bytes 524320 | tf_op jit(solution)/shard_map/ppermute | solution.py:393
  26.4 7.7 %collective-permute-done.4.c_two = f32[2,256,256]{2,1,0:T(8,128)S(1)} collective-permute-done((f32[2,256,256]{2,1,0:T(8,128)S(1)}, f32[2,256,256]{2,1,0:T(8,128)S(1)}, u32[]{:S(2)}, u32[]{:S(2)}) %collective-permute-start.4) | collective-permute-done | bytes 524320 | tf_op jit(solution)/shard_map/ppermute | solution.py:393
  34.1 4.6 %shard_map.66 = (f32[2,256,256]{2,1,0:T(8,128)S(1)}, f32[2,256,256]{2,1,0:T(8,128)S(1)}) custom-call(s32[2]{0:T(128)S(1)} %pad_add_fusion.place, f32[2,256,256]{2,1,0:T(8,128)S(1)} %get-tuple-element.11.b_own, f32[2,256,256]{2,1,0:T(8,128)S(1)} %collective-permute-done.b_x, f32[2,256,256]{2,1,0:T(8,128)S(1)} %collective-permute-done.1.b_y, ...), custom_call_target="tpu_custom_call" | custom-call | flops 2415919104 | bytes 5242880 | tf_op jit(solution)/shard_map/pallas_call | solution.py:346
  38.7 7.5 %shard_map.67 = (f32[4,256,256]{2,1,0:T(8,128)S(1)}, f32[4,256,256]{2,1,0:T(8,128)S(1)}) custom-call(s32[2]{0:T(128)S(1)} %pad_add_fusion.place, f32[2,256,256]{2,1,0:T(8,128)S(1)} %get-tuple-element.11.b_own, f32[2,256,256]{2,1,0:T(8,128)S(1)} %collective-permute-done.b_x, f32[2,256,256]{2,1,0:T(8,128)S(1)} %collective-permute-done.1.b_y, ...), custom_call_target="tpu_custom_call" | custom-call | flops 4831838208 | bytes 7340032 | tf_op jit(solution)/shard_map/pallas_call | solution.py:346
  46.2 1.4 %collective-permute-start.7 = (f32[4,256,256]{2,1,0:T(8,128)S(1)}, f32[4,256,256]{2,1,0:T(8,128)S(1)}, u32[]{:S(2)}, u32[]{:S(2)}) collective-permute-start(f32[4,256,256]{2,1,0:T(8,128)S(1)} %get-tuple-element.16), channel_id=1, source_target_pairs={{0,1},{2,3},{4,5},{6,7},{9,8},{11,10},{13,12},{15,14},{16,17},{18,... | collective-permute-start | bytes 3145736 | tf_op jit(solution)/shard_map/ppermute | solution.py:393
  47.6 2.2 %collective-permute-done.7 = f32[4,256,256]{2,1,0:T(8,128)S(1)} collective-permute-done((f32[4,256,256]{2,1,0:T(8,128)S(1)}, f32[4,256,256]{2,1,0:T(8,128)S(1)}, u32[]{:S(2)}, u32[]{:S(2)}) %collective-permute-start.7) | collective-permute-done | bytes 1048608 | tf_op jit(solution)/shard_map/ppermute | solution.py:393
  49.8 1.1 %broadcast_select_fusion.1 = f32[4,256,256]{2,1,0:T(8,128)} fusion(f32[4,256,256]{2,1,0:T(8,128)S(1)} %get-tuple-element.15, f32[4,256,256]{2,1,0:T(8,128)S(1)} %collective-permute-done.7, pred[]{:T(512)S(6)} %eq.48), kind=kLoop, calls=%fused_computation.1 | loop fusion | flops 262144 | bytes 3145729 | tf_op jit(solution)/shard_map/jit(_where)/select_n | solution.py:426
  50.9 5.5 %all-to-all-start = ((f32[16,64,256]{2,1,0:T(8,128)}), f32[16,64,256]{2,1,0:T(8,128)S(1)}, u32[]{:S(2)}, u32[]{:S(2)}) async-start(f32[16,64,256]{2,1,0:T(8,128)} %bitcast.9), calls=%async_computation | async-start | bytes 2097152 | tf_op jit(solution)/shard_map/all_to_all | solution.py:430
  56.4 0.6 copy-done.5
  57.1 0.1 iota_add_fusion
  57.1 0.1 add_reduce_fusion
  57.2 27.2 %all-to-all-done.parts_ref = f32[16,64,256]{2,1,0:T(8,128)S(1)} async-done(((f32[16,64,256]{2,1,0:T(8,128)}), f32[16,64,256]{2,1,0:T(8,128)S(1)}, u32[]{:S(2)}, u32[]{:S(2)}) %all-to-all-start) | async-done | bytes 1048608 | tf_op jit(solution)/shard_map/all_to_all | solution.py:430
  84.4 0.9 %shard_map.68 = f32[8,64,256]{2,1,0:T(8,128)S(1)} custom-call(f32[8,8]{1,0:T(8,128)S(1)} %broadcast_multiply_fusion.phonon, f32[16,64,256]{2,1,0:T(8,128)S(1)} %all-to-all-done.parts_ref), custom_call_target="tpu_custom_call" | custom-call | tf_op jit(solution)/shard_map/pallas_call | solution.py:434
  85.3 0.1 collective-permute-start.8
  85.4 1.9 %collective-permute-done.8 = f32[8,64,256]{2,1,0:T(8,128)S(1)} collective-permute-done((f32[8,64,256]{2,1,0:T(8,128)S(1)}, f32[8,64,256]{2,1,0:T(8,128)S(1)}, u32[]{:S(2)}, u32[]{:S(2)}) %collective-permute-start.8) | collective-permute-done | bytes 524320 | tf_op jit(solution)/shard_map/ppermute | solution.py:393
  87.3 1.1 %broadcast_select_fusion = f32[8,1,2,64,256]{4,3,2,1,0:T(8,128)} fusion(f32[8,64,256]{2,1,0:T(8,128)S(1)} %collective-permute-done.8, f32[8,64,256]{2,1,0:T(8,128)S(1)} %shard_map.68, pred[2]{0:T(512)(128)(4,1)S(1)} %iota_compare_fusion.2), kind=kLoop, calls=%fused_computation | loop fusion | flops 262144 | bytes 2097154 | tf_op jit(solution)/shard_map/jit(_where)/select_n | solution.py:443
  (14 shorter events, 0.1 us)
Async XLA Ops:
  0.2 0.7 copy-start.2
  0.8 1.2 %copy-start = (f32[2,1,2,256,256]{4,3,2,1,0:T(8,128)S(1)}, f32[2,1,2,256,256]{4,3,2,1,0:T(8,128)}, u32[]{:S(2)}) copy-start(f32[2,1,2,256,256]{4,3,2,1,0:T(8,128)} %param.9) | copy-start | bytes 3145732
  2.1 1.0 %copy-start.1 = (f32[1,1,2,256,256]{4,3,2,1,0:T(8,128)S(1)}, f32[1,1,2,256,256]{4,3,2,1,0:T(8,128)}, u32[]{:S(2)}) copy-start(f32[1,1,2,256,256]{4,3,2,1,0:T(8,128)} %param.7) | copy-start | bytes 1572868
  3.1 8.2 %copy-start.3 = (f32[1,1,2,256,256]{4,3,2,1,0:T(8,128)S(1)}, f32[1,1,2,256,256]{4,3,2,1,0:T(8,128)}, u32[]{:S(2)}) copy-start(f32[1,1,2,256,256]{4,3,2,1,0:T(8,128)} %param.8) | copy-start | bytes 1572868
  3.8 11.4 %collective-permute-start = (f32[2,256,256]{2,1,0:T(8,128)S(1)}, f32[2,256,256]{2,1,0:T(8,128)S(1)}, u32[]{:S(2)}, u32[]{:S(2)}) collective-permute-start(f32[2,256,256]{2,1,0:T(8,128)S(1)} %get-tuple-element.11.b_own), channel_id=1, source_target_pairs={{1,9},{3,11},{5,13},{7,15},{8,0},{10,2},{12,4},{14,6},{17,25},{19,... | collective-permute-start | bytes 1572872 | tf_op jit(solution)/shard_map/ppermute | solution.py:393
  5.1 17.2 %collective-permute-start.1 = (f32[2,256,256]{2,1,0:T(8,128)S(1)}, f32[2,256,256]{2,1,0:T(8,128)S(1)}, u32[]{:S(2)}, u32[]{:S(2)}) collective-permute-start(f32[2,256,256]{2,1,0:T(8,128)S(1)} %get-tuple-element.12), channel_id=1, source_target_pairs={{0,16},{2,18},{4,20},{6,22},{9,25},{11,27},{13,29},{15,31},{16,0},... | collective-permute-start | bytes 1572872 | tf_op jit(solution)/shard_map/ppermute | solution.py:393
  10.0 13.0 %collective-permute-start.2 = (f32[2,256,256]{2,1,0:T(8,128)S(1)}, f32[2,256,256]{2,1,0:T(8,128)S(1)}, u32[]{:S(2)}, u32[]{:S(2)}) collective-permute-start(f32[2,256,256]{2,1,0:T(8,128)S(1)} %get-tuple-element.12), channel_id=1, source_target_pairs={{1,25},{3,27},{5,29},{7,31},{8,16},{10,18},{12,20},{14,22},{17,9},... | collective-permute-start | bytes 1572872 | tf_op jit(solution)/shard_map/ppermute | solution.py:393
  11.3 15.2 %collective-permute-start.3 = (f32[2,256,256]{2,1,0:T(8,128)S(1)}, f32[2,256,256]{2,1,0:T(8,128)S(1)}, u32[]{:S(2)}, u32[]{:S(2)}) collective-permute-start(f32[2,256,256]{2,1,0:T(8,128)S(1)} %bitcast.15), channel_id=1, source_target_pairs={{8,0},{10,2},{12,4},{14,6},{9,25},{11,27},{13,29},{15,31},{17,9},{... | collective-permute-start | bytes 1572872 | tf_op jit(solution)/shard_map/ppermute | solution.py:393
  12.6 21.5 %collective-permute-start.4 = (f32[2,256,256]{2,1,0:T(8,128)S(1)}, f32[2,256,256]{2,1,0:T(8,128)S(1)}, u32[]{:S(2)}, u32[]{:S(2)}) collective-permute-start(f32[2,256,256]{2,1,0:T(8,128)S(1)} %bitcast.16), channel_id=1, source_target_pairs={{8,16},{10,18},{12,20},{14,22},{16,0},{18,2},{20,4},{22,6},{17,25}... | collective-permute-start | bytes 1572872 | tf_op jit(solution)/shard_map/ppermute | solution.py:393
  15.2 23.5 %collective-permute-start.5 = (f32[2,256,256]{2,1,0:T(8,128)S(1)}, f32[2,256,256]{2,1,0:T(8,128)S(1)}, u32[]{:S(2)}, u32[]{:S(2)}) collective-permute-start(f32[2,256,256]{2,1,0:T(8,128)S(1)} %bitcast.17), channel_id=1, source_target_pairs={{24,0},{26,2},{28,4},{30,6},{25,9},{27,11},{29,13},{31,15}} | collective-permute-start | bytes 1572872 | tf_op jit(solution)/shard_map/ppermute | solution.py:393
  22.3 16.4 %collective-permute-start.6 = (f32[2,256,256]{2,1,0:T(8,128)S(1)}, f32[2,256,256]{2,1,0:T(8,128)S(1)}, u32[]{:S(2)}, u32[]{:S(2)}) collective-permute-start(f32[2,256,256]{2,1,0:T(8,128)S(1)} %bitcast.18), channel_id=1, source_target_pairs={{24,16},{26,18},{28,20},{30,22}} | collective-permute-start | bytes 1572872 | tf_op jit(solution)/shard_map/ppermute | solution.py:393
  46.2 3.6 %collective-permute-start.7 = (f32[4,256,256]{2,1,0:T(8,128)S(1)}, f32[4,256,256]{2,1,0:T(8,128)S(1)}, u32[]{:S(2)}, u32[]{:S(2)}) collective-permute-start(f32[4,256,256]{2,1,0:T(8,128)S(1)} %get-tuple-element.16), channel_id=1, source_target_pairs={{0,1},{2,3},{4,5},{6,7},{9,8},{11,10},{13,12},{15,14},{16,17},{18,... | collective-permute-start | bytes 3145736 | tf_op jit(solution)/shard_map/ppermute | solution.py:393
  50.9 5.5 %copy-start.4 = (f32[2,4]{1,0:T(2,128)S(1)}, f32[2,4]{1,0:T(2,128)}, u32[]{:S(2)}) copy-start(f32[2,4]{1,0:T(2,128)} %param.11) | copy-start | bytes 100
  50.9 33.5 %all-to-all-start = ((f32[16,64,256]{2,1,0:T(8,128)}), f32[16,64,256]{2,1,0:T(8,128)S(1)}, u32[]{:S(2)}, u32[]{:S(2)}) async-start(f32[16,64,256]{2,1,0:T(8,128)} %bitcast.9), calls=%async_computation | async-start | bytes 2097152 | tf_op jit(solution)/shard_map/all_to_all | solution.py:430
  56.4 0.7 copy-start.5
  85.3 2.0 %collective-permute-start.8 = (f32[8,64,256]{2,1,0:T(8,128)S(1)}, f32[8,64,256]{2,1,0:T(8,128)S(1)}, u32[]{:S(2)}, u32[]{:S(2)}) collective-permute-start(f32[8,64,256]{2,1,0:T(8,128)S(1)} %shard_map.68), channel_id=1, source_target_pairs={{0,1},{1,0},{2,3},{3,2},{4,5},{5,4},{6,7},{7,6},{8,9},{9,8},{10,11... | collective-permute-start | bytes 1572872 | tf_op jit(solution)/shard_map/ppermute | solution.py:393

commit v5 on v4

--- a/solution.py
+++ b/solution.py
@@ -123,6 +123,7 @@
 
 
 VMEM_BYTES = 24 * 1024 * 1024
+ALL_VMEM_BYTES = 60 * 1024 * 1024
 
 
 BLOCKS = 2
@@ -268,26 +269,39 @@
     write(g_ref, inverse(split_rows(pick_block(y, x, 0, b_own, b_x, b_y, b_far))))
 
 
-def middle_coupling(y, x, slab, c_own, c_one, c_two):
+def two_halves(place, mine, theirs):
+    first = place[2] == 0
+    return tuple(
+        jnp.concatenate(
+            [jnp.where(first, mine[i], theirs[i]), jnp.where(first, theirs[i], mine[i])], axis=0
+        )
+        for i in range(2)
+    )
+
+
+def coupling_of(place, slab, c_own, *got):
+    y, x = place[0], place[1]
+    one, two, three = (two_halves(place, *got[i : i + 2]) for i in (0, 2, 4))
     if slab == 1:
-        return choose(x == y, read(c_one), choose(x == 1, read(c_own), read(c_two)))
-    return choose(x == y, read(c_two), choose(x == 1, read(c_one), read(c_own)))
-
-
-def forward_kernel(place, b_own, b_x, b_y, b_far, c_own, c_one, c_two, g0_ref, g1_ref, g2_ref):
+        return choose(x == y, one, choose(x == 1, read(c_own), two))
+    if slab == 2:
+        return choose(x == y, two, choose(x == 1, one, read(c_own)))
+    return choose(y == 0, choose(x == 0, three, two), choose(x == 0, one, read(c_own)))
+
+
+def forward_kernel(place, b_own, b_x, b_y, b_far, *refs):
+    *couplings, g0_ref, g1_ref, g2_ref = refs
     y, x = place[0], place[1]
     green_form = form(read(g0_ref))
     for slab, ref in ((1, g1_ref), (2, g2_ref)):
         block = pick_block(y, x, slab, b_own, b_x, b_y, b_far)
-        greens = forward(block, middle_coupling(y, x, slab, c_own, c_one, c_two), green_form)
+        greens = forward(block, coupling_of(place, slab, *couplings), green_form)
         write(ref, greens)
         green_form = whole_form(greens)
 
 
-def backward_kernel(
-    place, b_own, b_x, b_y, b_far, c_own, c_one, c_two, c_last, c_last_x,
-    g0_ref, g1_ref, g2_ref, keep_ref, give_ref,
-):
+def backward_kernel(place, b_own, b_x, b_y, b_far, *refs):
+    *couplings, g0_ref, g1_ref, g2_ref, keep_ref, give_ref = refs
     y, x = place[0], place[1]
 
     def finish(slab, blocks):
@@ -295,7 +309,7 @@
         keep_ref[slab] = jnp.where(x == 0, full[0], full[1])
         give_ref[slab] = jnp.where(x == 0, full[1], full[0])
 
-    coupling = choose(y == 0, read(c_last), choose(x == 0, read(c_last_x), read(c_own)))
+    coupling = coupling_of(place, 3, *couplings)
     block = pick_block(y, x, 3, b_own, b_x, b_y, b_far)
     fulls = forward(block, coupling, form(read(g2_ref)))
     finish(3, fulls)
@@ -304,7 +318,7 @@
         fulls = complete(split_rows(read(ref)), whole_form(coupled))
         finish(slab, fulls)
         if slab:
-            coupling = middle_coupling(y, x, slab, c_own, c_one, c_two)
+            coupling = coupling_of(place, slab, *couplings)
 
 
 def mix_kernel(phonon, parts_ref, out_ref):
@@ -329,15 +343,29 @@
             out_ref[energy, here, :] = total
 
 
-def prepare_kernel(place, scale, onsite_ref, hop_ref, sigma_ref, own_ref, other_ref):
-    width = hop_ref.shape[-1]
+def prepare_kernel(
+    place, scale, onsite_ref, hop_hbm, sigma_hbm, couple_hbm, other_ref, own_ref, part_ref,
+    hop_ref, sigma_ref, sems,
+):
+    width, rows = hop_ref.shape[-1], part_ref.shape[1]
+    order = (1 - place[0], place[0])
+    copies = [pltpu.make_async_copy(hop_hbm, hop_ref, sems.at[0])]
+    for i, local in enumerate(order):
+        copies.append(pltpu.make_async_copy(sigma_hbm.at[local], sigma_ref.at[i], sems.at[1 + i]))
+    start = pl.multiple_of(place[2] * rows, rows)
+    copies.append(pltpu.make_async_copy(couple_hbm.at[:, pl.ds(start, rows), :], part_ref, sems.at[3]))
+    for copy in copies:
+        copy.start()
     eye = lax.broadcasted_iota(jnp.int32, (width, width), 0) == lax.broadcasted_iota(
         jnp.int32, (width, width), 1
     )
-    for ref, local, energy in ((other_ref, 1 - place[0], scale[1]), (own_ref, place[0], scale[0])):
-        level = energy - onsite_ref[...]
-        ref[0] = jnp.where(eye, level, 0.0) - hop_ref[0] - sigma_ref[local, 0]
-        ref[1] = jnp.where(eye, ETA, 0.0) - hop_ref[1] - sigma_ref[local, 1]
+    copies[0].wait()
+    for i, ref in enumerate((other_ref, own_ref)):
+        copies[1 + i].wait()
+        level = scale[1 - i] - onsite_ref[...]
+        ref[0] = jnp.where(eye, level, 0.0) - hop_ref[0] - sigma_ref[i, 0]
+        ref[1] = jnp.where(eye, ETA, 0.0) - hop_ref[1] - sigma_ref[i, 1]
+    copies[3].wait()
 
 
 def call(kernel, place, arrays, shape, count, products):
@@ -368,7 +396,7 @@
     z = lax.axis_index("energy")
     k = lax.axis_index("mom")
     y, x = slab // 2, slab % 2
-    place = jnp.stack([y, x]).astype(jnp.int32)
+    place = jnp.stack([y, x, z % 2]).astype(jnp.int32)
     active = k == x
 
     def device(yy, xx, zz, kk):
@@ -386,6 +414,7 @@
             for zz in range(energy_count)
         ]
 
+    beside = [(device(a, b, c, b), device(a, b, c ^ 1, b)) for a, b, c in chips]
     siblings = [(device(a, b, c, d), device(a, b, c, 1 - d)) for a, b, c in chips for d in range(2)]
     gift = [(device(a, b, c, b), device(a, b, c, 1 - b)) for a, b, c in chips]
 
@@ -397,31 +426,40 @@
     smem = pl.BlockSpec(memory_space=pltpu.SMEM)
     vmem = pl.BlockSpec(memory_space=pltpu.VMEM)
     block_shape = jax.ShapeDtypeStruct((2, width, width), jnp.float32)
-    b_own, b_other = pl.pallas_call(
+    hbm = pl.BlockSpec(memory_space=pltpu.HBM)
+    coupling = couple[0, 0]
+    b_other, b_own, c_part = pl.pallas_call(
         prepare_kernel,
-        out_shape=[block_shape] * 2,
-        in_specs=[smem, smem, vmem, vmem, vmem],
-        out_specs=[vmem] * 2,
-        compiler_params=pltpu.CompilerParams(vmem_limit_bytes=VMEM_BYTES),
-    )(place, energies, onsite[0], hop[0, 0], sigma_in[:, 0])
-
-    coupling = couple[0, 0]
-    c_one = send(coupling, routes((1, 0), (1, 3), (2, 1)))
-    c_two = send(coupling, routes((1, 2), (2, 0), (2, 3)))
+        out_shape=[block_shape] * 2 + [jax.ShapeDtypeStruct((2, width // 2, width), jnp.float32)],
+        in_specs=[smem, smem, vmem, hbm, hbm, hbm],
+        out_specs=[vmem] * 3,
+        scratch_shapes=[
+            pltpu.VMEM((2, width, width), jnp.float32),
+            pltpu.VMEM((2, 2, width, width), jnp.float32),
+            pltpu.SemaphoreType.DMA((4,)),
+        ],
+        compiler_params=pltpu.CompilerParams(vmem_limit_bytes=ALL_VMEM_BYTES),
+    )(place, energies, onsite[0], hop[0, 0], sigma_in[:, 0], coupling)
+
+    couplings = [coupling]
+    for pairs in (
+        routes((1, 0), (1, 3), (2, 1), (3, 2)),
+        routes((2, 0), (2, 3), (1, 2), (3, 1)),
+        routes((3, 0)),
+    ):
+        mine = send(c_part, pairs)
+        couplings += [mine, send(mine, beside)]
     b_far = send(b_other, to_far)
     b_y = send(b_other, to_y)
     b_x = send(b_own, to_x)
-    c_last = send(coupling, routes((3, 0), (3, 1)))
-    c_last_x = send(coupling, routes((3, 2)))
 
     blocks = (b_own, b_x, b_y, b_far)
     shape = (2, width, width)
     (g0,) = call(first_kernel, place, blocks, shape, 1, 2)
-    middle = (coupling, c_one, c_two)
-    g1, g2 = call(forward_kernel, place, (*blocks, *middle, g0), shape, 2, 8)
+    g1, g2 = call(forward_kernel, place, (*blocks, *couplings, g0), shape, 2, 8)
     shape = (4, width, width)
     keep, give = call(
-        backward_kernel, place, (*blocks, *middle, c_last, c_last_x, g0, g1, g2), shape, 2, 16
+        backward_kernel, place, (*blocks, *couplings, g0, g1, g2), shape, 2, 16
     )
     half = jnp.where(active, keep, send(give, gift))
 

time: 88.9 us -> 100 us (1.12)
  starting transfers between devices: 18.9 us -> 27.4 us
  Pallas kernels: 15.2 us -> 18 us
  local copies, waits for them, and re-layouts: 3.59 us -> 1.69 us
  other arithmetic: 2.57 us -> 3.68 us
    ppermute x9 -> x11, starting transfers between devices: 13.4 us -> 22.7 us  [send(): return lax.ppermute(value, axes, pairs)]
    pallas_call x1, Pallas kernels: 0.67 us -> 3.19 us  [owner_body(): pl.pallas_call(prepare_kernel, out_shape=[block_shape] * 2 + [jax.ShapeDt...]
    unnamed x12 -> x10, local copies, waits for them, and re-layouts: 3.59 us -> 1.69 us
    ppermute x9 -> x11, waiting for transfers between devices: 20.8 us -> 21.3 us  [send(): return lax.ppermute(value, axes, pairs)]
  transfers between devices with their start and end apart: 10 -> 12, of which waited for: 7 -> 5; matrix products, arithmetic and copies ran while one was open for 0% -> 0% of each run, Pallas kernels for 7% -> 2%
where the time goes in v5:
time: 100 us; the launch traced here: 99.6 us
  waiting for transfers between devices  48.5 us (48%)
  starting transfers between devices  27.4 us (27%)
  Pallas kernels  18 us (18%)
  other arithmetic  3.68 us (4%)
  local copies, waits for them, and re-layouts  1.69 us (2%)
    all_to_all x1, waiting for transfers between devices, owner_body(): lax.all_to_all(half.reshape(slots, rows, width), ('slab', 'energy'), 0, 0...  27.2 us
    ppermute x11, starting transfers between devices, send(): return lax.ppermute(value, axes, pairs)  22.7 us
    ppermute x11, waiting for transfers between devices, send(): return lax.ppermute(value, axes, pairs)  21.3 us
    pallas_call x3, Pallas kernels, call(): pl.pallas_call(kernel, out_shape=[jax.ShapeDtypeStruct(shape, jnp.float32...  13.9 us
    all_to_all x1, starting transfers between devices, owner_body(): lax.all_to_all(half.reshape(slots, rows, width), ('slab', 'energy'), 0, 0...  4.7 us
    pallas_call x1, Pallas kernels, owner_body(): pl.pallas_call(prepare_kernel, out_shape=[block_shape] * 2 + [jax.ShapeDt...  3.19 us
  transfers between devices with their start and end apart: 12, of which 5 were waited for; matrix products, arithmetic and copies ran while one was open for 0% of the time, Pallas kernels for 2%

profile of v5, /device:TPU:0, one launch (start us, length us, event | category | flops | bytes accessed | tf_op | source)
XLA Modules:
  0.0 99.6 jit_solution(16083963087070215049)
XLA Ops:
  0.0 0.6 multiply_add_fusion.scale
  0.6 0.6 pad_add_fusion.place
  1.3 3.2 %shard_map.64 = (f32[2,256,256]{2,1,0:T(8,128)}, f32[2,256,256]{2,1,0:T(8,128)}, f32[2,128,256]{2,1,0:T(8,128)}) custom-call(s32[3]{0:T(128)} %pad_add_fusion.place, f32[2]{0:T(128)} %multiply_add_fusion.scale, f32[1,256]{1,0:T(1,128)} %bitcast.18, f32[2,256,256]{2,1,0:T(8,128)} %bitcast.17, f32[2,2,256,256]{3,2,1,0:T(8,128)} %bitcast.16, ...), custom_call_target="tpu_custom_call" | custom-call | tf_op jit(solution)/shard_map/pallas_call | solution.py:431
  4.5 1.3 %collective-permute-start.3 = (f32[2,128,256]{2,1,0:T(8,128)}, f32[2,128,256]{2,1,0:T(8,128)S(1)}, u32[]{:S(2)}, u32[]{:S(2)}) collective-permute-start(f32[2,128,256]{2,1,0:T(8,128)} %get-tuple-element.14), channel_id=1, source_target_pairs={{8,0},{10,2},{12,4},{14,6},{9,25},{11,27},{13,29},{15,31},{17,9},{... | collective-permute-start | bytes 786440 | tf_op jit(solution)/shard_map/ppermute | solution.py:422
  5.8 1.3 %collective-permute-start = (f32[2,256,256]{2,1,0:T(8,128)}, f32[2,256,256]{2,1,0:T(8,128)S(1)}, u32[]{:S(2)}, u32[]{:S(2)}) collective-permute-start(f32[2,256,256]{2,1,0:T(8,128)} %get-tuple-element.12.b_own), channel_id=1, source_target_pairs={{1,9},{3,11},{5,13},{7,15},{8,0},{10,2},{12,4},{14,6},{17,25},{19,... | collective-permute-start | bytes 1572872 | tf_op jit(solution)/shard_map/ppermute | solution.py:422
  7.1 0.0 copy-start
  7.1 5.0 %collective-permute-start.1 = (f32[2,256,256]{2,1,0:T(8,128)}, f32[2,256,256]{2,1,0:T(8,128)S(1)}, u32[]{:S(2)}, u32[]{:S(2)}) collective-permute-start(f32[2,256,256]{2,1,0:T(8,128)} %get-tuple-element.13), channel_id=1, source_target_pairs={{0,16},{2,18},{4,20},{6,22},{9,25},{11,27},{13,29},{15,31},{16,0},... | collective-permute-start | bytes 1572872 | tf_op jit(solution)/shard_map/ppermute | solution.py:422
  12.1 1.3 %collective-permute-start.2 = (f32[2,256,256]{2,1,0:T(8,128)}, f32[2,256,256]{2,1,0:T(8,128)S(1)}, u32[]{:S(2)}, u32[]{:S(2)}) collective-permute-start(f32[2,256,256]{2,1,0:T(8,128)} %get-tuple-element.13), channel_id=1, source_target_pairs={{1,25},{3,27},{5,29},{7,31},{8,16},{10,18},{12,20},{14,22},{17,9},... | collective-permute-start | bytes 1572872 | tf_op jit(solution)/shard_map/ppermute | solution.py:422
  13.4 1.3 %collective-permute-start.5 = (f32[2,128,256]{2,1,0:T(8,128)}, f32[2,128,256]{2,1,0:T(8,128)S(1)}, u32[]{:S(2)}, u32[]{:S(2)}) collective-permute-start(f32[2,128,256]{2,1,0:T(8,128)} %get-tuple-element.14), channel_id=1, source_target_pairs={{16,0},{18,2},{20,4},{22,6},{17,25},{19,27},{21,29},{23,31},{8,16}... | collective-permute-start | bytes 786440 | tf_op jit(solution)/shard_map/ppermute | solution.py:422
  14.7 1.3 %collective-permute-start.7 = (f32[2,128,256]{2,1,0:T(8,128)}, f32[2,128,256]{2,1,0:T(8,128)S(1)}, u32[]{:S(2)}, u32[]{:S(2)}) collective-permute-start(f32[2,128,256]{2,1,0:T(8,128)} %get-tuple-element.14), channel_id=1, source_target_pairs={{24,0},{26,2},{28,4},{30,6}} | collective-permute-start | bytes 786440 | tf_op jit(solution)/shard_map/ppermute | solution.py:422
  16.0 14.7 %collective-permute-done.5.refs_3_ = f32[2,128,256]{2,1,0:T(8,128)S(1)} collective-permute-done((f32[2,128,256]{2,1,0:T(8,128)}, f32[2,128,256]{2,1,0:T(8,128)S(1)}, u32[]{:S(2)}, u32[]{:S(2)}) %collective-permute-start.5) | collective-permute-done | bytes 262176 | tf_op jit(solution)/shard_map/ppermute | solution.py:422
  30.7 4.0 %collective-permute-start.4 = (f32[2,128,256]{2,1,0:T(8,128)S(1)}, f32[2,128,256]{2,1,0:T(8,128)S(1)}, u32[]{:S(2)}, u32[]{:S(2)}) collective-permute-start(f32[2,128,256]{2,1,0:T(8,128)S(1)} %collective-permute-done.3.refs_1_), channel_id=1, source_target_pairs={{0,2},{2,0},{4,6},{6,4},{9,11},{11,9},{13,15},{15,13},{16,18},{18,... | collective-permute-start | bytes 786440 | tf_op jit(solution)/shard_map/ppermute | solution.py:422
  34.7 1.9 %collective-permute-start.6 = (f32[2,128,256]{2,1,0:T(8,128)S(1)}, f32[2,128,256]{2,1,0:T(8,128)S(1)}, u32[]{:S(2)}, u32[]{:S(2)}) collective-permute-start(f32[2,128,256]{2,1,0:T(8,128)S(1)} %collective-permute-done.5.refs_3_), channel_id=1, source_target_pairs={{0,2},{2,0},{4,6},{6,4},{9,11},{11,9},{13,15},{15,13},{16,18},{18,... | collective-permute-start | bytes 786440 | tf_op jit(solution)/shard_map/ppermute | solution.py:422
  36.6 3.9 %collective-permute-start.8 = (f32[2,128,256]{2,1,0:T(8,128)S(1)}, f32[2,128,256]{2,1,0:T(8,128)S(1)}, u32[]{:S(2)}, u32[]{:S(2)}) collective-permute-start(f32[2,128,256]{2,1,0:T(8,128)S(1)} %collective-permute-done.7.refs_5_), channel_id=1, source_target_pairs={{0,2},{2,0},{4,6},{6,4},{9,11},{11,9},{13,15},{15,13},{16,18},{18,... | collective-permute-start | bytes 786440 | tf_op jit(solution)/shard_map/ppermute | solution.py:422
  40.6 1.0 %copy-done.1 = f32[2,256,256]{2,1,0:T(8,128)S(1)} copy-done((f32[2,256,256]{2,1,0:T(8,128)S(1)}, f32[2,256,256]{2,1,0:T(8,128)}, u32[]{:S(2)}) %copy-start.1) | copy-done | bytes 524312
  41.6 1.5 %shard_map.65.refs_7_ = f32[2,256,256]{2,1,0:T(8,128)S(1)} custom-call(s32[3]{0:T(128)S(1)} %copy-done.2, f32[2,256,256]{2,1,0:T(8,128)S(1)} %copy-done.1, f32[2,256,256]{2,1,0:T(8,128)S(1)} %collective-permute-done.b_x, f32[2,256,256]{2,1,0:T(8,128)S(1)} %collective-permute-done.1.b_y, f32[2,256,256]{2,1,0:T(8,128)S(1)} %collective-permute-done.2.b_far), custom_call_target="tpu_custom_call" | custom-call | flops 603979776 | bytes 2621440 | tf_op jit(solution)/shard_map/pallas_call | solution.py:374
  43.2 2.6 %collective-permute-done.8.refs_6_ = f32[2,128,256]{2,1,0:T(8,128)S(1)} collective-permute-done((f32[2,128,256]{2,1,0:T(8,128)S(1)}, f32[2,128,256]{2,1,0:T(8,128)S(1)}, u32[]{:S(2)}, u32[]{:S(2)}) %collective-permute-start.8) | collective-permute-done | bytes 262176 | tf_op jit(solution)/shard_map/ppermute | solution.py:422
  45.8 4.7 %shard_map.66 = (f32[2,256,256]{2,1,0:T(8,128)S(1)}, f32[2,256,256]{2,1,0:T(8,128)S(1)}) custom-call(s32[3]{0:T(128)S(1)} %copy-done.2, f32[2,256,256]{2,1,0:T(8,128)S(1)} %copy-done.1, f32[2,256,256]{2,1,0:T(8,128)S(1)} %collective-permute-done.b_x, f32[2,256,256]{2,1,0:T(8,128)S(1)} %collective-permute-done.1.b_y, ...), custom_call_target="tpu_custom_call" | custom-call | flops 2415919104 | bytes 7340032 | tf_op jit(solution)/shard_map/pallas_call | solution.py:374
  50.4 7.7 %shard_map.67 = (f32[4,256,256]{2,1,0:T(8,128)S(1)}, f32[4,256,256]{2,1,0:T(8,128)S(1)}) custom-call(s32[3]{0:T(128)S(1)} %copy-done.2, f32[2,256,256]{2,1,0:T(8,128)S(1)} %copy-done.1, f32[2,256,256]{2,1,0:T(8,128)S(1)} %collective-permute-done.b_x, f32[2,256,256]{2,1,0:T(8,128)S(1)} %collective-permute-done.1.b_y, ...), custom_call_target="tpu_custom_call" | custom-call | flops 4831838208 | bytes 8388608 | tf_op jit(solution)/shard_map/pallas_call | solution.py:374
  58.1 1.4 %collective-permute-start.9 = (f32[4,256,256]{2,1,0:T(8,128)S(1)}, f32[4,256,256]{2,1,0:T(8,128)S(1)}, u32[]{:S(2)}, u32[]{:S(2)}) collective-permute-start(f32[4,256,256]{2,1,0:T(8,128)S(1)} %get-tuple-element.18), channel_id=1, source_target_pairs={{0,1},{2,3},{4,5},{6,7},{9,8},{11,10},{13,12},{15,14},{16,17},{18,... | collective-permute-start | bytes 3145736 | tf_op jit(solution)/shard_map/ppermute | solution.py:422
  59.5 2.2 %collective-permute-done.9 = f32[4,256,256]{2,1,0:T(8,128)S(1)} collective-permute-done((f32[4,256,256]{2,1,0:T(8,128)S(1)}, f32[4,256,256]{2,1,0:T(8,128)S(1)}, u32[]{:S(2)}, u32[]{:S(2)}) %collective-permute-start.9) | collective-permute-done | bytes 1048608 | tf_op jit(solution)/shard_map/ppermute | solution.py:422
  61.7 1.1 %broadcast_select_fusion.1 = f32[4,256,256]{2,1,0:T(8,128)} fusion(f32[4,256,256]{2,1,0:T(8,128)S(1)} %get-tuple-element.17, f32[4,256,256]{2,1,0:T(8,128)S(1)} %collective-permute-done.9, pred[]{:T(512)S(6)} %eq.49), kind=kLoop, calls=%fused_computation.1 | loop fusion | flops 262144 | bytes 3145729 | tf_op jit(solution)/shard_map/jit(_where)/select_n | solution.py:464
  62.8 4.7 %all-to-all-start = ((f32[16,64,256]{2,1,0:T(8,128)}), f32[16,64,256]{2,1,0:T(8,128)S(1)}, u32[]{:S(2)}, u32[]{:S(2)}) async-start(f32[16,64,256]{2,1,0:T(8,128)} %bitcast.10), calls=%async_computation | async-start | bytes 2097152 | tf_op jit(solution)/shard_map/all_to_all | solution.py:468
  67.5 0.0 copy-start.4
  67.6 0.6 copy-done.4
  68.2 0.1 iota_add_fusion
  68.3 0.1 add_reduce_fusion
  68.4 27.2 %all-to-all-done.parts_ref = f32[16,64,256]{2,1,0:T(8,128)S(1)} async-done(((f32[16,64,256]{2,1,0:T(8,128)}), f32[16,64,256]{2,1,0:T(8,128)S(1)}, u32[]{:S(2)}, u32[]{:S(2)}) %all-to-all-start) | async-done | bytes 1048608 | tf_op jit(solution)/shard_map/all_to_all | solution.py:468
  95.5 0.9 shard_map.68
  96.4 0.1 collective-permute-start.10
  96.5 1.9 %collective-permute-done.10 = f32[8,64,256]{2,1,0:T(8,128)S(1)} collective-permute-done((f32[8,64,256]{2,1,0:T(8,128)S(1)}, f32[8,64,256]{2,1,0:T(8,128)S(1)}, u32[]{:S(2)}, u32[]{:S(2)}) %collective-permute-start.10) | collective-permute-done | bytes 524320 | tf_op jit(solution)/shard_map/ppermute | solution.py:422
  98.4 1.1 %broadcast_select_fusion = f32[8,1,2,64,256]{4,3,2,1,0:T(8,128)} fusion(f32[8,64,256]{2,1,0:T(8,128)S(1)} %collective-permute-done.10, f32[8,64,256]{2,1,0:T(8,128)S(1)} %shard_map.68, pred[2]{0:T(512)(128)(4,1)S(1)} %iota_compare_fusion.2), kind=kLoop, calls=%fused_computation | loop fusion | flops 262144 | bytes 2097154 | tf_op jit(solution)/shard_map/jit(_where)/select_n | solution.py:481
  (16 shorter events, 0.0 us)
Async XLA Ops:
  4.5 10.2 %collective-permute-start.3 = (f32[2,128,256]{2,1,0:T(8,128)}, f32[2,128,256]{2,1,0:T(8,128)S(1)}, u32[]{:S(2)}, u32[]{:S(2)}) collective-permute-start(f32[2,128,256]{2,1,0:T(8,128)} %get-tuple-element.14), channel_id=1, source_target_pairs={{8,0},{10,2},{12,4},{14,6},{9,25},{11,27},{13,29},{15,31},{17,9},{... | collective-permute-start | bytes 786440 | tf_op jit(solution)/shard_map/ppermute | solution.py:422
  5.8 34.8 %copy-start.2 = (s32[3]{0:T(128)S(1)}, s32[3]{0:T(128)}, u32[]{:S(2)}) copy-start(s32[3]{0:T(128)} %pad_add_fusion.place) | copy-start | bytes 40
  5.8 30.8 %collective-permute-start = (f32[2,256,256]{2,1,0:T(8,128)}, f32[2,256,256]{2,1,0:T(8,128)S(1)}, u32[]{:S(2)}, u32[]{:S(2)}) collective-permute-start(f32[2,256,256]{2,1,0:T(8,128)} %get-tuple-element.12.b_own), channel_id=1, source_target_pairs={{1,9},{3,11},{5,13},{7,15},{8,0},{10,2},{12,4},{14,6},{17,25},{19,... | collective-permute-start | bytes 1572872 | tf_op jit(solution)/shard_map/ppermute | solution.py:422
  7.1 38.7 %copy-start = (f32[1,1,2,256,256]{4,3,2,1,0:T(8,128)S(1)}, f32[1,1,2,256,256]{4,3,2,1,0:T(8,128)}, u32[]{:S(2)}) copy-start(f32[1,1,2,256,256]{4,3,2,1,0:T(8,128)} %param.8) | copy-start | bytes 1572868
  7.1 33.5 %collective-permute-start.1 = (f32[2,256,256]{2,1,0:T(8,128)}, f32[2,256,256]{2,1,0:T(8,128)S(1)}, u32[]{:S(2)}, u32[]{:S(2)}) collective-permute-start(f32[2,256,256]{2,1,0:T(8,128)} %get-tuple-element.13), channel_id=1, source_target_pairs={{0,16},{2,18},{4,20},{6,22},{9,25},{11,27},{13,29},{15,31},{16,0},... | collective-permute-start | bytes 1572872 | tf_op jit(solution)/shard_map/ppermute | solution.py:422
  12.1 28.5 %collective-permute-start.2 = (f32[2,256,256]{2,1,0:T(8,128)}, f32[2,256,256]{2,1,0:T(8,128)S(1)}, u32[]{:S(2)}, u32[]{:S(2)}) collective-permute-start(f32[2,256,256]{2,1,0:T(8,128)} %get-tuple-element.13), channel_id=1, source_target_pairs={{1,25},{3,27},{5,29},{7,31},{8,16},{10,18},{12,20},{14,22},{17,9},... | collective-permute-start | bytes 1572872 | tf_op jit(solution)/shard_map/ppermute | solution.py:422
  13.4 17.3 %collective-permute-start.5 = (f32[2,128,256]{2,1,0:T(8,128)}, f32[2,128,256]{2,1,0:T(8,128)S(1)}, u32[]{:S(2)}, u32[]{:S(2)}) collective-permute-start(f32[2,128,256]{2,1,0:T(8,128)} %get-tuple-element.14), channel_id=1, source_target_pairs={{16,0},{18,2},{20,4},{22,6},{17,25},{19,27},{21,29},{23,31},{8,16}... | collective-permute-start | bytes 786440 | tf_op jit(solution)/shard_map/ppermute | solution.py:422
  14.7 20.0 %collective-permute-start.7 = (f32[2,128,256]{2,1,0:T(8,128)}, f32[2,128,256]{2,1,0:T(8,128)S(1)}, u32[]{:S(2)}, u32[]{:S(2)}) collective-permute-start(f32[2,128,256]{2,1,0:T(8,128)} %get-tuple-element.14), channel_id=1, source_target_pairs={{24,0},{26,2},{28,4},{30,6}} | collective-permute-start | bytes 786440 | tf_op jit(solution)/shard_map/ppermute | solution.py:422
  30.7 12.5 %collective-permute-start.4 = (f32[2,128,256]{2,1,0:T(8,128)S(1)}, f32[2,128,256]{2,1,0:T(8,128)S(1)}, u32[]{:S(2)}, u32[]{:S(2)}) collective-permute-start(f32[2,128,256]{2,1,0:T(8,128)S(1)} %collective-permute-done.3.refs_1_), channel_id=1, source_target_pairs={{0,2},{2,0},{4,6},{6,4},{9,11},{11,9},{13,15},{15,13},{16,18},{18,... | collective-permute-start | bytes 786440 | tf_op jit(solution)/shard_map/ppermute | solution.py:422
  34.7 8.5 %collective-permute-start.6 = (f32[2,128,256]{2,1,0:T(8,128)S(1)}, f32[2,128,256]{2,1,0:T(8,128)S(1)}, u32[]{:S(2)}, u32[]{:S(2)}) collective-permute-start(f32[2,128,256]{2,1,0:T(8,128)S(1)} %collective-permute-done.5.refs_3_), channel_id=1, source_target_pairs={{0,2},{2,0},{4,6},{6,4},{9,11},{11,9},{13,15},{15,13},{16,18},{18,... | collective-permute-start | bytes 786440 | tf_op jit(solution)/shard_map/ppermute | solution.py:422
  36.6 9.1 %collective-permute-start.8 = (f32[2,128,256]{2,1,0:T(8,128)S(1)}, f32[2,128,256]{2,1,0:T(8,128)S(1)}, u32[]{:S(2)}, u32[]{:S(2)}) collective-permute-start(f32[2,128,256]{2,1,0:T(8,128)S(1)} %collective-permute-done.7.refs_5_), channel_id=1, source_target_pairs={{0,2},{2,0},{4,6},{6,4},{9,11},{11,9},{13,15},{15,13},{16,18},{18,... | collective-permute-start | bytes 786440 | tf_op jit(solution)/shard_map/ppermute | solution.py:422
  40.6 1.0 %copy-start.1 = (f32[2,256,256]{2,1,0:T(8,128)S(1)}, f32[2,256,256]{2,1,0:T(8,128)}, u32[]{:S(2)}) copy-start(f32[2,256,256]{2,1,0:T(8,128)} %get-tuple-element.12.b_own) | copy-start | bytes 1572868
  58.1 3.6 %collective-permute-start.9 = (f32[4,256,256]{2,1,0:T(8,128)S(1)}, f32[4,256,256]{2,1,0:T(8,128)S(1)}, u32[]{:S(2)}, u32[]{:S(2)}) collective-permute-start(f32[4,256,256]{2,1,0:T(8,128)S(1)} %get-tuple-element.18), channel_id=1, source_target_pairs={{0,1},{2,3},{4,5},{6,7},{9,8},{11,10},{13,12},{15,14},{16,17},{18,... | collective-permute-start | bytes 3145736 | tf_op jit(solution)/shard_map/ppermute | solution.py:422
  62.8 4.7 %copy-start.3 = (f32[2,4]{1,0:T(2,128)S(1)}, f32[2,4]{1,0:T(2,128)}, u32[]{:S(2)}) copy-start(f32[2,4]{1,0:T(2,128)} %param.11) | copy-start | bytes 100
  62.8 32.7 %all-to-all-start = ((f32[16,64,256]{2,1,0:T(8,128)}), f32[16,64,256]{2,1,0:T(8,128)S(1)}, u32[]{:S(2)}, u32[]{:S(2)}) async-start(f32[16,64,256]{2,1,0:T(8,128)} %bitcast.10), calls=%async_computation | async-start | bytes 2097152 | tf_op jit(solution)/shard_map/all_to_all | solution.py:468
  67.5 0.7 copy-start.4
  96.4 2.0 %collective-permute-start.10 = (f32[8,64,256]{2,1,0:T(8,128)S(1)}, f32[8,64,256]{2,1,0:T(8,128)S(1)}, u32[]{:S(2)}, u32[]{:S(2)}) collective-permute-start(f32[8,64,256]{2,1,0:T(8,128)S(1)} %shard_map.68), channel_id=1, source_target_pairs={{0,1},{1,0},{2,3},{3,2},{4,5},{5,4},{6,7},{7,6},{8,9},{9,8},{10,11... | collective-permute-start | bytes 1572872 | tf_op jit(solution)/shard_map/ppermute | solution.py:422

commit v6 on v4

--- a/solution.py
+++ b/solution.py
@@ -138,29 +138,24 @@
     return halves(pair[0]), halves(pair[1]), halves(pair[0] + pair[1])
 
 
-def adjoint_form(pair):
-    return halves(pair[0]), halves(-pair[1]), halves(pair[0] - pair[1])
-
-
-def real_dot(left, right, axis):
+def real_dot(left, right):
     rows = left[0].shape[0]
-    numbers = (((1,), (axis,)), ((), ()))
     both = jnp.concatenate([left[0], left[1]], axis=0)
-    main = lax.dot_general(both, right[0], numbers, preferred_element_type=jnp.float32)
-    rest = lax.dot_general(left[0], right[1], numbers, preferred_element_type=jnp.float32)
+    main = jnp.dot(both, right[0], preferred_element_type=jnp.float32)
+    rest = jnp.dot(left[0], right[1], preferred_element_type=jnp.float32)
     return main[:rows] + main[rows:] + rest
 
 
-def mul(left, right, axis=0):
-    first = real_dot(left[0], right[0], axis)
-    second = real_dot(left[1], right[1], axis)
-    third = real_dot(left[2], right[2], axis)
+def mul(left, right):
+    first = real_dot(left[0], right[0])
+    second = real_dot(left[1], right[1])
+    third = real_dot(left[2], right[2])
     return first - second, third - first - second
 
 
-def mul_twice(blocks, right, last, axis=0):
+def mul_twice(blocks, right, last):
     inner = [mul(block, right) for block in blocks]
-    return [mul(form(block), last, axis) for block in inner]
+    return [mul(form(block), last) for block in inner]
 
 
 def split_rows(pair):
@@ -239,72 +234,63 @@
     return choose(same_y, near, away)
 
 
-def forward(block, coupling, green_form):
-    lefts = [form(part) for part in split_rows(coupling)]
-    terms = mul_twice(lefts, green_form, adjoint_form(coupling), axis=1)
-    mats = [
-        (part[0] - term[0], part[1] - term[1]) for part, term in zip(split_rows(block), terms)
+def stored_form(ref, slab, side):
+    at = (slab - 1, side)
+    return tuple(tuple(ref[(*at, 2 * plane + term)] for term in range(2)) for plane in range(3))
+
+
+def stored_rows(ref, slab, side):
+    size = ref.shape[-2] // BLOCKS
+    at = (slab - 1, side)
+    return [
+        tuple(
+            tuple(ref[(*at, 2 * plane + term, slice(b * size, (b + 1) * size))] for term in range(2))
+            for plane in range(3)
+        )
+        for b in range(BLOCKS)
     ]
-    return inverse(mats)
-
-
-def couple_down(coupling, full_form):
-    lefts = [form(part) for part in split_rows((coupling[0].T, -coupling[1].T))]
-    return mul_twice(lefts, full_form, form(coupling))
-
-
-def complete(greens, coupled_form):
-    forms = [form(block) for block in greens]
-    extra = mul_twice(forms, coupled_form, form_rows(forms))
-    return [(g[0] + e[0], g[1] + e[1]) for g, e in zip(greens, extra)]
-
-
-def whole_form(blocks):
-    return form_rows([form(block) for block in blocks])
-
-
-def first_kernel(place, b_own, b_x, b_y, b_far, g_ref):
+
+
+def coupling_kernel(place, c_own, c_x, c_y, c_far, out_ref):
     y, x = place[0], place[1]
-    write(g_ref, inverse(split_rows(pick_block(y, x, 0, b_own, b_x, b_y, b_far))))
-
-
-def middle_coupling(y, x, slab, c_own, c_one, c_two):
-    if slab == 1:
-        return choose(x == y, read(c_one), choose(x == 1, read(c_own), read(c_two)))
-    return choose(x == y, read(c_two), choose(x == 1, read(c_one), read(c_own)))
-
-
-def forward_kernel(place, b_own, b_x, b_y, b_far, c_own, c_one, c_two, g0_ref, g1_ref, g2_ref):
+    for slab in (1, 2, 3):
+        real, imag = pick_block(y, x, slab, c_own, c_x, c_y, c_far)
+        for side, pair in enumerate(((real, imag), (real.T, -imag.T))):
+            for plane, terms in enumerate(form(pair)):
+                for term in range(2):
+                    out_ref[slab - 1, side, 2 * plane + term] = terms[term]
+
+
+def chain_kernel(place, b_own, b_x, b_y, b_far, c_forms, keep_ref, give_ref):
     y, x = place[0], place[1]
-    green_form = form(read(g0_ref))
-    for slab, ref in ((1, g1_ref), (2, g2_ref)):
-        block = pick_block(y, x, slab, b_own, b_x, b_y, b_far)
-        greens = forward(block, middle_coupling(y, x, slab, c_own, c_one, c_two), green_form)
-        write(ref, greens)
-        green_form = whole_form(greens)
-
-
-def backward_kernel(
-    place, b_own, b_x, b_y, b_far, c_own, c_one, c_two, c_last, c_last_x,
-    g0_ref, g1_ref, g2_ref, keep_ref, give_ref,
-):
-    y, x = place[0], place[1]
+    greens, forms = [], []
+    for slab in range(4):
+        mats = split_rows(pick_block(y, x, slab, b_own, b_x, b_y, b_far))
+        if slab:
+            terms = mul_twice(
+                stored_rows(c_forms, slab, 0), form_rows(forms[-1]), stored_form(c_forms, slab, 1)
+            )
+            mats = [(m[0] - t[0], m[1] - t[1]) for m, t in zip(mats, terms)]
+        greens.append(inverse(mats))
+        forms.append([form(block) for block in greens[-1]])
 
     def finish(slab, blocks):
         full = join_rows(blocks)
         keep_ref[slab] = jnp.where(x == 0, full[0], full[1])
         give_ref[slab] = jnp.where(x == 0, full[1], full[0])
 
-    coupling = choose(y == 0, read(c_last), choose(x == 0, read(c_last_x), read(c_own)))
-    block = pick_block(y, x, 3, b_own, b_x, b_y, b_far)
-    fulls = forward(block, coupling, form(read(g2_ref)))
-    finish(3, fulls)
-    for slab, ref in ((2, g2_ref), (1, g1_ref), (0, g0_ref)):
-        coupled = couple_down(coupling, whole_form(fulls))
-        fulls = complete(split_rows(read(ref)), whole_form(coupled))
+    finish(3, greens[3])
+    full_form = form_rows(forms[3])
+    for slab in (2, 1, 0):
+        coupled = mul_twice(
+            stored_rows(c_forms, slab + 1, 1), full_form, stored_form(c_forms, slab + 1, 0)
+        )
+        coupled_form = form_rows([form(block) for block in coupled])
+        extra = mul_twice(forms[slab], coupled_form, form_rows(forms[slab]))
+        fulls = [(g[0] + e[0], g[1] + e[1]) for g, e in zip(greens[slab], extra)]
         finish(slab, fulls)
         if slab:
-            coupling = middle_coupling(y, x, slab, c_own, c_one, c_two)
+            full_form = form_rows([form(block) for block in fulls])
 
 
 def mix_kernel(phonon, parts_ref, out_ref):
@@ -406,23 +392,22 @@
     )(place, energies, onsite[0], hop[0, 0], sigma_in[:, 0])
 
     coupling = couple[0, 0]
-    c_one = send(coupling, routes((1, 0), (1, 3), (2, 1)))
-    c_two = send(coupling, routes((1, 2), (2, 0), (2, 3)))
+    c_x = send(coupling, routes((1, 0), (2, 3), (3, 2)))
+    c_y = send(coupling, routes((1, 3), (2, 0), (3, 1)))
+    c_far = send(coupling, routes((1, 2), (2, 1), (3, 0)))
     b_far = send(b_other, to_far)
+    b_x = send(b_own, to_x)
     b_y = send(b_other, to_y)
-    b_x = send(b_own, to_x)
-    c_last = send(coupling, routes((3, 0), (3, 1)))
-    c_last_x = send(coupling, routes((3, 2)))
-
-    blocks = (b_own, b_x, b_y, b_far)
-    shape = (2, width, width)
-    (g0,) = call(first_kernel, place, blocks, shape, 1, 2)
-    middle = (coupling, c_one, c_two)
-    g1, g2 = call(forward_kernel, place, (*blocks, *middle, g0), shape, 2, 8)
+
+    c_forms = pl.pallas_call(
+        coupling_kernel,
+        out_shape=jax.ShapeDtypeStruct((3, 2, 6, width, width), jnp.bfloat16),
+        in_specs=[smem] + [vmem] * 4,
+        out_specs=vmem,
+        compiler_params=pltpu.CompilerParams(vmem_limit_bytes=VMEM_BYTES),
+    )(place, coupling, c_x, c_y, c_far)
     shape = (4, width, width)
-    keep, give = call(
-        backward_kernel, place, (*blocks, *middle, c_last, c_last_x, g0, g1, g2), shape, 2, 16
-    )
+    keep, give = call(chain_kernel, place, (b_own, b_x, b_y, b_far, c_forms), shape, 2, 26)
     half = jnp.where(active, keep, send(give, gift))
 
     rows = width // energy_count

time: 88.9 us -> 84.7 us (0.953)
  waiting for transfers between devices: 47.9 us -> 44.7 us
    ppermute x9 -> x8, waiting for transfers between devices: 20.8 us -> 16.9 us  [send(): return lax.ppermute(value, axes, pairs)]
    pallas_call x3 -> x1, Pallas kernels: 13.7 us -> 11.6 us  [call(): pl.pallas_call(kernel, out_shape=[jax.ShapeDtypeStruct(shape, jnp.float32...]
    pallas_call x0 -> x1, Pallas kernels: none -> 1.5 us  [owner_body(): pl.pallas_call(coupling_kernel, out_shape=jax.ShapeDtypeStruct((3, 2, 6,...]
    ppermute x9 -> x8, starting transfers between devices: 13.4 us -> 12.8 us  [send(): return lax.ppermute(value, axes, pairs)]
  transfers between devices with their start and end apart: 10 -> 9, of which waited for: 7 -> 7; matrix products, arithmetic and copies ran while one was open for 0% -> 0% of each run, Pallas kernels for 7% -> 3%
where the time goes in v6:
time: 84.7 us; the launch traced here: 84.2 us
  waiting for transfers between devices  44.7 us (53%)
  starting transfers between devices  18.1 us (21%)
  Pallas kernels  14.7 us (17%)
  local copies, waits for them, and re-layouts  4 us (5%)
  other arithmetic  2.57 us (3%)
    all_to_all x1, waiting for transfers between devices, owner_body(): lax.all_to_all(half.reshape(slots, rows, width), ('slab', 'energy'), 0, 0...  27.8 us
    ppermute x8, waiting for transfers between devices, send(): return lax.ppermute(value, axes, pairs)  16.9 us
    ppermute x8, starting transfers between devices, send(): return lax.ppermute(value, axes, pairs)  12.8 us
    pallas_call x1, Pallas kernels, call(): pl.pallas_call(kernel, out_shape=[jax.ShapeDtypeStruct(shape, jnp.float32...  11.6 us
    all_to_all x1, starting transfers between devices, owner_body(): lax.all_to_all(half.reshape(slots, rows, width), ('slab', 'energy'), 0, 0...  5.3 us
    unnamed x12, local copies, waits for them, and re-layouts  4 us
  transfers between devices with their start and end apart: 9, of which 7 were waited for; matrix products, arithmetic and copies ran while one was open for 0% of the time, Pallas kernels for 3%

profile of v6, /device:TPU:0, one launch (start us, length us, event | category | flops | bytes accessed | tf_op | source)
XLA Modules:
  0.0 84.2 jit_solution(3216068385898349204)
XLA Ops:
  0.0 1.3 %collective-permute-start.3 = (f32[2,256,256]{2,1,0:T(8,128)}, f32[2,256,256]{2,1,0:T(8,128)S(1)}, u32[]{:S(2)}, u32[]{:S(2)}) collective-permute-start(f32[2,256,256]{2,1,0:T(8,128)} %bitcast.14), channel_id=1, source_target_pairs={{8,0},{10,2},{12,4},{14,6},{17,25},{19,27},{21,29},{23,31},{24,16}... | collective-permute-start | bytes 1572872 | tf_op jit(solution)/shard_map/ppermute | solution.py:379
  1.3 1.3 %collective-permute-start.4 = (f32[2,256,256]{2,1,0:T(8,128)}, f32[2,256,256]{2,1,0:T(8,128)S(1)}, u32[]{:S(2)}, u32[]{:S(2)}) collective-permute-start(f32[2,256,256]{2,1,0:T(8,128)} %bitcast.15), channel_id=1, source_target_pairs={{9,25},{11,27},{13,29},{15,31},{16,0},{18,2},{20,4},{22,6},{25,9},... | collective-permute-start | bytes 1572872 | tf_op jit(solution)/shard_map/ppermute | solution.py:379
  2.6 1.3 %collective-permute-start.5 = (f32[2,256,256]{2,1,0:T(8,128)}, f32[2,256,256]{2,1,0:T(8,128)S(1)}, u32[]{:S(2)}, u32[]{:S(2)}) collective-permute-start(f32[2,256,256]{2,1,0:T(8,128)} %bitcast.16), channel_id=1, source_target_pairs={{8,16},{10,18},{12,20},{14,22},{17,9},{19,11},{21,13},{23,15},{24,... | collective-permute-start | bytes 1572872 | tf_op jit(solution)/shard_map/ppermute | solution.py:379
  3.9 0.1 pad_add_fusion.place
  4.0 0.1 multiply_add_fusion.scale
  4.1 1.2 %copy-done = f32[2,1,2,256,256]{4,3,2,1,0:T(8,128)S(1)} copy-done((f32[2,1,2,256,256]{4,3,2,1,0:T(8,128)S(1)}, f32[2,1,2,256,256]{4,3,2,1,0:T(8,128)}, u32[]{:S(2)}) %copy-start) | copy-done | bytes 1048600
  5.3 1.0 %copy-done.1 = f32[1,1,2,256,256]{4,3,2,1,0:T(8,128)S(1)} copy-done((f32[1,1,2,256,256]{4,3,2,1,0:T(8,128)S(1)}, f32[1,1,2,256,256]{4,3,2,1,0:T(8,128)}, u32[]{:S(2)}) %copy-start.1) | copy-done | bytes 524312
  6.3 0.7 copy-done.3
  7.0 0.7 shard_map.64
  7.7 1.3 %collective-permute-start = (f32[2,256,256]{2,1,0:T(8,128)S(1)}, f32[2,256,256]{2,1,0:T(8,128)S(1)}, u32[]{:S(2)}, u32[]{:S(2)}) collective-permute-start(f32[2,256,256]{2,1,0:T(8,128)S(1)} %get-tuple-element.9.b_own), channel_id=1, source_target_pairs={{1,9},{3,11},{5,13},{7,15},{8,0},{10,2},{12,4},{14,6},{17,25},{19,... | collective-permute-start | bytes 1572872 | tf_op jit(solution)/shard_map/ppermute | solution.py:379
  9.0 4.9 %collective-permute-start.1 = (f32[2,256,256]{2,1,0:T(8,128)S(1)}, f32[2,256,256]{2,1,0:T(8,128)S(1)}, u32[]{:S(2)}, u32[]{:S(2)}) collective-permute-start(f32[2,256,256]{2,1,0:T(8,128)S(1)} %get-tuple-element.10), channel_id=1, source_target_pairs={{0,16},{2,18},{4,20},{6,22},{9,25},{11,27},{13,29},{15,31},{16,0},... | collective-permute-start | bytes 1572872 | tf_op jit(solution)/shard_map/ppermute | solution.py:379
  13.9 1.3 %collective-permute-start.2 = (f32[2,256,256]{2,1,0:T(8,128)S(1)}, f32[2,256,256]{2,1,0:T(8,128)S(1)}, u32[]{:S(2)}, u32[]{:S(2)}) collective-permute-start(f32[2,256,256]{2,1,0:T(8,128)S(1)} %get-tuple-element.10), channel_id=1, source_target_pairs={{1,25},{3,27},{5,29},{7,31},{8,16},{10,18},{12,20},{14,22},{17,9},... | collective-permute-start | bytes 1572872 | tf_op jit(solution)/shard_map/ppermute | solution.py:379
  15.2 4.2 %collective-permute-done.5.c_far = f32[2,256,256]{2,1,0:T(8,128)S(1)} collective-permute-done((f32[2,256,256]{2,1,0:T(8,128)}, f32[2,256,256]{2,1,0:T(8,128)S(1)}, u32[]{:S(2)}, u32[]{:S(2)}) %collective-permute-start.5) | collective-permute-done | bytes 524320 | tf_op jit(solution)/shard_map/ppermute | solution.py:379
  19.4 1.0 %copy-done.2 = f32[1,1,2,256,256]{4,3,2,1,0:T(8,128)S(1)} copy-done((f32[1,1,2,256,256]{4,3,2,1,0:T(8,128)S(1)}, f32[1,1,2,256,256]{4,3,2,1,0:T(8,128)}, u32[]{:S(2)}) %copy-start.2) | copy-done | bytes 524312
  20.4 1.5 %shard_map.65.c_forms = bf16[3,2,6,256,256]{4,3,2,1,0:T(8,128)(2,1)S(1)} custom-call(s32[2]{0:T(128)S(1)} %pad_add_fusion.place, f32[2,256,256]{2,1,0:T(8,128)S(1)} %bitcast.17, f32[2,256,256]{2,1,0:T(8,128)S(1)} %collective-permute-done.3.c_x, f32[2,256,256]{2,1,0:T(8,128)S(1)} %collective-permute-done.4.c_y, f32[2,256,256]{2,1,0:T(8,128)S(1)} %collective-permute-done.5.c_far), custom_call_target="tpu_custom_call" | custom-call | tf_op jit(solution)/shard_map/pallas_call | solution.py:402
  21.9 0.9 %collective-permute-done.b_x = f32[2,256,256]{2,1,0:T(8,128)S(1)} collective-permute-done((f32[2,256,256]{2,1,0:T(8,128)S(1)}, f32[2,256,256]{2,1,0:T(8,128)S(1)}, u32[]{:S(2)}, u32[]{:S(2)}) %collective-permute-start) | collective-permute-done | bytes 524320 | tf_op jit(solution)/shard_map/ppermute | solution.py:379
  22.8 2.1 %collective-permute-done.1.b_y = f32[2,256,256]{2,1,0:T(8,128)S(1)} collective-permute-done((f32[2,256,256]{2,1,0:T(8,128)S(1)}, f32[2,256,256]{2,1,0:T(8,128)S(1)}, u32[]{:S(2)}, u32[]{:S(2)}) %collective-permute-start.1) | collective-permute-done | bytes 524320 | tf_op jit(solution)/shard_map/ppermute | solution.py:379
  24.9 5.7 %collective-permute-done.2.b_far = f32[2,256,256]{2,1,0:T(8,128)S(1)} collective-permute-done((f32[2,256,256]{2,1,0:T(8,128)S(1)}, f32[2,256,256]{2,1,0:T(8,128)S(1)}, u32[]{:S(2)}, u32[]{:S(2)}) %collective-permute-start.2) | collective-permute-done | bytes 524320 | tf_op jit(solution)/shard_map/ppermute | solution.py:379
  30.6 11.6 %shard_map.66 = (f32[4,256,256]{2,1,0:T(8,128)S(1)}, f32[4,256,256]{2,1,0:T(8,128)S(1)}) custom-call(s32[2]{0:T(128)S(1)} %pad_add_fusion.place, f32[2,256,256]{2,1,0:T(8,128)S(1)} %get-tuple-element.9.b_own, f32[2,256,256]{2,1,0:T(8,128)S(1)} %collective-permute-done.b_x, f32[2,256,256]{2,1,0:T(8,128)S(1)} %collective-permute-done.1.b_y, ...), custom_call_target="tpu_custom_call" | custom-call | flops 7851737088 | bytes 3670016 | tf_op jit(solution)/shard_map/pallas_call | solution.py:332
  42.2 0.0 copy-start.4
  42.2 0.0 copy-start.5
  42.2 1.4 %collective-permute-start.6 = (f32[4,256,256]{2,1,0:T(8,128)S(1)}, f32[4,256,256]{2,1,0:T(8,128)S(1)}, u32[]{:S(2)}, u32[]{:S(2)}) collective-permute-start(f32[4,256,256]{2,1,0:T(8,128)S(1)} %get-tuple-element.12), channel_id=1, source_target_pairs={{0,1},{2,3},{4,5},{6,7},{9,8},{11,10},{13,12},{15,14},{16,17},{18,... | collective-permute-start | bytes 3145736 | tf_op jit(solution)/shard_map/ppermute | solution.py:379
  43.6 2.2 %collective-permute-done.6 = f32[4,256,256]{2,1,0:T(8,128)S(1)} collective-permute-done((f32[4,256,256]{2,1,0:T(8,128)S(1)}, f32[4,256,256]{2,1,0:T(8,128)S(1)}, u32[]{:S(2)}, u32[]{:S(2)}) %collective-permute-start.6) | collective-permute-done | bytes 1048608 | tf_op jit(solution)/shard_map/ppermute | solution.py:379
  45.8 1.1 %broadcast_select_fusion.1 = f32[4,256,256]{2,1,0:T(8,128)} fusion(f32[4,256,256]{2,1,0:T(8,128)S(1)} %get-tuple-element.11, f32[4,256,256]{2,1,0:T(8,128)S(1)} %collective-permute-done.6, pred[]{:T(512)S(6)} %eq.48), kind=kLoop, calls=%fused_computation.1 | loop fusion | flops 262144 | bytes 3145729 | tf_op jit(solution)/shard_map/jit(_where)/select_n | solution.py:411
  46.9 5.3 %all-to-all-start = ((f32[16,64,256]{2,1,0:T(8,128)}), f32[16,64,256]{2,1,0:T(8,128)S(1)}, u32[]{:S(2)}, u32[]{:S(2)}) async-start(f32[16,64,256]{2,1,0:T(8,128)} %bitcast.9), calls=%async_computation | async-start | bytes 2097152 | tf_op jit(solution)/shard_map/all_to_all | solution.py:415
  52.2 0.1 iota_add_fusion
  52.3 0.1 add_reduce_fusion
  52.4 27.8 %all-to-all-done.parts_ref = f32[16,64,256]{2,1,0:T(8,128)S(1)} async-done(((f32[16,64,256]{2,1,0:T(8,128)}), f32[16,64,256]{2,1,0:T(8,128)S(1)}, u32[]{:S(2)}, u32[]{:S(2)}) %all-to-all-start) | async-done | bytes 1048608 | tf_op jit(solution)/shard_map/all_to_all | solution.py:415
  80.2 0.9 %shard_map.67 = f32[8,64,256]{2,1,0:T(8,128)S(1)} custom-call(f32[8,8]{1,0:T(8,128)S(1)} %broadcast_multiply_fusion.phonon, f32[16,64,256]{2,1,0:T(8,128)S(1)} %all-to-all-done.parts_ref), custom_call_target="tpu_custom_call" | custom-call | tf_op jit(solution)/shard_map/pallas_call | solution.py:419
  81.1 0.1 collective-permute-start.7
  81.2 1.9 %collective-permute-done.7 = f32[8,64,256]{2,1,0:T(8,128)S(1)} collective-permute-done((f32[8,64,256]{2,1,0:T(8,128)S(1)}, f32[8,64,256]{2,1,0:T(8,128)S(1)}, u32[]{:S(2)}, u32[]{:S(2)}) %collective-permute-start.7) | collective-permute-done | bytes 524320 | tf_op jit(solution)/shard_map/ppermute | solution.py:379
  83.1 1.1 %broadcast_select_fusion = f32[8,1,2,64,256]{4,3,2,1,0:T(8,128)} fusion(f32[8,64,256]{2,1,0:T(8,128)S(1)} %collective-permute-done.7, f32[8,64,256]{2,1,0:T(8,128)S(1)} %shard_map.67, pred[2]{0:T(512)(128)(4,1)S(1)} %iota_compare_fusion.2), kind=kLoop, calls=%fused_computation | loop fusion | flops 262144 | bytes 2097154 | tf_op jit(solution)/shard_map/jit(_where)/select_n | solution.py:428
  (11 shorter events, 0.0 us)
Async XLA Ops:
  0.0 13.9 %collective-permute-start.3 = (f32[2,256,256]{2,1,0:T(8,128)}, f32[2,256,256]{2,1,0:T(8,128)S(1)}, u32[]{:S(2)}, u32[]{:S(2)}) collective-permute-start(f32[2,256,256]{2,1,0:T(8,128)} %bitcast.14), channel_id=1, source_target_pairs={{8,0},{10,2},{12,4},{14,6},{17,25},{19,27},{21,29},{23,31},{24,16}... | collective-permute-start | bytes 1572872 | tf_op jit(solution)/shard_map/ppermute | solution.py:379
  1.3 13.9 %collective-permute-start.4 = (f32[2,256,256]{2,1,0:T(8,128)}, f32[2,256,256]{2,1,0:T(8,128)S(1)}, u32[]{:S(2)}, u32[]{:S(2)}) collective-permute-start(f32[2,256,256]{2,1,0:T(8,128)} %bitcast.15), channel_id=1, source_target_pairs={{9,25},{11,27},{13,29},{15,31},{16,0},{18,2},{20,4},{22,6},{25,9},... | collective-permute-start | bytes 1572872 | tf_op jit(solution)/shard_map/ppermute | solution.py:379
  2.6 16.8 %collective-permute-start.5 = (f32[2,256,256]{2,1,0:T(8,128)}, f32[2,256,256]{2,1,0:T(8,128)S(1)}, u32[]{:S(2)}, u32[]{:S(2)}) collective-permute-start(f32[2,256,256]{2,1,0:T(8,128)} %bitcast.16), channel_id=1, source_target_pairs={{8,16},{10,18},{12,20},{14,22},{17,9},{19,11},{21,13},{23,15},{24,... | collective-permute-start | bytes 1572872 | tf_op jit(solution)/shard_map/ppermute | solution.py:379
  4.1 1.2 %copy-start = (f32[2,1,2,256,256]{4,3,2,1,0:T(8,128)S(1)}, f32[2,1,2,256,256]{4,3,2,1,0:T(8,128)}, u32[]{:S(2)}) copy-start(f32[2,1,2,256,256]{4,3,2,1,0:T(8,128)} %param.9) | copy-start | bytes 3145732
  5.3 1.0 %copy-start.1 = (f32[1,1,2,256,256]{4,3,2,1,0:T(8,128)S(1)}, f32[1,1,2,256,256]{4,3,2,1,0:T(8,128)}, u32[]{:S(2)}) copy-start(f32[1,1,2,256,256]{4,3,2,1,0:T(8,128)} %param.7) | copy-start | bytes 1572868
  6.3 0.7 copy-start.3
  7.7 15.1 %collective-permute-start = (f32[2,256,256]{2,1,0:T(8,128)S(1)}, f32[2,256,256]{2,1,0:T(8,128)S(1)}, u32[]{:S(2)}, u32[]{:S(2)}) collective-permute-start(f32[2,256,256]{2,1,0:T(8,128)S(1)} %get-tuple-element.9.b_own), channel_id=1, source_target_pairs={{1,9},{3,11},{5,13},{7,15},{8,0},{10,2},{12,4},{14,6},{17,25},{19,... | collective-permute-start | bytes 1572872 | tf_op jit(solution)/shard_map/ppermute | solution.py:379
  9.0 15.9 %collective-permute-start.1 = (f32[2,256,256]{2,1,0:T(8,128)S(1)}, f32[2,256,256]{2,1,0:T(8,128)S(1)}, u32[]{:S(2)}, u32[]{:S(2)}) collective-permute-start(f32[2,256,256]{2,1,0:T(8,128)S(1)} %get-tuple-element.10), channel_id=1, source_target_pairs={{0,16},{2,18},{4,20},{6,22},{9,25},{11,27},{13,29},{15,31},{16,0},... | collective-permute-start | bytes 1572872 | tf_op jit(solution)/shard_map/ppermute | solution.py:379
  13.9 16.7 %collective-permute-start.2 = (f32[2,256,256]{2,1,0:T(8,128)S(1)}, f32[2,256,256]{2,1,0:T(8,128)S(1)}, u32[]{:S(2)}, u32[]{:S(2)}) collective-permute-start(f32[2,256,256]{2,1,0:T(8,128)S(1)} %get-tuple-element.10), channel_id=1, source_target_pairs={{1,25},{3,27},{5,29},{7,31},{8,16},{10,18},{12,20},{14,22},{17,9},... | collective-permute-start | bytes 1572872 | tf_op jit(solution)/shard_map/ppermute | solution.py:379
  19.4 1.0 %copy-start.2 = (f32[1,1,2,256,256]{4,3,2,1,0:T(8,128)S(1)}, f32[1,1,2,256,256]{4,3,2,1,0:T(8,128)}, u32[]{:S(2)}) copy-start(f32[1,1,2,256,256]{4,3,2,1,0:T(8,128)} %param.8) | copy-start | bytes 1572868
  42.2 10.0 %copy-start.4 = (f32[2,4]{1,0:T(2,128)S(1)}, f32[2,4]{1,0:T(2,128)}, u32[]{:S(2)}) copy-start(f32[2,4]{1,0:T(2,128)} %param.11) | copy-start | bytes 100
  42.2 10.0 %copy-start.5 = (s32[4]{0:T(128)S(1)}, s32[4]{0:T(128)}, u32[]{:S(2)}) copy-start(s32[4]{0:T(128)} %param.10) | copy-start | bytes 52
  42.2 3.6 %collective-permute-start.6 = (f32[4,256,256]{2,1,0:T(8,128)S(1)}, f32[4,256,256]{2,1,0:T(8,128)S(1)}, u32[]{:S(2)}, u32[]{:S(2)}) collective-permute-start(f32[4,256,256]{2,1,0:T(8,128)S(1)} %get-tuple-element.12), channel_id=1, source_target_pairs={{0,1},{2,3},{4,5},{6,7},{9,8},{11,10},{13,12},{15,14},{16,17},{18,... | collective-permute-start | bytes 3145736 | tf_op jit(solution)/shard_map/ppermute | solution.py:379
  46.9 33.3 %all-to-all-start = ((f32[16,64,256]{2,1,0:T(8,128)}), f32[16,64,256]{2,1,0:T(8,128)S(1)}, u32[]{:S(2)}, u32[]{:S(2)}) async-start(f32[16,64,256]{2,1,0:T(8,128)} %bitcast.9), calls=%async_computation | async-start | bytes 2097152 | tf_op jit(solution)/shard_map/all_to_all | solution.py:415
  81.1 2.0 %collective-permute-start.7 = (f32[8,64,256]{2,1,0:T(8,128)S(1)}, f32[8,64,256]{2,1,0:T(8,128)S(1)}, u32[]{:S(2)}, u32[]{:S(2)}) collective-permute-start(f32[8,64,256]{2,1,0:T(8,128)S(1)} %shard_map.67), channel_id=1, source_target_pairs={{0,1},{1,0},{2,3},{3,2},{4,5},{5,4},{6,7},{7,6},{8,9},{9,8},{10,11... | collective-permute-start | bytes 1572872 | tf_op jit(solution)/shard_map/ppermute | solution.py:379

commit v7 on v6

--- a/solution.py
+++ b/solution.py
@@ -139,11 +139,9 @@
 
 
 def real_dot(left, right):
-    rows = left[0].shape[0]
-    both = jnp.concatenate([left[0], left[1]], axis=0)
-    main = jnp.dot(both, right[0], preferred_element_type=jnp.float32)
-    rest = jnp.dot(left[0], right[1], preferred_element_type=jnp.float32)
-    return main[:rows] + main[rows:] + rest
+    lhs = jnp.concatenate([left[0], left[1], left[0]], axis=1)
+    rhs = jnp.concatenate([right[0], right[0], right[1]], axis=0)
+    return jnp.dot(lhs, rhs, preferred_element_type=jnp.float32)
 
 
 def mul(left, right):
@@ -251,8 +249,13 @@
     ]
 
 
-def coupling_kernel(place, c_own, c_x, c_y, c_far, out_ref):
+def coupling_kernel(place, c_own, c_x, c_y, far_mine, far_theirs, out_ref, c_far):
     y, x = place[0], place[1]
+    first, rows = place[2] == 0, far_mine.shape[1]
+    for part in range(2):
+        mine, theirs = far_mine[part], far_theirs[part]
+        c_far[part, :rows] = jnp.where(first, mine, theirs)
+        c_far[part, rows:] = jnp.where(first, theirs, mine)
     for slab in (1, 2, 3):
         real, imag = pick_block(y, x, slab, c_own, c_x, c_y, c_far)
         for side, pair in enumerate(((real, imag), (real.T, -imag.T))):
@@ -315,6 +318,18 @@
             out_ref[energy, here, :] = total
 
 
+def pick_kernel(active, keep_ref, got_ref, out_ref):
+    for slab in range(out_ref.shape[0]):
+        out_ref[slab] = jnp.where(active[0] == 1, keep_ref[slab], got_ref[slab])
+
+
+def join_kernel(core, mine_ref, other_ref, out_ref):
+    energy = pl.program_id(0)
+    mine, other = mine_ref[energy], other_ref[energy]
+    out_ref[0, 0] = jnp.where(core[0] == 0, mine, other)
+    out_ref[0, 1] = jnp.where(core[0] == 0, other, mine)
+
+
 def prepare_kernel(place, scale, onsite_ref, hop_ref, sigma_ref, own_ref, other_ref):
     width = hop_ref.shape[-1]
     eye = lax.broadcasted_iota(jnp.int32, (width, width), 0) == lax.broadcasted_iota(
@@ -354,7 +369,7 @@
     z = lax.axis_index("energy")
     k = lax.axis_index("mom")
     y, x = slab // 2, slab % 2
-    place = jnp.stack([y, x]).astype(jnp.int32)
+    place = jnp.stack([y, x, z % 2]).astype(jnp.int32)
     active = k == x
 
     def device(yy, xx, zz, kk):
@@ -372,6 +387,7 @@
             for zz in range(energy_count)
         ]
 
+    beside = [(device(a, b, c, b), device(a, b, c ^ 1, b)) for a, b, c in chips]
     siblings = [(device(a, b, c, d), device(a, b, c, 1 - d)) for a, b, c in chips for d in range(2)]
     gift = [(device(a, b, c, b), device(a, b, c, 1 - b)) for a, b, c in chips]
 
@@ -392,9 +408,12 @@
     )(place, energies, onsite[0], hop[0, 0], sigma_in[:, 0])
 
     coupling = couple[0, 0]
+    c_part = lax.dynamic_slice_in_dim(coupling, (z % 2) * (width // 2), width // 2, axis=1)
+    far_mine = send(c_part, routes((1, 2), (2, 1), (3, 0)))
     c_x = send(coupling, routes((1, 0), (2, 3), (3, 2)))
     c_y = send(coupling, routes((1, 3), (2, 0), (3, 1)))
-    c_far = send(coupling, routes((1, 2), (2, 1), (3, 0)))
+    far_mine, c_x, c_y = lax.optimization_barrier((far_mine, c_x, c_y))
+    far_theirs = send(far_mine, beside)
     b_far = send(b_other, to_far)
     b_x = send(b_own, to_x)
     b_y = send(b_other, to_y)
@@ -402,13 +421,20 @@
     c_forms = pl.pallas_call(
         coupling_kernel,
         out_shape=jax.ShapeDtypeStruct((3, 2, 6, width, width), jnp.bfloat16),
-        in_specs=[smem] + [vmem] * 4,
+        in_specs=[smem] + [vmem] * 5,
         out_specs=vmem,
-        compiler_params=pltpu.CompilerParams(vmem_limit_bytes=VMEM_BYTES),
-    )(place, coupling, c_x, c_y, c_far)
+        scratch_shapes=[pltpu.VMEM((2, width, width), jnp.float32)],
+        compiler_params=pltpu.CompilerParams(vmem_limit_bytes=VMEM_BYTES),
+    )(place, coupling, c_x, c_y, far_mine, far_theirs)
     shape = (4, width, width)
     keep, give = call(chain_kernel, place, (b_own, b_x, b_y, b_far, c_forms), shape, 2, 26)
-    half = jnp.where(active, keep, send(give, gift))
+    half = pl.pallas_call(
+        pick_kernel,
+        out_shape=jax.ShapeDtypeStruct(shape, jnp.float32),
+        in_specs=[smem, vmem, vmem],
+        out_specs=vmem,
+        compiler_params=pltpu.CompilerParams(vmem_limit_bytes=VMEM_BYTES),
+    )(active[None].astype(jnp.int32), keep, send(give, gift))
 
     rows = width // energy_count
     slots = 4 * energy_count
@@ -424,8 +450,14 @@
         compiler_params=pltpu.CompilerParams(vmem_limit_bytes=VMEM_BYTES),
     )(phonon, parts)
     other = send(mixed, siblings)
-    mine = jnp.arange(2)[:, None, None] == k
-    result = jnp.where(mine, mixed[:, None], other[:, None])
+    result = pl.pallas_call(
+        join_kernel,
+        grid=(total,),
+        out_shape=jax.ShapeDtypeStruct((total, 2, rows, width), jnp.float32),
+        in_specs=[smem, vmem, vmem],
+        out_specs=pl.BlockSpec((1, 2, rows, width), lambda energy: (energy, 0, 0, 0)),
+        compiler_params=pltpu.CompilerParams(vmem_limit_bytes=VMEM_BYTES),
+    )(k[None].astype(jnp.int32), mixed, other)
     return result[:, None]
 
 

time: 84.7 us -> 85.9 us (1.014)
  waiting for transfers between devices: 44.7 us -> 38.1 us
  starting transfers between devices: 18.1 us -> 23 us
  Pallas kernels: 14.7 us -> 18.7 us
  other arithmetic: 2.57 us -> 0.31 us
  local copies, waits for them, and re-layouts: 4 us -> 4.98 us
    ppermute x8 -> x9, waiting for transfers between devices: 16.9 us -> 10.4 us  [send(): return lax.ppermute(value, axes, pairs)]
    pallas_call x0 -> x2, Pallas kernels: none -> 3.79 us  [the longest x1 2.71 us: owner_body(): pl.pallas_call(join_kernel, grid=(total,), out_shape=jax.ShapeDtypeStruct...]
    ppermute x8 -> x9, starting transfers between devices: 12.8 us -> 16.4 us  [send(): return lax.ppermute(value, axes, pairs)]
    select_n x2 -> x0, other arithmetic: 2.25 us -> none  [the longest x1 1.15 us: owner_body(): result = jnp.where(mine, mixed[:, None], other[:, None])]
    all_to_all x1, starting transfers between devices: 5.3 us -> 6.59 us  [owner_body(): lax.all_to_all(half.reshape(slots, rows, width), ('slab', 'energy'), 0, 0...]
    dynamic_slice x0 -> x1, local copies, waits for them, and re-layouts: none -> 0.98 us  [owner_body(): lax.dynamic_slice_in_dim(coupling, z % 2 * (width // 2), width // 2, axis=1)]
  transfers between devices with their start and end apart: 9 -> 10, of which waited for: 7 -> 5; matrix products, arithmetic and copies ran while one was open for 0% -> 2% of each run, Pallas kernels for 3% -> 3%
where the time goes in v7:
time: 85.9 us; the launch traced here: 85.4 us
  waiting for transfers between devices  38.1 us (44%)
  starting transfers between devices  23 us (27%)
  Pallas kernels  18.7 us (22%)
  local copies, waits for them, and re-layouts  4.98 us (6%)
    all_to_all x1, waiting for transfers between devices, owner_body(): lax.all_to_all(half.reshape(slots, rows, width), ('slab', 'energy'), 0, 0...  27.8 us
    ppermute x9, starting transfers between devices, send(): return lax.ppermute(value, axes, pairs)  16.4 us
    pallas_call x1, Pallas kernels, call(): pl.pallas_call(kernel, out_shape=[jax.ShapeDtypeStruct(shape, jnp.float32...  11.8 us
    ppermute x9, waiting for transfers between devices, send(): return lax.ppermute(value, axes, pairs)  10.4 us
    all_to_all x1, starting transfers between devices, owner_body(): lax.all_to_all(half.reshape(slots, rows, width), ('slab', 'energy'), 0, 0...  6.59 us
    unnamed x12, local copies, waits for them, and re-layouts  4 us
    pallas_call x1, Pallas kernels, owner_body(): pl.pallas_call(join_kernel, grid=(total,), out_shape=jax.ShapeDtypeStruct...  2.71 us
  transfers between devices with their start and end apart: 10, of which 5 were waited for; matrix products, arithmetic and copies ran while one was open for 2% of the time, Pallas kernels for 3%

profile of v7, /device:TPU:0, one launch (start us, length us, event | category | flops | bytes accessed | tf_op | source)
XLA Modules:
  0.0 85.4 jit_solution(9570227515636497367)
XLA Ops:
  0.0 1.3 %collective-permute-start.4 = (f32[2,256,256]{2,1,0:T(8,128)}, f32[2,256,256]{2,1,0:T(8,128)S(1)}, u32[]{:S(2)}, u32[]{:S(2)}) collective-permute-start(f32[2,256,256]{2,1,0:T(8,128)} %bitcast.20), channel_id=1, source_target_pairs={{8,0},{10,2},{12,4},{14,6},{17,25},{19,27},{21,29},{23,31},{24,16}... | collective-permute-start | bytes 1572872 | tf_op jit(solution)/shard_map/ppermute | solution.py:395
  1.3 1.3 %collective-permute-start.5 = (f32[2,256,256]{2,1,0:T(8,128)}, f32[2,256,256]{2,1,0:T(8,128)S(1)}, u32[]{:S(2)}, u32[]{:S(2)}) collective-permute-start(f32[2,256,256]{2,1,0:T(8,128)} %bitcast.21), channel_id=1, source_target_pairs={{9,25},{11,27},{13,29},{15,31},{16,0},{18,2},{20,4},{22,6},{25,9},... | collective-permute-start | bytes 1572872 | tf_op jit(solution)/shard_map/ppermute | solution.py:395
  2.6 1.0 %dynamic-slice_bitcast_fusion = f32[2,128,256]{2,1,0:T(8,128)S(1)} fusion(f32[1,1,2,256,256]{4,3,2,1,0:T(8,128)} %param.8, s32[]{:T(128)S(6)} %select_n.23), kind=kLoop, calls=%fused_computation | loop fusion | bytes 524292 | tf_op jit(solution)/shard_map/dynamic_slice | solution.py:411
  3.6 1.3 %collective-permute-start.3 = (f32[2,128,256]{2,1,0:T(8,128)S(1)}, f32[2,128,256]{2,1,0:T(8,128)S(1)}, u32[]{:S(2)}, u32[]{:S(2)}) collective-permute-start(f32[2,128,256]{2,1,0:T(8,128)S(1)} %dynamic-slice_bitcast_fusion), channel_id=1, source_target_pairs={{8,16},{10,18},{12,20},{14,22},{17,9},{19,11},{21,13},{23,15},{24,... | collective-permute-start | bytes 786440 | tf_op jit(solution)/shard_map/ppermute | solution.py:395
  4.9 0.1 pad_add_fusion.place
  5.0 0.1 multiply_add_fusion.scale
  5.1 1.2 %copy-done.1 = f32[2,1,2,256,256]{4,3,2,1,0:T(8,128)S(1)} copy-done((f32[2,1,2,256,256]{4,3,2,1,0:T(8,128)S(1)}, f32[2,1,2,256,256]{4,3,2,1,0:T(8,128)}, u32[]{:S(2)}) %copy-start.1) | copy-done | bytes 1048600
  6.3 1.0 %copy-done.2 = f32[1,1,2,256,256]{4,3,2,1,0:T(8,128)S(1)} copy-done((f32[1,1,2,256,256]{4,3,2,1,0:T(8,128)S(1)}, f32[1,1,2,256,256]{4,3,2,1,0:T(8,128)}, u32[]{:S(2)}) %copy-start.2) | copy-done | bytes 524312
  7.3 0.7 copy-done.3
  8.0 0.7 shard_map.64
  8.7 1.3 %collective-permute-start = (f32[2,256,256]{2,1,0:T(8,128)S(1)}, f32[2,256,256]{2,1,0:T(8,128)S(1)}, u32[]{:S(2)}, u32[]{:S(2)}) collective-permute-start(f32[2,256,256]{2,1,0:T(8,128)S(1)} %get-tuple-element.12.b_own), channel_id=1, source_target_pairs={{1,9},{3,11},{5,13},{7,15},{8,0},{10,2},{12,4},{14,6},{17,25},{19,... | collective-permute-start | bytes 1572872 | tf_op jit(solution)/shard_map/ppermute | solution.py:395
  10.0 4.9 %collective-permute-start.1 = (f32[2,256,256]{2,1,0:T(8,128)S(1)}, f32[2,256,256]{2,1,0:T(8,128)S(1)}, u32[]{:S(2)}, u32[]{:S(2)}) collective-permute-start(f32[2,256,256]{2,1,0:T(8,128)S(1)} %get-tuple-element.13), channel_id=1, source_target_pairs={{0,16},{2,18},{4,20},{6,22},{9,25},{11,27},{13,29},{15,31},{16,0},... | collective-permute-start | bytes 1572872 | tf_op jit(solution)/shard_map/ppermute | solution.py:395
  14.9 1.6 %collective-permute-done.3.far_mine = f32[2,128,256]{2,1,0:T(8,128)S(1)} collective-permute-done((f32[2,128,256]{2,1,0:T(8,128)S(1)}, f32[2,128,256]{2,1,0:T(8,128)S(1)}, u32[]{:S(2)}, u32[]{:S(2)}) %collective-permute-start.3) | collective-permute-done | bytes 262176 | tf_op jit(solution)/shard_map/ppermute | solution.py:395
  16.5 1.3 %collective-permute-start.2 = (f32[2,256,256]{2,1,0:T(8,128)S(1)}, f32[2,256,256]{2,1,0:T(8,128)S(1)}, u32[]{:S(2)}, u32[]{:S(2)}) collective-permute-start(f32[2,256,256]{2,1,0:T(8,128)S(1)} %get-tuple-element.13), channel_id=1, source_target_pairs={{1,25},{3,27},{5,29},{7,31},{8,16},{10,18},{12,20},{14,22},{17,9},... | collective-permute-start | bytes 1572872 | tf_op jit(solution)/shard_map/ppermute | solution.py:395
  17.8 3.6 %collective-permute-start.6 = (f32[2,128,256]{2,1,0:T(8,128)S(1)}, f32[2,128,256]{2,1,0:T(8,128)S(1)}, u32[]{:S(2)}, u32[]{:S(2)}) collective-permute-start(f32[2,128,256]{2,1,0:T(8,128)S(1)} %collective-permute-done.3.far_mine), channel_id=1, source_target_pairs={{0,2},{2,0},{4,6},{6,4},{9,11},{11,9},{13,15},{15,13},{16,18},{18,... | collective-permute-start | bytes 786440 | tf_op jit(solution)/shard_map/ppermute | solution.py:395
  21.4 4.7 %collective-permute-done.6.far_theirs = f32[2,128,256]{2,1,0:T(8,128)S(1)} collective-permute-done((f32[2,128,256]{2,1,0:T(8,128)S(1)}, f32[2,128,256]{2,1,0:T(8,128)S(1)}, u32[]{:S(2)}, u32[]{:S(2)}) %collective-permute-start.6) | collective-permute-done | bytes 262176 | tf_op jit(solution)/shard_map/ppermute | solution.py:395
  26.1 1.0 %copy-done = f32[1,1,2,256,256]{4,3,2,1,0:T(8,128)S(1)} copy-done((f32[1,1,2,256,256]{4,3,2,1,0:T(8,128)S(1)}, f32[1,1,2,256,256]{4,3,2,1,0:T(8,128)}, u32[]{:S(2)}) %copy-start) | copy-done | bytes 524312
  27.1 1.5 %shard_map.65.c_forms = bf16[3,2,6,256,256]{4,3,2,1,0:T(8,128)(2,1)S(1)} custom-call(s32[3]{0:T(128)S(1)} %pad_add_fusion.place, f32[2,256,256]{2,1,0:T(8,128)S(1)} %bitcast.22, f32[2,256,256]{2,1,0:T(8,128)S(1)} %collective-permute-done.4.c_x, f32[2,256,256]{2,1,0:T(8,128)S(1)} %collective-permute-done.5.c_y, ...), custom_call_target="tpu_custom_call" | custom-call | tf_op jit(solution)/shard_map/pallas_call | solution.py:421
  28.6 11.8 %shard_map.66 = (f32[4,256,256]{2,1,0:T(8,128)S(1)}, f32[4,256,256]{2,1,0:T(8,128)S(1)}) custom-call(s32[3]{0:T(128)S(1)} %pad_add_fusion.place, f32[2,256,256]{2,1,0:T(8,128)S(1)} %get-tuple-element.12.b_own, f32[2,256,256]{2,1,0:T(8,128)S(1)} %collective-permute-done.b_x, f32[2,256,256]{2,1,0:T(8,128)S(1)} %collective-permute-done.1.b_y, ...), custom_call_target="tpu_custom_call" | custom-call | flops 7851737088 | bytes 3670016 | tf_op jit(solution)/shard_map/pallas_call | solution.py:347
  40.5 0.0 copy-start.4
  40.5 0.0 copy-start.5
  40.5 1.4 %collective-permute-start.7 = (f32[4,256,256]{2,1,0:T(8,128)S(1)}, f32[4,256,256]{2,1,0:T(8,128)S(1)}, u32[]{:S(2)}, u32[]{:S(2)}) collective-permute-start(f32[4,256,256]{2,1,0:T(8,128)S(1)} %get-tuple-element.18), channel_id=1, source_target_pairs={{0,1},{2,3},{4,5},{6,7},{9,8},{11,10},{13,12},{15,14},{16,17},{18,... | collective-permute-start | bytes 3145736 | tf_op jit(solution)/shard_map/ppermute | solution.py:395
  41.9 2.2 %collective-permute-done.7.got_ref = f32[4,256,256]{2,1,0:T(8,128)S(1)} collective-permute-done((f32[4,256,256]{2,1,0:T(8,128)S(1)}, f32[4,256,256]{2,1,0:T(8,128)S(1)}, u32[]{:S(2)}, u32[]{:S(2)}) %collective-permute-start.7) | collective-permute-done | bytes 1048608 | tf_op jit(solution)/shard_map/ppermute | solution.py:395
  44.1 1.1 %shard_map.67 = f32[4,256,256]{2,1,0:T(8,128)} custom-call(s32[1]{0:T(128)} %bitcast.3.active, f32[4,256,256]{2,1,0:T(8,128)S(1)} %get-tuple-element.17.keep_ref, f32[4,256,256]{2,1,0:T(8,128)S(1)} %collective-permute-done.7.got_ref), custom_call_target="tpu_custom_call" | custom-call | tf_op jit(solution)/shard_map/pallas_call | solution.py:431
  45.2 6.6 %all-to-all-start = ((f32[16,64,256]{2,1,0:T(8,128)}), f32[16,64,256]{2,1,0:T(8,128)S(1)}, u32[]{:S(2)}, u32[]{:S(2)}) async-start(f32[16,64,256]{2,1,0:T(8,128)} %bitcast.13), calls=%async_computation | async-start | bytes 2097152 | tf_op jit(solution)/shard_map/all_to_all | solution.py:441
  51.8 0.1 iota_add_fusion
  51.9 0.1 add_reduce_fusion
  52.0 27.8 %all-to-all-done.parts_ref = f32[16,64,256]{2,1,0:T(8,128)S(1)} async-done(((f32[16,64,256]{2,1,0:T(8,128)}), f32[16,64,256]{2,1,0:T(8,128)S(1)}, u32[]{:S(2)}, u32[]{:S(2)}) %all-to-all-start) | async-done | bytes 1048608 | tf_op jit(solution)/shard_map/all_to_all | solution.py:441
  79.8 0.9 %shard_map.68.mine_ref = f32[8,64,256]{2,1,0:T(8,128)S(1)} custom-call(f32[8,8]{1,0:T(8,128)S(1)} %broadcast_multiply_fusion.phonon, f32[16,64,256]{2,1,0:T(8,128)S(1)} %all-to-all-done.parts_ref), custom_call_target="tpu_custom_call" | custom-call | tf_op jit(solution)/shard_map/pallas_call | solution.py:445
  80.7 0.1 collective-permute-start.8
  80.8 1.9 %collective-permute-done.8.other_ref = f32[8,64,256]{2,1,0:T(8,128)S(1)} collective-permute-done((f32[8,64,256]{2,1,0:T(8,128)S(1)}, f32[8,64,256]{2,1,0:T(8,128)S(1)}, u32[]{:S(2)}, u32[]{:S(2)}) %collective-permute-start.8) | collective-permute-done | bytes 524320 | tf_op jit(solution)/shard_map/ppermute | solution.py:395
  82.7 2.7 %shard_map.69 = f32[8,2,64,256]{3,2,1,0:T(8,128)} custom-call(s32[1]{0:T(128)} %bitcast.core, f32[8,64,256]{2,1,0:T(8,128)S(1)} %shard_map.68.mine_ref, f32[8,64,256]{2,1,0:T(8,128)S(1)} %collective-permute-done.8.other_ref), custom_call_target="tpu_custom_call" | custom-call | tf_op jit(solution)/shard_map/pallas_call | solution.py:453
  (13 shorter events, 0.0 us)
Async XLA Ops:
  0.0 17.8 %collective-permute-start.4 = (f32[2,256,256]{2,1,0:T(8,128)}, f32[2,256,256]{2,1,0:T(8,128)S(1)}, u32[]{:S(2)}, u32[]{:S(2)}) collective-permute-start(f32[2,256,256]{2,1,0:T(8,128)} %bitcast.20), channel_id=1, source_target_pairs={{8,0},{10,2},{12,4},{14,6},{17,25},{19,27},{21,29},{23,31},{24,16}... | collective-permute-start | bytes 1572872 | tf_op jit(solution)/shard_map/ppermute | solution.py:395
  1.3 16.5 %collective-permute-start.5 = (f32[2,256,256]{2,1,0:T(8,128)}, f32[2,256,256]{2,1,0:T(8,128)S(1)}, u32[]{:S(2)}, u32[]{:S(2)}) collective-permute-start(f32[2,256,256]{2,1,0:T(8,128)} %bitcast.21), channel_id=1, source_target_pairs={{9,25},{11,27},{13,29},{15,31},{16,0},{18,2},{20,4},{22,6},{25,9},... | collective-permute-start | bytes 1572872 | tf_op jit(solution)/shard_map/ppermute | solution.py:395
  3.6 12.9 %collective-permute-start.3 = (f32[2,128,256]{2,1,0:T(8,128)S(1)}, f32[2,128,256]{2,1,0:T(8,128)S(1)}, u32[]{:S(2)}, u32[]{:S(2)}) collective-permute-start(f32[2,128,256]{2,1,0:T(8,128)S(1)} %dynamic-slice_bitcast_fusion), channel_id=1, source_target_pairs={{8,16},{10,18},{12,20},{14,22},{17,9},{19,11},{21,13},{23,15},{24,... | collective-permute-start | bytes 786440 | tf_op jit(solution)/shard_map/ppermute | solution.py:395
  5.1 1.2 %copy-start.1 = (f32[2,1,2,256,256]{4,3,2,1,0:T(8,128)S(1)}, f32[2,1,2,256,256]{4,3,2,1,0:T(8,128)}, u32[]{:S(2)}) copy-start(f32[2,1,2,256,256]{4,3,2,1,0:T(8,128)} %param.9) | copy-start | bytes 3145732
  6.3 1.0 %copy-start.2 = (f32[1,1,2,256,256]{4,3,2,1,0:T(8,128)S(1)}, f32[1,1,2,256,256]{4,3,2,1,0:T(8,128)}, u32[]{:S(2)}) copy-start(f32[1,1,2,256,256]{4,3,2,1,0:T(8,128)} %param.7) | copy-start | bytes 1572868
  7.3 0.7 copy-start.3
  8.7 19.9 %collective-permute-start = (f32[2,256,256]{2,1,0:T(8,128)S(1)}, f32[2,256,256]{2,1,0:T(8,128)S(1)}, u32[]{:S(2)}, u32[]{:S(2)}) collective-permute-start(f32[2,256,256]{2,1,0:T(8,128)S(1)} %get-tuple-element.12.b_own), channel_id=1, source_target_pairs={{1,9},{3,11},{5,13},{7,15},{8,0},{10,2},{12,4},{14,6},{17,25},{19,... | collective-permute-start | bytes 1572872 | tf_op jit(solution)/shard_map/ppermute | solution.py:395
  10.0 18.6 %collective-permute-start.1 = (f32[2,256,256]{2,1,0:T(8,128)S(1)}, f32[2,256,256]{2,1,0:T(8,128)S(1)}, u32[]{:S(2)}, u32[]{:S(2)}) collective-permute-start(f32[2,256,256]{2,1,0:T(8,128)S(1)} %get-tuple-element.13), channel_id=1, source_target_pairs={{0,16},{2,18},{4,20},{6,22},{9,25},{11,27},{13,29},{15,31},{16,0},... | collective-permute-start | bytes 1572872 | tf_op jit(solution)/shard_map/ppermute | solution.py:395
  16.5 12.1 %collective-permute-start.2 = (f32[2,256,256]{2,1,0:T(8,128)S(1)}, f32[2,256,256]{2,1,0:T(8,128)S(1)}, u32[]{:S(2)}, u32[]{:S(2)}) collective-permute-start(f32[2,256,256]{2,1,0:T(8,128)S(1)} %get-tuple-element.13), channel_id=1, source_target_pairs={{1,25},{3,27},{5,29},{7,31},{8,16},{10,18},{12,20},{14,22},{17,9},... | collective-permute-start | bytes 1572872 | tf_op jit(solution)/shard_map/ppermute | solution.py:395
  17.8 8.3 %collective-permute-start.6 = (f32[2,128,256]{2,1,0:T(8,128)S(1)}, f32[2,128,256]{2,1,0:T(8,128)S(1)}, u32[]{:S(2)}, u32[]{:S(2)}) collective-permute-start(f32[2,128,256]{2,1,0:T(8,128)S(1)} %collective-permute-done.3.far_mine), channel_id=1, source_target_pairs={{0,2},{2,0},{4,6},{6,4},{9,11},{11,9},{13,15},{15,13},{16,18},{18,... | collective-permute-start | bytes 786440 | tf_op jit(solution)/shard_map/ppermute | solution.py:395
  26.1 1.0 %copy-start = (f32[1,1,2,256,256]{4,3,2,1,0:T(8,128)S(1)}, f32[1,1,2,256,256]{4,3,2,1,0:T(8,128)}, u32[]{:S(2)}) copy-start(f32[1,1,2,256,256]{4,3,2,1,0:T(8,128)} %param.8) | copy-start | bytes 1572868
  40.5 11.3 %copy-start.4 = (f32[2,4]{1,0:T(2,128)S(1)}, f32[2,4]{1,0:T(2,128)}, u32[]{:S(2)}) copy-start(f32[2,4]{1,0:T(2,128)} %param.11) | copy-start | bytes 100
  40.5 11.3 %copy-start.5 = (s32[4]{0:T(128)S(1)}, s32[4]{0:T(128)}, u32[]{:S(2)}) copy-start(s32[4]{0:T(128)} %param.10) | copy-start | bytes 52
  40.5 3.6 %collective-permute-start.7 = (f32[4,256,256]{2,1,0:T(8,128)S(1)}, f32[4,256,256]{2,1,0:T(8,128)S(1)}, u32[]{:S(2)}, u32[]{:S(2)}) collective-permute-start(f32[4,256,256]{2,1,0:T(8,128)S(1)} %get-tuple-element.18), channel_id=1, source_target_pairs={{0,1},{2,3},{4,5},{6,7},{9,8},{11,10},{13,12},{15,14},{16,17},{18,... | collective-permute-start | bytes 3145736 | tf_op jit(solution)/shard_map/ppermute | solution.py:395
  45.2 34.6 %all-to-all-start = ((f32[16,64,256]{2,1,0:T(8,128)}), f32[16,64,256]{2,1,0:T(8,128)S(1)}, u32[]{:S(2)}, u32[]{:S(2)}) async-start(f32[16,64,256]{2,1,0:T(8,128)} %bitcast.13), calls=%async_computation | async-start | bytes 2097152 | tf_op jit(solution)/shard_map/all_to_all | solution.py:441
  80.7 2.0 %collective-permute-start.8 = (f32[8,64,256]{2,1,0:T(8,128)S(1)}, f32[8,64,256]{2,1,0:T(8,128)S(1)}, u32[]{:S(2)}, u32[]{:S(2)}) collective-permute-start(f32[8,64,256]{2,1,0:T(8,128)S(1)} %shard_map.68.mine_ref), channel_id=1, source_target_pairs={{0,1},{1,0},{2,3},{3,2},{4,5},{5,4},{6,7},{7,6},{8,9},{9,8},{10,11... | collective-permute-start | bytes 1572872 | tf_op jit(solution)/shard_map/ppermute | solution.py:395

commit v8 on v6

--- a/solution.py
+++ b/solution.py
@@ -125,7 +125,7 @@
 VMEM_BYTES = 24 * 1024 * 1024
 
 
-BLOCKS = 2
+BLOCKS = 4
 
 
 def halves(value):
@@ -313,17 +313,6 @@
             for other in range(1, energies):
                 total = total + phonon[energy, other] * values[other]
             out_ref[energy, here, :] = total
-
-
-def prepare_kernel(place, scale, onsite_ref, hop_ref, sigma_ref, own_ref, other_ref):
-    width = hop_ref.shape[-1]
-    eye = lax.broadcasted_iota(jnp.int32, (width, width), 0) == lax.broadcasted_iota(
-        jnp.int32, (width, width), 1
-    )
-    for ref, local, energy in ((other_ref, 1 - place[0], scale[1]), (own_ref, place[0], scale[0])):
-        level = energy - onsite_ref[...]
-        ref[0] = jnp.where(eye, level, 0.0) - hop_ref[0] - sigma_ref[local, 0]
-        ref[1] = jnp.where(eye, ETA, 0.0) - hop_ref[1] - sigma_ref[local, 1]
 
 
 def call(kernel, place, arrays, shape, count, products):
@@ -378,26 +367,26 @@
     def send(value, pairs):
         return lax.ppermute(value, axes, pairs)
 
-    locals_ = jnp.stack([y, 1 - y])
-    energies = -0.5 + ((z * e_local + locals_).astype(jnp.float32) + 0.5) / total
     smem = pl.BlockSpec(memory_space=pltpu.SMEM)
     vmem = pl.BlockSpec(memory_space=pltpu.VMEM)
-    block_shape = jax.ShapeDtypeStruct((2, width, width), jnp.float32)
-    b_own, b_other = pl.pallas_call(
-        prepare_kernel,
-        out_shape=[block_shape] * 2,
-        in_specs=[smem, smem, vmem, vmem, vmem],
-        out_specs=[vmem] * 2,
-        compiler_params=pltpu.CompilerParams(vmem_limit_bytes=VMEM_BYTES),
-    )(place, energies, onsite[0], hop[0, 0], sigma_in[:, 0])
-
+    eye = jnp.eye(width, dtype=bool)
+
+    def block(local):
+        index = (z * e_local + local).astype(jnp.float32)
+        energy = -0.5 + (index + 0.5) / total
+        sigma = lax.dynamic_index_in_dim(sigma_in[:, 0], local, 0, keepdims=False)
+        real = jnp.where(eye, (energy - onsite[0, 0])[None, :], 0.0) - hop[0, 0, 0] - sigma[0]
+        imag = jnp.where(eye, ETA, 0.0) - hop[0, 0, 1] - sigma[1]
+        return jnp.stack([real, imag])
+
+    b_other, b_own = block(1 - y), block(y)
     coupling = couple[0, 0]
     c_x = send(coupling, routes((1, 0), (2, 3), (3, 2)))
     c_y = send(coupling, routes((1, 3), (2, 0), (3, 1)))
     c_far = send(coupling, routes((1, 2), (2, 1), (3, 0)))
     b_far = send(b_other, to_far)
     b_x = send(b_own, to_x)
-    b_y = send(b_other, to_y)
+    b_y = send(lax.optimization_barrier((b_other, c_y))[0], to_y)
 
     c_forms = pl.pallas_call(
         coupling_kernel,

time: 84.7 us -> 93.1 us (1.099)
  waiting for transfers between devices: 44.7 us -> 50 us
  Pallas kernels: 14.7 us -> 19.9 us
  local copies, waits for them, and re-layouts: 4 us -> 0.02 us
  other arithmetic: 2.57 us -> 5.53 us
  starting transfers between devices: 18.1 us -> 17 us
    pallas_call x1, Pallas kernels: 11.6 us -> 17.6 us  [call(): pl.pallas_call(kernel, out_shape=[jax.ShapeDtypeStruct(shape, jnp.float32...]
    ppermute x8, waiting for transfers between devices: 16.9 us -> 22.2 us  [send(): return lax.ppermute(value, axes, pairs)]
    unnamed x12 -> x6, local copies, waits for them, and re-layouts: 4 us -> 0.02 us
    sub x0 -> x2, other arithmetic: none -> 2.16 us  [the longest x1 1.48 us: block(): jnp.where(eye, (energy - onsite[0, 0])[None, :], 0.0) - hop[0, 0, 0]]
    ppermute x8, starting transfers between devices: 12.8 us -> 10.9 us  [send(): return lax.ppermute(value, axes, pairs)]
  transfers between devices with their start and end apart: 9 -> 9, of which waited for: 7 -> 8; matrix products, arithmetic and copies ran while one was open for 0% -> 4% of each run, Pallas kernels for 3% -> 1%
where the time goes in v8:
time: 93.1 us; the launch traced here: 92.7 us
  waiting for transfers between devices  50 us (54%)
  Pallas kernels  19.9 us (21%)
  starting transfers between devices  17 us (18%)
  other arithmetic  5.53 us (6%)
    all_to_all x1, waiting for transfers between devices, owner_body(): lax.all_to_all(half.reshape(slots, rows, width), ('slab', 'energy'), 0, 0...  27.8 us
    ppermute x8, waiting for transfers between devices, send(): return lax.ppermute(value, axes, pairs)  22.2 us
    pallas_call x1, Pallas kernels, call(): pl.pallas_call(kernel, out_shape=[jax.ShapeDtypeStruct(shape, jnp.float32...  17.6 us
    ppermute x8, starting transfers between devices, send(): return lax.ppermute(value, axes, pairs)  10.9 us
    all_to_all x1, starting transfers between devices, owner_body(): lax.all_to_all(half.reshape(slots, rows, width), ('slab', 'energy'), 0, 0...  6.16 us
  transfers between devices with their start and end apart: 9, of which 8 were waited for; matrix products, arithmetic and copies ran while one was open for 4% of the time, Pallas kernels for 1%

profile of v8, /device:TPU:0, one launch (start us, length us, event | category | flops | bytes accessed | tf_op | source)
XLA Modules:
  0.0 92.7 jit_solution(12684154717711995784)
XLA Ops:
  0.0 1.4 %collective-permute-start.1 = (f32[2,256,256]{2,1,0:T(8,128)}, f32[2,256,256]{2,1,0:T(8,128)S(1)}, u32[]{:S(2)}, u32[]{:S(2)}) collective-permute-start(f32[2,256,256]{2,1,0:T(8,128)} %bitcast.39), channel_id=1, source_target_pairs={{9,25},{11,27},{13,29},{15,31},{16,0},{18,2},{20,4},{22,6},{25,9},... | collective-permute-start | bytes 1572872 | tf_op jit(solution)/shard_map/ppermute | solution.py:368
  1.4 1.3 %collective-permute-start.4 = (f32[2,256,256]{2,1,0:T(8,128)}, f32[2,256,256]{2,1,0:T(8,128)S(1)}, u32[]{:S(2)}, u32[]{:S(2)}) collective-permute-start(f32[2,256,256]{2,1,0:T(8,128)} %bitcast.40), channel_id=1, source_target_pairs={{8,0},{10,2},{12,4},{14,6},{17,25},{19,27},{21,29},{23,31},{24,16}... | collective-permute-start | bytes 1572872 | tf_op jit(solution)/shard_map/ppermute | solution.py:368
  2.7 1.3 %collective-permute-start.5 = (f32[2,256,256]{2,1,0:T(8,128)}, f32[2,256,256]{2,1,0:T(8,128)S(1)}, u32[]{:S(2)}, u32[]{:S(2)}) collective-permute-start(f32[2,256,256]{2,1,0:T(8,128)} %bitcast.41), channel_id=1, source_target_pairs={{8,16},{10,18},{12,20},{14,22},{17,9},{19,11},{21,13},{23,15},{24,... | collective-permute-start | bytes 1572872 | tf_op jit(solution)/shard_map/ppermute | solution.py:368
  4.0 0.7 broadcast_subtract_fusion
  4.7 1.5 %fusion.1 = (f32[1,256,256]{2,1,0:T(8,128)S(1)}, f32[1,256,256]{2,1,0:T(8,128)S(1)}, f32[1,256,256]{2,1,0:T(8,128)S(1)}, f32[1,256,256]{2,1,0:T(8,128)S(1)}) fusion(f32[2,1,2,256,256]{4,3,2,1,0:T(8,128)} %param.9, s32[]{:T(128)S(6)} %select_n.81, f32[1,1,2,256,256]{4,3,2,1,0:T(8,128)} %param.7, f32[256]{0:T(256)S(1)} %bitcast.43, s32[]{:T(128)S(6)} %select_n.78, ...), kind=kLoop, calls=%fused_computation.7 | loop fusion | flops 720896 | bytes 2623500 | tf_op jit(solution)/shard_map/sub | solution.py:378
  6.2 0.8 pad_maximum_fusion.1
  7.0 1.3 %collective-permute-start.3 = (f32[2,256,256]{2,1,0:T(8,128)}, f32[2,256,256]{2,1,0:T(8,128)S(1)}, u32[]{:S(2)}, u32[]{:S(2)}) collective-permute-start(f32[2,256,256]{2,1,0:T(8,128)} %pad_maximum_fusion.1), channel_id=1, source_target_pairs={{1,25},{3,27},{5,29},{7,31},{8,16},{10,18},{12,20},{14,22},{17,9},... | collective-permute-start | bytes 1572872 | tf_op jit(solution)/shard_map/ppermute | solution.py:368
  8.4 1.3 %collective-permute-start = (f32[2,256,256]{2,1,0:T(8,128)S(1)}, f32[2,256,256]{2,1,0:T(8,128)}, u32[]{:S(2)}, u32[]{:S(2)}) collective-permute-start(f32[2,256,256]{2,1,0:T(8,128)S(1)} %pad_maximum_fusion.b_own), channel_id=1, source_target_pairs={{1,9},{3,11},{5,13},{7,15},{8,0},{10,2},{12,4},{14,6},{17,25},{19,... | collective-permute-start | bytes 1572872 | tf_op jit(solution)/shard_map/ppermute | solution.py:368
  9.7 2.1 %collective-permute-done.1.c_y = f32[2,256,256]{2,1,0:T(8,128)S(1)} collective-permute-done((f32[2,256,256]{2,1,0:T(8,128)}, f32[2,256,256]{2,1,0:T(8,128)S(1)}, u32[]{:S(2)}, u32[]{:S(2)}) %collective-permute-start.1) | collective-permute-done | bytes 524320 | tf_op jit(solution)/shard_map/ppermute | solution.py:368
  11.7 2.9 %collective-permute-start.2 = (f32[2,256,256]{2,1,0:T(8,128)}, f32[2,256,256]{2,1,0:T(8,128)}, u32[]{:S(2)}, u32[]{:S(2)}) collective-permute-start(f32[2,256,256]{2,1,0:T(8,128)} %pad_maximum_fusion.1), channel_id=1, source_target_pairs={{0,16},{2,18},{4,20},{6,22},{9,25},{11,27},{13,29},{15,31},{16,0},... | collective-permute-start | bytes 1572872 | tf_op jit(solution)/shard_map/ppermute | solution.py:368
  14.6 0.1 pad_add_fusion.place
  14.7 0.0 collective-permute-done.4.c_x
  14.7 6.2 %collective-permute-done.5.c_far = f32[2,256,256]{2,1,0:T(8,128)S(1)} collective-permute-done((f32[2,256,256]{2,1,0:T(8,128)}, f32[2,256,256]{2,1,0:T(8,128)S(1)}, u32[]{:S(2)}, u32[]{:S(2)}) %collective-permute-start.5) | collective-permute-done | bytes 524320 | tf_op jit(solution)/shard_map/ppermute | solution.py:368
  20.9 1.4 %shard_map.64.c_forms = bf16[3,2,6,256,256]{4,3,2,1,0:T(8,128)(2,1)S(1)} custom-call(s32[2]{0:T(128)S(1)} %pad_add_fusion.place, f32[2,256,256]{2,1,0:T(8,128)S(1)} %bitcast.42, f32[2,256,256]{2,1,0:T(8,128)S(1)} %collective-permute-done.4.c_x, f32[2,256,256]{2,1,0:T(8,128)S(1)} %collective-permute-done.1.c_y, f32[2,256,256]{2,1,0:T(8,128)S(1)} %collective-permute-done.5.c_far), custom_call_target="tpu_custom_call" | custom-call | tf_op jit(solution)/shard_map/pallas_call | solution.py:391
  22.2 4.3 %collective-permute-done.3.b_far = f32[2,256,256]{2,1,0:T(8,128)S(1)} collective-permute-done((f32[2,256,256]{2,1,0:T(8,128)}, f32[2,256,256]{2,1,0:T(8,128)S(1)}, u32[]{:S(2)}, u32[]{:S(2)}) %collective-permute-start.3) | collective-permute-done | bytes 524320 | tf_op jit(solution)/shard_map/ppermute | solution.py:368
  26.5 3.2 %collective-permute-done.b_x = f32[2,256,256]{2,1,0:T(8,128)} collective-permute-done((f32[2,256,256]{2,1,0:T(8,128)S(1)}, f32[2,256,256]{2,1,0:T(8,128)}, u32[]{:S(2)}, u32[]{:S(2)}) %collective-permute-start) | collective-permute-done | bytes 524320 | tf_op jit(solution)/shard_map/ppermute | solution.py:368
  29.7 2.4 %collective-permute-done.2.b_y = f32[2,256,256]{2,1,0:T(8,128)} collective-permute-done((f32[2,256,256]{2,1,0:T(8,128)}, f32[2,256,256]{2,1,0:T(8,128)}, u32[]{:S(2)}, u32[]{:S(2)}) %collective-permute-start.2) | collective-permute-done | bytes 524320 | tf_op jit(solution)/shard_map/ppermute | solution.py:368
  32.1 17.6 %shard_map.65 = (f32[4,256,256]{2,1,0:T(8,128)S(1)}, f32[4,256,256]{2,1,0:T(8,128)S(1)}) custom-call(s32[2]{0:T(128)S(1)} %pad_add_fusion.place, f32[2,256,256]{2,1,0:T(8,128)S(1)} %pad_maximum_fusion.b_own, f32[2,256,256]{2,1,0:T(8,128)} %collective-permute-done.b_x, f32[2,256,256]{2,1,0:T(8,128)} %collective-permute-done.2.b_y, ...), custom_call_target="tpu_custom_call" | custom-call | flops 7851737088 | bytes 3670016 | tf_op jit(solution)/shard_map/pallas_call | solution.py:321
  49.8 0.0 copy-start.1
  49.8 0.0 copy-start.2
  49.8 1.4 %collective-permute-start.6 = (f32[4,256,256]{2,1,0:T(8,128)S(1)}, f32[4,256,256]{2,1,0:T(8,128)S(1)}, u32[]{:S(2)}, u32[]{:S(2)}) collective-permute-start(f32[4,256,256]{2,1,0:T(8,128)S(1)} %get-tuple-element.10), channel_id=1, source_target_pairs={{0,1},{2,3},{4,5},{6,7},{9,8},{11,10},{13,12},{15,14},{16,17},{18,... | collective-permute-start | bytes 3145736 | tf_op jit(solution)/shard_map/ppermute | solution.py:368
  51.1 2.2 %collective-permute-done.6 = f32[4,256,256]{2,1,0:T(8,128)S(1)} collective-permute-done((f32[4,256,256]{2,1,0:T(8,128)S(1)}, f32[4,256,256]{2,1,0:T(8,128)S(1)}, u32[]{:S(2)}, u32[]{:S(2)}) %collective-permute-start.6) | collective-permute-done | bytes 1048608 | tf_op jit(solution)/shard_map/ppermute | solution.py:368
  53.3 1.1 %broadcast_select_fusion.1 = f32[4,256,256]{2,1,0:T(8,128)} fusion(f32[4,256,256]{2,1,0:T(8,128)S(1)} %get-tuple-element.9, f32[4,256,256]{2,1,0:T(8,128)S(1)} %collective-permute-done.6, pred[]{:T(512)S(6)} %eq.74), kind=kLoop, calls=%fused_computation.3 | loop fusion | flops 262144 | bytes 3145729 | tf_op jit(solution)/shard_map/jit(_where)/select_n | solution.py:400
  54.5 6.2 %all-to-all-start = ((f32[16,64,256]{2,1,0:T(8,128)}), f32[16,64,256]{2,1,0:T(8,128)S(1)}, u32[]{:S(2)}, u32[]{:S(2)}) async-start(f32[16,64,256]{2,1,0:T(8,128)} %bitcast.13), calls=%async_computation | async-start | bytes 2097152 | tf_op jit(solution)/shard_map/all_to_all | solution.py:404
  60.6 0.0 copy-done.1
  60.7 0.1 iota_add_fusion
  60.7 0.1 add_reduce_fusion
  60.8 27.8 %all-to-all-done.parts_ref = f32[16,64,256]{2,1,0:T(8,128)S(1)} async-done(((f32[16,64,256]{2,1,0:T(8,128)}), f32[16,64,256]{2,1,0:T(8,128)S(1)}, u32[]{:S(2)}, u32[]{:S(2)}) %all-to-all-start) | async-done | bytes 1048608 | tf_op jit(solution)/shard_map/all_to_all | solution.py:404
  88.6 0.9 shard_map.66
  89.5 0.1 collective-permute-start.7
  89.6 1.9 %collective-permute-done.7 = f32[8,64,256]{2,1,0:T(8,128)S(1)} collective-permute-done((f32[8,64,256]{2,1,0:T(8,128)S(1)}, f32[8,64,256]{2,1,0:T(8,128)S(1)}, u32[]{:S(2)}, u32[]{:S(2)}) %collective-permute-start.7) | collective-permute-done | bytes 524320 | tf_op jit(solution)/shard_map/ppermute | solution.py:368
  91.5 1.1 %broadcast_select_fusion = f32[8,1,2,64,256]{4,3,2,1,0:T(8,128)} fusion(f32[8,64,256]{2,1,0:T(8,128)S(1)} %collective-permute-done.7, f32[8,64,256]{2,1,0:T(8,128)S(1)} %shard_map.66, pred[2]{0:T(512)(128)(4,1)S(1)} %iota_compare_fusion.3), kind=kLoop, calls=%fused_computation.2 | loop fusion | flops 262144 | bytes 2097154 | tf_op jit(solution)/shard_map/jit(_where)/select_n | solution.py:417
  (7 shorter events, 0.1 us)
Async XLA Ops:
  0.0 20.9 %copy-start = (f32[1,1,2,256,256]{4,3,2,1,0:T(8,128)S(1)}, f32[1,1,2,256,256]{4,3,2,1,0:T(8,128)}, u32[]{:S(2)}) copy-start(f32[1,1,2,256,256]{4,3,2,1,0:T(8,128)} %param.8) | copy-start | bytes 1572868
  0.0 11.7 %collective-permute-start.1 = (f32[2,256,256]{2,1,0:T(8,128)}, f32[2,256,256]{2,1,0:T(8,128)S(1)}, u32[]{:S(2)}, u32[]{:S(2)}) collective-permute-start(f32[2,256,256]{2,1,0:T(8,128)} %bitcast.39), channel_id=1, source_target_pairs={{9,25},{11,27},{13,29},{15,31},{16,0},{18,2},{20,4},{22,6},{25,9},... | collective-permute-start | bytes 1572872 | tf_op jit(solution)/shard_map/ppermute | solution.py:368
  1.4 13.3 %collective-permute-start.4 = (f32[2,256,256]{2,1,0:T(8,128)}, f32[2,256,256]{2,1,0:T(8,128)S(1)}, u32[]{:S(2)}, u32[]{:S(2)}) collective-permute-start(f32[2,256,256]{2,1,0:T(8,128)} %bitcast.40), channel_id=1, source_target_pairs={{8,0},{10,2},{12,4},{14,6},{17,25},{19,27},{21,29},{23,31},{24,16}... | collective-permute-start | bytes 1572872 | tf_op jit(solution)/shard_map/ppermute | solution.py:368
  2.7 18.1 %collective-permute-start.5 = (f32[2,256,256]{2,1,0:T(8,128)}, f32[2,256,256]{2,1,0:T(8,128)S(1)}, u32[]{:S(2)}, u32[]{:S(2)}) collective-permute-start(f32[2,256,256]{2,1,0:T(8,128)} %bitcast.41), channel_id=1, source_target_pairs={{8,16},{10,18},{12,20},{14,22},{17,9},{19,11},{21,13},{23,15},{24,... | collective-permute-start | bytes 1572872 | tf_op jit(solution)/shard_map/ppermute | solution.py:368
  7.0 19.4 %collective-permute-start.3 = (f32[2,256,256]{2,1,0:T(8,128)}, f32[2,256,256]{2,1,0:T(8,128)S(1)}, u32[]{:S(2)}, u32[]{:S(2)}) collective-permute-start(f32[2,256,256]{2,1,0:T(8,128)} %pad_maximum_fusion.1), channel_id=1, source_target_pairs={{1,25},{3,27},{5,29},{7,31},{8,16},{10,18},{12,20},{14,22},{17,9},... | collective-permute-start | bytes 1572872 | tf_op jit(solution)/shard_map/ppermute | solution.py:368
  8.4 21.3 %collective-permute-start = (f32[2,256,256]{2,1,0:T(8,128)S(1)}, f32[2,256,256]{2,1,0:T(8,128)}, u32[]{:S(2)}, u32[]{:S(2)}) collective-permute-start(f32[2,256,256]{2,1,0:T(8,128)S(1)} %pad_maximum_fusion.b_own), channel_id=1, source_target_pairs={{1,9},{3,11},{5,13},{7,15},{8,0},{10,2},{12,4},{14,6},{17,25},{19,... | collective-permute-start | bytes 1572872 | tf_op jit(solution)/shard_map/ppermute | solution.py:368
  11.7 20.4 %collective-permute-start.2 = (f32[2,256,256]{2,1,0:T(8,128)}, f32[2,256,256]{2,1,0:T(8,128)}, u32[]{:S(2)}, u32[]{:S(2)}) collective-permute-start(f32[2,256,256]{2,1,0:T(8,128)} %pad_maximum_fusion.1), channel_id=1, source_target_pairs={{0,16},{2,18},{4,20},{6,22},{9,25},{11,27},{13,29},{15,31},{16,0},... | collective-permute-start | bytes 1572872 | tf_op jit(solution)/shard_map/ppermute | solution.py:368
  49.8 10.9 %copy-start.1 = (f32[2,4]{1,0:T(2,128)S(1)}, f32[2,4]{1,0:T(2,128)}, u32[]{:S(2)}) copy-start(f32[2,4]{1,0:T(2,128)} %param.11) | copy-start | bytes 100
  49.8 10.9 %copy-start.2 = (s32[4]{0:T(128)S(1)}, s32[4]{0:T(128)}, u32[]{:S(2)}) copy-start(s32[4]{0:T(128)} %param.10) | copy-start | bytes 52
  49.8 3.6 %collective-permute-start.6 = (f32[4,256,256]{2,1,0:T(8,128)S(1)}, f32[4,256,256]{2,1,0:T(8,128)S(1)}, u32[]{:S(2)}, u32[]{:S(2)}) collective-permute-start(f32[4,256,256]{2,1,0:T(8,128)S(1)} %get-tuple-element.10), channel_id=1, source_target_pairs={{0,1},{2,3},{4,5},{6,7},{9,8},{11,10},{13,12},{15,14},{16,17},{18,... | collective-permute-start | bytes 3145736 | tf_op jit(solution)/shard_map/ppermute | solution.py:368
  54.5 34.2 %all-to-all-start = ((f32[16,64,256]{2,1,0:T(8,128)}), f32[16,64,256]{2,1,0:T(8,128)S(1)}, u32[]{:S(2)}, u32[]{:S(2)}) async-start(f32[16,64,256]{2,1,0:T(8,128)} %bitcast.13), calls=%async_computation | async-start | bytes 2097152 | tf_op jit(solution)/shard_map/all_to_all | solution.py:404
  89.5 2.0 %collective-permute-start.7 = (f32[8,64,256]{2,1,0:T(8,128)S(1)}, f32[8,64,256]{2,1,0:T(8,128)S(1)}, u32[]{:S(2)}, u32[]{:S(2)}) collective-permute-start(f32[8,64,256]{2,1,0:T(8,128)S(1)} %shard_map.66), channel_id=1, source_target_pairs={{0,1},{1,0},{2,3},{3,2},{4,5},{5,4},{6,7},{7,6},{8,9},{9,8},{10,11... | collective-permute-start | bytes 1572872 | tf_op jit(solution)/shard_map/ppermute | solution.py:368

commit v9 on v8

--- a/solution.py
+++ b/solution.py
@@ -125,7 +125,7 @@
 VMEM_BYTES = 24 * 1024 * 1024
 
 
-BLOCKS = 4
+BLOCKS = 1
 
 
 def halves(value):
@@ -251,8 +251,9 @@
     ]
 
 
-def coupling_kernel(place, c_own, c_x, c_y, c_far, out_ref):
+def coupling_kernel(place, c_own, c_x, c_y, far, out_ref):
     y, x = place[0], place[1]
+    c_far = far.at[2:]
     for slab in (1, 2, 3):
         real, imag = pick_block(y, x, slab, c_own, c_x, c_y, c_far)
         for side, pair in enumerate(((real, imag), (real.T, -imag.T))):
@@ -383,10 +384,9 @@
     coupling = couple[0, 0]
     c_x = send(coupling, routes((1, 0), (2, 3), (3, 2)))
     c_y = send(coupling, routes((1, 3), (2, 0), (3, 1)))
-    c_far = send(coupling, routes((1, 2), (2, 1), (3, 0)))
-    b_far = send(b_other, to_far)
+    far = send(jnp.concatenate([b_other, coupling]), to_far)
     b_x = send(b_own, to_x)
-    b_y = send(lax.optimization_barrier((b_other, c_y))[0], to_y)
+    b_y = send(b_other, to_y)
 
     c_forms = pl.pallas_call(
         coupling_kernel,
@@ -394,9 +394,9 @@
         in_specs=[smem] + [vmem] * 4,
         out_specs=vmem,
         compiler_params=pltpu.CompilerParams(vmem_limit_bytes=VMEM_BYTES),
-    )(place, coupling, c_x, c_y, c_far)
+    )(place, coupling, c_x, c_y, far)
     shape = (4, width, width)
-    keep, give = call(chain_kernel, place, (b_own, b_x, b_y, b_far, c_forms), shape, 2, 26)
+    keep, give = call(chain_kernel, place, (b_own, b_x, b_y, far, c_forms), shape, 2, 26)
     half = jnp.where(active, keep, send(give, gift))
 
     rows = width // energy_count

time: 93.1 us -> 91.6 us (0.984)
  Pallas kernels: 19.9 us -> 16.3 us
  other arithmetic: 5.53 us -> 7.7 us
    pallas_call x1, Pallas kernels: 17.6 us -> 14 us  [call(): pl.pallas_call(kernel, out_shape=[jax.ShapeDtypeStruct(shape, jnp.float32...]
    concatenate x0 -> x1, other arithmetic: none -> 2.11 us  [owner_body(): far = send(jnp.concatenate([b_other, coupling]), to_far)]
    ppermute x8 -> x7, starting transfers between devices: 10.9 us -> 11.6 us  [send(): return lax.ppermute(value, axes, pairs)]
    ppermute x8 -> x7, waiting for transfers between devices: 22.2 us -> 22.5 us  [send(): return lax.ppermute(value, axes, pairs)]
  transfers between devices with their start and end apart: 9 -> 8, of which waited for: 8 -> 6; matrix products, arithmetic and copies ran while one was open for 4% -> 1% of each run, Pallas kernels for 1% -> 1%
where the time goes in v9:
time: 91.6 us; the launch traced here: 91.2 us
  waiting for transfers between devices  50.1 us (55%)
  starting transfers between devices  16.9 us (18%)
  Pallas kernels  16.3 us (18%)
  other arithmetic  7.7 us (8%)
    all_to_all x1, waiting for transfers between devices, owner_body(): lax.all_to_all(half.reshape(slots, rows, width), ('slab', 'energy'), 0, 0...  27.6 us
    ppermute x7, waiting for transfers between devices, send(): return lax.ppermute(value, axes, pairs)  22.5 us
    pallas_call x1, Pallas kernels, call(): pl.pallas_call(kernel, out_shape=[jax.ShapeDtypeStruct(shape, jnp.float32...  14 us
    ppermute x7, starting transfers between devices, send(): return lax.ppermute(value, axes, pairs)  11.6 us
    all_to_all x1, starting transfers between devices, owner_body(): lax.all_to_all(half.reshape(slots, rows, width), ('slab', 'energy'), 0, 0...  5.32 us
    concatenate x1, other arithmetic, owner_body(): far = send(jnp.concatenate([b_other, coupling]), to_far)  2.11 us
  transfers between devices with their start and end apart: 8, of which 6 were waited for; matrix products, arithmetic and copies ran while one was open for 1% of the time, Pallas kernels for 1%

profile of v9, /device:TPU:0, one launch (start us, length us, event | category | flops | bytes accessed | tf_op | source)
XLA Modules:
  0.0 91.2 jit_solution(11578424884385978852)
XLA Ops:
  0.0 0.7 broadcast_subtract_fusion
  0.7 1.5 %fusion.1 = (f32[1,256,256]{2,1,0:T(8,128)S(1)}, f32[1,256,256]{2,1,0:T(8,128)S(1)}, f32[1,256,256]{2,1,0:T(8,128)S(1)}, f32[1,256,256]{2,1,0:T(8,128)S(1)}) fusion(f32[2,1,2,256,256]{4,3,2,1,0:T(8,128)} %param.9, s32[]{:T(128)S(6)} %select_n.81, f32[1,1,2,256,256]{4,3,2,1,0:T(8,128)} %param.7, f32[256]{0:T(256)S(1)} %bitcast.43, s32[]{:T(128)S(6)} %select_n.78, ...), kind=kLoop, calls=%fused_computation.8 | loop fusion | flops 720896 | bytes 2623500 | tf_op jit(solution)/shard_map/sub | solution.py:379
  2.2 2.1 %pad_maximum_fusion = f32[4,256,256]{2,1,0:T(8,128)} fusion(f32[2,256,256]{2,1,0:T(8,128)} %bitcast.39, f32[1,256,256]{2,1,0:T(8,128)S(1)} %get-tuple-element.11, f32[1,256,256]{2,1,0:T(8,128)S(1)} %get-tuple-element.9), kind=kLoop, calls=%fused_computation | loop fusion | flops 524288 | bytes 2097152 | tf_op jit(solution)/shard_map/concatenate | solution.py:387
  4.3 1.3 %collective-permute-start.2 = (f32[4,256,256]{2,1,0:T(8,128)}, f32[4,256,256]{2,1,0:T(8,128)S(1)}, u32[]{:S(2)}, u32[]{:S(2)}) collective-permute-start(f32[4,256,256]{2,1,0:T(8,128)} %pad_maximum_fusion), channel_id=1, source_target_pairs={{1,25},{3,27},{5,29},{7,31},{8,16},{10,18},{12,20},{14,22},{17,9},... | collective-permute-start | bytes 3145736 | tf_op jit(solution)/shard_map/ppermute | solution.py:369
  5.6 0.0 copy-done
  5.6 1.3 %collective-permute-start.3 = (f32[2,256,256]{2,1,0:T(8,128)S(1)}, f32[2,256,256]{2,1,0:T(8,128)S(1)}, u32[]{:S(2)}, u32[]{:S(2)}) collective-permute-start(f32[2,256,256]{2,1,0:T(8,128)S(1)} %bitcast.40), channel_id=1, source_target_pairs={{8,0},{10,2},{12,4},{14,6},{17,25},{19,27},{21,29},{23,31},{24,16}... | collective-permute-start | bytes 1572872 | tf_op jit(solution)/shard_map/ppermute | solution.py:369
  6.9 1.3 %collective-permute-start.4 = (f32[2,256,256]{2,1,0:T(8,128)S(1)}, f32[2,256,256]{2,1,0:T(8,128)S(1)}, u32[]{:S(2)}, u32[]{:S(2)}) collective-permute-start(f32[2,256,256]{2,1,0:T(8,128)S(1)} %bitcast.41), channel_id=1, source_target_pairs={{9,25},{11,27},{13,29},{15,31},{16,0},{18,2},{20,4},{22,6},{25,9},... | collective-permute-start | bytes 1572872 | tf_op jit(solution)/shard_map/ppermute | solution.py:369
  8.2 0.8 pad_maximum_fusion.2
  9.1 4.9 %collective-permute-start.1 = (f32[2,256,256]{2,1,0:T(8,128)}, f32[2,256,256]{2,1,0:T(8,128)}, u32[]{:S(2)}, u32[]{:S(2)}) collective-permute-start(f32[2,256,256]{2,1,0:T(8,128)} %pad_maximum_fusion.2), channel_id=1, source_target_pairs={{0,16},{2,18},{4,20},{6,22},{9,25},{11,27},{13,29},{15,31},{16,0},... | collective-permute-start | bytes 1572872 | tf_op jit(solution)/shard_map/ppermute | solution.py:369
  14.0 1.3 %collective-permute-start = (f32[2,256,256]{2,1,0:T(8,128)S(1)}, f32[2,256,256]{2,1,0:T(8,128)}, u32[]{:S(2)}, u32[]{:S(2)}) collective-permute-start(f32[2,256,256]{2,1,0:T(8,128)S(1)} %pad_maximum_fusion.1.b_own), channel_id=1, source_target_pairs={{1,9},{3,11},{5,13},{7,15},{8,0},{10,2},{12,4},{14,6},{17,25},{19,... | collective-permute-start | bytes 1572872 | tf_op jit(solution)/shard_map/ppermute | solution.py:369
  15.3 0.1 pad_add_fusion.place
  15.4 13.9 %collective-permute-done.3.c_x = f32[2,256,256]{2,1,0:T(8,128)S(1)} collective-permute-done((f32[2,256,256]{2,1,0:T(8,128)S(1)}, f32[2,256,256]{2,1,0:T(8,128)S(1)}, u32[]{:S(2)}, u32[]{:S(2)}) %collective-permute-start.3) | collective-permute-done | bytes 524320 | tf_op jit(solution)/shard_map/ppermute | solution.py:369
  29.3 0.0 collective-permute-done.4.c_y
  29.3 0.0 collective-permute-done.2.far.b_far
  29.3 1.4 %shard_map.64.c_forms = bf16[3,2,6,256,256]{4,3,2,1,0:T(8,128)(2,1)S(1)} custom-call(s32[2]{0:T(128)S(1)} %pad_add_fusion.place, f32[2,256,256]{2,1,0:T(8,128)S(1)} %bitcast.42, f32[2,256,256]{2,1,0:T(8,128)S(1)} %collective-permute-done.3.c_x, f32[2,256,256]{2,1,0:T(8,128)S(1)} %collective-permute-done.4.c_y, ...), custom_call_target="tpu_custom_call" | custom-call | tf_op jit(solution)/shard_map/pallas_call | solution.py:391
  30.7 3.2 %collective-permute-done.1.b_y = f32[2,256,256]{2,1,0:T(8,128)} collective-permute-done((f32[2,256,256]{2,1,0:T(8,128)}, f32[2,256,256]{2,1,0:T(8,128)}, u32[]{:S(2)}, u32[]{:S(2)}) %collective-permute-start.1) | collective-permute-done | bytes 524320 | tf_op jit(solution)/shard_map/ppermute | solution.py:369
  33.8 1.2 %collective-permute-done.b_x = f32[2,256,256]{2,1,0:T(8,128)} collective-permute-done((f32[2,256,256]{2,1,0:T(8,128)S(1)}, f32[2,256,256]{2,1,0:T(8,128)}, u32[]{:S(2)}, u32[]{:S(2)}) %collective-permute-start) | collective-permute-done | bytes 524320 | tf_op jit(solution)/shard_map/ppermute | solution.py:369
  35.0 14.0 %shard_map.65 = (f32[4,256,256]{2,1,0:T(8,128)S(1)}, f32[4,256,256]{2,1,0:T(8,128)}) custom-call(s32[2]{0:T(128)S(1)} %pad_add_fusion.place, f32[2,256,256]{2,1,0:T(8,128)S(1)} %pad_maximum_fusion.1.b_own, f32[2,256,256]{2,1,0:T(8,128)} %collective-permute-done.b_x, f32[2,256,256]{2,1,0:T(8,128)} %collective-permute-done.1.b_y, ...), custom_call_target="tpu_custom_call" | custom-call | flops 7851737088 | bytes 3670016 | tf_op jit(solution)/shard_map/pallas_call | solution.py:322
  49.1 0.0 copy-start.1
  49.1 1.5 %collective-permute-start.5 = (f32[4,256,256]{2,1,0:T(8,128)}, f32[4,256,256]{2,1,0:T(8,128)S(1)}, u32[]{:S(2)}, u32[]{:S(2)}) collective-permute-start(f32[4,256,256]{2,1,0:T(8,128)} %get-tuple-element.8), channel_id=1, source_target_pairs={{0,1},{2,3},{4,5},{6,7},{9,8},{11,10},{13,12},{15,14},{16,17},{18,... | collective-permute-start | bytes 3145736 | tf_op jit(solution)/shard_map/ppermute | solution.py:369
  50.6 2.4 %collective-permute-done.5 = f32[4,256,256]{2,1,0:T(8,128)S(1)} collective-permute-done((f32[4,256,256]{2,1,0:T(8,128)}, f32[4,256,256]{2,1,0:T(8,128)S(1)}, u32[]{:S(2)}, u32[]{:S(2)}) %collective-permute-start.5) | collective-permute-done | bytes 1048608 | tf_op jit(solution)/shard_map/ppermute | solution.py:369
  53.0 1.1 %broadcast_select_fusion.1 = f32[4,256,256]{2,1,0:T(8,128)} fusion(f32[4,256,256]{2,1,0:T(8,128)S(1)} %get-tuple-element.7, f32[4,256,256]{2,1,0:T(8,128)S(1)} %collective-permute-done.5, pred[]{:T(512)S(6)} %eq.74), kind=kLoop, calls=%fused_computation.4 | loop fusion | flops 262144 | bytes 3145729 | tf_op jit(solution)/shard_map/jit(_where)/select_n | solution.py:400
  54.1 5.3 %all-to-all-start = ((f32[16,64,256]{2,1,0:T(8,128)}), f32[16,64,256]{2,1,0:T(8,128)S(1)}, u32[]{:S(2)}, u32[]{:S(2)}) async-start(f32[16,64,256]{2,1,0:T(8,128)} %bitcast.13), calls=%async_computation | async-start | bytes 2097152 | tf_op jit(solution)/shard_map/all_to_all | solution.py:404
  59.4 0.0 copy-done.1
  59.4 0.0 copy-done.2
  59.4 0.1 iota_add_fusion
  59.5 0.1 add_reduce_fusion
  59.6 27.6 %all-to-all-done.parts_ref = f32[16,64,256]{2,1,0:T(8,128)S(1)} async-done(((f32[16,64,256]{2,1,0:T(8,128)}), f32[16,64,256]{2,1,0:T(8,128)S(1)}, u32[]{:S(2)}, u32[]{:S(2)}) %all-to-all-start) | async-done | bytes 1048608 | tf_op jit(solution)/shard_map/all_to_all | solution.py:404
  87.2 0.9 %shard_map.66 = f32[8,64,256]{2,1,0:T(8,128)S(1)} custom-call(f32[8,8]{1,0:T(8,128)S(1)} %broadcast_multiply_fusion.phonon, f32[16,64,256]{2,1,0:T(8,128)S(1)} %all-to-all-done.parts_ref), custom_call_target="tpu_custom_call" | custom-call | tf_op jit(solution)/shard_map/pallas_call | solution.py:408
  88.1 0.1 collective-permute-start.6
  88.2 1.9 %collective-permute-done.6 = f32[8,64,256]{2,1,0:T(8,128)S(1)} collective-permute-done((f32[8,64,256]{2,1,0:T(8,128)S(1)}, f32[8,64,256]{2,1,0:T(8,128)S(1)}, u32[]{:S(2)}, u32[]{:S(2)}) %collective-permute-start.6) | collective-permute-done | bytes 524320 | tf_op jit(solution)/shard_map/ppermute | solution.py:369
  90.1 1.1 %broadcast_select_fusion = f32[8,1,2,64,256]{4,3,2,1,0:T(8,128)} fusion(f32[8,64,256]{2,1,0:T(8,128)S(1)} %collective-permute-done.6, f32[8,64,256]{2,1,0:T(8,128)S(1)} %shard_map.66, pred[2]{0:T(512)(128)(4,1)S(1)} %iota_compare_fusion.3), kind=kLoop, calls=%fused_computation.3 | loop fusion | flops 262144 | bytes 2097154 | tf_op jit(solution)/shard_map/jit(_where)/select_n | solution.py:417
  (6 shorter events, 0.1 us)
Async XLA Ops:
  0.0 5.6 %copy-start = (f32[1,1,2,256,256]{4,3,2,1,0:T(8,128)S(1)}, f32[1,1,2,256,256]{4,3,2,1,0:T(8,128)}, u32[]{:S(2)}) copy-start(f32[1,1,2,256,256]{4,3,2,1,0:T(8,128)} %param.8) | copy-start | bytes 1572868
  4.3 25.0 %collective-permute-start.2 = (f32[4,256,256]{2,1,0:T(8,128)}, f32[4,256,256]{2,1,0:T(8,128)S(1)}, u32[]{:S(2)}, u32[]{:S(2)}) collective-permute-start(f32[4,256,256]{2,1,0:T(8,128)} %pad_maximum_fusion), channel_id=1, source_target_pairs={{1,25},{3,27},{5,29},{7,31},{8,16},{10,18},{12,20},{14,22},{17,9},... | collective-permute-start | bytes 3145736 | tf_op jit(solution)/shard_map/ppermute | solution.py:369
  5.6 23.7 %collective-permute-start.3 = (f32[2,256,256]{2,1,0:T(8,128)S(1)}, f32[2,256,256]{2,1,0:T(8,128)S(1)}, u32[]{:S(2)}, u32[]{:S(2)}) collective-permute-start(f32[2,256,256]{2,1,0:T(8,128)S(1)} %bitcast.40), channel_id=1, source_target_pairs={{8,0},{10,2},{12,4},{14,6},{17,25},{19,27},{21,29},{23,31},{24,16}... | collective-permute-start | bytes 1572872 | tf_op jit(solution)/shard_map/ppermute | solution.py:369
  6.9 22.4 %collective-permute-start.4 = (f32[2,256,256]{2,1,0:T(8,128)S(1)}, f32[2,256,256]{2,1,0:T(8,128)S(1)}, u32[]{:S(2)}, u32[]{:S(2)}) collective-permute-start(f32[2,256,256]{2,1,0:T(8,128)S(1)} %bitcast.41), channel_id=1, source_target_pairs={{9,25},{11,27},{13,29},{15,31},{16,0},{18,2},{20,4},{22,6},{25,9},... | collective-permute-start | bytes 1572872 | tf_op jit(solution)/shard_map/ppermute | solution.py:369
  9.1 24.7 %collective-permute-start.1 = (f32[2,256,256]{2,1,0:T(8,128)}, f32[2,256,256]{2,1,0:T(8,128)}, u32[]{:S(2)}, u32[]{:S(2)}) collective-permute-start(f32[2,256,256]{2,1,0:T(8,128)} %pad_maximum_fusion.2), channel_id=1, source_target_pairs={{0,16},{2,18},{4,20},{6,22},{9,25},{11,27},{13,29},{15,31},{16,0},... | collective-permute-start | bytes 1572872 | tf_op jit(solution)/shard_map/ppermute | solution.py:369
  14.0 21.0 %collective-permute-start = (f32[2,256,256]{2,1,0:T(8,128)S(1)}, f32[2,256,256]{2,1,0:T(8,128)}, u32[]{:S(2)}, u32[]{:S(2)}) collective-permute-start(f32[2,256,256]{2,1,0:T(8,128)S(1)} %pad_maximum_fusion.1.b_own), channel_id=1, source_target_pairs={{1,9},{3,11},{5,13},{7,15},{8,0},{10,2},{12,4},{14,6},{17,25},{19,... | collective-permute-start | bytes 1572872 | tf_op jit(solution)/shard_map/ppermute | solution.py:369
  49.1 10.3 %copy-start.1 = (f32[2,4]{1,0:T(2,128)S(1)}, f32[2,4]{1,0:T(2,128)}, u32[]{:S(2)}) copy-start(f32[2,4]{1,0:T(2,128)} %param.11) | copy-start | bytes 100
  49.1 10.4 %copy-start.2 = (s32[4]{0:T(128)S(1)}, s32[4]{0:T(128)}, u32[]{:S(2)}) copy-start(s32[4]{0:T(128)} %param.10) | copy-start | bytes 52
  49.1 3.9 %collective-permute-start.5 = (f32[4,256,256]{2,1,0:T(8,128)}, f32[4,256,256]{2,1,0:T(8,128)S(1)}, u32[]{:S(2)}, u32[]{:S(2)}) collective-permute-start(f32[4,256,256]{2,1,0:T(8,128)} %get-tuple-element.8), channel_id=1, source_target_pairs={{0,1},{2,3},{4,5},{6,7},{9,8},{11,10},{13,12},{15,14},{16,17},{18,... | collective-permute-start | bytes 3145736 | tf_op jit(solution)/shard_map/ppermute | solution.py:369
  54.1 33.1 %all-to-all-start = ((f32[16,64,256]{2,1,0:T(8,128)}), f32[16,64,256]{2,1,0:T(8,128)S(1)}, u32[]{:S(2)}, u32[]{:S(2)}) async-start(f32[16,64,256]{2,1,0:T(8,128)} %bitcast.13), calls=%async_computation | async-start | bytes 2097152 | tf_op jit(solution)/shard_map/all_to_all | solution.py:404
  88.1 2.0 %collective-permute-start.6 = (f32[8,64,256]{2,1,0:T(8,128)S(1)}, f32[8,64,256]{2,1,0:T(8,128)S(1)}, u32[]{:S(2)}, u32[]{:S(2)}) collective-permute-start(f32[8,64,256]{2,1,0:T(8,128)S(1)} %shard_map.66), channel_id=1, source_target_pairs={{0,1},{1,0},{2,3},{3,2},{4,5},{5,4},{6,7},{7,6},{8,9},{9,8},{10,11... | collective-permute-start | bytes 1572872 | tf_op jit(solution)/shard_map/ppermute | solution.py:369

commit v10 on v8

--- a/solution.py
+++ b/solution.py
@@ -125,7 +125,7 @@
 VMEM_BYTES = 24 * 1024 * 1024
 
 
-BLOCKS = 4
+BLOCKS = 2
 
 
 def halves(value):
@@ -154,8 +154,8 @@
 
 
 def mul_twice(blocks, right, last):
-    inner = [mul(block, right) for block in blocks]
-    return [mul(form(block), last) for block in inner]
+    inner = mul(form_rows(blocks), right)
+    return [mul(form(block), last) for block in split_rows(inner)]
 
 
 def split_rows(pair):
@@ -216,7 +216,7 @@
         scaled.append(times(down, off))
     forms = [form(block) for block in scaled]
     right = form_rows(forms)
-    squares = [mul(block, right) for block in forms]
+    squares = split_rows(mul(right, right))
     cubes = [mul(form(block), right) for block in squares]
     factor = invert(*across)
     out = []
@@ -251,8 +251,13 @@
     ]
 
 
-def coupling_kernel(place, c_own, c_x, c_y, c_far, out_ref):
+def coupling_kernel(place, c_own, c_x, c_y, far_mine, far_theirs, out_ref, c_far):
     y, x = place[0], place[1]
+    first, rows = place[2] == 0, far_mine.shape[1]
+    for part in range(2):
+        mine, theirs = far_mine[part], far_theirs[part]
+        c_far[part, :rows] = jnp.where(first, mine, theirs)
+        c_far[part, rows:] = jnp.where(first, theirs, mine)
     for slab in (1, 2, 3):
         real, imag = pick_block(y, x, slab, c_own, c_x, c_y, c_far)
         for side, pair in enumerate(((real, imag), (real.T, -imag.T))):
@@ -343,7 +348,7 @@
     z = lax.axis_index("energy")
     k = lax.axis_index("mom")
     y, x = slab // 2, slab % 2
-    place = jnp.stack([y, x]).astype(jnp.int32)
+    place = jnp.stack([y, x, z % 2]).astype(jnp.int32)
     active = k == x
 
     def device(yy, xx, zz, kk):
@@ -361,6 +366,7 @@
             for zz in range(energy_count)
         ]
 
+    beside = [(device(a, b, c, b), device(a, b, c ^ 1, b)) for a, b, c in chips]
     siblings = [(device(a, b, c, d), device(a, b, c, 1 - d)) for a, b, c in chips for d in range(2)]
     gift = [(device(a, b, c, b), device(a, b, c, 1 - b)) for a, b, c in chips]
 
@@ -381,20 +387,24 @@
 
     b_other, b_own = block(1 - y), block(y)
     coupling = couple[0, 0]
+    c_part = lax.dynamic_slice_in_dim(coupling, (z % 2) * (width // 2), width // 2, axis=1)
+    far_mine = send(c_part, routes((1, 2), (2, 1), (3, 0)))
     c_x = send(coupling, routes((1, 0), (2, 3), (3, 2)))
     c_y = send(coupling, routes((1, 3), (2, 0), (3, 1)))
-    c_far = send(coupling, routes((1, 2), (2, 1), (3, 0)))
+    far_mine, c_x, c_y = lax.optimization_barrier((far_mine, c_x, c_y))
+    far_theirs = send(far_mine, beside)
     b_far = send(b_other, to_far)
     b_x = send(b_own, to_x)
-    b_y = send(lax.optimization_barrier((b_other, c_y))[0], to_y)
+    b_y = send(b_other, to_y)
 
     c_forms = pl.pallas_call(
         coupling_kernel,
         out_shape=jax.ShapeDtypeStruct((3, 2, 6, width, width), jnp.bfloat16),
-        in_specs=[smem] + [vmem] * 4,
+        in_specs=[smem] + [vmem] * 5,
         out_specs=vmem,
+        scratch_shapes=[pltpu.VMEM((2, width, width), jnp.float32)],
         compiler_params=pltpu.CompilerParams(vmem_limit_bytes=VMEM_BYTES),
-    )(place, coupling, c_x, c_y, c_far)
+    )(place, coupling, c_x, c_y, far_mine, far_theirs)
     shape = (4, width, width)
     keep, give = call(chain_kernel, place, (b_own, b_x, b_y, b_far, c_forms), shape, 2, 26)
     half = jnp.where(active, keep, send(give, gift))

time: 93.1 us -> 89.3 us (0.959)
  waiting for transfers between devices: 50 us -> 40.1 us
  starting transfers between devices: 17 us -> 25.9 us
  Pallas kernels: 19.9 us -> 16 us
  local copies, waits for them, and re-layouts: 0.02 us -> 1 us
    ppermute x8 -> x9, waiting for transfers between devices: 22.2 us -> 12.2 us  [send(): return lax.ppermute(value, axes, pairs)]
    ppermute x8 -> x9, starting transfers between devices: 10.9 us -> 17.8 us  [send(): return lax.ppermute(value, axes, pairs)]
    pallas_call x1, Pallas kernels: 17.6 us -> 13.7 us  [call(): pl.pallas_call(kernel, out_shape=[jax.ShapeDtypeStruct(shape, jnp.float32...]
    all_to_all x1, starting transfers between devices: 6.16 us -> 8.07 us  [owner_body(): lax.all_to_all(half.reshape(slots, rows, width), ('slab', 'energy'), 0, 0...]
    dynamic_slice x0 -> x1, local copies, waits for them, and re-layouts: none -> 0.98 us  [owner_body(): lax.dynamic_slice_in_dim(coupling, z % 2 * (width // 2), width // 2, axis=1)]
  transfers between devices with their start and end apart: 9 -> 10, of which waited for: 8 -> 7; matrix products, arithmetic and copies ran while one was open for 4% -> 5% of each run, Pallas kernels for 1% -> 2%
where the time goes in v10:
time: 89.3 us; the launch traced here: 88.8 us
  waiting for transfers between devices  40.1 us (45%)
  starting transfers between devices  25.9 us (29%)
  Pallas kernels  16 us (18%)
  other arithmetic  5.53 us (6%)
  local copies, waits for them, and re-layouts  1 us (1%)
    all_to_all x1, waiting for transfers between devices, owner_body(): lax.all_to_all(half.reshape(slots, rows, width), ('slab', 'energy'), 0, 0...  28 us
    ppermute x9, starting transfers between devices, send(): return lax.ppermute(value, axes, pairs)  17.8 us
    pallas_call x1, Pallas kernels, call(): pl.pallas_call(kernel, out_shape=[jax.ShapeDtypeStruct(shape, jnp.float32...  13.7 us
    ppermute x9, waiting for transfers between devices, send(): return lax.ppermute(value, axes, pairs)  12.2 us
    all_to_all x1, starting transfers between devices, owner_body(): lax.all_to_all(half.reshape(slots, rows, width), ('slab', 'energy'), 0, 0...  8.07 us
  transfers between devices with their start and end apart: 10, of which 7 were waited for; matrix products, arithmetic and copies ran while one was open for 5% of the time, Pallas kernels for 2%

profile of v10, /device:TPU:0, one launch (start us, length us, event | category | flops | bytes accessed | tf_op | source)
XLA Modules:
  0.0 88.8 jit_solution(17673109675112979296)
XLA Ops:
  0.0 1.4 %collective-permute-start.4 = (f32[2,256,256]{2,1,0:T(8,128)}, f32[2,256,256]{2,1,0:T(8,128)S(1)}, u32[]{:S(2)}, u32[]{:S(2)}) collective-permute-start(f32[2,256,256]{2,1,0:T(8,128)} %bitcast.42), channel_id=1, source_target_pairs={{8,0},{10,2},{12,4},{14,6},{17,25},{19,27},{21,29},{23,31},{24,16}... | collective-permute-start | bytes 1572872 | tf_op jit(solution)/shard_map/ppermute | solution.py:374
  1.4 1.3 %collective-permute-start.5 = (f32[2,256,256]{2,1,0:T(8,128)}, f32[2,256,256]{2,1,0:T(8,128)S(1)}, u32[]{:S(2)}, u32[]{:S(2)}) collective-permute-start(f32[2,256,256]{2,1,0:T(8,128)} %bitcast.43), channel_id=1, source_target_pairs={{9,25},{11,27},{13,29},{15,31},{16,0},{18,2},{20,4},{22,6},{25,9},... | collective-permute-start | bytes 1572872 | tf_op jit(solution)/shard_map/ppermute | solution.py:374
  2.7 1.0 %dynamic-slice_bitcast_fusion.4 = f32[2,128,256]{2,1,0:T(8,128)S(1)} fusion(f32[1,1,2,256,256]{4,3,2,1,0:T(8,128)} %param.8, s32[]{:T(128)S(6)} %select_n.92), kind=kLoop, calls=%fused_computation.15 | loop fusion | bytes 524292 | tf_op jit(solution)/shard_map/dynamic_slice | solution.py:390
  3.7 1.3 %collective-permute-start.3 = (f32[2,128,256]{2,1,0:T(8,128)S(1)}, f32[2,128,256]{2,1,0:T(8,128)S(1)}, u32[]{:S(2)}, u32[]{:S(2)}) collective-permute-start(f32[2,128,256]{2,1,0:T(8,128)S(1)} %dynamic-slice_bitcast_fusion.4), channel_id=1, source_target_pairs={{8,16},{10,18},{12,20},{14,22},{17,9},{19,11},{21,13},{23,15},{24,... | collective-permute-start | bytes 786440 | tf_op jit(solution)/shard_map/ppermute | solution.py:374
  5.1 0.7 broadcast_subtract_fusion
  5.7 1.5 %fusion.1 = (f32[1,256,256]{2,1,0:T(8,128)S(1)}, f32[1,256,256]{2,1,0:T(8,128)S(1)}, f32[1,256,256]{2,1,0:T(8,128)S(1)}, f32[1,256,256]{2,1,0:T(8,128)S(1)}) fusion(f32[2,1,2,256,256]{4,3,2,1,0:T(8,128)} %param.9, s32[]{:T(128)S(6)} %select_n.91, f32[1,1,2,256,256]{4,3,2,1,0:T(8,128)} %param.7, f32[256]{0:T(256)S(1)} %bitcast.45, s32[]{:T(128)S(6)} %select_n.88, ...), kind=kLoop, calls=%fused_computation.7 | loop fusion | flops 720896 | bytes 2623500 | tf_op jit(solution)/shard_map/sub | solution.py:384
  7.2 0.8 pad_maximum_fusion.1
  8.1 4.9 %collective-permute-start.1 = (f32[2,256,256]{2,1,0:T(8,128)}, f32[2,256,256]{2,1,0:T(8,128)S(1)}, u32[]{:S(2)}, u32[]{:S(2)}) collective-permute-start(f32[2,256,256]{2,1,0:T(8,128)} %pad_maximum_fusion.1), channel_id=1, source_target_pairs={{0,16},{2,18},{4,20},{6,22},{9,25},{11,27},{13,29},{15,31},{16,0},... | collective-permute-start | bytes 1572872 | tf_op jit(solution)/shard_map/ppermute | solution.py:374
  13.0 1.3 %collective-permute-start.2 = (f32[2,256,256]{2,1,0:T(8,128)}, f32[2,256,256]{2,1,0:T(8,128)}, u32[]{:S(2)}, u32[]{:S(2)}) collective-permute-start(f32[2,256,256]{2,1,0:T(8,128)} %pad_maximum_fusion.1), channel_id=1, source_target_pairs={{1,25},{3,27},{5,29},{7,31},{8,16},{10,18},{12,20},{14,22},{17,9},... | collective-permute-start | bytes 1572872 | tf_op jit(solution)/shard_map/ppermute | solution.py:374
  14.3 2.4 %collective-permute-done.3.far_mine = f32[2,128,256]{2,1,0:T(8,128)S(1)} collective-permute-done((f32[2,128,256]{2,1,0:T(8,128)S(1)}, f32[2,128,256]{2,1,0:T(8,128)S(1)}, u32[]{:S(2)}, u32[]{:S(2)}) %collective-permute-start.3) | collective-permute-done | bytes 262176 | tf_op jit(solution)/shard_map/ppermute | solution.py:374
  16.7 1.3 %collective-permute-start = (f32[2,256,256]{2,1,0:T(8,128)S(1)}, f32[2,256,256]{2,1,0:T(8,128)}, u32[]{:S(2)}, u32[]{:S(2)}) collective-permute-start(f32[2,256,256]{2,1,0:T(8,128)S(1)} %pad_maximum_fusion.b_own), channel_id=1, source_target_pairs={{1,9},{3,11},{5,13},{7,15},{8,0},{10,2},{12,4},{14,6},{17,25},{19,... | collective-permute-start | bytes 1572872 | tf_op jit(solution)/shard_map/ppermute | solution.py:374
  18.0 0.0 collective-permute-done.4.c_x
  18.0 3.5 %collective-permute-start.6 = (f32[2,128,256]{2,1,0:T(8,128)S(1)}, f32[2,128,256]{2,1,0:T(8,128)S(1)}, u32[]{:S(2)}, u32[]{:S(2)}) collective-permute-start(f32[2,128,256]{2,1,0:T(8,128)S(1)} %collective-permute-done.3.far_mine), channel_id=1, source_target_pairs={{0,2},{2,0},{4,6},{6,4},{9,11},{11,9},{13,15},{15,13},{16,18},{18,... | collective-permute-start | bytes 786440 | tf_op jit(solution)/shard_map/ppermute | solution.py:374
  21.5 0.1 pad_add_fusion.place
  21.6 4.7 %collective-permute-done.6.far_theirs = f32[2,128,256]{2,1,0:T(8,128)S(1)} collective-permute-done((f32[2,128,256]{2,1,0:T(8,128)S(1)}, f32[2,128,256]{2,1,0:T(8,128)S(1)}, u32[]{:S(2)}, u32[]{:S(2)}) %collective-permute-start.6) | collective-permute-done | bytes 262176 | tf_op jit(solution)/shard_map/ppermute | solution.py:374
  26.3 1.4 %shard_map.64.c_forms = bf16[3,2,6,256,256]{4,3,2,1,0:T(8,128)(2,1)S(1)} custom-call(s32[3]{0:T(128)S(1)} %pad_add_fusion.place, f32[2,256,256]{2,1,0:T(8,128)S(1)} %bitcast.44, f32[2,256,256]{2,1,0:T(8,128)S(1)} %collective-permute-done.4.c_x, f32[2,256,256]{2,1,0:T(8,128)S(1)} %collective-permute-done.5.c_y, ...), custom_call_target="tpu_custom_call" | custom-call | tf_op jit(solution)/shard_map/pallas_call | solution.py:400
  27.7 0.2 collective-permute-done.1.b_y
  27.9 1.6 %collective-permute-done.b_x = f32[2,256,256]{2,1,0:T(8,128)} collective-permute-done((f32[2,256,256]{2,1,0:T(8,128)S(1)}, f32[2,256,256]{2,1,0:T(8,128)}, u32[]{:S(2)}, u32[]{:S(2)}) %collective-permute-start) | collective-permute-done | bytes 524320 | tf_op jit(solution)/shard_map/ppermute | solution.py:374
  29.5 13.7 %shard_map.65 = (f32[4,256,256]{2,1,0:T(8,128)S(1)}, f32[4,256,256]{2,1,0:T(8,128)S(1)}) custom-call(s32[3]{0:T(128)S(1)} %pad_add_fusion.place, f32[2,256,256]{2,1,0:T(8,128)S(1)} %pad_maximum_fusion.b_own, f32[2,256,256]{2,1,0:T(8,128)} %collective-permute-done.b_x, f32[2,256,256]{2,1,0:T(8,128)S(1)} %collective-permute-done.1.b_y, ...), custom_call_target="tpu_custom_call" | custom-call | flops 7851737088 | bytes 3670016 | tf_op jit(solution)/shard_map/pallas_call | solution.py:326
  43.2 0.0 copy-start.1
  43.2 0.0 copy-start.2
  43.2 2.8 %collective-permute-start.7 = (f32[4,256,256]{2,1,0:T(8,128)S(1)}, f32[4,256,256]{2,1,0:T(8,128)}, u32[]{:S(2)}, u32[]{:S(2)}) collective-permute-start(f32[4,256,256]{2,1,0:T(8,128)S(1)} %get-tuple-element.14), channel_id=1, source_target_pairs={{0,1},{2,3},{4,5},{6,7},{9,8},{11,10},{13,12},{15,14},{16,17},{18,... | collective-permute-start | bytes 3145736 | tf_op jit(solution)/shard_map/ppermute | solution.py:374
  46.0 1.4 %collective-permute-done.7 = f32[4,256,256]{2,1,0:T(8,128)} collective-permute-done((f32[4,256,256]{2,1,0:T(8,128)S(1)}, f32[4,256,256]{2,1,0:T(8,128)}, u32[]{:S(2)}, u32[]{:S(2)}) %collective-permute-start.7) | collective-permute-done | bytes 1048608 | tf_op jit(solution)/shard_map/ppermute | solution.py:374
  47.4 1.1 %broadcast_select_fusion.1 = f32[4,256,256]{2,1,0:T(8,128)} fusion(f32[4,256,256]{2,1,0:T(8,128)S(1)} %get-tuple-element.13, f32[4,256,256]{2,1,0:T(8,128)} %collective-permute-done.7, pred[]{:T(512)S(6)} %eq.76), kind=kLoop, calls=%fused_computation.3 | loop fusion | flops 262144 | bytes 3145729 | tf_op jit(solution)/shard_map/jit(_where)/select_n | solution.py:410
  48.5 8.1 %all-to-all-start = ((f32[16,64,256]{2,1,0:T(8,128)}), f32[16,64,256]{2,1,0:T(8,128)S(1)}, u32[]{:S(2)}, u32[]{:S(2)}) async-start(f32[16,64,256]{2,1,0:T(8,128)} %bitcast.15), calls=%async_computation | async-start | bytes 2097152 | tf_op jit(solution)/shard_map/all_to_all | solution.py:414
  56.7 0.1 iota_add_fusion
  56.7 0.1 add_reduce_fusion
  56.8 28.0 %all-to-all-done.parts_ref = f32[16,64,256]{2,1,0:T(8,128)S(1)} async-done(((f32[16,64,256]{2,1,0:T(8,128)}), f32[16,64,256]{2,1,0:T(8,128)S(1)}, u32[]{:S(2)}, u32[]{:S(2)}) %all-to-all-start) | async-done | bytes 1048608 | tf_op jit(solution)/shard_map/all_to_all | solution.py:414
  84.8 0.9 %shard_map.66 = f32[8,64,256]{2,1,0:T(8,128)S(1)} custom-call(f32[8,8]{1,0:T(8,128)S(1)} %broadcast_multiply_fusion.phonon, f32[16,64,256]{2,1,0:T(8,128)S(1)} %all-to-all-done.parts_ref), custom_call_target="tpu_custom_call" | custom-call | tf_op jit(solution)/shard_map/pallas_call | solution.py:418
  85.7 0.1 collective-permute-start.8
  85.8 1.9 %collective-permute-done.8 = f32[8,64,256]{2,1,0:T(8,128)S(1)} collective-permute-done((f32[8,64,256]{2,1,0:T(8,128)S(1)}, f32[8,64,256]{2,1,0:T(8,128)S(1)}, u32[]{:S(2)}, u32[]{:S(2)}) %collective-permute-start.8) | collective-permute-done | bytes 524320 | tf_op jit(solution)/shard_map/ppermute | solution.py:374
  87.7 1.1 %broadcast_select_fusion = f32[8,1,2,64,256]{4,3,2,1,0:T(8,128)} fusion(f32[8,64,256]{2,1,0:T(8,128)S(1)} %collective-permute-done.8, f32[8,64,256]{2,1,0:T(8,128)S(1)} %shard_map.66, pred[2]{0:T(512)(128)(4,1)S(1)} %iota_compare_fusion.3), kind=kLoop, calls=%fused_computation.2 | loop fusion | flops 262144 | bytes 2097154 | tf_op jit(solution)/shard_map/jit(_where)/select_n | solution.py:427
  (10 shorter events, 0.1 us)
Async XLA Ops:
  0.0 26.3 %copy-start = (f32[1,1,2,256,256]{4,3,2,1,0:T(8,128)S(1)}, f32[1,1,2,256,256]{4,3,2,1,0:T(8,128)}, u32[]{:S(2)}) copy-start(f32[1,1,2,256,256]{4,3,2,1,0:T(8,128)} %param.8) | copy-start | bytes 1572868
  0.0 18.0 %collective-permute-start.4 = (f32[2,256,256]{2,1,0:T(8,128)}, f32[2,256,256]{2,1,0:T(8,128)S(1)}, u32[]{:S(2)}, u32[]{:S(2)}) collective-permute-start(f32[2,256,256]{2,1,0:T(8,128)} %bitcast.42), channel_id=1, source_target_pairs={{8,0},{10,2},{12,4},{14,6},{17,25},{19,27},{21,29},{23,31},{24,16}... | collective-permute-start | bytes 1572872 | tf_op jit(solution)/shard_map/ppermute | solution.py:374
  1.4 16.6 %collective-permute-start.5 = (f32[2,256,256]{2,1,0:T(8,128)}, f32[2,256,256]{2,1,0:T(8,128)S(1)}, u32[]{:S(2)}, u32[]{:S(2)}) collective-permute-start(f32[2,256,256]{2,1,0:T(8,128)} %bitcast.43), channel_id=1, source_target_pairs={{9,25},{11,27},{13,29},{15,31},{16,0},{18,2},{20,4},{22,6},{25,9},... | collective-permute-start | bytes 1572872 | tf_op jit(solution)/shard_map/ppermute | solution.py:374
  3.7 13.0 %collective-permute-start.3 = (f32[2,128,256]{2,1,0:T(8,128)S(1)}, f32[2,128,256]{2,1,0:T(8,128)S(1)}, u32[]{:S(2)}, u32[]{:S(2)}) collective-permute-start(f32[2,128,256]{2,1,0:T(8,128)S(1)} %dynamic-slice_bitcast_fusion.4), channel_id=1, source_target_pairs={{8,16},{10,18},{12,20},{14,22},{17,9},{19,11},{21,13},{23,15},{24,... | collective-permute-start | bytes 786440 | tf_op jit(solution)/shard_map/ppermute | solution.py:374
  8.1 19.8 %collective-permute-start.1 = (f32[2,256,256]{2,1,0:T(8,128)}, f32[2,256,256]{2,1,0:T(8,128)S(1)}, u32[]{:S(2)}, u32[]{:S(2)}) collective-permute-start(f32[2,256,256]{2,1,0:T(8,128)} %pad_maximum_fusion.1), channel_id=1, source_target_pairs={{0,16},{2,18},{4,20},{6,22},{9,25},{11,27},{13,29},{15,31},{16,0},... | collective-permute-start | bytes 1572872 | tf_op jit(solution)/shard_map/ppermute | solution.py:374
  13.0 14.9 %collective-permute-start.2 = (f32[2,256,256]{2,1,0:T(8,128)}, f32[2,256,256]{2,1,0:T(8,128)}, u32[]{:S(2)}, u32[]{:S(2)}) collective-permute-start(f32[2,256,256]{2,1,0:T(8,128)} %pad_maximum_fusion.1), channel_id=1, source_target_pairs={{1,25},{3,27},{5,29},{7,31},{8,16},{10,18},{12,20},{14,22},{17,9},... | collective-permute-start | bytes 1572872 | tf_op jit(solution)/shard_map/ppermute | solution.py:374
  16.7 12.7 %collective-permute-start = (f32[2,256,256]{2,1,0:T(8,128)S(1)}, f32[2,256,256]{2,1,0:T(8,128)}, u32[]{:S(2)}, u32[]{:S(2)}) collective-permute-start(f32[2,256,256]{2,1,0:T(8,128)S(1)} %pad_maximum_fusion.b_own), channel_id=1, source_target_pairs={{1,9},{3,11},{5,13},{7,15},{8,0},{10,2},{12,4},{14,6},{17,25},{19,... | collective-permute-start | bytes 1572872 | tf_op jit(solution)/shard_map/ppermute | solution.py:374
  18.0 8.3 %collective-permute-start.6 = (f32[2,128,256]{2,1,0:T(8,128)S(1)}, f32[2,128,256]{2,1,0:T(8,128)S(1)}, u32[]{:S(2)}, u32[]{:S(2)}) collective-permute-start(f32[2,128,256]{2,1,0:T(8,128)S(1)} %collective-permute-done.3.far_mine), channel_id=1, source_target_pairs={{0,2},{2,0},{4,6},{6,4},{9,11},{11,9},{13,15},{15,13},{16,18},{18,... | collective-permute-start | bytes 786440 | tf_op jit(solution)/shard_map/ppermute | solution.py:374
  43.2 13.5 %copy-start.1 = (f32[2,4]{1,0:T(2,128)S(1)}, f32[2,4]{1,0:T(2,128)}, u32[]{:S(2)}) copy-start(f32[2,4]{1,0:T(2,128)} %param.11) | copy-start | bytes 100
  43.2 13.5 %copy-start.2 = (s32[4]{0:T(128)S(1)}, s32[4]{0:T(128)}, u32[]{:S(2)}) copy-start(s32[4]{0:T(128)} %param.10) | copy-start | bytes 52
  43.2 4.3 %collective-permute-start.7 = (f32[4,256,256]{2,1,0:T(8,128)S(1)}, f32[4,256,256]{2,1,0:T(8,128)}, u32[]{:S(2)}, u32[]{:S(2)}) collective-permute-start(f32[4,256,256]{2,1,0:T(8,128)S(1)} %get-tuple-element.14), channel_id=1, source_target_pairs={{0,1},{2,3},{4,5},{6,7},{9,8},{11,10},{13,12},{15,14},{16,17},{18,... | collective-permute-start | bytes 3145736 | tf_op jit(solution)/shard_map/ppermute | solution.py:374
  48.5 36.2 %all-to-all-start = ((f32[16,64,256]{2,1,0:T(8,128)}), f32[16,64,256]{2,1,0:T(8,128)S(1)}, u32[]{:S(2)}, u32[]{:S(2)}) async-start(f32[16,64,256]{2,1,0:T(8,128)} %bitcast.15), calls=%async_computation | async-start | bytes 2097152 | tf_op jit(solution)/shard_map/all_to_all | solution.py:414
  85.7 2.0 %collective-permute-start.8 = (f32[8,64,256]{2,1,0:T(8,128)S(1)}, f32[8,64,256]{2,1,0:T(8,128)S(1)}, u32[]{:S(2)}, u32[]{:S(2)}) collective-permute-start(f32[8,64,256]{2,1,0:T(8,128)S(1)} %shard_map.66), channel_id=1, source_target_pairs={{0,1},{1,0},{2,3},{3,2},{4,5},{5,4},{6,7},{7,6},{8,9},{9,8},{10,11... | collective-permute-start | bytes 1572872 | tf_op jit(solution)/shard_map/ppermute | solution.py:374

commit v11 on v7

--- a/solution.py
+++ b/solution.py
@@ -139,9 +139,11 @@
 
 
 def real_dot(left, right):
-    lhs = jnp.concatenate([left[0], left[1], left[0]], axis=1)
-    rhs = jnp.concatenate([right[0], right[0], right[1]], axis=0)
-    return jnp.dot(lhs, rhs, preferred_element_type=jnp.float32)
+    rows = left[0].shape[0]
+    both = jnp.concatenate([left[0], left[1]], axis=0)
+    main = jnp.dot(both, right[0], preferred_element_type=jnp.float32)
+    rest = jnp.dot(left[0], right[1], preferred_element_type=jnp.float32)
+    return main[:rows] + main[rows:] + rest
 
 
 def mul(left, right):
@@ -321,13 +323,6 @@
 def pick_kernel(active, keep_ref, got_ref, out_ref):
     for slab in range(out_ref.shape[0]):
         out_ref[slab] = jnp.where(active[0] == 1, keep_ref[slab], got_ref[slab])
-
-
-def join_kernel(core, mine_ref, other_ref, out_ref):
-    energy = pl.program_id(0)
-    mine, other = mine_ref[energy], other_ref[energy]
-    out_ref[0, 0] = jnp.where(core[0] == 0, mine, other)
-    out_ref[0, 1] = jnp.where(core[0] == 0, other, mine)
 
 
 def prepare_kernel(place, scale, onsite_ref, hop_ref, sigma_ref, own_ref, other_ref):
@@ -450,14 +445,8 @@
         compiler_params=pltpu.CompilerParams(vmem_limit_bytes=VMEM_BYTES),
     )(phonon, parts)
     other = send(mixed, siblings)
-    result = pl.pallas_call(
-        join_kernel,
-        grid=(total,),
-        out_shape=jax.ShapeDtypeStruct((total, 2, rows, width), jnp.float32),
-        in_specs=[smem, vmem, vmem],
-        out_specs=pl.BlockSpec((1, 2, rows, width), lambda energy: (energy, 0, 0, 0)),
-        compiler_params=pltpu.CompilerParams(vmem_limit_bytes=VMEM_BYTES),
-    )(k[None].astype(jnp.int32), mixed, other)
+    mine = jnp.arange(2)[:, None, None] == k
+    result = jnp.where(mine, mixed[:, None], other[:, None])
     return result[:, None]
 
 

time: 85.9 us -> 84.1 us (0.979)
  Pallas kernels: 18.7 us -> 15.8 us
  other arithmetic: 0.31 us -> 1.47 us
    pallas_call x1 -> x0, Pallas kernels: 2.71 us -> none  [owner_body(): pl.pallas_call(join_kernel, grid=(total,), out_shape=jax.ShapeDtypeStruct...]
    select_n x0 -> x1, other arithmetic: none -> 1.15 us  [owner_body(): result = jnp.where(mine, mixed[:, None], other[:, None])]
where the time goes in v11:
time: 84.1 us; the launch traced here: 83.6 us
  waiting for transfers between devices  38.1 us (45%)
  starting transfers between devices  23 us (27%)
  Pallas kernels  15.8 us (19%)
  local copies, waits for them, and re-layouts  4.98 us (6%)
  other arithmetic  1.47 us (2%)
    all_to_all x1, waiting for transfers between devices, owner_body(): lax.all_to_all(half.reshape(slots, rows, width), ('slab', 'energy'), 0, 0...  27.8 us
    ppermute x9, starting transfers between devices, send(): return lax.ppermute(value, axes, pairs)  16.4 us
    pallas_call x1, Pallas kernels, call(): pl.pallas_call(kernel, out_shape=[jax.ShapeDtypeStruct(shape, jnp.float32...  11.6 us
    ppermute x9, waiting for transfers between devices, send(): return lax.ppermute(value, axes, pairs)  10.3 us
    all_to_all x1, starting transfers between devices, owner_body(): lax.all_to_all(half.reshape(slots, rows, width), ('slab', 'energy'), 0, 0...  6.59 us
    unnamed x12, local copies, waits for them, and re-layouts  4 us
  transfers between devices with their start and end apart: 10, of which 5 were waited for; matrix products, arithmetic and copies ran while one was open for 2% of the time, Pallas kernels for 3%

profile of v11, /device:TPU:0, one launch (start us, length us, event | category | flops | bytes accessed | tf_op | source)
XLA Modules:
  0.0 83.6 jit_solution(9533999110393650237)
XLA Ops:
  0.0 1.3 %collective-permute-start.4 = (f32[2,256,256]{2,1,0:T(8,128)}, f32[2,256,256]{2,1,0:T(8,128)S(1)}, u32[]{:S(2)}, u32[]{:S(2)}) collective-permute-start(f32[2,256,256]{2,1,0:T(8,128)} %bitcast.16), channel_id=1, source_target_pairs={{8,0},{10,2},{12,4},{14,6},{17,25},{19,27},{21,29},{23,31},{24,16}... | collective-permute-start | bytes 1572872 | tf_op jit(solution)/shard_map/ppermute | solution.py:390
  1.3 1.3 %collective-permute-start.5 = (f32[2,256,256]{2,1,0:T(8,128)}, f32[2,256,256]{2,1,0:T(8,128)S(1)}, u32[]{:S(2)}, u32[]{:S(2)}) collective-permute-start(f32[2,256,256]{2,1,0:T(8,128)} %bitcast.17), channel_id=1, source_target_pairs={{9,25},{11,27},{13,29},{15,31},{16,0},{18,2},{20,4},{22,6},{25,9},... | collective-permute-start | bytes 1572872 | tf_op jit(solution)/shard_map/ppermute | solution.py:390
  2.6 1.0 %dynamic-slice_bitcast_fusion = f32[2,128,256]{2,1,0:T(8,128)S(1)} fusion(f32[1,1,2,256,256]{4,3,2,1,0:T(8,128)} %param.8, s32[]{:T(128)S(6)} %select_n.34), kind=kLoop, calls=%fused_computation.1 | loop fusion | bytes 524292 | tf_op jit(solution)/shard_map/dynamic_slice | solution.py:406
  3.6 1.3 %collective-permute-start.3 = (f32[2,128,256]{2,1,0:T(8,128)S(1)}, f32[2,128,256]{2,1,0:T(8,128)S(1)}, u32[]{:S(2)}, u32[]{:S(2)}) collective-permute-start(f32[2,128,256]{2,1,0:T(8,128)S(1)} %dynamic-slice_bitcast_fusion), channel_id=1, source_target_pairs={{8,16},{10,18},{12,20},{14,22},{17,9},{19,11},{21,13},{23,15},{24,... | collective-permute-start | bytes 786440 | tf_op jit(solution)/shard_map/ppermute | solution.py:390
  4.9 0.1 pad_add_fusion.place
  5.0 0.1 multiply_add_fusion.scale
  5.1 1.2 %copy-done.1 = f32[2,1,2,256,256]{4,3,2,1,0:T(8,128)S(1)} copy-done((f32[2,1,2,256,256]{4,3,2,1,0:T(8,128)S(1)}, f32[2,1,2,256,256]{4,3,2,1,0:T(8,128)}, u32[]{:S(2)}) %copy-start.1) | copy-done | bytes 1048600
  6.3 1.0 %copy-done.2 = f32[1,1,2,256,256]{4,3,2,1,0:T(8,128)S(1)} copy-done((f32[1,1,2,256,256]{4,3,2,1,0:T(8,128)S(1)}, f32[1,1,2,256,256]{4,3,2,1,0:T(8,128)}, u32[]{:S(2)}) %copy-start.2) | copy-done | bytes 524312
  7.3 0.7 copy-done.3
  8.0 0.7 shard_map.64
  8.7 1.3 %collective-permute-start = (f32[2,256,256]{2,1,0:T(8,128)S(1)}, f32[2,256,256]{2,1,0:T(8,128)S(1)}, u32[]{:S(2)}, u32[]{:S(2)}) collective-permute-start(f32[2,256,256]{2,1,0:T(8,128)S(1)} %get-tuple-element.12.b_own), channel_id=1, source_target_pairs={{1,9},{3,11},{5,13},{7,15},{8,0},{10,2},{12,4},{14,6},{17,25},{19,... | collective-permute-start | bytes 1572872 | tf_op jit(solution)/shard_map/ppermute | solution.py:390
  10.0 4.9 %collective-permute-start.1 = (f32[2,256,256]{2,1,0:T(8,128)S(1)}, f32[2,256,256]{2,1,0:T(8,128)S(1)}, u32[]{:S(2)}, u32[]{:S(2)}) collective-permute-start(f32[2,256,256]{2,1,0:T(8,128)S(1)} %get-tuple-element.13), channel_id=1, source_target_pairs={{0,16},{2,18},{4,20},{6,22},{9,25},{11,27},{13,29},{15,31},{16,0},... | collective-permute-start | bytes 1572872 | tf_op jit(solution)/shard_map/ppermute | solution.py:390
  14.9 1.6 %collective-permute-done.3.far_mine = f32[2,128,256]{2,1,0:T(8,128)S(1)} collective-permute-done((f32[2,128,256]{2,1,0:T(8,128)S(1)}, f32[2,128,256]{2,1,0:T(8,128)S(1)}, u32[]{:S(2)}, u32[]{:S(2)}) %collective-permute-start.3) | collective-permute-done | bytes 262176 | tf_op jit(solution)/shard_map/ppermute | solution.py:390
  16.5 1.3 %collective-permute-start.2 = (f32[2,256,256]{2,1,0:T(8,128)S(1)}, f32[2,256,256]{2,1,0:T(8,128)S(1)}, u32[]{:S(2)}, u32[]{:S(2)}) collective-permute-start(f32[2,256,256]{2,1,0:T(8,128)S(1)} %get-tuple-element.13), channel_id=1, source_target_pairs={{1,25},{3,27},{5,29},{7,31},{8,16},{10,18},{12,20},{14,22},{17,9},... | collective-permute-start | bytes 1572872 | tf_op jit(solution)/shard_map/ppermute | solution.py:390
  17.8 3.6 %collective-permute-start.6 = (f32[2,128,256]{2,1,0:T(8,128)S(1)}, f32[2,128,256]{2,1,0:T(8,128)S(1)}, u32[]{:S(2)}, u32[]{:S(2)}) collective-permute-start(f32[2,128,256]{2,1,0:T(8,128)S(1)} %collective-permute-done.3.far_mine), channel_id=1, source_target_pairs={{0,2},{2,0},{4,6},{6,4},{9,11},{11,9},{13,15},{15,13},{16,18},{18,... | collective-permute-start | bytes 786440 | tf_op jit(solution)/shard_map/ppermute | solution.py:390
  21.4 4.7 %collective-permute-done.6.far_theirs = f32[2,128,256]{2,1,0:T(8,128)S(1)} collective-permute-done((f32[2,128,256]{2,1,0:T(8,128)S(1)}, f32[2,128,256]{2,1,0:T(8,128)S(1)}, u32[]{:S(2)}, u32[]{:S(2)}) %collective-permute-start.6) | collective-permute-done | bytes 262176 | tf_op jit(solution)/shard_map/ppermute | solution.py:390
  26.1 1.0 %copy-done = f32[1,1,2,256,256]{4,3,2,1,0:T(8,128)S(1)} copy-done((f32[1,1,2,256,256]{4,3,2,1,0:T(8,128)S(1)}, f32[1,1,2,256,256]{4,3,2,1,0:T(8,128)}, u32[]{:S(2)}) %copy-start) | copy-done | bytes 524312
  27.1 1.5 %shard_map.65.c_forms = bf16[3,2,6,256,256]{4,3,2,1,0:T(8,128)(2,1)S(1)} custom-call(s32[3]{0:T(128)S(1)} %pad_add_fusion.place, f32[2,256,256]{2,1,0:T(8,128)S(1)} %bitcast.18, f32[2,256,256]{2,1,0:T(8,128)S(1)} %collective-permute-done.4.c_x, f32[2,256,256]{2,1,0:T(8,128)S(1)} %collective-permute-done.5.c_y, ...), custom_call_target="tpu_custom_call" | custom-call | tf_op jit(solution)/shard_map/pallas_call | solution.py:416
  28.6 11.6 %shard_map.66 = (f32[4,256,256]{2,1,0:T(8,128)S(1)}, f32[4,256,256]{2,1,0:T(8,128)S(1)}) custom-call(s32[3]{0:T(128)S(1)} %pad_add_fusion.place, f32[2,256,256]{2,1,0:T(8,128)S(1)} %get-tuple-element.12.b_own, f32[2,256,256]{2,1,0:T(8,128)S(1)} %collective-permute-done.b_x, f32[2,256,256]{2,1,0:T(8,128)S(1)} %collective-permute-done.1.b_y, ...), custom_call_target="tpu_custom_call" | custom-call | flops 7851737088 | bytes 3670016 | tf_op jit(solution)/shard_map/pallas_call | solution.py:342
  40.3 0.0 copy-start.4
  40.3 0.0 copy-start.5
  40.3 1.4 %collective-permute-start.7 = (f32[4,256,256]{2,1,0:T(8,128)S(1)}, f32[4,256,256]{2,1,0:T(8,128)S(1)}, u32[]{:S(2)}, u32[]{:S(2)}) collective-permute-start(f32[4,256,256]{2,1,0:T(8,128)S(1)} %get-tuple-element.18), channel_id=1, source_target_pairs={{0,1},{2,3},{4,5},{6,7},{9,8},{11,10},{13,12},{15,14},{16,17},{18,... | collective-permute-start | bytes 3145736 | tf_op jit(solution)/shard_map/ppermute | solution.py:390
  41.6 2.2 %collective-permute-done.7.got_ref = f32[4,256,256]{2,1,0:T(8,128)S(1)} collective-permute-done((f32[4,256,256]{2,1,0:T(8,128)S(1)}, f32[4,256,256]{2,1,0:T(8,128)S(1)}, u32[]{:S(2)}, u32[]{:S(2)}) %collective-permute-start.7) | collective-permute-done | bytes 1048608 | tf_op jit(solution)/shard_map/ppermute | solution.py:390
  43.8 1.1 %shard_map.67 = f32[4,256,256]{2,1,0:T(8,128)} custom-call(s32[1]{0:T(128)} %bitcast.2.active, f32[4,256,256]{2,1,0:T(8,128)S(1)} %get-tuple-element.17.keep_ref, f32[4,256,256]{2,1,0:T(8,128)S(1)} %collective-permute-done.7.got_ref), custom_call_target="tpu_custom_call" | custom-call | tf_op jit(solution)/shard_map/pallas_call | solution.py:426
  44.9 6.6 %all-to-all-start = ((f32[16,64,256]{2,1,0:T(8,128)}), f32[16,64,256]{2,1,0:T(8,128)S(1)}, u32[]{:S(2)}, u32[]{:S(2)}) async-start(f32[16,64,256]{2,1,0:T(8,128)} %bitcast.12), calls=%async_computation | async-start | bytes 2097152 | tf_op jit(solution)/shard_map/all_to_all | solution.py:436
  51.6 0.1 iota_add_fusion
  51.6 0.1 add_reduce_fusion
  51.7 27.8 %all-to-all-done.parts_ref = f32[16,64,256]{2,1,0:T(8,128)S(1)} async-done(((f32[16,64,256]{2,1,0:T(8,128)}), f32[16,64,256]{2,1,0:T(8,128)S(1)}, u32[]{:S(2)}, u32[]{:S(2)}) %all-to-all-start) | async-done | bytes 1048608 | tf_op jit(solution)/shard_map/all_to_all | solution.py:436
  79.5 0.9 %shard_map.68 = f32[8,64,256]{2,1,0:T(8,128)S(1)} custom-call(f32[8,8]{1,0:T(8,128)S(1)} %broadcast_multiply_fusion.phonon, f32[16,64,256]{2,1,0:T(8,128)S(1)} %all-to-all-done.parts_ref), custom_call_target="tpu_custom_call" | custom-call | tf_op jit(solution)/shard_map/pallas_call | solution.py:440
  80.4 0.1 collective-permute-start.8
  80.5 1.9 %collective-permute-done.8 = f32[8,64,256]{2,1,0:T(8,128)S(1)} collective-permute-done((f32[8,64,256]{2,1,0:T(8,128)S(1)}, f32[8,64,256]{2,1,0:T(8,128)S(1)}, u32[]{:S(2)}, u32[]{:S(2)}) %collective-permute-start.8) | collective-permute-done | bytes 524320 | tf_op jit(solution)/shard_map/ppermute | solution.py:390
  82.4 1.1 %broadcast_select_fusion = f32[8,1,2,64,256]{4,3,2,1,0:T(8,128)} fusion(f32[8,64,256]{2,1,0:T(8,128)S(1)} %collective-permute-done.8, f32[8,64,256]{2,1,0:T(8,128)S(1)} %shard_map.68, pred[2]{0:T(512)(128)(4,1)S(1)} %iota_compare_fusion.2), kind=kLoop, calls=%fused_computation | loop fusion | flops 262144 | bytes 2097154 | tf_op jit(solution)/shard_map/jit(_where)/select_n | solution.py:449
  (14 shorter events, 0.0 us)
Async XLA Ops:
  0.0 17.8 %collective-permute-start.4 = (f32[2,256,256]{2,1,0:T(8,128)}, f32[2,256,256]{2,1,0:T(8,128)S(1)}, u32[]{:S(2)}, u32[]{:S(2)}) collective-permute-start(f32[2,256,256]{2,1,0:T(8,128)} %bitcast.16), channel_id=1, source_target_pairs={{8,0},{10,2},{12,4},{14,6},{17,25},{19,27},{21,29},{23,31},{24,16}... | collective-permute-start | bytes 1572872 | tf_op jit(solution)/shard_map/ppermute | solution.py:390
  1.3 16.5 %collective-permute-start.5 = (f32[2,256,256]{2,1,0:T(8,128)}, f32[2,256,256]{2,1,0:T(8,128)S(1)}, u32[]{:S(2)}, u32[]{:S(2)}) collective-permute-start(f32[2,256,256]{2,1,0:T(8,128)} %bitcast.17), channel_id=1, source_target_pairs={{9,25},{11,27},{13,29},{15,31},{16,0},{18,2},{20,4},{22,6},{25,9},... | collective-permute-start | bytes 1572872 | tf_op jit(solution)/shard_map/ppermute | solution.py:390
  3.6 12.9 %collective-permute-start.3 = (f32[2,128,256]{2,1,0:T(8,128)S(1)}, f32[2,128,256]{2,1,0:T(8,128)S(1)}, u32[]{:S(2)}, u32[]{:S(2)}) collective-permute-start(f32[2,128,256]{2,1,0:T(8,128)S(1)} %dynamic-slice_bitcast_fusion), channel_id=1, source_target_pairs={{8,16},{10,18},{12,20},{14,22},{17,9},{19,11},{21,13},{23,15},{24,... | collective-permute-start | bytes 786440 | tf_op jit(solution)/shard_map/ppermute | solution.py:390
  5.1 1.2 %copy-start.1 = (f32[2,1,2,256,256]{4,3,2,1,0:T(8,128)S(1)}, f32[2,1,2,256,256]{4,3,2,1,0:T(8,128)}, u32[]{:S(2)}) copy-start(f32[2,1,2,256,256]{4,3,2,1,0:T(8,128)} %param.9) | copy-start | bytes 3145732
  6.3 1.0 %copy-start.2 = (f32[1,1,2,256,256]{4,3,2,1,0:T(8,128)S(1)}, f32[1,1,2,256,256]{4,3,2,1,0:T(8,128)}, u32[]{:S(2)}) copy-start(f32[1,1,2,256,256]{4,3,2,1,0:T(8,128)} %param.7) | copy-start | bytes 1572868
  7.3 0.7 copy-start.3
  8.7 19.9 %collective-permute-start = (f32[2,256,256]{2,1,0:T(8,128)S(1)}, f32[2,256,256]{2,1,0:T(8,128)S(1)}, u32[]{:S(2)}, u32[]{:S(2)}) collective-permute-start(f32[2,256,256]{2,1,0:T(8,128)S(1)} %get-tuple-element.12.b_own), channel_id=1, source_target_pairs={{1,9},{3,11},{5,13},{7,15},{8,0},{10,2},{12,4},{14,6},{17,25},{19,... | collective-permute-start | bytes 1572872 | tf_op jit(solution)/shard_map/ppermute | solution.py:390
  10.0 18.6 %collective-permute-start.1 = (f32[2,256,256]{2,1,0:T(8,128)S(1)}, f32[2,256,256]{2,1,0:T(8,128)S(1)}, u32[]{:S(2)}, u32[]{:S(2)}) collective-permute-start(f32[2,256,256]{2,1,0:T(8,128)S(1)} %get-tuple-element.13), channel_id=1, source_target_pairs={{0,16},{2,18},{4,20},{6,22},{9,25},{11,27},{13,29},{15,31},{16,0},... | collective-permute-start | bytes 1572872 | tf_op jit(solution)/shard_map/ppermute | solution.py:390
  16.5 12.1 %collective-permute-start.2 = (f32[2,256,256]{2,1,0:T(8,128)S(1)}, f32[2,256,256]{2,1,0:T(8,128)S(1)}, u32[]{:S(2)}, u32[]{:S(2)}) collective-permute-start(f32[2,256,256]{2,1,0:T(8,128)S(1)} %get-tuple-element.13), channel_id=1, source_target_pairs={{1,25},{3,27},{5,29},{7,31},{8,16},{10,18},{12,20},{14,22},{17,9},... | collective-permute-start | bytes 1572872 | tf_op jit(solution)/shard_map/ppermute | solution.py:390
  17.8 8.3 %collective-permute-start.6 = (f32[2,128,256]{2,1,0:T(8,128)S(1)}, f32[2,128,256]{2,1,0:T(8,128)S(1)}, u32[]{:S(2)}, u32[]{:S(2)}) collective-permute-start(f32[2,128,256]{2,1,0:T(8,128)S(1)} %collective-permute-done.3.far_mine), channel_id=1, source_target_pairs={{0,2},{2,0},{4,6},{6,4},{9,11},{11,9},{13,15},{15,13},{16,18},{18,... | collective-permute-start | bytes 786440 | tf_op jit(solution)/shard_map/ppermute | solution.py:390
  26.1 1.0 %copy-start = (f32[1,1,2,256,256]{4,3,2,1,0:T(8,128)S(1)}, f32[1,1,2,256,256]{4,3,2,1,0:T(8,128)}, u32[]{:S(2)}) copy-start(f32[1,1,2,256,256]{4,3,2,1,0:T(8,128)} %param.8) | copy-start | bytes 1572868
  40.3 11.3 %copy-start.4 = (f32[2,4]{1,0:T(2,128)S(1)}, f32[2,4]{1,0:T(2,128)}, u32[]{:S(2)}) copy-start(f32[2,4]{1,0:T(2,128)} %param.11) | copy-start | bytes 100
  40.3 11.3 %copy-start.5 = (s32[4]{0:T(128)S(1)}, s32[4]{0:T(128)}, u32[]{:S(2)}) copy-start(s32[4]{0:T(128)} %param.10) | copy-start | bytes 52
  40.3 3.6 %collective-permute-start.7 = (f32[4,256,256]{2,1,0:T(8,128)S(1)}, f32[4,256,256]{2,1,0:T(8,128)S(1)}, u32[]{:S(2)}, u32[]{:S(2)}) collective-permute-start(f32[4,256,256]{2,1,0:T(8,128)S(1)} %get-tuple-element.18), channel_id=1, source_target_pairs={{0,1},{2,3},{4,5},{6,7},{9,8},{11,10},{13,12},{15,14},{16,17},{18,... | collective-permute-start | bytes 3145736 | tf_op jit(solution)/shard_map/ppermute | solution.py:390
  44.9 34.6 %all-to-all-start = ((f32[16,64,256]{2,1,0:T(8,128)}), f32[16,64,256]{2,1,0:T(8,128)S(1)}, u32[]{:S(2)}, u32[]{:S(2)}) async-start(f32[16,64,256]{2,1,0:T(8,128)} %bitcast.12), calls=%async_computation | async-start | bytes 2097152 | tf_op jit(solution)/shard_map/all_to_all | solution.py:436
  80.4 2.0 %collective-permute-start.8 = (f32[8,64,256]{2,1,0:T(8,128)S(1)}, f32[8,64,256]{2,1,0:T(8,128)S(1)}, u32[]{:S(2)}, u32[]{:S(2)}) collective-permute-start(f32[8,64,256]{2,1,0:T(8,128)S(1)} %shard_map.68), channel_id=1, source_target_pairs={{0,1},{1,0},{2,3},{3,2},{4,5},{5,4},{6,7},{7,6},{8,9},{9,8},{10,11... | collective-permute-start | bytes 1572872 | tf_op jit(solution)/shard_map/ppermute | solution.py:390

commit v12 on v11

--- a/solution.py
+++ b/solution.py
@@ -251,9 +251,14 @@
     ]
 
 
-def coupling_kernel(place, c_own, c_x, c_y, far_mine, far_theirs, out_ref, c_far):
-    y, x = place[0], place[1]
-    first, rows = place[2] == 0, far_mine.shape[1]
+def place_of():
+    slab = lax.axis_index("slab")
+    return slab // 2, slab % 2
+
+
+def coupling_kernel(c_own, c_x, c_y, far_mine, far_theirs, out_ref, c_far):
+    y, x = place_of()
+    first, rows = lax.axis_index("energy") % 2 == 0, far_mine.shape[1]
     for part in range(2):
         mine, theirs = far_mine[part], far_theirs[part]
         c_far[part, :rows] = jnp.where(first, mine, theirs)
@@ -266,8 +271,8 @@
                     out_ref[slab - 1, side, 2 * plane + term] = terms[term]
 
 
-def chain_kernel(place, b_own, b_x, b_y, b_far, c_forms, keep_ref, give_ref):
-    y, x = place[0], place[1]
+def chain_kernel(b_own, b_x, b_y, b_far, c_forms, keep_ref, give_ref):
+    y, x = place_of()
     greens, forms = [], []
     for slab in range(4):
         mats = split_rows(pick_block(y, x, slab, b_own, b_x, b_y, b_far))
@@ -320,29 +325,33 @@
             out_ref[energy, here, :] = total
 
 
-def pick_kernel(active, keep_ref, got_ref, out_ref):
+def pick_kernel(keep_ref, got_ref, out_ref):
+    owner = lax.axis_index("mom") == place_of()[1]
     for slab in range(out_ref.shape[0]):
-        out_ref[slab] = jnp.where(active[0] == 1, keep_ref[slab], got_ref[slab])
-
-
-def prepare_kernel(place, scale, onsite_ref, hop_ref, sigma_ref, own_ref, other_ref):
+        out_ref[slab] = jnp.where(owner, keep_ref[slab], got_ref[slab])
+
+
+def prepare_kernel(planes, onsite_ref, hop_ref, sigma_ref, own_ref, other_ref):
     width = hop_ref.shape[-1]
+    y, _ = place_of()
     eye = lax.broadcasted_iota(jnp.int32, (width, width), 0) == lax.broadcasted_iota(
         jnp.int32, (width, width), 1
     )
-    for ref, local, energy in ((other_ref, 1 - place[0], scale[1]), (own_ref, place[0], scale[0])):
-        level = energy - onsite_ref[...]
+    count = sigma_ref.shape[0]
+    for ref, local in ((other_ref, 1 - y), (own_ref, y)):
+        index = (lax.axis_index("energy") * count + local).astype(jnp.float32)
+        level = (-0.5 + (index + 0.5) / (count * planes)) - onsite_ref[...]
         ref[0] = jnp.where(eye, level, 0.0) - hop_ref[0] - sigma_ref[local, 0]
         ref[1] = jnp.where(eye, ETA, 0.0) - hop_ref[1] - sigma_ref[local, 1]
 
 
-def call(kernel, place, arrays, shape, count, products):
+def call(kernel, arrays, shape, count, products):
     width = arrays[0].shape[-1]
     vmem = pl.BlockSpec(memory_space=pltpu.VMEM)
     return pl.pallas_call(
         kernel,
         out_shape=[jax.ShapeDtypeStruct(shape, jnp.float32)] * count,
-        in_specs=[pl.BlockSpec(memory_space=pltpu.SMEM)] + [vmem] * len(arrays),
+        in_specs=[vmem] * len(arrays),
         out_specs=[vmem] * count,
         compiler_params=pltpu.CompilerParams(vmem_limit_bytes=VMEM_BYTES),
         cost_estimate=pl.CostEstimate(
@@ -350,7 +359,7 @@
             bytes_accessed=(len(arrays) + count) * 2 * width * width * 4,
             transcendentals=0,
         ),
-    )(place, *arrays)
+    )(*arrays)
 
 
 def owner_body(onsite, hop, couple, sigma_in, shifts, mode_weight):
@@ -364,8 +373,6 @@
     z = lax.axis_index("energy")
     k = lax.axis_index("mom")
     y, x = slab // 2, slab % 2
-    place = jnp.stack([y, x, z % 2]).astype(jnp.int32)
-    active = k == x
 
     def device(yy, xx, zz, kk):
         return ((2 * yy + xx) * energy_count + zz) * mom_count + kk
@@ -389,18 +396,16 @@
     def send(value, pairs):
         return lax.ppermute(value, axes, pairs)
 
-    locals_ = jnp.stack([y, 1 - y])
-    energies = -0.5 + ((z * e_local + locals_).astype(jnp.float32) + 0.5) / total
     smem = pl.BlockSpec(memory_space=pltpu.SMEM)
     vmem = pl.BlockSpec(memory_space=pltpu.VMEM)
     block_shape = jax.ShapeDtypeStruct((2, width, width), jnp.float32)
     b_own, b_other = pl.pallas_call(
-        prepare_kernel,
+        functools.partial(prepare_kernel, energy_count),
         out_shape=[block_shape] * 2,
-        in_specs=[smem, smem, vmem, vmem, vmem],
+        in_specs=[vmem] * 3,
         out_specs=[vmem] * 2,
         compiler_params=pltpu.CompilerParams(vmem_limit_bytes=VMEM_BYTES),
-    )(place, energies, onsite[0], hop[0, 0], sigma_in[:, 0])
+    )(onsite[0], hop[0, 0], sigma_in[:, 0])
 
     coupling = couple[0, 0]
     c_part = lax.dynamic_slice_in_dim(coupling, (z % 2) * (width // 2), width // 2, axis=1)
@@ -416,20 +421,20 @@
     c_forms = pl.pallas_call(
         coupling_kernel,
         out_shape=jax.ShapeDtypeStruct((3, 2, 6, width, width), jnp.bfloat16),
-        in_specs=[smem] + [vmem] * 5,
+        in_specs=[vmem] * 5,
         out_specs=vmem,
         scratch_shapes=[pltpu.VMEM((2, width, width), jnp.float32)],
         compiler_params=pltpu.CompilerParams(vmem_limit_bytes=VMEM_BYTES),
-    )(place, coupling, c_x, c_y, far_mine, far_theirs)
+    )(coupling, c_x, c_y, far_mine, far_theirs)
     shape = (4, width, width)
-    keep, give = call(chain_kernel, place, (b_own, b_x, b_y, b_far, c_forms), shape, 2, 26)
+    keep, give = call(chain_kernel, (b_own, b_x, b_y, b_far, c_forms), shape, 2, 26)
     half = pl.pallas_call(
         pick_kernel,
         out_shape=jax.ShapeDtypeStruct(shape, jnp.float32),
-        in_specs=[smem, vmem, vmem],
+        in_specs=[vmem, vmem],
         out_specs=vmem,
         compiler_params=pltpu.CompilerParams(vmem_limit_bytes=VMEM_BYTES),
-    )(active[None].astype(jnp.int32), keep, send(give, gift))
+    )(keep, send(give, gift))
 
     rows = width // energy_count
     slots = 4 * energy_count

time: 84.1 us -> 82.6 us (0.982)
  Pallas kernels: 15.8 us -> 13.8 us
  waiting for transfers between devices: 38.1 us -> 39.4 us
    ppermute x9, waiting for transfers between devices: 10.3 us -> 11.6 us  [send(): return lax.ppermute(value, axes, pairs)]
  transfers between devices with their start and end apart: 10 -> 10, of which waited for: 5 -> 6; matrix products, arithmetic and copies ran while one was open for 2% -> 1% of each run, Pallas kernels for 3% -> 1%
where the time goes in v12:
time: 82.6 us; the launch traced here: 82.1 us
  waiting for transfers between devices  39.4 us (48%)
  starting transfers between devices  22.3 us (27%)
  Pallas kernels  13.8 us (17%)
  local copies, waits for them, and re-layouts  4.98 us (6%)
  other arithmetic  1.32 us (2%)
    all_to_all x1, waiting for transfers between devices, owner_body(): lax.all_to_all(half.reshape(slots, rows, width), ('slab', 'energy'), 0, 0...  27.8 us
    ppermute x9, starting transfers between devices, send(): return lax.ppermute(value, axes, pairs)  16.3 us
    ppermute x9, waiting for transfers between devices, send(): return lax.ppermute(value, axes, pairs)  11.6 us
    pallas_call x1, Pallas kernels, call(): pl.pallas_call(kernel, out_shape=[jax.ShapeDtypeStruct(shape, jnp.float32...  10.8 us
    all_to_all x1, starting transfers between devices, owner_body(): lax.all_to_all(half.reshape(slots, rows, width), ('slab', 'energy'), 0, 0...  6.02 us
    unnamed x12, local copies, waits for them, and re-layouts  3.99 us
  transfers between devices with their start and end apart: 10, of which 6 were waited for; matrix products, arithmetic and copies ran while one was open for 1% of the time, Pallas kernels for 1%

profile of v12, /device:TPU:0, one launch (start us, length us, event | category | flops | bytes accessed | tf_op | source)
XLA Modules:
  0.0 82.1 jit_solution(15714145606415971685)
XLA Ops:
  0.0 1.3 %collective-permute-start.4 = (f32[2,256,256]{2,1,0:T(8,128)}, f32[2,256,256]{2,1,0:T(8,128)S(1)}, u32[]{:S(2)}, u32[]{:S(2)}) collective-permute-start(f32[2,256,256]{2,1,0:T(8,128)} %bitcast.11), channel_id=1, source_target_pairs={{8,0},{10,2},{12,4},{14,6},{17,25},{19,27},{21,29},{23,31},{24,16}... | collective-permute-start | bytes 1572872 | tf_op jit(solution)/shard_map/ppermute | solution.py:397
  1.3 1.3 %collective-permute-start.5 = (f32[2,256,256]{2,1,0:T(8,128)}, f32[2,256,256]{2,1,0:T(8,128)S(1)}, u32[]{:S(2)}, u32[]{:S(2)}) collective-permute-start(f32[2,256,256]{2,1,0:T(8,128)} %bitcast.12), channel_id=1, source_target_pairs={{9,25},{11,27},{13,29},{15,31},{16,0},{18,2},{20,4},{22,6},{25,9},... | collective-permute-start | bytes 1572872 | tf_op jit(solution)/shard_map/ppermute | solution.py:397
  2.6 1.0 %dynamic-slice_bitcast_fusion = f32[2,128,256]{2,1,0:T(8,128)S(1)} fusion(f32[1,1,2,256,256]{4,3,2,1,0:T(8,128)} %param.8, s32[]{:T(128)S(6)} %select_n.22), kind=kLoop, calls=%fused_computation.1 | loop fusion | bytes 524292 | tf_op jit(solution)/shard_map/dynamic_slice | solution.py:411
  3.6 1.3 %collective-permute-start.3 = (f32[2,128,256]{2,1,0:T(8,128)S(1)}, f32[2,128,256]{2,1,0:T(8,128)S(1)}, u32[]{:S(2)}, u32[]{:S(2)}) collective-permute-start(f32[2,128,256]{2,1,0:T(8,128)S(1)} %dynamic-slice_bitcast_fusion), channel_id=1, source_target_pairs={{8,16},{10,18},{12,20},{14,22},{17,9},{19,11},{21,13},{23,15},{24,... | collective-permute-start | bytes 786440 | tf_op jit(solution)/shard_map/ppermute | solution.py:397
  4.9 0.0 copy-start.1
  4.9 1.2 %copy-done.1 = f32[2,1,2,256,256]{4,3,2,1,0:T(8,128)S(1)} copy-done((f32[2,1,2,256,256]{4,3,2,1,0:T(8,128)S(1)}, f32[2,1,2,256,256]{4,3,2,1,0:T(8,128)}, u32[]{:S(2)}) %copy-start.1) | copy-done | bytes 1048600
  6.1 1.0 %copy-done.2 = f32[1,1,2,256,256]{4,3,2,1,0:T(8,128)S(1)} copy-done((f32[1,1,2,256,256]{4,3,2,1,0:T(8,128)S(1)}, f32[1,1,2,256,256]{4,3,2,1,0:T(8,128)}, u32[]{:S(2)}) %copy-start.2) | copy-done | bytes 524312
  7.2 0.7 copy-done.3
  7.8 0.2 shard_map.64
  8.0 1.3 %collective-permute-start = (f32[2,256,256]{2,1,0:T(8,128)S(1)}, f32[2,256,256]{2,1,0:T(8,128)S(1)}, u32[]{:S(2)}, u32[]{:S(2)}) collective-permute-start(f32[2,256,256]{2,1,0:T(8,128)S(1)} %get-tuple-element.12.b_own), channel_id=1, source_target_pairs={{1,9},{3,11},{5,13},{7,15},{8,0},{10,2},{12,4},{14,6},{17,25},{19,... | collective-permute-start | bytes 1572872 | tf_op jit(solution)/shard_map/ppermute | solution.py:397
  9.3 4.9 %collective-permute-start.1 = (f32[2,256,256]{2,1,0:T(8,128)S(1)}, f32[2,256,256]{2,1,0:T(8,128)S(1)}, u32[]{:S(2)}, u32[]{:S(2)}) collective-permute-start(f32[2,256,256]{2,1,0:T(8,128)S(1)} %get-tuple-element.13), channel_id=1, source_target_pairs={{0,16},{2,18},{4,20},{6,22},{9,25},{11,27},{13,29},{15,31},{16,0},... | collective-permute-start | bytes 1572872 | tf_op jit(solution)/shard_map/ppermute | solution.py:397
  14.2 2.4 %collective-permute-done.3.far_mine = f32[2,128,256]{2,1,0:T(8,128)S(1)} collective-permute-done((f32[2,128,256]{2,1,0:T(8,128)S(1)}, f32[2,128,256]{2,1,0:T(8,128)S(1)}, u32[]{:S(2)}, u32[]{:S(2)}) %collective-permute-start.3) | collective-permute-done | bytes 262176 | tf_op jit(solution)/shard_map/ppermute | solution.py:397
  16.6 1.3 %collective-permute-start.2 = (f32[2,256,256]{2,1,0:T(8,128)S(1)}, f32[2,256,256]{2,1,0:T(8,128)S(1)}, u32[]{:S(2)}, u32[]{:S(2)}) collective-permute-start(f32[2,256,256]{2,1,0:T(8,128)S(1)} %get-tuple-element.13), channel_id=1, source_target_pairs={{1,25},{3,27},{5,29},{7,31},{8,16},{10,18},{12,20},{14,22},{17,9},... | collective-permute-start | bytes 1572872 | tf_op jit(solution)/shard_map/ppermute | solution.py:397
  17.9 3.5 %collective-permute-start.6 = (f32[2,128,256]{2,1,0:T(8,128)S(1)}, f32[2,128,256]{2,1,0:T(8,128)S(1)}, u32[]{:S(2)}, u32[]{:S(2)}) collective-permute-start(f32[2,128,256]{2,1,0:T(8,128)S(1)} %collective-permute-done.3.far_mine), channel_id=1, source_target_pairs={{0,2},{2,0},{4,6},{6,4},{9,11},{11,9},{13,15},{15,13},{16,18},{18,... | collective-permute-start | bytes 786440 | tf_op jit(solution)/shard_map/ppermute | solution.py:397
  21.4 4.7 %collective-permute-done.6.far_theirs = f32[2,128,256]{2,1,0:T(8,128)S(1)} collective-permute-done((f32[2,128,256]{2,1,0:T(8,128)S(1)}, f32[2,128,256]{2,1,0:T(8,128)S(1)}, u32[]{:S(2)}, u32[]{:S(2)}) %collective-permute-start.6) | collective-permute-done | bytes 262176 | tf_op jit(solution)/shard_map/ppermute | solution.py:397
  26.1 1.0 %copy-done = f32[1,1,2,256,256]{4,3,2,1,0:T(8,128)S(1)} copy-done((f32[1,1,2,256,256]{4,3,2,1,0:T(8,128)S(1)}, f32[1,1,2,256,256]{4,3,2,1,0:T(8,128)}, u32[]{:S(2)}) %copy-start) | copy-done | bytes 524312
  27.2 0.9 %shard_map.65.c_forms = bf16[3,2,6,256,256]{4,3,2,1,0:T(8,128)(2,1)S(1)} custom-call(f32[2,256,256]{2,1,0:T(8,128)S(1)} %bitcast.13, f32[2,256,256]{2,1,0:T(8,128)S(1)} %collective-permute-done.4.c_x, f32[2,256,256]{2,1,0:T(8,128)S(1)} %collective-permute-done.5.c_y, f32[2,128,256]{2,1,0:T(8,128)S(1)} %collective-permute-done.3.far_mine, ...), custom_call_target="tpu_custom_call" | custom-call | tf_op jit(solution)/shard_map/pallas_call | solution.py:421
  28.1 0.4 collective-permute-done.2.b_far
  28.5 10.8 %shard_map.66 = (f32[4,256,256]{2,1,0:T(8,128)S(1)}, f32[4,256,256]{2,1,0:T(8,128)S(1)}) custom-call(f32[2,256,256]{2,1,0:T(8,128)S(1)} %get-tuple-element.12.b_own, f32[2,256,256]{2,1,0:T(8,128)S(1)} %collective-permute-done.b_x, f32[2,256,256]{2,1,0:T(8,128)S(1)} %collective-permute-done.1.b_y, f32[2,256,256]{2,1,0:T(8,128)S(1)} %collective-permute-done.2.b_far, ...), custom_call_target="tpu_custom_call" | custom-call | flops 7851737088 | bytes 3670016 | tf_op jit(solution)/shard_map/pallas_call | solution.py:351
  39.3 0.0 copy-start.4
  39.3 0.0 copy-start.5
  39.4 1.4 %collective-permute-start.7 = (f32[4,256,256]{2,1,0:T(8,128)S(1)}, f32[4,256,256]{2,1,0:T(8,128)S(1)}, u32[]{:S(2)}, u32[]{:S(2)}) collective-permute-start(f32[4,256,256]{2,1,0:T(8,128)S(1)} %get-tuple-element.18), channel_id=1, source_target_pairs={{0,1},{2,3},{4,5},{6,7},{9,8},{11,10},{13,12},{15,14},{16,17},{18,... | collective-permute-start | bytes 3145736 | tf_op jit(solution)/shard_map/ppermute | solution.py:397
  40.7 2.2 %collective-permute-done.7.got_ref = f32[4,256,256]{2,1,0:T(8,128)S(1)} collective-permute-done((f32[4,256,256]{2,1,0:T(8,128)S(1)}, f32[4,256,256]{2,1,0:T(8,128)S(1)}, u32[]{:S(2)}, u32[]{:S(2)}) %collective-permute-start.7) | collective-permute-done | bytes 1048608 | tf_op jit(solution)/shard_map/ppermute | solution.py:397
  42.9 1.1 %shard_map.67 = f32[4,256,256]{2,1,0:T(8,128)} custom-call(f32[4,256,256]{2,1,0:T(8,128)S(1)} %get-tuple-element.17.keep_ref, f32[4,256,256]{2,1,0:T(8,128)S(1)} %collective-permute-done.7.got_ref), custom_call_target="tpu_custom_call" | custom-call | tf_op jit(solution)/shard_map/pallas_call | solution.py:431
  44.0 6.0 %all-to-all-start = ((f32[16,64,256]{2,1,0:T(8,128)}), f32[16,64,256]{2,1,0:T(8,128)S(1)}, u32[]{:S(2)}, u32[]{:S(2)}) async-start(f32[16,64,256]{2,1,0:T(8,128)} %bitcast.7), calls=%async_computation | async-start | bytes 2097152 | tf_op jit(solution)/shard_map/all_to_all | solution.py:441
  50.1 0.1 iota_add_fusion
  50.1 0.1 add_reduce_fusion
  50.2 27.8 %all-to-all-done.parts_ref = f32[16,64,256]{2,1,0:T(8,128)S(1)} async-done(((f32[16,64,256]{2,1,0:T(8,128)}), f32[16,64,256]{2,1,0:T(8,128)S(1)}, u32[]{:S(2)}, u32[]{:S(2)}) %all-to-all-start) | async-done | bytes 1048608 | tf_op jit(solution)/shard_map/all_to_all | solution.py:441
  78.0 0.9 %shard_map.68 = f32[8,64,256]{2,1,0:T(8,128)S(1)} custom-call(f32[8,8]{1,0:T(8,128)S(1)} %broadcast_multiply_fusion.phonon, f32[16,64,256]{2,1,0:T(8,128)S(1)} %all-to-all-done.parts_ref), custom_call_target="tpu_custom_call" | custom-call | tf_op jit(solution)/shard_map/pallas_call | solution.py:445
  78.9 0.1 collective-permute-start.8
  79.0 1.9 %collective-permute-done.8 = f32[8,64,256]{2,1,0:T(8,128)S(1)} collective-permute-done((f32[8,64,256]{2,1,0:T(8,128)S(1)}, f32[8,64,256]{2,1,0:T(8,128)S(1)}, u32[]{:S(2)}, u32[]{:S(2)}) %collective-permute-start.8) | collective-permute-done | bytes 524320 | tf_op jit(solution)/shard_map/ppermute | solution.py:397
  80.9 1.2 %broadcast_select_fusion = f32[8,1,2,64,256]{4,3,2,1,0:T(8,128)} fusion(f32[8,64,256]{2,1,0:T(8,128)S(1)} %collective-permute-done.8, f32[8,64,256]{2,1,0:T(8,128)S(1)} %shard_map.68, pred[2]{0:T(512)(128)(4,1)S(1)} %iota_compare_fusion.2), kind=kLoop, calls=%fused_computation | loop fusion | flops 262144 | bytes 2097154 | tf_op jit(solution)/shard_map/jit(_where)/select_n | solution.py:454
  (12 shorter events, 0.0 us)
Async XLA Ops:
  0.0 17.9 %collective-permute-start.4 = (f32[2,256,256]{2,1,0:T(8,128)}, f32[2,256,256]{2,1,0:T(8,128)S(1)}, u32[]{:S(2)}, u32[]{:S(2)}) collective-permute-start(f32[2,256,256]{2,1,0:T(8,128)} %bitcast.11), channel_id=1, source_target_pairs={{8,0},{10,2},{12,4},{14,6},{17,25},{19,27},{21,29},{23,31},{24,16}... | collective-permute-start | bytes 1572872 | tf_op jit(solution)/shard_map/ppermute | solution.py:397
  1.3 16.6 %collective-permute-start.5 = (f32[2,256,256]{2,1,0:T(8,128)}, f32[2,256,256]{2,1,0:T(8,128)S(1)}, u32[]{:S(2)}, u32[]{:S(2)}) collective-permute-start(f32[2,256,256]{2,1,0:T(8,128)} %bitcast.12), channel_id=1, source_target_pairs={{9,25},{11,27},{13,29},{15,31},{16,0},{18,2},{20,4},{22,6},{25,9},... | collective-permute-start | bytes 1572872 | tf_op jit(solution)/shard_map/ppermute | solution.py:397
  3.6 13.0 %collective-permute-start.3 = (f32[2,128,256]{2,1,0:T(8,128)S(1)}, f32[2,128,256]{2,1,0:T(8,128)S(1)}, u32[]{:S(2)}, u32[]{:S(2)}) collective-permute-start(f32[2,128,256]{2,1,0:T(8,128)S(1)} %dynamic-slice_bitcast_fusion), channel_id=1, source_target_pairs={{8,16},{10,18},{12,20},{14,22},{17,9},{19,11},{21,13},{23,15},{24,... | collective-permute-start | bytes 786440 | tf_op jit(solution)/shard_map/ppermute | solution.py:397
  4.9 1.2 %copy-start.1 = (f32[2,1,2,256,256]{4,3,2,1,0:T(8,128)S(1)}, f32[2,1,2,256,256]{4,3,2,1,0:T(8,128)}, u32[]{:S(2)}) copy-start(f32[2,1,2,256,256]{4,3,2,1,0:T(8,128)} %param.9) | copy-start | bytes 3145732
  6.1 1.0 %copy-start.2 = (f32[1,1,2,256,256]{4,3,2,1,0:T(8,128)S(1)}, f32[1,1,2,256,256]{4,3,2,1,0:T(8,128)}, u32[]{:S(2)}) copy-start(f32[1,1,2,256,256]{4,3,2,1,0:T(8,128)} %param.7) | copy-start | bytes 1572868
  7.2 0.7 copy-start.3
  8.0 20.1 %collective-permute-start = (f32[2,256,256]{2,1,0:T(8,128)S(1)}, f32[2,256,256]{2,1,0:T(8,128)S(1)}, u32[]{:S(2)}, u32[]{:S(2)}) collective-permute-start(f32[2,256,256]{2,1,0:T(8,128)S(1)} %get-tuple-element.12.b_own), channel_id=1, source_target_pairs={{1,9},{3,11},{5,13},{7,15},{8,0},{10,2},{12,4},{14,6},{17,25},{19,... | collective-permute-start | bytes 1572872 | tf_op jit(solution)/shard_map/ppermute | solution.py:397
  9.3 18.8 %collective-permute-start.1 = (f32[2,256,256]{2,1,0:T(8,128)S(1)}, f32[2,256,256]{2,1,0:T(8,128)S(1)}, u32[]{:S(2)}, u32[]{:S(2)}) collective-permute-start(f32[2,256,256]{2,1,0:T(8,128)S(1)} %get-tuple-element.13), channel_id=1, source_target_pairs={{0,16},{2,18},{4,20},{6,22},{9,25},{11,27},{13,29},{15,31},{16,0},... | collective-permute-start | bytes 1572872 | tf_op jit(solution)/shard_map/ppermute | solution.py:397
  16.6 12.0 %collective-permute-start.2 = (f32[2,256,256]{2,1,0:T(8,128)S(1)}, f32[2,256,256]{2,1,0:T(8,128)S(1)}, u32[]{:S(2)}, u32[]{:S(2)}) collective-permute-start(f32[2,256,256]{2,1,0:T(8,128)S(1)} %get-tuple-element.13), channel_id=1, source_target_pairs={{1,25},{3,27},{5,29},{7,31},{8,16},{10,18},{12,20},{14,22},{17,9},... | collective-permute-start | bytes 1572872 | tf_op jit(solution)/shard_map/ppermute | solution.py:397
  17.9 8.3 %collective-permute-start.6 = (f32[2,128,256]{2,1,0:T(8,128)S(1)}, f32[2,128,256]{2,1,0:T(8,128)S(1)}, u32[]{:S(2)}, u32[]{:S(2)}) collective-permute-start(f32[2,128,256]{2,1,0:T(8,128)S(1)} %collective-permute-done.3.far_mine), channel_id=1, source_target_pairs={{0,2},{2,0},{4,6},{6,4},{9,11},{11,9},{13,15},{15,13},{16,18},{18,... | collective-permute-start | bytes 786440 | tf_op jit(solution)/shard_map/ppermute | solution.py:397
  26.1 1.0 %copy-start = (f32[1,1,2,256,256]{4,3,2,1,0:T(8,128)S(1)}, f32[1,1,2,256,256]{4,3,2,1,0:T(8,128)}, u32[]{:S(2)}) copy-start(f32[1,1,2,256,256]{4,3,2,1,0:T(8,128)} %param.8) | copy-start | bytes 1572868
  39.3 10.7 %copy-start.4 = (f32[2,4]{1,0:T(2,128)S(1)}, f32[2,4]{1,0:T(2,128)}, u32[]{:S(2)}) copy-start(f32[2,4]{1,0:T(2,128)} %param.11) | copy-start | bytes 100
  39.3 10.7 %copy-start.5 = (s32[4]{0:T(128)S(1)}, s32[4]{0:T(128)}, u32[]{:S(2)}) copy-start(s32[4]{0:T(128)} %param.10) | copy-start | bytes 52
  39.4 3.6 %collective-permute-start.7 = (f32[4,256,256]{2,1,0:T(8,128)S(1)}, f32[4,256,256]{2,1,0:T(8,128)S(1)}, u32[]{:S(2)}, u32[]{:S(2)}) collective-permute-start(f32[4,256,256]{2,1,0:T(8,128)S(1)} %get-tuple-element.18), channel_id=1, source_target_pairs={{0,1},{2,3},{4,5},{6,7},{9,8},{11,10},{13,12},{15,14},{16,17},{18,... | collective-permute-start | bytes 3145736 | tf_op jit(solution)/shard_map/ppermute | solution.py:397
  44.0 34.0 %all-to-all-start = ((f32[16,64,256]{2,1,0:T(8,128)}), f32[16,64,256]{2,1,0:T(8,128)S(1)}, u32[]{:S(2)}, u32[]{:S(2)}) async-start(f32[16,64,256]{2,1,0:T(8,128)} %bitcast.7), calls=%async_computation | async-start | bytes 2097152 | tf_op jit(solution)/shard_map/all_to_all | solution.py:441
  78.9 2.0 %collective-permute-start.8 = (f32[8,64,256]{2,1,0:T(8,128)S(1)}, f32[8,64,256]{2,1,0:T(8,128)S(1)}, u32[]{:S(2)}, u32[]{:S(2)}) collective-permute-start(f32[8,64,256]{2,1,0:T(8,128)S(1)} %shard_map.68), channel_id=1, source_target_pairs={{0,1},{1,0},{2,3},{3,2},{4,5},{5,4},{6,7},{7,6},{8,9},{9,8},{10,11... | collective-permute-start | bytes 1572872 | tf_op jit(solution)/shard_map/ppermute | solution.py:397

commit v13 on v12

--- a/solution.py
+++ b/solution.py
@@ -256,13 +256,14 @@
     return slab // 2, slab % 2
 
 
-def coupling_kernel(c_own, c_x, c_y, far_mine, far_theirs, out_ref, c_far):
+def coupling_kernel(c_part, c_rest, c_x, c_y, far_mine, far_theirs, out_ref, c_own, c_far):
     y, x = place_of()
     first, rows = lax.axis_index("energy") % 2 == 0, far_mine.shape[1]
-    for part in range(2):
-        mine, theirs = far_mine[part], far_theirs[part]
-        c_far[part, :rows] = jnp.where(first, mine, theirs)
-        c_far[part, rows:] = jnp.where(first, theirs, mine)
+    for ref, here, beside in ((c_own, c_part, c_rest), (c_far, far_mine, far_theirs)):
+        for part in range(2):
+            mine, theirs = here[part], beside[part]
+            ref[part, :rows] = jnp.where(first, mine, theirs)
+            ref[part, rows:] = jnp.where(first, theirs, mine)
     for slab in (1, 2, 3):
         real, imag = pick_block(y, x, slab, c_own, c_x, c_y, c_far)
         for side, pair in enumerate(((real, imag), (real.T, -imag.T))):
@@ -303,32 +304,44 @@
             full_form = form_rows([form(block) for block in fulls])
 
 
-def mix_kernel(phonon, parts_ref, out_ref):
-    slots, rows, _ = parts_ref.shape
+def mix_kernel(weight, parts_ref, out_ref):
+    slots, rows, width = parts_ref.shape
     energies = out_ref.shape[0]
-    planes, step = slots // 4, 8
+    planes = slots // 4
+    high, wide = weight.shape[2:]
 
     def source(slot):
         return 2 * (slot % planes) + slot // planes // 2
 
-    for row in range(0, rows, step):
-        here = slice(row, row + step)
-        values = [None] * energies
-        for slot in range(slots):
-            value = parts_ref[slot, here, :]
-            held = values[source(slot)]
-            values[source(slot)] = value if held is None else held + value
-        for energy in range(energies):
-            total = phonon[energy, 0] * values[0]
-            for other in range(1, energies):
-                total = total + phonon[energy, other] * values[other]
-            out_ref[energy, here, :] = total
-
-
-def pick_kernel(keep_ref, got_ref, out_ref):
+    for row in range(0, rows, high):
+        for column in range(0, width, wide):
+            here = (slice(row, row + high), slice(column, column + wide))
+            values = [None] * energies
+            for slot in range(slots):
+                value = parts_ref[(slot, *here)]
+                held = values[source(slot)]
+                values[source(slot)] = value if held is None else held + value
+            for energy in range(energies):
+                total = weight[energy, 0] * values[0]
+                for other in range(1, energies):
+                    total = total + weight[energy, other] * values[other]
+                out_ref[(energy, *here)] = total
+
+
+def pick_kernel(keep_ref, got_ref, out_ref, sem):
     owner = lax.axis_index("mom") == place_of()[1]
-    for slab in range(out_ref.shape[0]):
-        out_ref[slab] = jnp.where(owner, keep_ref[slab], got_ref[slab])
+
+    @pl.when(owner)
+    def _():
+        copy = pltpu.make_async_copy(keep_ref, out_ref, sem)
+        copy.start()
+        copy.wait()
+
+    @pl.when(jnp.logical_not(owner))
+    def _():
+        copy = pltpu.make_async_copy(got_ref, out_ref, sem)
+        copy.start()
+        copy.wait()
 
 
 def prepare_kernel(planes, onsite_ref, hop_ref, sigma_ref, own_ref, other_ref):
@@ -396,7 +409,6 @@
     def send(value, pairs):
         return lax.ppermute(value, axes, pairs)
 
-    smem = pl.BlockSpec(memory_space=pltpu.SMEM)
     vmem = pl.BlockSpec(memory_space=pltpu.VMEM)
     block_shape = jax.ShapeDtypeStruct((2, width, width), jnp.float32)
     b_own, b_other = pl.pallas_call(
@@ -408,7 +420,9 @@
     )(onsite[0], hop[0, 0], sigma_in[:, 0])
 
     coupling = couple[0, 0]
-    c_part = lax.dynamic_slice_in_dim(coupling, (z % 2) * (width // 2), width // 2, axis=1)
+    size = width // 2
+    c_part = lax.dynamic_slice_in_dim(coupling, (z % 2) * size, size, axis=1)
+    c_rest = lax.dynamic_slice_in_dim(coupling, (1 - z % 2) * size, size, axis=1)
     far_mine = send(c_part, routes((1, 2), (2, 1), (3, 0)))
     c_x = send(coupling, routes((1, 0), (2, 3), (3, 2)))
     c_y = send(coupling, routes((1, 3), (2, 0), (3, 1)))
@@ -421,18 +435,20 @@
     c_forms = pl.pallas_call(
         coupling_kernel,
         out_shape=jax.ShapeDtypeStruct((3, 2, 6, width, width), jnp.bfloat16),
-        in_specs=[vmem] * 5,
+        in_specs=[vmem] * 6,
         out_specs=vmem,
-        scratch_shapes=[pltpu.VMEM((2, width, width), jnp.float32)],
+        scratch_shapes=[pltpu.VMEM((2, width, width), jnp.float32)] * 2,
         compiler_params=pltpu.CompilerParams(vmem_limit_bytes=VMEM_BYTES),
-    )(coupling, c_x, c_y, far_mine, far_theirs)
+    )(c_part, c_rest, c_x, c_y, far_mine, far_theirs)
     shape = (4, width, width)
     keep, give = call(chain_kernel, (b_own, b_x, b_y, b_far, c_forms), shape, 2, 26)
+    anywhere = pl.BlockSpec(memory_space=pl.ANY)
     half = pl.pallas_call(
         pick_kernel,
         out_shape=jax.ShapeDtypeStruct(shape, jnp.float32),
-        in_specs=[vmem, vmem],
-        out_specs=vmem,
+        in_specs=[anywhere] * 2,
+        out_specs=anywhere,
+        scratch_shapes=[pltpu.SemaphoreType.DMA],
         compiler_params=pltpu.CompilerParams(vmem_limit_bytes=VMEM_BYTES),
     )(keep, send(give, gift))
 
@@ -442,13 +458,14 @@
         half.reshape(slots, rows, width), ("slab", "energy"), 0, 0, tiled=True
     )
     phonon = phonon_matrix(shifts, mode_weight, total) / mom_count
+    weight = jnp.broadcast_to(phonon[:, :, None, None], (total, total, 8, 128))
     mixed = pl.pallas_call(
         mix_kernel,
         out_shape=jax.ShapeDtypeStruct((total, rows, width), jnp.float32),
-        in_specs=[smem, vmem],
+        in_specs=[vmem, vmem],
         out_specs=vmem,
         compiler_params=pltpu.CompilerParams(vmem_limit_bytes=VMEM_BYTES),
-    )(phonon, parts)
+    )(weight, parts)
     other = send(mixed, siblings)
     mine = jnp.arange(2)[:, None, None] == k
     result = jnp.where(mine, mixed[:, None], other[:, None])

time: 82.6 us -> 82.1 us (level)
  waiting for transfers between devices: 39.4 us -> 40.3 us
  local copies, waits for them, and re-layouts: 4.98 us -> 4.15 us
    unnamed x12 -> x10, local copies, waits for them, and re-layouts: 3.99 us -> 2.95 us
    ppermute x9, waiting for transfers between devices: 11.6 us -> 12.5 us  [send(): return lax.ppermute(value, axes, pairs)]
  transfers between devices with their start and end apart: 10 -> 10, of which waited for: 6 -> 6; matrix products, arithmetic and copies ran while one was open for 1% -> 2% of each run, Pallas kernels for 1% -> 1%
where the time goes in v13:
time: 82.1 us; the launch traced here: 81.7 us
  waiting for transfers between devices  40.3 us (49%)
  starting transfers between devices  22.4 us (27%)
  Pallas kernels  13.2 us (16%)
  local copies, waits for them, and re-layouts  4.15 us (5%)
  other arithmetic  1.32 us (2%)
    all_to_all x1, waiting for transfers between devices, owner_body(): lax.all_to_all(half.reshape(slots, rows, width), ('slab', 'energy'), 0, 0...  27.8 us
    ppermute x9, starting transfers between devices, send(): return lax.ppermute(value, axes, pairs)  16.3 us
    ppermute x9, waiting for transfers between devices, send(): return lax.ppermute(value, axes, pairs)  12.5 us
    pallas_call x1, Pallas kernels, call(): pl.pallas_call(kernel, out_shape=[jax.ShapeDtypeStruct(shape, jnp.float32...  10.8 us
    all_to_all x1, starting transfers between devices, owner_body(): lax.all_to_all(half.reshape(slots, rows, width), ('slab', 'energy'), 0, 0...  6.13 us
    unnamed x10, local copies, waits for them, and re-layouts  2.95 us
  transfers between devices with their start and end apart: 10, of which 6 were waited for; matrix products, arithmetic and copies ran while one was open for 2% of the time, Pallas kernels for 1%

profile of v13, /device:TPU:0, one launch (start us, length us, event | category | flops | bytes accessed | tf_op | source)
XLA Modules:
  0.0 81.7 jit_solution(14585965498033719642)
XLA Ops:
  0.0 1.3 %collective-permute-start.4 = (f32[2,256,256]{2,1,0:T(8,128)}, f32[2,256,256]{2,1,0:T(8,128)S(1)}, u32[]{:S(2)}, u32[]{:S(2)}) collective-permute-start(f32[2,256,256]{2,1,0:T(8,128)} %bitcast.16), channel_id=1, source_target_pairs={{8,0},{10,2},{12,4},{14,6},{17,25},{19,27},{21,29},{23,31},{24,16}... | collective-permute-start | bytes 1572872 | tf_op jit(solution)/shard_map/ppermute | solution.py:410
  1.3 1.3 %collective-permute-start.5 = (f32[2,256,256]{2,1,0:T(8,128)}, f32[2,256,256]{2,1,0:T(8,128)S(1)}, u32[]{:S(2)}, u32[]{:S(2)}) collective-permute-start(f32[2,256,256]{2,1,0:T(8,128)} %bitcast.17), channel_id=1, source_target_pairs={{9,25},{11,27},{13,29},{15,31},{16,0},{18,2},{20,4},{22,6},{25,9},... | collective-permute-start | bytes 1572872 | tf_op jit(solution)/shard_map/ppermute | solution.py:410
  2.6 1.1 %dynamic-slice_bitcast_fusion = (f32[2,128,256]{2,1,0:T(8,128)S(1)}, f32[2,128,256]{2,1,0:T(8,128)S(1)}) fusion(f32[1,1,2,256,256]{4,3,2,1,0:T(8,128)} %param.8, s32[]{:T(128)S(6)} %select_n.28, s32[]{:T(128)S(6)} %select_n.27), kind=kLoop, calls=%fused_computation.1 | loop fusion | bytes 1048584 | tf_op jit(solution)/shard_map/dynamic_slice | solution.py:425
  3.7 1.3 %collective-permute-start.3 = (f32[2,128,256]{2,1,0:T(8,128)S(1)}, f32[2,128,256]{2,1,0:T(8,128)S(1)}, u32[]{:S(2)}, u32[]{:S(2)}) collective-permute-start(f32[2,128,256]{2,1,0:T(8,128)S(1)} %get-tuple-element.20.c_part), channel_id=1, source_target_pairs={{8,16},{10,18},{12,20},{14,22},{17,9},{19,11},{21,13},{23,15},{24,... | collective-permute-start | bytes 786440 | tf_op jit(solution)/shard_map/ppermute | solution.py:410
  5.0 0.0 copy-start
  5.0 1.2 %copy-done = f32[2,1,2,256,256]{4,3,2,1,0:T(8,128)S(1)} copy-done((f32[2,1,2,256,256]{4,3,2,1,0:T(8,128)S(1)}, f32[2,1,2,256,256]{4,3,2,1,0:T(8,128)}, u32[]{:S(2)}) %copy-start) | copy-done | bytes 1048600
  6.2 1.0 %copy-done.1 = f32[1,1,2,256,256]{4,3,2,1,0:T(8,128)S(1)} copy-done((f32[1,1,2,256,256]{4,3,2,1,0:T(8,128)S(1)}, f32[1,1,2,256,256]{4,3,2,1,0:T(8,128)}, u32[]{:S(2)}) %copy-start.1) | copy-done | bytes 524312
  7.3 0.7 copy-done.2
  7.9 0.2 shard_map.64
  8.1 1.3 %collective-permute-start = (f32[2,256,256]{2,1,0:T(8,128)S(1)}, f32[2,256,256]{2,1,0:T(8,128)S(1)}, u32[]{:S(2)}, u32[]{:S(2)}) collective-permute-start(f32[2,256,256]{2,1,0:T(8,128)S(1)} %get-tuple-element.12.b_own), channel_id=1, source_target_pairs={{1,9},{3,11},{5,13},{7,15},{8,0},{10,2},{12,4},{14,6},{17,25},{19,... | collective-permute-start | bytes 1572872 | tf_op jit(solution)/shard_map/ppermute | solution.py:410
  9.4 4.9 %collective-permute-start.1 = (f32[2,256,256]{2,1,0:T(8,128)S(1)}, f32[2,256,256]{2,1,0:T(8,128)S(1)}, u32[]{:S(2)}, u32[]{:S(2)}) collective-permute-start(f32[2,256,256]{2,1,0:T(8,128)S(1)} %get-tuple-element.13), channel_id=1, source_target_pairs={{0,16},{2,18},{4,20},{6,22},{9,25},{11,27},{13,29},{15,31},{16,0},... | collective-permute-start | bytes 1572872 | tf_op jit(solution)/shard_map/ppermute | solution.py:410
  14.3 2.2 %collective-permute-done.3.far_mine = f32[2,128,256]{2,1,0:T(8,128)S(1)} collective-permute-done((f32[2,128,256]{2,1,0:T(8,128)S(1)}, f32[2,128,256]{2,1,0:T(8,128)S(1)}, u32[]{:S(2)}, u32[]{:S(2)}) %collective-permute-start.3) | collective-permute-done | bytes 262176 | tf_op jit(solution)/shard_map/ppermute | solution.py:410
  16.6 1.3 %collective-permute-start.2 = (f32[2,256,256]{2,1,0:T(8,128)S(1)}, f32[2,256,256]{2,1,0:T(8,128)S(1)}, u32[]{:S(2)}, u32[]{:S(2)}) collective-permute-start(f32[2,256,256]{2,1,0:T(8,128)S(1)} %get-tuple-element.13), channel_id=1, source_target_pairs={{1,25},{3,27},{5,29},{7,31},{8,16},{10,18},{12,20},{14,22},{17,9},... | collective-permute-start | bytes 1572872 | tf_op jit(solution)/shard_map/ppermute | solution.py:410
  17.9 3.5 %collective-permute-start.6 = (f32[2,128,256]{2,1,0:T(8,128)S(1)}, f32[2,128,256]{2,1,0:T(8,128)S(1)}, u32[]{:S(2)}, u32[]{:S(2)}) collective-permute-start(f32[2,128,256]{2,1,0:T(8,128)S(1)} %collective-permute-done.3.far_mine), channel_id=1, source_target_pairs={{0,2},{2,0},{4,6},{6,4},{9,11},{11,9},{13,15},{15,13},{16,18},{18,... | collective-permute-start | bytes 786440 | tf_op jit(solution)/shard_map/ppermute | solution.py:410
  21.4 4.7 %collective-permute-done.6.far_theirs = f32[2,128,256]{2,1,0:T(8,128)S(1)} collective-permute-done((f32[2,128,256]{2,1,0:T(8,128)S(1)}, f32[2,128,256]{2,1,0:T(8,128)S(1)}, u32[]{:S(2)}, u32[]{:S(2)}) %collective-permute-start.6) | collective-permute-done | bytes 262176 | tf_op jit(solution)/shard_map/ppermute | solution.py:410
  26.1 1.0 %shard_map.65.c_forms = bf16[3,2,6,256,256]{4,3,2,1,0:T(8,128)(2,1)S(1)} custom-call(f32[2,128,256]{2,1,0:T(8,128)S(1)} %get-tuple-element.20.c_part, f32[2,128,256]{2,1,0:T(8,128)S(1)} %get-tuple-element.19.c_rest, f32[2,256,256]{2,1,0:T(8,128)S(1)} %collective-permute-done.4.c_x, f32[2,256,256]{2,1,0:T(8,128)S(1)} %collective-permute-done.5.c_y, ...), custom_call_target="tpu_custom_call" | custom-call | tf_op jit(solution)/shard_map/pallas_call | solution.py:435
  27.1 1.4 %collective-permute-done.2.b_far = f32[2,256,256]{2,1,0:T(8,128)S(1)} collective-permute-done((f32[2,256,256]{2,1,0:T(8,128)S(1)}, f32[2,256,256]{2,1,0:T(8,128)S(1)}, u32[]{:S(2)}, u32[]{:S(2)}) %collective-permute-start.2) | collective-permute-done | bytes 524320 | tf_op jit(solution)/shard_map/ppermute | solution.py:410
  28.5 10.8 %shard_map.66 = (f32[4,256,256]{2,1,0:T(8,128)S(1)}, f32[4,256,256]{2,1,0:T(8,128)S(1)}) custom-call(f32[2,256,256]{2,1,0:T(8,128)S(1)} %get-tuple-element.12.b_own, f32[2,256,256]{2,1,0:T(8,128)S(1)} %collective-permute-done.b_x, f32[2,256,256]{2,1,0:T(8,128)S(1)} %collective-permute-done.1.b_y, f32[2,256,256]{2,1,0:T(8,128)S(1)} %collective-permute-done.2.b_far, ...), custom_call_target="tpu_custom_call" | custom-call | flops 7851737088 | bytes 3670016 | tf_op jit(solution)/shard_map/pallas_call | solution.py:364
  39.4 0.0 copy-start.3
  39.4 0.0 copy-start.4
  39.4 1.4 %collective-permute-start.7 = (f32[4,256,256]{2,1,0:T(8,128)S(1)}, f32[4,256,256]{2,1,0:T(8,128)S(1)}, u32[]{:S(2)}, u32[]{:S(2)}) collective-permute-start(f32[4,256,256]{2,1,0:T(8,128)S(1)} %get-tuple-element.18), channel_id=1, source_target_pairs={{0,1},{2,3},{4,5},{6,7},{9,8},{11,10},{13,12},{15,14},{16,17},{18,... | collective-permute-start | bytes 3145736 | tf_op jit(solution)/shard_map/ppermute | solution.py:410
  40.7 2.2 %collective-permute-done.7.got_ref = f32[4,256,256]{2,1,0:T(8,128)S(1)} collective-permute-done((f32[4,256,256]{2,1,0:T(8,128)S(1)}, f32[4,256,256]{2,1,0:T(8,128)S(1)}, u32[]{:S(2)}, u32[]{:S(2)}) %collective-permute-start.7) | collective-permute-done | bytes 1048608 | tf_op jit(solution)/shard_map/ppermute | solution.py:410
  43.0 1.0 %shard_map.67 = f32[4,256,256]{2,1,0:T(8,128)} custom-call(f32[4,256,256]{2,1,0:T(8,128)S(1)} %get-tuple-element.17.keep_ref, f32[4,256,256]{2,1,0:T(8,128)S(1)} %collective-permute-done.7.got_ref), custom_call_target="tpu_custom_call" | custom-call | tf_op jit(solution)/shard_map/pallas_call | solution.py:446
  43.9 6.1 %all-to-all-start = ((f32[16,64,256]{2,1,0:T(8,128)}), f32[16,64,256]{2,1,0:T(8,128)S(1)}, u32[]{:S(2)}, u32[]{:S(2)}) async-start(f32[16,64,256]{2,1,0:T(8,128)} %bitcast.8), calls=%async_computation | async-start | bytes 2097152 | tf_op jit(solution)/shard_map/all_to_all | solution.py:457
  50.1 0.1 iota_add_fusion
  50.2 0.1 add_reduce_fusion
  50.3 27.8 %all-to-all-done.parts_ref = f32[16,64,256]{2,1,0:T(8,128)S(1)} async-done(((f32[16,64,256]{2,1,0:T(8,128)}), f32[16,64,256]{2,1,0:T(8,128)S(1)}, u32[]{:S(2)}, u32[]{:S(2)}) %all-to-all-start) | async-done | bytes 1048608 | tf_op jit(solution)/shard_map/all_to_all | solution.py:457
  78.1 0.1 broadcast_in_dim.18.weight
  78.2 0.3 shard_map.68
  78.5 0.1 collective-permute-start.8
  78.6 1.9 %collective-permute-done.8 = f32[8,64,256]{2,1,0:T(8,128)S(1)} collective-permute-done((f32[8,64,256]{2,1,0:T(8,128)S(1)}, f32[8,64,256]{2,1,0:T(8,128)S(1)}, u32[]{:S(2)}, u32[]{:S(2)}) %collective-permute-start.8) | collective-permute-done | bytes 524320 | tf_op jit(solution)/shard_map/ppermute | solution.py:410
  80.5 1.2 %broadcast_select_fusion = f32[8,1,2,64,256]{4,3,2,1,0:T(8,128)} fusion(f32[8,64,256]{2,1,0:T(8,128)S(1)} %collective-permute-done.8, f32[8,64,256]{2,1,0:T(8,128)S(1)} %shard_map.68, pred[2]{0:T(512)(128)(4,1)S(1)} %iota_compare_fusion.2), kind=kLoop, calls=%fused_computation | loop fusion | flops 262144 | bytes 2097154 | tf_op jit(solution)/shard_map/jit(_where)/select_n | solution.py:471
  (11 shorter events, 0.0 us)
Async XLA Ops:
  0.0 17.8 %collective-permute-start.4 = (f32[2,256,256]{2,1,0:T(8,128)}, f32[2,256,256]{2,1,0:T(8,128)S(1)}, u32[]{:S(2)}, u32[]{:S(2)}) collective-permute-start(f32[2,256,256]{2,1,0:T(8,128)} %bitcast.16), channel_id=1, source_target_pairs={{8,0},{10,2},{12,4},{14,6},{17,25},{19,27},{21,29},{23,31},{24,16}... | collective-permute-start | bytes 1572872 | tf_op jit(solution)/shard_map/ppermute | solution.py:410
  1.3 16.6 %collective-permute-start.5 = (f32[2,256,256]{2,1,0:T(8,128)}, f32[2,256,256]{2,1,0:T(8,128)S(1)}, u32[]{:S(2)}, u32[]{:S(2)}) collective-permute-start(f32[2,256,256]{2,1,0:T(8,128)} %bitcast.17), channel_id=1, source_target_pairs={{9,25},{11,27},{13,29},{15,31},{16,0},{18,2},{20,4},{22,6},{25,9},... | collective-permute-start | bytes 1572872 | tf_op jit(solution)/shard_map/ppermute | solution.py:410
  3.7 12.9 %collective-permute-start.3 = (f32[2,128,256]{2,1,0:T(8,128)S(1)}, f32[2,128,256]{2,1,0:T(8,128)S(1)}, u32[]{:S(2)}, u32[]{:S(2)}) collective-permute-start(f32[2,128,256]{2,1,0:T(8,128)S(1)} %get-tuple-element.20.c_part), channel_id=1, source_target_pairs={{8,16},{10,18},{12,20},{14,22},{17,9},{19,11},{21,13},{23,15},{24,... | collective-permute-start | bytes 786440 | tf_op jit(solution)/shard_map/ppermute | solution.py:410
  5.0 1.2 %copy-start = (f32[2,1,2,256,256]{4,3,2,1,0:T(8,128)S(1)}, f32[2,1,2,256,256]{4,3,2,1,0:T(8,128)}, u32[]{:S(2)}) copy-start(f32[2,1,2,256,256]{4,3,2,1,0:T(8,128)} %param.9) | copy-start | bytes 3145732
  6.2 1.0 %copy-start.1 = (f32[1,1,2,256,256]{4,3,2,1,0:T(8,128)S(1)}, f32[1,1,2,256,256]{4,3,2,1,0:T(8,128)}, u32[]{:S(2)}) copy-start(f32[1,1,2,256,256]{4,3,2,1,0:T(8,128)} %param.7) | copy-start | bytes 1572868
  7.3 0.7 copy-start.2
  8.1 19.0 %collective-permute-start = (f32[2,256,256]{2,1,0:T(8,128)S(1)}, f32[2,256,256]{2,1,0:T(8,128)S(1)}, u32[]{:S(2)}, u32[]{:S(2)}) collective-permute-start(f32[2,256,256]{2,1,0:T(8,128)S(1)} %get-tuple-element.12.b_own), channel_id=1, source_target_pairs={{1,9},{3,11},{5,13},{7,15},{8,0},{10,2},{12,4},{14,6},{17,25},{19,... | collective-permute-start | bytes 1572872 | tf_op jit(solution)/shard_map/ppermute | solution.py:410
  9.4 17.7 %collective-permute-start.1 = (f32[2,256,256]{2,1,0:T(8,128)S(1)}, f32[2,256,256]{2,1,0:T(8,128)S(1)}, u32[]{:S(2)}, u32[]{:S(2)}) collective-permute-start(f32[2,256,256]{2,1,0:T(8,128)S(1)} %get-tuple-element.13), channel_id=1, source_target_pairs={{0,16},{2,18},{4,20},{6,22},{9,25},{11,27},{13,29},{15,31},{16,0},... | collective-permute-start | bytes 1572872 | tf_op jit(solution)/shard_map/ppermute | solution.py:410
  16.6 12.0 %collective-permute-start.2 = (f32[2,256,256]{2,1,0:T(8,128)S(1)}, f32[2,256,256]{2,1,0:T(8,128)S(1)}, u32[]{:S(2)}, u32[]{:S(2)}) collective-permute-start(f32[2,256,256]{2,1,0:T(8,128)S(1)} %get-tuple-element.13), channel_id=1, source_target_pairs={{1,25},{3,27},{5,29},{7,31},{8,16},{10,18},{12,20},{14,22},{17,9},... | collective-permute-start | bytes 1572872 | tf_op jit(solution)/shard_map/ppermute | solution.py:410
  17.9 8.3 %collective-permute-start.6 = (f32[2,128,256]{2,1,0:T(8,128)S(1)}, f32[2,128,256]{2,1,0:T(8,128)S(1)}, u32[]{:S(2)}, u32[]{:S(2)}) collective-permute-start(f32[2,128,256]{2,1,0:T(8,128)S(1)} %collective-permute-done.3.far_mine), channel_id=1, source_target_pairs={{0,2},{2,0},{4,6},{6,4},{9,11},{11,9},{13,15},{15,13},{16,18},{18,... | collective-permute-start | bytes 786440 | tf_op jit(solution)/shard_map/ppermute | solution.py:410
  39.4 10.7 %copy-start.3 = (f32[2,4]{1,0:T(2,128)S(1)}, f32[2,4]{1,0:T(2,128)}, u32[]{:S(2)}) copy-start(f32[2,4]{1,0:T(2,128)} %param.11) | copy-start | bytes 100
  39.4 10.7 %copy-start.4 = (s32[4]{0:T(128)S(1)}, s32[4]{0:T(128)}, u32[]{:S(2)}) copy-start(s32[4]{0:T(128)} %param.10) | copy-start | bytes 52
  39.4 3.6 %collective-permute-start.7 = (f32[4,256,256]{2,1,0:T(8,128)S(1)}, f32[4,256,256]{2,1,0:T(8,128)S(1)}, u32[]{:S(2)}, u32[]{:S(2)}) collective-permute-start(f32[4,256,256]{2,1,0:T(8,128)S(1)} %get-tuple-element.18), channel_id=1, source_target_pairs={{0,1},{2,3},{4,5},{6,7},{9,8},{11,10},{13,12},{15,14},{16,17},{18,... | collective-permute-start | bytes 3145736 | tf_op jit(solution)/shard_map/ppermute | solution.py:410
  43.9 34.1 %all-to-all-start = ((f32[16,64,256]{2,1,0:T(8,128)}), f32[16,64,256]{2,1,0:T(8,128)S(1)}, u32[]{:S(2)}, u32[]{:S(2)}) async-start(f32[16,64,256]{2,1,0:T(8,128)} %bitcast.8), calls=%async_computation | async-start | bytes 2097152 | tf_op jit(solution)/shard_map/all_to_all | solution.py:457
  78.5 2.0 %collective-permute-start.8 = (f32[8,64,256]{2,1,0:T(8,128)S(1)}, f32[8,64,256]{2,1,0:T(8,128)S(1)}, u32[]{:S(2)}, u32[]{:S(2)}) collective-permute-start(f32[8,64,256]{2,1,0:T(8,128)S(1)} %shard_map.68), channel_id=1, source_target_pairs={{0,1},{1,0},{2,3},{3,2},{4,5},{5,4},{6,7},{7,6},{8,9},{9,8},{10,11... | collective-permute-start | bytes 1572872 | tf_op jit(solution)/shard_map/ppermute | solution.py:410

commit v14 on v13

--- a/solution.py
+++ b/solution.py
@@ -344,6 +344,16 @@
         copy.wait()
 
 
+def join_kernel(mine_ref, other_ref, out_ref, sems):
+    core = lax.axis_index("mom")
+    mine = pltpu.make_async_copy(mine_ref, out_ref.at[:, core], sems.at[0])
+    other = pltpu.make_async_copy(other_ref, out_ref.at[:, 1 - core], sems.at[1])
+    mine.start()
+    other.start()
+    mine.wait()
+    other.wait()
+
+
 def prepare_kernel(planes, onsite_ref, hop_ref, sigma_ref, own_ref, other_ref):
     width = hop_ref.shape[-1]
     y, _ = place_of()
@@ -384,7 +394,6 @@
     axes = ("slab", "energy", "mom")
     slab = lax.axis_index("slab")
     z = lax.axis_index("energy")
-    k = lax.axis_index("mom")
     y, x = slab // 2, slab % 2
 
     def device(yy, xx, zz, kk):
@@ -467,8 +476,14 @@
         compiler_params=pltpu.CompilerParams(vmem_limit_bytes=VMEM_BYTES),
     )(weight, parts)
     other = send(mixed, siblings)
-    mine = jnp.arange(2)[:, None, None] == k
-    result = jnp.where(mine, mixed[:, None], other[:, None])
+    result = pl.pallas_call(
+        join_kernel,
+        out_shape=jax.ShapeDtypeStruct((total, 2, rows, width), jnp.float32),
+        in_specs=[anywhere] * 2,
+        out_specs=anywhere,
+        scratch_shapes=[pltpu.SemaphoreType.DMA((2,))],
+        compiler_params=pltpu.CompilerParams(vmem_limit_bytes=VMEM_BYTES),
+    )(mixed, other)
     return result[:, None]
 
 

time: 82.1 us -> 82 us (level)
  other arithmetic: 1.32 us -> 0.16 us
  Pallas kernels: 13.2 us -> 14.2 us
    select_n x1 -> x0, other arithmetic: 1.16 us -> none  [owner_body(): result = jnp.where(mine, mixed[:, None], other[:, None])]
    pallas_call x0 -> x1, Pallas kernels: none -> 0.98 us  [owner_body(): pl.pallas_call(join_kernel, out_shape=jax.ShapeDtypeStruct((total, 2, row...]
where the time goes in v14:
time: 82 us; the launch traced here: 81.5 us
  waiting for transfers between devices  40.3 us (49%)
  starting transfers between devices  22.4 us (27%)
  Pallas kernels  14.2 us (17%)
  local copies, waits for them, and re-layouts  4.15 us (5%)
    all_to_all x1, waiting for transfers between devices, owner_body(): lax.all_to_all(half.reshape(slots, rows, width), ('slab', 'energy'), 0, 0...  27.8 us
    ppermute x9, starting transfers between devices, send(): return lax.ppermute(value, axes, pairs)  16.3 us
    ppermute x9, waiting for transfers between devices, send(): return lax.ppermute(value, axes, pairs)  12.5 us
    pallas_call x1, Pallas kernels, call(): pl.pallas_call(kernel, out_shape=[jax.ShapeDtypeStruct(shape, jnp.float32...  10.8 us
    all_to_all x1, starting transfers between devices, owner_body(): lax.all_to_all(half.reshape(slots, rows, width), ('slab', 'energy'), 0, 0...  6.13 us
    unnamed x10, local copies, waits for them, and re-layouts  2.95 us
  transfers between devices with their start and end apart: 10, of which 6 were waited for; matrix products, arithmetic and copies ran while one was open for 2% of the time, Pallas kernels for 1%

profile of v14, /device:TPU:0, one launch (start us, length us, event | category | flops | bytes accessed | tf_op | source)
XLA Modules:
  0.0 81.5 jit_solution(8090600636149425957)
XLA Ops:
  0.0 1.3 %collective-permute-start.4 = (f32[2,256,256]{2,1,0:T(8,128)}, f32[2,256,256]{2,1,0:T(8,128)S(1)}, u32[]{:S(2)}, u32[]{:S(2)}) collective-permute-start(f32[2,256,256]{2,1,0:T(8,128)} %bitcast.19), channel_id=1, source_target_pairs={{8,0},{10,2},{12,4},{14,6},{17,25},{19,27},{21,29},{23,31},{24,16}... | collective-permute-start | bytes 1572872 | tf_op jit(solution)/shard_map/ppermute | solution.py:419
  1.3 1.3 %collective-permute-start.5 = (f32[2,256,256]{2,1,0:T(8,128)}, f32[2,256,256]{2,1,0:T(8,128)S(1)}, u32[]{:S(2)}, u32[]{:S(2)}) collective-permute-start(f32[2,256,256]{2,1,0:T(8,128)} %bitcast.20), channel_id=1, source_target_pairs={{9,25},{11,27},{13,29},{15,31},{16,0},{18,2},{20,4},{22,6},{25,9},... | collective-permute-start | bytes 1572872 | tf_op jit(solution)/shard_map/ppermute | solution.py:419
  2.6 1.1 %dynamic-slice_bitcast_fusion = (f32[2,128,256]{2,1,0:T(8,128)S(1)}, f32[2,128,256]{2,1,0:T(8,128)S(1)}) fusion(f32[1,1,2,256,256]{4,3,2,1,0:T(8,128)} %param.8, s32[]{:T(128)S(6)} %select_n.17, s32[]{:T(128)S(6)} %select_n.16), kind=kLoop, calls=%fused_computation | loop fusion | bytes 1048584 | tf_op jit(solution)/shard_map/dynamic_slice | solution.py:434
  3.7 1.3 %collective-permute-start.3 = (f32[2,128,256]{2,1,0:T(8,128)S(1)}, f32[2,128,256]{2,1,0:T(8,128)S(1)}, u32[]{:S(2)}, u32[]{:S(2)}) collective-permute-start(f32[2,128,256]{2,1,0:T(8,128)S(1)} %get-tuple-element.20.c_part), channel_id=1, source_target_pairs={{8,16},{10,18},{12,20},{14,22},{17,9},{19,11},{21,13},{23,15},{24,... | collective-permute-start | bytes 786440 | tf_op jit(solution)/shard_map/ppermute | solution.py:419
  5.0 0.0 copy-start
  5.0 1.2 %copy-done = f32[2,1,2,256,256]{4,3,2,1,0:T(8,128)S(1)} copy-done((f32[2,1,2,256,256]{4,3,2,1,0:T(8,128)S(1)}, f32[2,1,2,256,256]{4,3,2,1,0:T(8,128)}, u32[]{:S(2)}) %copy-start) | copy-done | bytes 1048600
  6.2 1.0 %copy-done.1 = f32[1,1,2,256,256]{4,3,2,1,0:T(8,128)S(1)} copy-done((f32[1,1,2,256,256]{4,3,2,1,0:T(8,128)S(1)}, f32[1,1,2,256,256]{4,3,2,1,0:T(8,128)}, u32[]{:S(2)}) %copy-start.1) | copy-done | bytes 524312
  7.3 0.7 copy-done.2
  7.9 0.2 shard_map.64
  8.1 1.3 %collective-permute-start = (f32[2,256,256]{2,1,0:T(8,128)S(1)}, f32[2,256,256]{2,1,0:T(8,128)S(1)}, u32[]{:S(2)}, u32[]{:S(2)}) collective-permute-start(f32[2,256,256]{2,1,0:T(8,128)S(1)} %get-tuple-element.12.b_own), channel_id=1, source_target_pairs={{1,9},{3,11},{5,13},{7,15},{8,0},{10,2},{12,4},{14,6},{17,25},{19,... | collective-permute-start | bytes 1572872 | tf_op jit(solution)/shard_map/ppermute | solution.py:419
  9.4 4.9 %collective-permute-start.1 = (f32[2,256,256]{2,1,0:T(8,128)S(1)}, f32[2,256,256]{2,1,0:T(8,128)S(1)}, u32[]{:S(2)}, u32[]{:S(2)}) collective-permute-start(f32[2,256,256]{2,1,0:T(8,128)S(1)} %get-tuple-element.13), channel_id=1, source_target_pairs={{0,16},{2,18},{4,20},{6,22},{9,25},{11,27},{13,29},{15,31},{16,0},... | collective-permute-start | bytes 1572872 | tf_op jit(solution)/shard_map/ppermute | solution.py:419
  14.3 2.2 %collective-permute-done.3.far_mine = f32[2,128,256]{2,1,0:T(8,128)S(1)} collective-permute-done((f32[2,128,256]{2,1,0:T(8,128)S(1)}, f32[2,128,256]{2,1,0:T(8,128)S(1)}, u32[]{:S(2)}, u32[]{:S(2)}) %collective-permute-start.3) | collective-permute-done | bytes 262176 | tf_op jit(solution)/shard_map/ppermute | solution.py:419
  16.6 1.3 %collective-permute-start.2 = (f32[2,256,256]{2,1,0:T(8,128)S(1)}, f32[2,256,256]{2,1,0:T(8,128)S(1)}, u32[]{:S(2)}, u32[]{:S(2)}) collective-permute-start(f32[2,256,256]{2,1,0:T(8,128)S(1)} %get-tuple-element.13), channel_id=1, source_target_pairs={{1,25},{3,27},{5,29},{7,31},{8,16},{10,18},{12,20},{14,22},{17,9},... | collective-permute-start | bytes 1572872 | tf_op jit(solution)/shard_map/ppermute | solution.py:419
  17.9 3.5 %collective-permute-start.6 = (f32[2,128,256]{2,1,0:T(8,128)S(1)}, f32[2,128,256]{2,1,0:T(8,128)S(1)}, u32[]{:S(2)}, u32[]{:S(2)}) collective-permute-start(f32[2,128,256]{2,1,0:T(8,128)S(1)} %collective-permute-done.3.far_mine), channel_id=1, source_target_pairs={{0,2},{2,0},{4,6},{6,4},{9,11},{11,9},{13,15},{15,13},{16,18},{18,... | collective-permute-start | bytes 786440 | tf_op jit(solution)/shard_map/ppermute | solution.py:419
  21.4 4.7 %collective-permute-done.6.far_theirs = f32[2,128,256]{2,1,0:T(8,128)S(1)} collective-permute-done((f32[2,128,256]{2,1,0:T(8,128)S(1)}, f32[2,128,256]{2,1,0:T(8,128)S(1)}, u32[]{:S(2)}, u32[]{:S(2)}) %collective-permute-start.6) | collective-permute-done | bytes 262176 | tf_op jit(solution)/shard_map/ppermute | solution.py:419
  26.1 1.0 %shard_map.65.c_forms = bf16[3,2,6,256,256]{4,3,2,1,0:T(8,128)(2,1)S(1)} custom-call(f32[2,128,256]{2,1,0:T(8,128)S(1)} %get-tuple-element.20.c_part, f32[2,128,256]{2,1,0:T(8,128)S(1)} %get-tuple-element.19.c_rest, f32[2,256,256]{2,1,0:T(8,128)S(1)} %collective-permute-done.4.c_x, f32[2,256,256]{2,1,0:T(8,128)S(1)} %collective-permute-done.5.c_y, ...), custom_call_target="tpu_custom_call" | custom-call | tf_op jit(solution)/shard_map/pallas_call | solution.py:444
  27.1 1.4 %collective-permute-done.2.b_far = f32[2,256,256]{2,1,0:T(8,128)S(1)} collective-permute-done((f32[2,256,256]{2,1,0:T(8,128)S(1)}, f32[2,256,256]{2,1,0:T(8,128)S(1)}, u32[]{:S(2)}, u32[]{:S(2)}) %collective-permute-start.2) | collective-permute-done | bytes 524320 | tf_op jit(solution)/shard_map/ppermute | solution.py:419
  28.5 10.8 %shard_map.66 = (f32[4,256,256]{2,1,0:T(8,128)S(1)}, f32[4,256,256]{2,1,0:T(8,128)S(1)}) custom-call(f32[2,256,256]{2,1,0:T(8,128)S(1)} %get-tuple-element.12.b_own, f32[2,256,256]{2,1,0:T(8,128)S(1)} %collective-permute-done.b_x, f32[2,256,256]{2,1,0:T(8,128)S(1)} %collective-permute-done.1.b_y, f32[2,256,256]{2,1,0:T(8,128)S(1)} %collective-permute-done.2.b_far, ...), custom_call_target="tpu_custom_call" | custom-call | flops 7851737088 | bytes 3670016 | tf_op jit(solution)/shard_map/pallas_call | solution.py:374
  39.4 0.0 copy-start.3
  39.4 0.0 copy-start.4
  39.4 1.4 %collective-permute-start.7 = (f32[4,256,256]{2,1,0:T(8,128)S(1)}, f32[4,256,256]{2,1,0:T(8,128)S(1)}, u32[]{:S(2)}, u32[]{:S(2)}) collective-permute-start(f32[4,256,256]{2,1,0:T(8,128)S(1)} %get-tuple-element.18), channel_id=1, source_target_pairs={{0,1},{2,3},{4,5},{6,7},{9,8},{11,10},{13,12},{15,14},{16,17},{18,... | collective-permute-start | bytes 3145736 | tf_op jit(solution)/shard_map/ppermute | solution.py:419
  40.7 2.2 %collective-permute-done.7.got_ref = f32[4,256,256]{2,1,0:T(8,128)S(1)} collective-permute-done((f32[4,256,256]{2,1,0:T(8,128)S(1)}, f32[4,256,256]{2,1,0:T(8,128)S(1)}, u32[]{:S(2)}, u32[]{:S(2)}) %collective-permute-start.7) | collective-permute-done | bytes 1048608 | tf_op jit(solution)/shard_map/ppermute | solution.py:419
  43.0 1.0 %shard_map.67 = f32[4,256,256]{2,1,0:T(8,128)} custom-call(f32[4,256,256]{2,1,0:T(8,128)S(1)} %get-tuple-element.17.keep_ref, f32[4,256,256]{2,1,0:T(8,128)S(1)} %collective-permute-done.7.got_ref), custom_call_target="tpu_custom_call" | custom-call | tf_op jit(solution)/shard_map/pallas_call | solution.py:455
  43.9 6.1 %all-to-all-start = ((f32[16,64,256]{2,1,0:T(8,128)}), f32[16,64,256]{2,1,0:T(8,128)S(1)}, u32[]{:S(2)}, u32[]{:S(2)}) async-start(f32[16,64,256]{2,1,0:T(8,128)} %bitcast.8), calls=%async_computation | async-start | bytes 2097152 | tf_op jit(solution)/shard_map/all_to_all | solution.py:466
  50.1 0.1 iota_add_fusion
  50.2 0.1 add_reduce_fusion
  50.3 27.8 %all-to-all-done.parts_ref = f32[16,64,256]{2,1,0:T(8,128)S(1)} async-done(((f32[16,64,256]{2,1,0:T(8,128)}), f32[16,64,256]{2,1,0:T(8,128)S(1)}, u32[]{:S(2)}, u32[]{:S(2)}) %all-to-all-start) | async-done | bytes 1048608 | tf_op jit(solution)/shard_map/all_to_all | solution.py:466
  78.1 0.1 broadcast_in_dim.4.weight
  78.2 0.3 shard_map.68.mine_ref
  78.5 0.1 collective-permute-start.8
  78.6 1.9 %collective-permute-done.8.other_ref = f32[8,64,256]{2,1,0:T(8,128)S(1)} collective-permute-done((f32[8,64,256]{2,1,0:T(8,128)S(1)}, f32[8,64,256]{2,1,0:T(8,128)S(1)}, u32[]{:S(2)}, u32[]{:S(2)}) %collective-permute-start.8) | collective-permute-done | bytes 524320 | tf_op jit(solution)/shard_map/ppermute | solution.py:419
  80.5 1.0 %shard_map.69 = f32[8,2,64,256]{3,2,1,0:T(8,128)} custom-call(f32[8,64,256]{2,1,0:T(8,128)S(1)} %shard_map.68.mine_ref, f32[8,64,256]{2,1,0:T(8,128)S(1)} %collective-permute-done.8.other_ref), custom_call_target="tpu_custom_call" | custom-call | tf_op jit(solution)/shard_map/pallas_call | solution.py:479
  (10 shorter events, 0.0 us)
Async XLA Ops:
  0.0 17.8 %collective-permute-start.4 = (f32[2,256,256]{2,1,0:T(8,128)}, f32[2,256,256]{2,1,0:T(8,128)S(1)}, u32[]{:S(2)}, u32[]{:S(2)}) collective-permute-start(f32[2,256,256]{2,1,0:T(8,128)} %bitcast.19), channel_id=1, source_target_pairs={{8,0},{10,2},{12,4},{14,6},{17,25},{19,27},{21,29},{23,31},{24,16}... | collective-permute-start | bytes 1572872 | tf_op jit(solution)/shard_map/ppermute | solution.py:419
  1.3 16.6 %collective-permute-start.5 = (f32[2,256,256]{2,1,0:T(8,128)}, f32[2,256,256]{2,1,0:T(8,128)S(1)}, u32[]{:S(2)}, u32[]{:S(2)}) collective-permute-start(f32[2,256,256]{2,1,0:T(8,128)} %bitcast.20), channel_id=1, source_target_pairs={{9,25},{11,27},{13,29},{15,31},{16,0},{18,2},{20,4},{22,6},{25,9},... | collective-permute-start | bytes 1572872 | tf_op jit(solution)/shard_map/ppermute | solution.py:419
  3.7 12.9 %collective-permute-start.3 = (f32[2,128,256]{2,1,0:T(8,128)S(1)}, f32[2,128,256]{2,1,0:T(8,128)S(1)}, u32[]{:S(2)}, u32[]{:S(2)}) collective-permute-start(f32[2,128,256]{2,1,0:T(8,128)S(1)} %get-tuple-element.20.c_part), channel_id=1, source_target_pairs={{8,16},{10,18},{12,20},{14,22},{17,9},{19,11},{21,13},{23,15},{24,... | collective-permute-start | bytes 786440 | tf_op jit(solution)/shard_map/ppermute | solution.py:419
  5.0 1.2 %copy-start = (f32[2,1,2,256,256]{4,3,2,1,0:T(8,128)S(1)}, f32[2,1,2,256,256]{4,3,2,1,0:T(8,128)}, u32[]{:S(2)}) copy-start(f32[2,1,2,256,256]{4,3,2,1,0:T(8,128)} %param.9) | copy-start | bytes 3145732
  6.2 1.0 %copy-start.1 = (f32[1,1,2,256,256]{4,3,2,1,0:T(8,128)S(1)}, f32[1,1,2,256,256]{4,3,2,1,0:T(8,128)}, u32[]{:S(2)}) copy-start(f32[1,1,2,256,256]{4,3,2,1,0:T(8,128)} %param.7) | copy-start | bytes 1572868
  7.3 0.7 copy-start.2
  8.1 19.0 %collective-permute-start = (f32[2,256,256]{2,1,0:T(8,128)S(1)}, f32[2,256,256]{2,1,0:T(8,128)S(1)}, u32[]{:S(2)}, u32[]{:S(2)}) collective-permute-start(f32[2,256,256]{2,1,0:T(8,128)S(1)} %get-tuple-element.12.b_own), channel_id=1, source_target_pairs={{1,9},{3,11},{5,13},{7,15},{8,0},{10,2},{12,4},{14,6},{17,25},{19,... | collective-permute-start | bytes 1572872 | tf_op jit(solution)/shard_map/ppermute | solution.py:419
  9.4 17.7 %collective-permute-start.1 = (f32[2,256,256]{2,1,0:T(8,128)S(1)}, f32[2,256,256]{2,1,0:T(8,128)S(1)}, u32[]{:S(2)}, u32[]{:S(2)}) collective-permute-start(f32[2,256,256]{2,1,0:T(8,128)S(1)} %get-tuple-element.13), channel_id=1, source_target_pairs={{0,16},{2,18},{4,20},{6,22},{9,25},{11,27},{13,29},{15,31},{16,0},... | collective-permute-start | bytes 1572872 | tf_op jit(solution)/shard_map/ppermute | solution.py:419
  16.6 12.0 %collective-permute-start.2 = (f32[2,256,256]{2,1,0:T(8,128)S(1)}, f32[2,256,256]{2,1,0:T(8,128)S(1)}, u32[]{:S(2)}, u32[]{:S(2)}) collective-permute-start(f32[2,256,256]{2,1,0:T(8,128)S(1)} %get-tuple-element.13), channel_id=1, source_target_pairs={{1,25},{3,27},{5,29},{7,31},{8,16},{10,18},{12,20},{14,22},{17,9},... | collective-permute-start | bytes 1572872 | tf_op jit(solution)/shard_map/ppermute | solution.py:419
  17.9 8.3 %collective-permute-start.6 = (f32[2,128,256]{2,1,0:T(8,128)S(1)}, f32[2,128,256]{2,1,0:T(8,128)S(1)}, u32[]{:S(2)}, u32[]{:S(2)}) collective-permute-start(f32[2,128,256]{2,1,0:T(8,128)S(1)} %collective-permute-done.3.far_mine), channel_id=1, source_target_pairs={{0,2},{2,0},{4,6},{6,4},{9,11},{11,9},{13,15},{15,13},{16,18},{18,... | collective-permute-start | bytes 786440 | tf_op jit(solution)/shard_map/ppermute | solution.py:419
  39.4 10.7 %copy-start.3 = (f32[2,4]{1,0:T(2,128)S(1)}, f32[2,4]{1,0:T(2,128)}, u32[]{:S(2)}) copy-start(f32[2,4]{1,0:T(2,128)} %param.11) | copy-start | bytes 100
  39.4 10.7 %copy-start.4 = (s32[4]{0:T(128)S(1)}, s32[4]{0:T(128)}, u32[]{:S(2)}) copy-start(s32[4]{0:T(128)} %param.10) | copy-start | bytes 52
  39.4 3.6 %collective-permute-start.7 = (f32[4,256,256]{2,1,0:T(8,128)S(1)}, f32[4,256,256]{2,1,0:T(8,128)S(1)}, u32[]{:S(2)}, u32[]{:S(2)}) collective-permute-start(f32[4,256,256]{2,1,0:T(8,128)S(1)} %get-tuple-element.18), channel_id=1, source_target_pairs={{0,1},{2,3},{4,5},{6,7},{9,8},{11,10},{13,12},{15,14},{16,17},{18,... | collective-permute-start | bytes 3145736 | tf_op jit(solution)/shard_map/ppermute | solution.py:419
  43.9 34.1 %all-to-all-start = ((f32[16,64,256]{2,1,0:T(8,128)}), f32[16,64,256]{2,1,0:T(8,128)S(1)}, u32[]{:S(2)}, u32[]{:S(2)}) async-start(f32[16,64,256]{2,1,0:T(8,128)} %bitcast.8), calls=%async_computation | async-start | bytes 2097152 | tf_op jit(solution)/shard_map/all_to_all | solution.py:466
  78.5 2.0 %collective-permute-start.8 = (f32[8,64,256]{2,1,0:T(8,128)S(1)}, f32[8,64,256]{2,1,0:T(8,128)S(1)}, u32[]{:S(2)}, u32[]{:S(2)}) collective-permute-start(f32[8,64,256]{2,1,0:T(8,128)S(1)} %shard_map.68.mine_ref), channel_id=1, source_target_pairs={{0,1},{1,0},{2,3},{3,2},{4,5},{5,4},{6,7},{7,6},{8,9},{9,8},{10,11... | collective-permute-start | bytes 1572872 | tf_op jit(solution)/shard_map/ppermute | solution.py:419

commit v15 on v14

--- a/solution.py
+++ b/solution.py
@@ -272,7 +272,7 @@
                     out_ref[slab - 1, side, 2 * plane + term] = terms[term]
 
 
-def chain_kernel(b_own, b_x, b_y, b_far, c_forms, keep_ref, give_ref):
+def chain_kernel(b_own, b_y, b_x, b_far, c_forms, keep_ref, give_ref):
     y, x = place_of()
     greens, forms = [], []
     for slab in range(4):
@@ -438,8 +438,8 @@
     far_mine, c_x, c_y = lax.optimization_barrier((far_mine, c_x, c_y))
     far_theirs = send(far_mine, beside)
     b_far = send(b_other, to_far)
+    b_y = send(b_other, to_y)
     b_x = send(b_own, to_x)
-    b_y = send(b_other, to_y)
 
     c_forms = pl.pallas_call(
         coupling_kernel,
@@ -450,7 +450,7 @@
         compiler_params=pltpu.CompilerParams(vmem_limit_bytes=VMEM_BYTES),
     )(c_part, c_rest, c_x, c_y, far_mine, far_theirs)
     shape = (4, width, width)
-    keep, give = call(chain_kernel, (b_own, b_x, b_y, b_far, c_forms), shape, 2, 26)
+    keep, give = call(chain_kernel, (b_own, b_y, b_x, b_far, c_forms), shape, 2, 26)
     anywhere = pl.BlockSpec(memory_space=pl.ANY)
     half = pl.pallas_call(
         pick_kernel,

time: 82 us -> 84 us (1.024)
  starting transfers between devices: 22.4 us -> 23.8 us
    all_to_all x1, starting transfers between devices: 6.13 us -> 7.57 us  [owner_body(): lax.all_to_all(half.reshape(slots, rows, width), ('slab', 'energy'), 0, 0...]
  transfers between devices with their start and end apart: 10 -> 10, of which waited for: 6 -> 6; matrix products, arithmetic and copies ran while one was open for 2% -> 1% of each run, Pallas kernels for 1% -> 1%
where the time goes in v15:
time: 84 us; the launch traced here: 83.5 us
  waiting for transfers between devices  41 us (49%)
  starting transfers between devices  23.8 us (28%)
  Pallas kernels  14.2 us (17%)
  local copies, waits for them, and re-layouts  4.15 us (5%)
    all_to_all x1, waiting for transfers between devices, owner_body(): lax.all_to_all(half.reshape(slots, rows, width), ('slab', 'energy'), 0, 0...  27.8 us
    ppermute x9, starting transfers between devices, send(): return lax.ppermute(value, axes, pairs)  16.3 us
    ppermute x9, waiting for transfers between devices, send(): return lax.ppermute(value, axes, pairs)  13.2 us
    pallas_call x1, Pallas kernels, call(): pl.pallas_call(kernel, out_shape=[jax.ShapeDtypeStruct(shape, jnp.float32...  10.8 us
    all_to_all x1, starting transfers between devices, owner_body(): lax.all_to_all(half.reshape(slots, rows, width), ('slab', 'energy'), 0, 0...  7.57 us
    unnamed x10, local copies, waits for them, and re-layouts  2.95 us
  transfers between devices with their start and end apart: 10, of which 6 were waited for; matrix products, arithmetic and copies ran while one was open for 1% of the time, Pallas kernels for 1%

profile of v15, /device:TPU:0, one launch (start us, length us, event | category | flops | bytes accessed | tf_op | source)
XLA Modules:
  0.0 83.5 jit_solution(14903694969493928243)
XLA Ops:
  0.0 1.3 %collective-permute-start.4 = (f32[2,256,256]{2,1,0:T(8,128)}, f32[2,256,256]{2,1,0:T(8,128)S(1)}, u32[]{:S(2)}, u32[]{:S(2)}) collective-permute-start(f32[2,256,256]{2,1,0:T(8,128)} %bitcast.19), channel_id=1, source_target_pairs={{8,0},{10,2},{12,4},{14,6},{17,25},{19,27},{21,29},{23,31},{24,16}... | collective-permute-start | bytes 1572872 | tf_op jit(solution)/shard_map/ppermute | solution.py:419
  1.3 1.3 %collective-permute-start.5 = (f32[2,256,256]{2,1,0:T(8,128)}, f32[2,256,256]{2,1,0:T(8,128)S(1)}, u32[]{:S(2)}, u32[]{:S(2)}) collective-permute-start(f32[2,256,256]{2,1,0:T(8,128)} %bitcast.20), channel_id=1, source_target_pairs={{9,25},{11,27},{13,29},{15,31},{16,0},{18,2},{20,4},{22,6},{25,9},... | collective-permute-start | bytes 1572872 | tf_op jit(solution)/shard_map/ppermute | solution.py:419
  2.6 1.1 %dynamic-slice_bitcast_fusion = (f32[2,128,256]{2,1,0:T(8,128)S(1)}, f32[2,128,256]{2,1,0:T(8,128)S(1)}) fusion(f32[1,1,2,256,256]{4,3,2,1,0:T(8,128)} %param.8, s32[]{:T(128)S(6)} %select_n.17, s32[]{:T(128)S(6)} %select_n.16), kind=kLoop, calls=%fused_computation | loop fusion | bytes 1048584 | tf_op jit(solution)/shard_map/dynamic_slice | solution.py:434
  3.7 1.3 %collective-permute-start.3 = (f32[2,128,256]{2,1,0:T(8,128)S(1)}, f32[2,128,256]{2,1,0:T(8,128)S(1)}, u32[]{:S(2)}, u32[]{:S(2)}) collective-permute-start(f32[2,128,256]{2,1,0:T(8,128)S(1)} %get-tuple-element.20.c_part), channel_id=1, source_target_pairs={{8,16},{10,18},{12,20},{14,22},{17,9},{19,11},{21,13},{23,15},{24,... | collective-permute-start | bytes 786440 | tf_op jit(solution)/shard_map/ppermute | solution.py:419
  5.0 0.0 copy-start
  5.0 1.2 %copy-done = f32[2,1,2,256,256]{4,3,2,1,0:T(8,128)S(1)} copy-done((f32[2,1,2,256,256]{4,3,2,1,0:T(8,128)S(1)}, f32[2,1,2,256,256]{4,3,2,1,0:T(8,128)}, u32[]{:S(2)}) %copy-start) | copy-done | bytes 1048600
  6.2 1.0 %copy-done.1 = f32[1,1,2,256,256]{4,3,2,1,0:T(8,128)S(1)} copy-done((f32[1,1,2,256,256]{4,3,2,1,0:T(8,128)S(1)}, f32[1,1,2,256,256]{4,3,2,1,0:T(8,128)}, u32[]{:S(2)}) %copy-start.1) | copy-done | bytes 524312
  7.3 0.7 copy-done.2
  7.9 0.2 shard_map.64
  8.1 4.9 %collective-permute-start = (f32[2,256,256]{2,1,0:T(8,128)S(1)}, f32[2,256,256]{2,1,0:T(8,128)S(1)}, u32[]{:S(2)}, u32[]{:S(2)}) collective-permute-start(f32[2,256,256]{2,1,0:T(8,128)S(1)} %get-tuple-element.13), channel_id=1, source_target_pairs={{0,16},{2,18},{4,20},{6,22},{9,25},{11,27},{13,29},{15,31},{16,0},... | collective-permute-start | bytes 1572872 | tf_op jit(solution)/shard_map/ppermute | solution.py:419
  13.0 1.3 %collective-permute-start.1 = (f32[2,256,256]{2,1,0:T(8,128)S(1)}, f32[2,256,256]{2,1,0:T(8,128)S(1)}, u32[]{:S(2)}, u32[]{:S(2)}) collective-permute-start(f32[2,256,256]{2,1,0:T(8,128)S(1)} %get-tuple-element.12.b_own), channel_id=1, source_target_pairs={{1,9},{3,11},{5,13},{7,15},{8,0},{10,2},{12,4},{14,6},{17,25},{19,... | collective-permute-start | bytes 1572872 | tf_op jit(solution)/shard_map/ppermute | solution.py:419
  14.3 2.3 %collective-permute-done.3.far_mine = f32[2,128,256]{2,1,0:T(8,128)S(1)} collective-permute-done((f32[2,128,256]{2,1,0:T(8,128)S(1)}, f32[2,128,256]{2,1,0:T(8,128)S(1)}, u32[]{:S(2)}, u32[]{:S(2)}) %collective-permute-start.3) | collective-permute-done | bytes 262176 | tf_op jit(solution)/shard_map/ppermute | solution.py:419
  16.6 1.3 %collective-permute-start.2 = (f32[2,256,256]{2,1,0:T(8,128)S(1)}, f32[2,256,256]{2,1,0:T(8,128)S(1)}, u32[]{:S(2)}, u32[]{:S(2)}) collective-permute-start(f32[2,256,256]{2,1,0:T(8,128)S(1)} %get-tuple-element.13), channel_id=1, source_target_pairs={{1,25},{3,27},{5,29},{7,31},{8,16},{10,18},{12,20},{14,22},{17,9},... | collective-permute-start | bytes 1572872 | tf_op jit(solution)/shard_map/ppermute | solution.py:419
  17.9 3.5 %collective-permute-start.6 = (f32[2,128,256]{2,1,0:T(8,128)S(1)}, f32[2,128,256]{2,1,0:T(8,128)S(1)}, u32[]{:S(2)}, u32[]{:S(2)}) collective-permute-start(f32[2,128,256]{2,1,0:T(8,128)S(1)} %collective-permute-done.3.far_mine), channel_id=1, source_target_pairs={{0,2},{2,0},{4,6},{6,4},{9,11},{11,9},{13,15},{15,13},{16,18},{18,... | collective-permute-start | bytes 786440 | tf_op jit(solution)/shard_map/ppermute | solution.py:419
  21.4 4.8 %collective-permute-done.6.far_theirs = f32[2,128,256]{2,1,0:T(8,128)S(1)} collective-permute-done((f32[2,128,256]{2,1,0:T(8,128)S(1)}, f32[2,128,256]{2,1,0:T(8,128)S(1)}, u32[]{:S(2)}, u32[]{:S(2)}) %collective-permute-start.6) | collective-permute-done | bytes 262176 | tf_op jit(solution)/shard_map/ppermute | solution.py:419
  26.2 1.0 %shard_map.65.c_forms = bf16[3,2,6,256,256]{4,3,2,1,0:T(8,128)(2,1)S(1)} custom-call(f32[2,128,256]{2,1,0:T(8,128)S(1)} %get-tuple-element.20.c_part, f32[2,128,256]{2,1,0:T(8,128)S(1)} %get-tuple-element.19.c_rest, f32[2,256,256]{2,1,0:T(8,128)S(1)} %collective-permute-done.4.c_x, f32[2,256,256]{2,1,0:T(8,128)S(1)} %collective-permute-done.5.c_y, ...), custom_call_target="tpu_custom_call" | custom-call | tf_op jit(solution)/shard_map/pallas_call | solution.py:444
  27.1 2.0 %collective-permute-done.2.b_far = f32[2,256,256]{2,1,0:T(8,128)S(1)} collective-permute-done((f32[2,256,256]{2,1,0:T(8,128)S(1)}, f32[2,256,256]{2,1,0:T(8,128)S(1)}, u32[]{:S(2)}, u32[]{:S(2)}) %collective-permute-start.2) | collective-permute-done | bytes 524320 | tf_op jit(solution)/shard_map/ppermute | solution.py:419
  29.2 10.8 %shard_map.66 = (f32[4,256,256]{2,1,0:T(8,128)S(1)}, f32[4,256,256]{2,1,0:T(8,128)S(1)}) custom-call(f32[2,256,256]{2,1,0:T(8,128)S(1)} %get-tuple-element.12.b_own, f32[2,256,256]{2,1,0:T(8,128)S(1)} %collective-permute-done.b_y, f32[2,256,256]{2,1,0:T(8,128)S(1)} %collective-permute-done.1.b_x, f32[2,256,256]{2,1,0:T(8,128)S(1)} %collective-permute-done.2.b_far, ...), custom_call_target="tpu_custom_call" | custom-call | flops 7851737088 | bytes 3670016 | tf_op jit(solution)/shard_map/pallas_call | solution.py:374
  40.0 0.0 copy-start.3
  40.0 0.0 copy-start.4
  40.0 1.4 %collective-permute-start.7 = (f32[4,256,256]{2,1,0:T(8,128)S(1)}, f32[4,256,256]{2,1,0:T(8,128)S(1)}, u32[]{:S(2)}, u32[]{:S(2)}) collective-permute-start(f32[4,256,256]{2,1,0:T(8,128)S(1)} %get-tuple-element.18), channel_id=1, source_target_pairs={{0,1},{2,3},{4,5},{6,7},{9,8},{11,10},{13,12},{15,14},{16,17},{18,... | collective-permute-start | bytes 3145736 | tf_op jit(solution)/shard_map/ppermute | solution.py:419
  41.4 2.2 %collective-permute-done.7.got_ref = f32[4,256,256]{2,1,0:T(8,128)S(1)} collective-permute-done((f32[4,256,256]{2,1,0:T(8,128)S(1)}, f32[4,256,256]{2,1,0:T(8,128)S(1)}, u32[]{:S(2)}, u32[]{:S(2)}) %collective-permute-start.7) | collective-permute-done | bytes 1048608 | tf_op jit(solution)/shard_map/ppermute | solution.py:419
  43.6 1.0 %shard_map.67 = f32[4,256,256]{2,1,0:T(8,128)} custom-call(f32[4,256,256]{2,1,0:T(8,128)S(1)} %get-tuple-element.17.keep_ref, f32[4,256,256]{2,1,0:T(8,128)S(1)} %collective-permute-done.7.got_ref), custom_call_target="tpu_custom_call" | custom-call | tf_op jit(solution)/shard_map/pallas_call | solution.py:455
  44.6 7.6 %all-to-all-start = ((f32[16,64,256]{2,1,0:T(8,128)}), f32[16,64,256]{2,1,0:T(8,128)S(1)}, u32[]{:S(2)}, u32[]{:S(2)}) async-start(f32[16,64,256]{2,1,0:T(8,128)} %bitcast.8), calls=%async_computation | async-start | bytes 2097152 | tf_op jit(solution)/shard_map/all_to_all | solution.py:466
  52.2 0.1 iota_add_fusion
  52.2 0.1 add_reduce_fusion
  52.3 27.8 %all-to-all-done.parts_ref = f32[16,64,256]{2,1,0:T(8,128)S(1)} async-done(((f32[16,64,256]{2,1,0:T(8,128)}), f32[16,64,256]{2,1,0:T(8,128)S(1)}, u32[]{:S(2)}, u32[]{:S(2)}) %all-to-all-start) | async-done | bytes 1048608 | tf_op jit(solution)/shard_map/all_to_all | solution.py:466
  80.1 0.1 broadcast_in_dim.4.weight
  80.3 0.3 shard_map.68.mine_ref
  80.6 0.1 collective-permute-start.8
  80.7 1.9 %collective-permute-done.8.other_ref = f32[8,64,256]{2,1,0:T(8,128)S(1)} collective-permute-done((f32[8,64,256]{2,1,0:T(8,128)S(1)}, f32[8,64,256]{2,1,0:T(8,128)S(1)}, u32[]{:S(2)}, u32[]{:S(2)}) %collective-permute-start.8) | collective-permute-done | bytes 524320 | tf_op jit(solution)/shard_map/ppermute | solution.py:419
  82.6 1.0 %shard_map.69 = f32[8,2,64,256]{3,2,1,0:T(8,128)} custom-call(f32[8,64,256]{2,1,0:T(8,128)S(1)} %shard_map.68.mine_ref, f32[8,64,256]{2,1,0:T(8,128)S(1)} %collective-permute-done.8.other_ref), custom_call_target="tpu_custom_call" | custom-call | tf_op jit(solution)/shard_map/pallas_call | solution.py:479
  (10 shorter events, 0.0 us)
Async XLA Ops:
  0.0 17.9 %collective-permute-start.4 = (f32[2,256,256]{2,1,0:T(8,128)}, f32[2,256,256]{2,1,0:T(8,128)S(1)}, u32[]{:S(2)}, u32[]{:S(2)}) collective-permute-start(f32[2,256,256]{2,1,0:T(8,128)} %bitcast.19), channel_id=1, source_target_pairs={{8,0},{10,2},{12,4},{14,6},{17,25},{19,27},{21,29},{23,31},{24,16}... | collective-permute-start | bytes 1572872 | tf_op jit(solution)/shard_map/ppermute | solution.py:419
  1.3 16.6 %collective-permute-start.5 = (f32[2,256,256]{2,1,0:T(8,128)}, f32[2,256,256]{2,1,0:T(8,128)S(1)}, u32[]{:S(2)}, u32[]{:S(2)}) collective-permute-start(f32[2,256,256]{2,1,0:T(8,128)} %bitcast.20), channel_id=1, source_target_pairs={{9,25},{11,27},{13,29},{15,31},{16,0},{18,2},{20,4},{22,6},{25,9},... | collective-permute-start | bytes 1572872 | tf_op jit(solution)/shard_map/ppermute | solution.py:419
  3.7 12.9 %collective-permute-start.3 = (f32[2,128,256]{2,1,0:T(8,128)S(1)}, f32[2,128,256]{2,1,0:T(8,128)S(1)}, u32[]{:S(2)}, u32[]{:S(2)}) collective-permute-start(f32[2,128,256]{2,1,0:T(8,128)S(1)} %get-tuple-element.20.c_part), channel_id=1, source_target_pairs={{8,16},{10,18},{12,20},{14,22},{17,9},{19,11},{21,13},{23,15},{24,... | collective-permute-start | bytes 786440 | tf_op jit(solution)/shard_map/ppermute | solution.py:419
  5.0 1.2 %copy-start = (f32[2,1,2,256,256]{4,3,2,1,0:T(8,128)S(1)}, f32[2,1,2,256,256]{4,3,2,1,0:T(8,128)}, u32[]{:S(2)}) copy-start(f32[2,1,2,256,256]{4,3,2,1,0:T(8,128)} %param.9) | copy-start | bytes 3145732
  6.2 1.0 %copy-start.1 = (f32[1,1,2,256,256]{4,3,2,1,0:T(8,128)S(1)}, f32[1,1,2,256,256]{4,3,2,1,0:T(8,128)}, u32[]{:S(2)}) copy-start(f32[1,1,2,256,256]{4,3,2,1,0:T(8,128)} %param.7) | copy-start | bytes 1572868
  7.3 0.7 copy-start.2
  8.1 19.0 %collective-permute-start = (f32[2,256,256]{2,1,0:T(8,128)S(1)}, f32[2,256,256]{2,1,0:T(8,128)S(1)}, u32[]{:S(2)}, u32[]{:S(2)}) collective-permute-start(f32[2,256,256]{2,1,0:T(8,128)S(1)} %get-tuple-element.13), channel_id=1, source_target_pairs={{0,16},{2,18},{4,20},{6,22},{9,25},{11,27},{13,29},{15,31},{16,0},... | collective-permute-start | bytes 1572872 | tf_op jit(solution)/shard_map/ppermute | solution.py:419
  13.0 14.1 %collective-permute-start.1 = (f32[2,256,256]{2,1,0:T(8,128)S(1)}, f32[2,256,256]{2,1,0:T(8,128)S(1)}, u32[]{:S(2)}, u32[]{:S(2)}) collective-permute-start(f32[2,256,256]{2,1,0:T(8,128)S(1)} %get-tuple-element.12.b_own), channel_id=1, source_target_pairs={{1,9},{3,11},{5,13},{7,15},{8,0},{10,2},{12,4},{14,6},{17,25},{19,... | collective-permute-start | bytes 1572872 | tf_op jit(solution)/shard_map/ppermute | solution.py:419
  16.6 12.6 %collective-permute-start.2 = (f32[2,256,256]{2,1,0:T(8,128)S(1)}, f32[2,256,256]{2,1,0:T(8,128)S(1)}, u32[]{:S(2)}, u32[]{:S(2)}) collective-permute-start(f32[2,256,256]{2,1,0:T(8,128)S(1)} %get-tuple-element.13), channel_id=1, source_target_pairs={{1,25},{3,27},{5,29},{7,31},{8,16},{10,18},{12,20},{14,22},{17,9},... | collective-permute-start | bytes 1572872 | tf_op jit(solution)/shard_map/ppermute | solution.py:419
  17.9 8.3 %collective-permute-start.6 = (f32[2,128,256]{2,1,0:T(8,128)S(1)}, f32[2,128,256]{2,1,0:T(8,128)S(1)}, u32[]{:S(2)}, u32[]{:S(2)}) collective-permute-start(f32[2,128,256]{2,1,0:T(8,128)S(1)} %collective-permute-done.3.far_mine), channel_id=1, source_target_pairs={{0,2},{2,0},{4,6},{6,4},{9,11},{11,9},{13,15},{15,13},{16,18},{18,... | collective-permute-start | bytes 786440 | tf_op jit(solution)/shard_map/ppermute | solution.py:419
  40.0 12.2 %copy-start.3 = (f32[2,4]{1,0:T(2,128)S(1)}, f32[2,4]{1,0:T(2,128)}, u32[]{:S(2)}) copy-start(f32[2,4]{1,0:T(2,128)} %param.11) | copy-start | bytes 100
  40.0 12.2 %copy-start.4 = (s32[4]{0:T(128)S(1)}, s32[4]{0:T(128)}, u32[]{:S(2)}) copy-start(s32[4]{0:T(128)} %param.10) | copy-start | bytes 52
  40.0 3.6 %collective-permute-start.7 = (f32[4,256,256]{2,1,0:T(8,128)S(1)}, f32[4,256,256]{2,1,0:T(8,128)S(1)}, u32[]{:S(2)}, u32[]{:S(2)}) collective-permute-start(f32[4,256,256]{2,1,0:T(8,128)S(1)} %get-tuple-element.18), channel_id=1, source_target_pairs={{0,1},{2,3},{4,5},{6,7},{9,8},{11,10},{13,12},{15,14},{16,17},{18,... | collective-permute-start | bytes 3145736 | tf_op jit(solution)/shard_map/ppermute | solution.py:419
  44.6 35.6 %all-to-all-start = ((f32[16,64,256]{2,1,0:T(8,128)}), f32[16,64,256]{2,1,0:T(8,128)S(1)}, u32[]{:S(2)}, u32[]{:S(2)}) async-start(f32[16,64,256]{2,1,0:T(8,128)} %bitcast.8), calls=%async_computation | async-start | bytes 2097152 | tf_op jit(solution)/shard_map/all_to_all | solution.py:466
  80.6 2.0 %collective-permute-start.8 = (f32[8,64,256]{2,1,0:T(8,128)S(1)}, f32[8,64,256]{2,1,0:T(8,128)S(1)}, u32[]{:S(2)}, u32[]{:S(2)}) collective-permute-start(f32[8,64,256]{2,1,0:T(8,128)S(1)} %shard_map.68.mine_ref), channel_id=1, source_target_pairs={{0,1},{1,0},{2,3},{3,2},{4,5},{5,4},{6,7},{7,6},{8,9},{9,8},{10,11... | collective-permute-start | bytes 1572872 | tf_op jit(solution)/shard_map/ppermute | solution.py:419
